TPU v7x, 32 devices: a whole 2x2x4 slice. The times are simulated.
32 devices in a mesh: dp: 2 (over y), seq: 16 (over z, x, core).
Axes of the slice: x: 2, y: 2, z: 4, core: 2. Of those that a mesh axis runs over, the one named last changes fastest.
Arguments:
- block_input: bfloat16 [2, 2048, 2048], P('dp', 'seq'), may hold values from -6 to 6
- attention_gain: bfloat16 [2048], P(('dp', 'seq')), may hold values from 0.5 to 1.5
- query_weight: bfloat16 [2048, 2048], P(('dp', 'seq')), may hold values from -0.125 to 0.125
- keyvalue_weight: bfloat16 [2048, 256], P(('dp', 'seq')), may hold values from -0.125 to 0.125
- output_weight: bfloat16 [2048, 2048], P(('dp', 'seq')), may hold values from -0.5 to 0.5
- feedforward_gain: bfloat16 [2048], P(('dp', 'seq')), may hold values from 0.5 to 1.5
- gate_weight: bfloat16 [2048, 5632], P(('dp', 'seq')), may hold values from -0.125 to 0.125
- up_weight: bfloat16 [2048, 5632], P(('dp', 'seq')), may hold values from -0.125 to 0.125
- down_weight: bfloat16 [2048, 5632], P(('dp', 'seq')), may hold values from -0.078125 to 0.078125
- document_lengths: int32 [2, 32], P('dp'), may hold values from 1 to 1024, 2048 in all within a row
- piece_order: int32 [32], replicated, may hold values from 0 to 31, each once
- output_grad: bfloat16 [2, 2048, 2048], P('dp', 'seq'), may hold values from -6 to 6
- shared_grad: bfloat16 [2, 2048, 256], P('dp', 'seq'), may hold values from -6 to 6
Outputs:
- block_output: bfloat16 [2, 2048, 2048], P('dp', 'seq')
- shared_keyvalue: bfloat16 [2, 2048, 256], P('dp', 'seq')
- input_grad: float32 [2, 2048, 2048], P('dp', 'seq')
- attention_gain_grad: float32 [2048], P(('dp', 'seq'))
- query_weight_grad: float32 [2048, 2048], P(('dp', 'seq'))
- keyvalue_weight_grad: float32 [2048, 256], P(('dp', 'seq'))
- output_weight_grad: float32 [2048, 2048], P(('dp', 'seq'))
- feedforward_gain_grad: float32 [2048], P(('dp', 'seq'))
- gate_weight_grad: float32 [2048, 5632], P(('dp', 'seq'))
- up_weight_grad: float32 [2048, 5632], P(('dp', 'seq'))
- down_weight_grad: float32 [2048, 5632], P(('dp', 'seq'))
Inputs may be any that keep to these rules, and one draw needn't show every extreme that they name: `document_lengths`: each row sums to 2048, and its largest entry is 1024. `piece_order`: a permutation: every piece of the stream appears once.
All inputs are finite; a program needn't handle non-finite values.
Results may differ from a plain program's by a relative error of at most 0.015.
Values may be sent and summed in bfloat16 or wider, within the bound.
No kernel may reach another device: no remote copies, remote signals or barrier semaphores. Data moves between devices by JAX's collectives and lax.ppermute only.
A program may use at most 512 MiB of HBM per device.

v0:
```python
import math

import jax
import jax.numpy as jnp
from jax import lax
from jax.sharding import PartitionSpec as P

HEADS = 16
HEAD_DIM = 128


EPSILON = 1e-05
NEGATIVE = -1e30


def layout(lengths, order, piece_len):
    position = (
        order[:, None] * piece_len + jnp.arange(piece_len, dtype=jnp.int32)[None, :]
    ).reshape(-1)
    finish = jnp.cumsum(lengths)
    starts = finish - lengths
    segment = jnp.sum((finish[None, :] <= position[:, None]).astype(jnp.int32), axis=1)
    begins = jnp.max(jnp.where(starts[None, :] <= position[:, None], starts[None, :], 0), axis=1)
    return (position, segment, position - begins)


def angles(offset):
    half_dim = HEAD_DIM // 2
    frequency = jnp.exp(
        jnp.arange(half_dim, dtype=jnp.float32) * (-2.0 * math.log(10000.0) / HEAD_DIM)
    )
    phases = offset.astype(jnp.float32)[:, None] * frequency[None, :]
    return (jnp.cos(phases), jnp.sin(phases))


def rotate(vectors, cosine, sine_part):
    half_dim = vectors.shape[-1] // 2
    first_half = vectors[..., :half_dim]
    second_half = vectors[..., half_dim:]
    return jnp.concatenate(
        [
            first_half * cosine - second_half * sine_part,
            second_half * cosine + first_half * sine_part,
        ],
        -1,
    )


def unrotate(vectors, cosine, sine_part):
    half_dim = vectors.shape[-1] // 2
    first_half = vectors[..., :half_dim]
    second_half = vectors[..., half_dim:]
    return jnp.concatenate(
        [
            first_half * cosine + second_half * sine_part,
            second_half * cosine - first_half * sine_part,
        ],
        -1,
    )


def contract_last(left, right):
    return lax.dot_general(
        left, right, (((1,), (1,)), ((), ())), preferred_element_type=jnp.float32
    )


def contract_first(left, right):
    return lax.dot_general(
        left, right, (((0,), (0,)), ((), ())), preferred_element_type=jnp.float32
    )


def norm_back(grad_normed, normed, scale_rows):
    return scale_rows * (
        grad_normed - normed * jnp.mean(grad_normed * normed, axis=-1, keepdims=True)
    )


def on_device(
    block_input,
    attention_gain,
    query_weight,
    keyvalue_weight,
    output_weight,
    feedforward_gain,
    gate_weight,
    up_weight,
    down_weight,
    document_lengths,
    piece_order,
    output_grad,
    shared_grad,
):
    tokens = block_input.shape[1]
    query_width = query_weight.shape[1]
    my_index = lax.axis_index("seq")
    position_all, segment_all, offset_all = layout(document_lengths[0], piece_order, tokens // 2)
    position = lax.dynamic_slice_in_dim(position_all, my_index * tokens, tokens)
    segment = lax.dynamic_slice_in_dim(segment_all, my_index * tokens, tokens)
    offset = lax.dynamic_slice_in_dim(offset_all, my_index * tokens, tokens)
    cosine, sine_part = angles(offset)
    score_scale = 1.0 / math.sqrt(HEAD_DIM)
    inputs = block_input[0].astype(jnp.float32)
    scale_one = lax.rsqrt(jnp.mean(inputs * inputs, axis=-1, keepdims=True) + EPSILON)
    normed_one = inputs * scale_one
    gain_piece = lax.all_gather(attention_gain, ("dp", "seq"), axis=0, tiled=True)
    query_piece = lax.all_gather(query_weight, ("dp", "seq"), axis=0, tiled=True)
    keyvalue_piece = lax.all_gather(keyvalue_weight, ("dp", "seq"), axis=0, tiled=True)
    gain_float = gain_piece.astype(jnp.float32)
    columns = (normed_one * gain_float).astype(jnp.bfloat16)
    query_sum = jnp.dot(columns, query_piece, preferred_element_type=jnp.float32)
    keyvalue_sum = jnp.dot(columns, keyvalue_piece, preferred_element_type=jnp.float32)
    gain_full = gain_float
    gain_one = gain_full
    normed_one_low = (normed_one * gain_one).astype(jnp.bfloat16)
    query_rot = rotate(
        query_sum.reshape(tokens, HEADS, HEAD_DIM), cosine[:, None, :], sine_part[:, None, :]
    ).astype(jnp.bfloat16)
    shared_mine = jnp.concatenate(
        [rotate(keyvalue_sum[:, :HEAD_DIM], cosine, sine_part), keyvalue_sum[:, HEAD_DIM:]], -1
    ).astype(jnp.bfloat16)
    gathered = lax.all_gather(shared_mine, "seq", axis=0, tiled=True)
    stream_len = gathered.shape[0]
    key_block_len = min(512, stream_len)
    block_count = stream_len // key_block_len
    key_blocks = gathered.reshape(block_count, key_block_len, 2 * HEAD_DIM)
    place_blocks = position_all.reshape(block_count, key_block_len)
    segment_blocks = segment_all.reshape(block_count, key_block_len)

    def allowed_mask(place_row, segment_row):
        return (
            (segment_row[None, :] == segment[:, None]) & (place_row[None, :] <= position[:, None])
        )[None]

    def forward_step(running, block_item):
        running_max, running_sum, running_out = running
        key_block, place_row, segment_row = block_item
        allowed = allowed_mask(place_row, segment_row)
        scores = (
            jnp.einsum(
                "thd,kd->htk",
                query_rot,
                key_block[:, :HEAD_DIM],
                preferred_element_type=jnp.float32,
            )
            * score_scale
        )
        scores = jnp.where(allowed, scores, NEGATIVE)
        new_max = jnp.maximum(running_max, jnp.max(scores, axis=-1))
        weights = jnp.where(allowed, jnp.exp(scores - new_max[..., None]), 0.0)
        factor = jnp.exp(running_max - new_max)
        running_sum = running_sum * factor + jnp.sum(weights, axis=-1)
        running_out = running_out * factor[..., None] + jnp.einsum(
            "htk,kd->htd", weights, key_block[:, HEAD_DIM:], preferred_element_type=jnp.float32
        )
        return ((new_max, running_sum, running_out), None)

    start_state = (
        jnp.full((HEADS, tokens), NEGATIVE, jnp.float32),
        jnp.zeros((HEADS, tokens), jnp.float32),
        jnp.zeros((HEADS, tokens, HEAD_DIM), jnp.float32),
    )
    (final_max, final_sum, final_out), unused = lax.scan(
        forward_step, start_state, (key_blocks, place_blocks, segment_blocks)
    )
    output_heads = final_out / final_sum[..., None]
    log_total = final_max + jnp.log(final_sum)
    attended_low = output_heads.transpose(1, 0, 2).reshape(tokens, query_width).astype(jnp.bfloat16)
    branch_out = contract_last(
        attended_low, lax.all_gather(output_weight, ("dp", "seq"), axis=0, tiled=True)
    )
    hidden = inputs + branch_out
    scale_two = lax.rsqrt(jnp.mean(hidden * hidden, axis=-1, keepdims=True) + EPSILON)
    normed_two = hidden * scale_two
    gain_piece = lax.all_gather(feedforward_gain, ("dp", "seq"), axis=0, tiled=True)
    gate_piece = lax.all_gather(gate_weight, ("dp", "seq"), axis=0, tiled=True)
    up_piece = lax.all_gather(up_weight, ("dp", "seq"), axis=0, tiled=True)
    gain_float = gain_piece.astype(jnp.float32)
    columns = (normed_two * gain_float).astype(jnp.bfloat16)
    gate_sum = jnp.dot(columns, gate_piece, preferred_element_type=jnp.float32)
    up_sum = jnp.dot(columns, up_piece, preferred_element_type=jnp.float32)
    gain_full = gain_float
    normed_two_low = (normed_two * gain_full).astype(jnp.bfloat16)
    sigmoid_gate = jax.nn.sigmoid(gate_sum)
    silu_gate = gate_sum * sigmoid_gate
    mixed_low = (silu_gate * up_sum).astype(jnp.bfloat16)
    feed_out = contract_last(
        mixed_low, lax.all_gather(down_weight, ("dp", "seq"), axis=0, tiled=True)
    )
    block_output = (hidden + feed_out).astype(jnp.bfloat16)[None]
    grad_low = output_grad[0]
    grad_out = grad_low.astype(jnp.float32)
    grad_mixed = jnp.dot(
        grad_low,
        lax.all_gather(down_weight, ("dp", "seq"), axis=0, tiled=True),
        preferred_element_type=jnp.float32,
    )
    grad_gate = (
        grad_mixed * up_sum * sigmoid_gate * (1.0 + gate_sum * (1.0 - sigmoid_gate))
    ).astype(jnp.bfloat16)
    grad_up = (grad_mixed * silu_gate).astype(jnp.bfloat16)
    weight_rows = lax.all_gather((gate_weight, up_weight), ("dp", "seq"), axis=0, tiled=True)
    grad_two = contract_last(grad_gate, weight_rows[0]) + contract_last(grad_up, weight_rows[1])
    gain_two_grad = jnp.sum(grad_two * normed_two, axis=0)
    grad_hidden = grad_out + norm_back(grad_two * gain_full, normed_two, scale_two)
    grad_hidden_low = grad_hidden.astype(jnp.bfloat16)
    grad_attended = jnp.dot(
        grad_hidden_low,
        lax.all_gather(output_weight, ("dp", "seq"), axis=0, tiled=True),
        preferred_element_type=jnp.float32,
    )
    grad_heads = grad_attended.astype(jnp.bfloat16).reshape(tokens, HEADS, HEAD_DIM)
    delta = jnp.einsum("thd,htd->ht", grad_heads, output_heads, preferred_element_type=jnp.float32)

    def backward_step(query_acc, block_item):
        key_block, place_row, segment_row = block_item
        key_part = key_block[:, :HEAD_DIM]
        value_part = key_block[:, HEAD_DIM:]
        allowed = allowed_mask(place_row, segment_row)
        scores = (
            jnp.einsum("thd,kd->htk", query_rot, key_part, preferred_element_type=jnp.float32)
            * score_scale
        )
        weights = jnp.where(allowed, jnp.exp(scores - log_total[..., None]), 0.0)
        grad_weights = jnp.einsum(
            "thd,kd->htk", grad_heads, value_part, preferred_element_type=jnp.float32
        )
        grad_scores = (weights * (grad_weights - delta[..., None])).astype(jnp.bfloat16)
        query_acc = query_acc + jnp.einsum(
            "htk,kd->thd", grad_scores, key_part, preferred_element_type=jnp.float32
        )
        key_grad = jnp.einsum(
            "htk,thd->kd", grad_scores, query_rot, preferred_element_type=jnp.float32
        )
        value_grad = jnp.einsum(
            "htk,thd->kd", weights, grad_heads, preferred_element_type=jnp.float32
        )
        return (query_acc, (key_grad, value_grad))

    query_acc, (key_grads, value_grads) = lax.scan(
        backward_step,
        jnp.zeros((tokens, HEADS, HEAD_DIM), jnp.float32),
        (key_blocks, place_blocks, segment_blocks),
    )
    key_all = key_grads.reshape(stream_len, HEAD_DIM) * score_scale
    value_all = value_grads.reshape(stream_len, HEAD_DIM)
    key_mine, value_mine = (
        lax.psum_scatter(key_all, "seq", scatter_dimension=0, tiled=True),
        lax.psum_scatter(value_all, "seq", scatter_dimension=0, tiled=True),
    )
    shared_float = shared_grad[0].astype(jnp.float32)
    key_total = key_mine + shared_float[:, :HEAD_DIM]
    value_total = value_mine + shared_float[:, HEAD_DIM:]
    query_grad_low = (
        unrotate(query_acc * score_scale, cosine[:, None, :], sine_part[:, None, :])
        .reshape(tokens, query_width)
        .astype(jnp.bfloat16)
    )
    keyvalue_grad_low = jnp.concatenate(
        [unrotate(key_total, cosine, sine_part), value_total], -1
    ).astype(jnp.bfloat16)
    weight_rows = lax.all_gather((query_weight, keyvalue_weight), ("dp", "seq"), axis=0, tiled=True)
    grad_one = contract_last(query_grad_low, weight_rows[0]) + contract_last(
        keyvalue_grad_low, weight_rows[1]
    )
    gain_one_grad = jnp.sum(grad_one * normed_one, axis=0)
    input_grad = (grad_hidden + norm_back(grad_one * gain_one, normed_one, scale_one))[None]
    query_term = contract_first(normed_one_low, query_grad_low)
    keyvalue_term = contract_first(normed_one_low, keyvalue_grad_low)
    output_term = contract_first(grad_hidden_low, attended_low)
    gate_term = contract_first(normed_two_low, grad_gate)
    up_term = contract_first(normed_two_low, grad_up)
    down_term = contract_first(grad_low, mixed_low)
    (
        query_weight_grad,
        keyvalue_weight_grad,
        output_weight_grad,
        gate_weight_grad,
        up_weight_grad,
        down_weight_grad,
    ) = (
        lax.psum_scatter(query_term, ("dp", "seq"), scatter_dimension=0, tiled=True),
        lax.psum_scatter(keyvalue_term, ("dp", "seq"), scatter_dimension=0, tiled=True),
        lax.psum_scatter(output_term, ("dp", "seq"), scatter_dimension=0, tiled=True),
        lax.psum_scatter(gate_term, ("dp", "seq"), scatter_dimension=0, tiled=True),
        lax.psum_scatter(up_term, ("dp", "seq"), scatter_dimension=0, tiled=True),
        lax.psum_scatter(down_term, ("dp", "seq"), scatter_dimension=0, tiled=True),
    )
    gain_one_mine, gain_two_mine = (
        lax.psum_scatter(gain_one_grad, ("dp", "seq"), scatter_dimension=0, tiled=True),
        lax.psum_scatter(gain_two_grad, ("dp", "seq"), scatter_dimension=0, tiled=True),
    )
    return (
        block_output,
        shared_mine[None],
        input_grad,
        gain_one_mine,
        query_weight_grad,
        keyvalue_weight_grad,
        output_weight_grad,
        gain_two_mine,
        gate_weight_grad,
        up_weight_grad,
        down_weight_grad,
    )


def solution(mesh):
    in_specs = (
        P("dp", "seq", None),
        P(("dp", "seq")),
        P(("dp", "seq"), None),
        P(("dp", "seq"), None),
        P(("dp", "seq"), None),
        P(("dp", "seq")),
        P(("dp", "seq"), None),
        P(("dp", "seq"), None),
        P(("dp", "seq"), None),
        P("dp", None),
        P(),
        P("dp", "seq", None),
        P("dp", "seq", None),
    )
    out_specs = (
        P("dp", "seq", None),
        P("dp", "seq", None),
        P("dp", "seq", None),
        P(("dp", "seq")),
        P(("dp", "seq"), None),
        P(("dp", "seq"), None),
        P(("dp", "seq"), None),
        P(("dp", "seq")),
        P(("dp", "seq"), None),
        P(("dp", "seq"), None),
        P(("dp", "seq"), None),
    )
    return jax.shard_map(
        on_device, mesh=mesh, in_specs=in_specs, out_specs=out_specs, check_vma=False
    )
```

profile of v0, /device:TPU:0, one launch (start us, length us, event | category | flops | bytes accessed | tf_op | source)
XLA Modules:
  0.0 2905.4 jit_solution(7875601891863448938)
XLA Ops:
  12.2 42.1 %all-reduce.5 = (bf16[2048]{0:T(1024)(128)(2,1)S(1)}, bf16[2048]{0:T(1024)(128)(2,1)S(1)}) all-reduce(bf16[2048]{0:T(1024)(128)(2,1)S(1)} %dynamic-update-slice, bf16[2048]{0:T(1024)(128)(2,1)S(1)} %dynamic-update-slice.1), channel_id=1, replica_groups=mesh['dp'=2,'seq'=16] {'dp','seq'}, use_global_device_ids=true, to_apply=%add | all-reduce | flops 4096 | bytes 16384
  56.4 10.9 all-gather.8.cloned.1.call-done
  67.3 1.7 fusion.69
  75.2 71.5 %all-gather.12.cloned.1.call-done = bf16[2048,2048]{1,0:T(8,128)(2,1)} async-done(((bf16[64,2048]{1,0:T(8,128)(2,1)}), bf16[2048,2048]{1,0:T(8,128)(2,1)}) %all-gather.12.cloned.1.call-update) | async-done | bytes 8388624 | tf_op jit(solution)/shard_map/all_gather | solution.py:108
  146.7 12.3 copy.63
  159.0 5.9 fusion.57
  165.4 20.6 all-gather.10.cloned.1.call-done
  186.0 40.6 %while.30 = (s32[]{:T(128)}, f32[16,128]{1,0:T(8,128)S(1)}, f32[16,128]{1,0:T(8,128)S(1)}, f32[16,128,128]{2,1,0:T(8,128)S(1)}, s32[4,512]{1,0:T(4,128)S(1)}, /*...) while((s32[]{:T(128)}, f32[16,128]{1,0:T(8,128)S(1)}, ...), condition=%wide.region_7.8_spmd.clone, body=%wide.region_4.7_spmd.clone.sunk | while | flops 550447104 | bytes 33174700 | solution.py:164
  187.9 2.8 fusion.150
  190.6 3.3 fusion.151
  194.1 1.9 fusion.153
  197.9 2.8 fusion.150
  200.7 3.4 fusion.151
  204.1 1.9 fusion.153
  207.9 2.8 fusion.150
  210.7 3.3 fusion.151
  214.1 1.9 fusion.153
  218.0 2.8 fusion.150
  220.7 3.3 fusion.151
  224.2 1.9 fusion.153
  227.1 38.0 %all-gather.14.cloned.1.call-done = bf16[2048,2048]{1,0:T(8,128)(2,1)} async-done(((bf16[64,2048]{1,0:T(8,128)(2,1)}), bf16[2048,2048]{1,0:T(8,128)(2,1)}) %all-gather.14.cloned.1.call-update) | async-done | bytes 8388624 | tf_op jit(solution)/shard_map/all_gather | solution.py:171
  265.0 6.4 multiply_reduce_fusion.3
  272.3 138.8 %all-gather.16.cloned.1.call-done = bf16[2048,5632]{1,0:T(8,128)(2,1)} async-done(((bf16[64,5632]{1,0:T(8,128)(2,1)}), bf16[2048,5632]{1,0:T(8,128)(2,1)}) %all-gather.16.cloned.1.call-update) | async-done | bytes 23068688 | tf_op jit(solution)/shard_map/all_gather | solution.py:177
  411.0 12.3 fusion.92
  423.3 133.3 %all-gather.18.cloned.1.call-done = bf16[2048,5632]{1,0:T(8,128)(2,1)} async-done(((bf16[64,5632]{1,0:T(8,128)(2,1)}), bf16[2048,5632]{1,0:T(8,128)(2,1)}) %all-gather.18.cloned.1.call-update) | async-done | bytes 23068688 | tf_op jit(solution)/shard_map/all_gather | solution.py:178
  556.6 12.3 fusion.93
  569.0 133.4 %all-gather.20.cloned.1.call-done = bf16[2048,5632]{1,0:T(8,128)(2,1)} async-done(((bf16[64,5632]{1,0:T(8,128)(2,1)}), bf16[2048,5632]{1,0:T(8,128)(2,1)}) %all-gather.20.cloned.1.call-update) | async-done | bytes 23068688 | tf_op jit(solution)/shard_map/all_gather | solution.py:189
  702.4 14.7 multiply_convert_fusion
  717.0 12.8 fusion.94
  729.9 13.8 multiply_reduce_fusion.1
  743.7 1.7 multiply_add_fusion
  745.4 5.0 convolution_convert_fusion
  752.6 1.6 copy.78
  755.0 44.7 %while.31 = (s32[]{:T(128)}, f32[128,16,128]{0,2,1:T(8,128)}, f32[4,512,128]{2,1,0:T(8,128)}, f32[4,512,128]{2,1,0:T(8,128)}, bf16[4,512,256]{2,1,0:T(8,128)(2,1...) while((s32[]{:T(128)}, f32[128,16,128]{0,2,1:T(8,128)}, ...), condition=%wide.region_11.12_spmd.clone, body=%wide.region_10.11_spmd.clone.sunk | while | flops 1352335360 | bytes 62600676 | solution.py:241
  760.7 1.5 fusion.163
  762.2 1.4 fusion.164
  763.6 1.5 fusion.165
  770.9 2.9 fusion.163
  773.8 1.4 fusion.164
  775.2 1.5 fusion.165
  782.4 2.9 fusion.163
  785.3 1.4 fusion.164
  786.7 1.5 fusion.165
  793.9 2.9 fusion.163
  796.8 1.4 fusion.164
  798.2 1.5 fusion.165
  799.8 2.3 broadcast_multiply_fusion
  802.9 54.9 %reduce-scatter.11.cloned.1.call-done = f32[128,128]{1,0:T(8,128)} async-done(((f32[2048,128]{1,0:T(8,128)}), f32[128,128]{1,0:T(8,128)}) %reduce-scatter.11.cloned.1.call-update) | async-done | bytes 65552 | tf_op jit(solution)/shard_map/reduce_scatter | solution.py:249
  857.8 60.5 %reduce-scatter.13.cloned.1.call-done = f32[128,128]{1,0:T(8,128)} async-done(((f32[2048,128]{1,0:T(8,128)}), f32[128,128]{1,0:T(8,128)}) %reduce-scatter.13.cloned.1.call-update) | async-done | bytes 65552 | tf_op jit(solution)/shard_map/reduce_scatter | solution.py:250
  919.5 1.9 fusion.67
  922.8 8.2 fusion.59
  932.4 8.1 fusion.62
  941.5 19.2 fusion.96
  960.9 19.3 fusion.97
  981.5 18.9 convolution_bitcast_fusion.2
  1000.4 42.4 %copy.80 = f32[2048,5632]{1,0:T(8,128)} copy(f32[2048,5632]{0,1:T(8,128)} %convolution_bitcast_fusion.2) | data formatting | bytes 92274688
  1044.4 6.6 fusion.95
  1051.0 12.9 fusion.37
  1064.5 47.1 %all-reduce.4 = (f32[2048]{0:T(1024)S(1)}, f32[2048]{0:T(1024)S(1)}) all-reduce(f32[2048]{0:T(1024)S(1)} %get-tuple-element.353, f32[2048]{0:T(1024)S(1)} %copy-done.33), channel_id=4, replica_groups=mesh['dp'=2,'seq'=16] {'dp','seq'}, use_global_device_ids=true, to_apply=%region_16.17.clone | all-reduce | flops 4096 | bytes 32768
  1114.1 129.2 %reduce-scatter.15.cloned.1.call-done = f32[64,2048]{1,0:T(8,128)} async-done(((f32[2048,2048]{1,0:T(8,128)}), f32[64,2048]{1,0:T(8,128)}) %reduce-scatter.15.cloned.1.call-update) | async-done | bytes 524304 | tf_op jit(solution)/shard_map/reduce_scatter | solution.py:283
  1243.3 183.3 %reduce-scatter.19.cloned.1.call-done = f32[64,2048]{1,0:T(8,128)} async-done(((f32[2048,2048]{1,0:T(8,128)}), f32[64,2048]{1,0:T(8,128)}) %reduce-scatter.19.cloned.1.call-update) | async-done | bytes 524304 | tf_op jit(solution)/shard_map/reduce_scatter | solution.py:285
  1426.6 489.2 %reduce-scatter.21.cloned.1.call-done = f32[64,5632]{1,0:T(8,128)} async-done(((f32[2048,5632]{1,0:T(8,128)}), f32[64,5632]{1,0:T(8,128)}) %reduce-scatter.21.cloned.1.call-update) | async-done | bytes 1441808 | tf_op jit(solution)/shard_map/reduce_scatter | solution.py:286
  1915.8 491.3 %reduce-scatter.23.cloned.1.call-done = f32[64,5632]{1,0:T(8,128)} async-done(((f32[2048,5632]{1,0:T(8,128)}), f32[64,5632]{1,0:T(8,128)}) %reduce-scatter.23.cloned.1.call-update) | async-done | bytes 1441808 | tf_op jit(solution)/shard_map/reduce_scatter | solution.py:287
  2407.2 491.3 %reduce-scatter.25.cloned.1.call-done = f32[64,5632]{1,0:T(8,128)} async-done(((f32[2048,5632]{1,0:T(8,128)}), f32[64,5632]{1,0:T(8,128)}) %reduce-scatter.25.cloned.1.call-update) | async-done | bytes 1441808
  (296 shorter events, 60.2 us)
Async XLA Ops:
  7.2 60.2 %all-gather.8.cloned.1.call-start = ((), (), s32[]{:S(2)}) async-start(), calls=%async_computation.8 | async-start | bytes 1081344 | tf_op jit(solution)/shard_map/all_gather | solution.py:109
  7.9 138.8 %all-gather.12.cloned.1.call-start = ((), (), s32[]{:S(2)}) async-start(), calls=%async_computation.10 | async-start | bytes 8650752 | tf_op jit(solution)/shard_map/all_gather | solution.py:108
  8.7 177.3 %all-gather.10.cloned.1.call-start = ((), (), s32[]{:S(2)}) async-start(), calls=%async_computation.9 | async-start | bytes 1114112 | tf_op jit(solution)/shard_map/all_gather | solution.py:123
  54.2 20.0 copy-start.41
  55.2 103.8 %copy-start.39 = (f32[128]{0:T(128)}, f32[128]{0:T(128)S(1)}, u32[]{:S(2)}) copy-start(f32[128]{0:T(128)S(1)} %get-tuple-element.409) | copy-start | bytes 1540
  56.4 102.6 %copy-start.34 = (f32[128]{0:T(128)}, f32[128]{0:T(128)S(1)}, u32[]{:S(2)}) copy-start(f32[128]{0:T(128)S(1)} %add_rsqrt_fusion.1) | copy-start | bytes 1540
  71.4 193.6 %all-gather.14.cloned.1.call-start = ((), (), s32[]{:S(2)}) async-start(), calls=%async_computation.11 | async-start | bytes 8650752 | tf_op jit(solution)/shard_map/all_gather | solution.py:171
  72.0 339.0 %all-gather.16.cloned.1.call-start = ((), (), s32[]{:S(2)}) async-start(), calls=%async_computation.12 | async-start | bytes 23789568 | tf_op jit(solution)/shard_map/all_gather | solution.py:177
  72.6 484.0 %all-gather.18.cloned.1.call-start = ((), (), s32[]{:S(2)}) async-start(), calls=%async_computation.13 | async-start | bytes 23789568 | tf_op jit(solution)/shard_map/all_gather | solution.py:178
  73.2 629.2 %all-gather.20.cloned.1.call-start = ((), (), s32[]{:S(2)}) async-start(), calls=%async_computation.14 | async-start | bytes 23789568 | tf_op jit(solution)/shard_map/all_gather | solution.py:189
  73.9 783.8 %reduce-scatter.11.cloned.1.call-start = ((), (), s32[]{:S(2)}) async-start(), calls=%async_computation.15 | async-start | bytes 1114112 | tf_op jit(solution)/shard_map/reduce_scatter | solution.py:249
  146.7 12.3 copy-start.4
  190.6 3.4 copy-start
  200.6 3.5 copy-start
  210.7 3.5 copy-start
  220.7 3.5 copy-start
  226.9 38.1 %copy-start.14 = (f32[16,128,128]{1,2,0:T(8,128)}, f32[16,128,128]{1,2,0:T(8,128)S(1)}, u32[]{:S(2)}) copy-start(f32[16,128,128]{1,2,0:T(8,128)S(1)} %copy.67) | copy-start | bytes 3145732
  227.0 44.4 %copy-start.17 = (bf16[16,128,128]{1,2,0:T(8,128)(2,1)}, bf16[16,128,128]{1,2,0:T(8,128)(2,1)S(1)}, u32[]{:S(2)}) copy-start(bf16[16,128,128]{1,2,0:T(8,128)(2,1)S(1)} %fusion.61) | copy-start | bytes 1572868
  271.4 472.3 %copy-start.5 = (f32[128,2048]{1,0:T(8,128)}, f32[128,2048]{1,0:T(8,128)S(1)}, u32[]{:S(2)}) copy-start(f32[128,2048]{1,0:T(8,128)S(1)} %get-tuple-element.435) | copy-start | bytes 3145732
  272.3 284.4 %copy-start.9 = (bf16[128,2048]{1,0:T(8,128)(2,1)}, bf16[128,2048]{1,0:T(8,128)(2,1)S(1)}, u32[]{:S(2)}) copy-start(bf16[128,2048]{1,0:T(8,128)(2,1)S(1)} %multiply_convert_fusion.3) | copy-start | bytes 1572868
  423.3 279.0 %copy-start.19 = (bf16[1,128,2048]{2,1,0:T(8,128)(2,1)S(1)}, bf16[1,128,2048]{2,1,0:T(8,128)(2,1)}, u32[]{:S(2)}) copy-start(bf16[1,128,2048]{2,1,0:T(8,128)(2,1)} %param.28) | copy-start | bytes 1572868
  717.0 12.8 copy-start.13
  717.0 12.8 copy-start.12
  745.4 5.0 copy-start.7
  750.4 3.8 copy-start.15
  755.0 4.3 copy-start.21
  755.0 4.3 copy-start.36
  755.0 4.3 copy-start.37
  760.7 3.0 copy-start.2
  762.2 3.0 copy-start.30
  762.2 3.0 copy-start.32
  765.2 4.3 copy-start.21
  765.2 4.2 copy-start.36
  765.2 4.2 copy-start.37
  770.8 4.3 copy-start.2
  770.9 4.3 copy-start.22
  770.9 4.3 copy-start.38
  776.7 4.3 copy-start.21
  776.7 4.2 copy-start.36
  776.7 4.2 copy-start.37
  782.4 4.3 copy-start.2
  782.4 4.3 copy-start.22
  782.4 4.3 copy-start.38
  788.2 4.3 copy-start.21
  788.2 4.2 copy-start.36
  788.2 4.2 copy-start.37
  793.9 4.3 copy-start.2
  793.9 4.3 copy-start.22
  793.9 4.3 copy-start.38
  799.7 3.1 copy-start.28
  799.7 119.4 %copy-start.40 = (f32[128]{0:T(128)S(1)}, f32[128]{0:T(128)}, u32[]{:S(2)}) copy-start(f32[128]{0:T(128)} %copy-done.39) | copy-start | bytes 1540
  799.7 119.4 %copy-start.42 = (f32[64]{0:T(128)S(1)}, f32[64]{0:T(128)}, u32[]{:S(2)}) copy-start(f32[64]{0:T(128)} %copy-done.41) | copy-start | bytes 772
  799.7 119.8 %copy-start.35 = (f32[128]{0:T(128)S(1)}, f32[128]{0:T(128)}, u32[]{:S(2)}) copy-start(f32[128]{0:T(128)} %copy-done.34) | copy-start | bytes 1540
  802.0 119.6 %copy-start.3 = (f32[128,16,128]{0,2,1:T(8,128)S(1)}, f32[128,16,128]{0,2,1:T(8,128)}, u32[]{:S(2)}) copy-start(f32[128,16,128]{0,2,1:T(8,128)} %get-tuple-element.137) | copy-start | bytes 3145732
  802.1 116.2 %reduce-scatter.13.cloned.1.call-start = ((), (), s32[]{:S(2)}) async-start(), calls=%async_computation.16 | async-start | bytes 1114112 | tf_op jit(solution)/shard_map/reduce_scatter | solution.py:250
  802.8 311.3 %reduce-scatter.17.cloned.1.call-start = ((), (), s32[]{:S(2)}) async-start(), calls=%async_computation.18 | async-start | bytes 2162688 | tf_op jit(solution)/shard_map/reduce_scatter | solution.py:284
  921.4 321.9 %reduce-scatter.15.cloned.1.call-start = ((), (), s32[]{:S(2)}) async-start(), calls=%async_computation.17 | async-start | bytes 17301504 | tf_op jit(solution)/shard_map/reduce_scatter | solution.py:283
  931.1 495.6 %reduce-scatter.19.cloned.1.call-start = ((), (), s32[]{:S(2)}) async-start(), calls=%async_computation.19 | async-start | bytes 17301504 | tf_op jit(solution)/shard_map/reduce_scatter | solution.py:285
  940.5 975.3 %reduce-scatter.21.cloned.1.call-start = ((), (), s32[]{:S(2)}) async-start(), calls=%async_computation.20 | async-start | bytes 47579136 | tf_op jit(solution)/shard_map/reduce_scatter | solution.py:286
  960.8 1446.4 %reduce-scatter.23.cloned.1.call-start = ((), (), s32[]{:S(2)}) async-start(), calls=%async_computation.21 | async-start | bytes 47579136 | tf_op jit(solution)/shard_map/reduce_scatter | solution.py:287
  980.1 1918.3 %reduce-scatter.25.cloned.1.call-start = ((), (), s32[]{:S(2)}) async-start(), calls=%async_computation.22 | async-start | bytes 47579136
  1044.4 6.6 copy-start.6
  1051.0 12.9 copy-start.20
  1051.0 13.5 copy-start.33
  (30 other events, 45.3 us)
Sparse Core Ops, SparseCore 0:
  10.8 56.4 all-gather.7
  70.2 76.4 all-gather.11
  149.4 36.5 all-gather.9
  188.7 76.3 all-gather.13
  267.8 143.1 all-gather.15
  413.8 142.7 all-gather.17
  559.6 142.7 all-gather.19
  802.2 55.5 reduce-scatter.10
  861.9 56.3 reduce-scatter.12
  921.5 135.8 reduce-scatter.16
  1060.4 182.9 reduce-scatter.14
  1246.1 180.4 reduce-scatter.18
  1429.6 486.1 reduce-scatter.20
  1918.7 488.4 reduce-scatter.22
  2410.0 488.4 reduce-scatter.24
where the time goes:
time: 2920 us; the launch traced here: 2910 us
  waiting for transfers between devices  2450 us (84%)
  matrix products  229 us (8%)
  blocking collectives  89.1 us (3%)
  local copies, waits for them, and re-layouts  86 us (3%)
  other arithmetic  33.2 us (1%)
    unnamed x16, waiting for transfers between devices  496 us
    reduce_scatter x1, waiting for transfers between devices, on_device(): lax.psum_scatter(up_term, ('dp', 'seq'), scatter_dimension=0, tiled=True)  491 us
    reduce_scatter x1, waiting for transfers between devices, on_device(): lax.psum_scatter(gate_term, ('dp', 'seq'), scatter_dimension=0, tiled=True)  489 us
    reduce_scatter x1, waiting for transfers between devices, on_device(): lax.psum_scatter(output_term, ('dp', 'seq'), scatter_dimension=0, tiled=T...  183 us
    all_gather x1, waiting for transfers between devices, on_device(): gate_piece = lax.all_gather(gate_weight, ('dp', 'seq'), axis=0, tiled=True)  139 us
    all_gather x1, waiting for transfers between devices, on_device(): lax.all_gather(down_weight, ('dp', 'seq'), axis=0, tiled=True)  133 us
    all_gather x1, waiting for transfers between devices, on_device(): up_piece = lax.all_gather(up_weight, ('dp', 'seq'), axis=0, tiled=True)  133 us
    reduce_scatter x1, waiting for transfers between devices, on_device(): lax.psum_scatter(query_term, ('dp', 'seq'), scatter_dimension=0, tiled=True)  129 us
  transfers between devices with their start and end apart: 15, of which 14 were waited for; matrix products, arithmetic and copies ran while one was open for 8% of the time, Pallas kernels for 0%

commit v1 on v0

v1 whole, which is shorter than its diff:
```python
import math

import jax
import jax.numpy as jnp
from jax import lax
from jax.sharding import Mesh
from jax.sharding import PartitionSpec as P

HEAD_DIM = 128
EPSILON = 1e-05
NEGATIVE = -1e30
Z = 4
BF16 = jnp.bfloat16
F32 = jnp.float32


def angles(offset):
    half_dim = HEAD_DIM // 2
    frequency = jnp.exp(
        jnp.arange(half_dim, dtype=F32) * (-2.0 * math.log(10000.0) / HEAD_DIM)
    )
    phases = offset.astype(F32)[:, None] * frequency[None, :]
    return (jnp.cos(phases), jnp.sin(phases))


def rotate(vectors, cosine, sine_part):
    half_dim = vectors.shape[-1] // 2
    first, second = vectors[..., :half_dim], vectors[..., half_dim:]
    return jnp.concatenate(
        [first * cosine - second * sine_part, second * cosine + first * sine_part], -1
    )


def dot(left, right):
    return jnp.dot(left, right, preferred_element_type=F32)


def contract_last(left, right):
    return lax.dot_general(left, right, (((1,), (1,)), ((), ())), preferred_element_type=F32)


def contract_first(left, right):
    return lax.dot_general(left, right, (((0,), (0,)), ((), ())), preferred_element_type=F32)


def norm_back(grad_normed, normed, scale_rows):
    return scale_rows * (
        grad_normed - normed * jnp.mean(grad_normed * normed, axis=-1, keepdims=True)
    )


def swap(value, axis):
    return lax.ppermute(value, axis, [(0, 1), (1, 0)])


def hop(value, k):
    return lax.ppermute(value, "z", [(i, i ^ k) for i in range(Z)])


def pick(stacked, index, axis=0):
    return lax.dynamic_index_in_dim(stacked, index, axis, keepdims=False)


def put(pieces, indices, axis):
    shape = list(pieces[0].shape)
    shape.insert(axis, len(pieces))
    result = jnp.zeros(shape, pieces[0].dtype)
    for piece, index in zip(pieces, indices):
        result = lax.dynamic_update_index_in_dim(result, piece, index, axis)
    return result


def pair(own, other, index, axis=0):
    return jnp.where(
        index == 0, jnp.stack([own, other], axis), jnp.stack([other, own], axis)
    )


def on_device(
    block_input,
    attention_gain,
    query_weight,
    keyvalue_weight,
    output_weight,
    feedforward_gain,
    gate_weight,
    up_weight,
    down_weight,
    document_lengths,
    piece_order,
    output_grad,
    shared_grad,
):
    y, z, m, x, c = (lax.axis_index(a) for a in "yzmxc")
    M = lax.axis_size("m")
    tokens, width = block_input.shape[1:]
    rows = query_weight.shape[0]
    query_width = query_weight.shape[1]
    half_width = query_width // 2
    heads = half_width // HEAD_DIM
    hidden_units = gate_weight.shape[1]
    part = hidden_units // Z
    piece_len = tokens // 2
    others = [z ^ k for k in range(Z)]

    def inward(value):
        value = value.reshape(tokens, 2, Z, M, 2, 2, rows).transpose(0, 5, 1, 4, 3, 2, 6)
        value = jnp.where(c == 0, value, value[:, ::-1])
        value = jnp.where(y == 0, value, value[:, :, ::-1])
        return value.reshape(tokens, width)

    def outward(value):
        value = value.reshape(tokens, 2, 2, 2, M, Z, rows)
        value = jnp.where(y == 0, value, value[:, :, ::-1])
        value = jnp.where(c == 0, value, value[:, ::-1])
        return value.transpose(0, 2, 5, 4, 3, 1, 6).reshape(tokens, width)

    def turn(value):
        parts = value.reshape(tokens, 4, 2, width // 8)
        return jnp.where(x == 0, parts, parts[:, :, ::-1]).reshape(tokens, width)

    def gather_z(value):
        return [value] + [hop(value, k) for k in range(1, Z)]

    def gather_m(value, axis):
        return lax.all_gather(value, "m", axis=axis) if M > 1 else jnp.expand_dims(value, axis)

    def scatter_m(value, axis):
        if M > 1:
            return lax.psum_scatter(value, "m", scatter_dimension=axis)
        return lax.squeeze(value, (axis,))

    finish = jnp.cumsum(document_lengths[0])
    starts = finish - document_lengths[0]

    def places(slots):
        order = piece_order[(slots[:, None] * 2 + jnp.arange(2)[None, :]).reshape(-1)]
        position = (
            order[:, None] * piece_len + jnp.arange(piece_len, dtype=jnp.int32)[None, :]
        ).reshape(-1)
        segment = jnp.sum((finish[None, :] <= position[:, None]).astype(jnp.int32), axis=1)
        begins = jnp.max(
            jnp.where(starts[None, :] <= position[:, None], starts[None, :], 0), axis=1
        )
        return position, segment, position - begins

    def slot(z_at, m_at, x_at, c_at):
        return ((z_at * M + m_at) * 2 + x_at) * 2 + c_at

    query_slots = jnp.stack([slot(z, m, x, c), slot(z, m, 1 - x, c)])
    position, segment, offset = places(query_slots)
    key_slots = jnp.stack(
        [
            slot(z ^ k, m_at, x ^ i, c ^ j)
            for j in range(2)
            for i in range(2)
            for m_at in range(M)
            for k in range(Z)
        ]
    )
    key_position, key_segment, _ = places(key_slots)
    allowed = (key_segment[None, :] == segment[:, None]) & (
        key_position[None, :] <= position[:, None]
    )
    cosine, sine_part = angles(offset)

    gains = jnp.stack([attention_gain, feedforward_gain])
    gains = jnp.pad(gains, ((0, 14), (0, 2 * HEAD_DIM - rows)))
    small = jnp.concatenate([keyvalue_weight, gains])
    small = put(gather_z(small), others, 0)
    small = gather_m(small, 0)
    small_x = swap(small, "x")
    small_y = swap(small, "y")
    small_d = swap(small_x, "y")
    small = jnp.stack([pair(small, small_x, x), pair(small_y, small_d, x)])
    small = jnp.stack([small, swap(small, "c")])
    small = small.reshape(width // rows, rows + 16, 2 * HEAD_DIM)
    keyvalue_full = small[:, :rows].reshape(width, 2 * HEAD_DIM)
    gain_one = small[:, rows, :rows].reshape(1, width).astype(F32)
    gain_two = small[:, rows + 1, :rows].reshape(1, width).astype(F32)

    def gather_heads(weight):
        parts = weight.reshape(rows, 2, half_width).transpose(1, 0, 2)
        got = pair(pick(parts, x), swap(pick(parts, 1 - x), "x"), x)
        got = put(gather_z(got), others, 1)
        got = gather_m(got, 1).reshape(-1, half_width)
        got = jnp.concatenate([got, swap(got, "y")])
        return jnp.concatenate([got, swap(got, "c")])

    def scatter_heads(grad):
        grad = grad.astype(BF16)
        half = width // 2
        grad = grad[:half].astype(F32) + swap(grad[half:], "c").astype(F32)
        quarter = half // 2
        grad = grad[:quarter] + swap(grad[quarter:].astype(BF16), "y").astype(F32)
        grad = scatter_m(grad.reshape(2, M, Z, rows, half_width), 1)
        low = grad.astype(BF16)
        total = pick(grad, z, 1)
        for k in range(1, Z):
            total = total + hop(pick(low, z ^ k, 1), k).astype(F32)
        own = pick(total, x)
        other = swap(pick(total, 1 - x).astype(BF16), "x").astype(F32)
        return pair(own, other, x, 1).reshape(rows, query_width)

    query_full = gather_heads(query_weight)
    output_full = gather_heads(output_weight)

    stacked = jnp.stack([gate_weight, up_weight, down_weight])
    stacked = stacked.reshape(3, rows, Z, part).transpose(2, 0, 1, 3)
    got = [pick(stacked, z)] + [hop(pick(stacked, z ^ k), k) for k in range(1, Z)]
    got = put(got, others, 1)
    got = gather_m(got, 1).reshape(3, width // 8, part)
    got_x = swap(got, "x")
    got_y = swap(got, "y")
    mid = width // 16
    got_da = swap(got_x[:, :mid], "y")
    got_db = swap(got_y[:, mid:], "x")
    pieces = [got, got_x, got_y, got_da, got_db]
    pieces = pieces + [swap(piece, "c") for piece in pieces]
    gate_full, up_full, down_full = (
        jnp.concatenate([piece[i] for piece in pieces]) for i in range(3)
    )

    score_scale = 1.0 / math.sqrt(HEAD_DIM)
    input_mine = inward(block_input[0])
    input_pair = jnp.concatenate([input_mine, swap(input_mine, "x")])
    inputs = input_pair.astype(F32)
    scale_one = lax.rsqrt(jnp.mean(inputs * inputs, axis=-1, keepdims=True) + EPSILON)
    normed_one = inputs * scale_one
    normed_one_low = (normed_one * gain_one).astype(BF16)
    keyvalue_sum = dot(normed_one_low[:tokens], keyvalue_full)
    shared_mine = jnp.concatenate(
        [
            rotate(keyvalue_sum[:, :HEAD_DIM], cosine[:tokens], sine_part[:tokens]),
            keyvalue_sum[:, HEAD_DIM:],
        ],
        -1,
    ).astype(BF16)
    gathered = gather_m(jnp.stack(gather_z(shared_mine)), 0)
    gathered = jnp.stack([gathered, swap(gathered, "x")])
    gathered = jnp.stack([gathered, swap(gathered, "c")])
    gathered = gathered.reshape(-1, 2 * HEAD_DIM)
    key_all, value_all = gathered[:, :HEAD_DIM], gathered[:, HEAD_DIM:]
    query_rot = rotate(
        dot(normed_one_low, query_full).reshape(2 * tokens, heads, HEAD_DIM),
        cosine[:, None, :],
        sine_part[:, None, :],
    ).astype(BF16)
    scores = (
        jnp.einsum("thd,kd->htk", query_rot, key_all, preferred_element_type=F32) * score_scale
    )
    scores = jnp.where(allowed[None], scores, NEGATIVE)
    top = jnp.max(scores, axis=-1, keepdims=True)
    weights = jnp.exp(scores - top)
    total = jnp.sum(weights, axis=-1, keepdims=True)
    log_total = top + jnp.log(total)
    output_heads = (
        jnp.einsum("htk,kd->htd", weights.astype(BF16), value_all, preferred_element_type=F32)
        / total
    )
    attended_low = output_heads.transpose(1, 0, 2).reshape(2 * tokens, half_width).astype(BF16)
    branch = contract_last(attended_low, output_full)
    branch = branch[:tokens] + swap(branch[tokens:].astype(BF16), "x").astype(F32)
    hidden = inputs[:tokens] + branch

    scale_two = lax.rsqrt(jnp.mean(hidden * hidden, axis=-1, keepdims=True) + EPSILON)
    normed_two = hidden * scale_two
    normed_two_low = jnp.concatenate(gather_z(turn((normed_two * gain_two).astype(BF16))))
    grad_mine = inward(output_grad[0])
    grad_low = jnp.concatenate(gather_z(turn(grad_mine)))
    gate_sum = dot(normed_two_low, gate_full)
    up_sum = dot(normed_two_low, up_full)
    sigmoid_gate = jax.nn.sigmoid(gate_sum)
    silu_gate = gate_sum * sigmoid_gate
    mixed_low = (silu_gate * up_sum).astype(BF16)
    grad_mixed = dot(grad_low, down_full)
    grad_gate = (
        grad_mixed * up_sum * sigmoid_gate * (1.0 + gate_sum * (1.0 - sigmoid_gate))
    ).astype(BF16)
    grad_up = (grad_mixed * silu_gate).astype(BF16)

    def scatter_z(value):
        value = value.reshape(Z, tokens, width)
        low = value.astype(BF16)
        result = value[0]
        for k in range(1, Z):
            result = result + hop(low[k], k).astype(F32)
        return turn(result)

    grad_two = scatter_z(contract_last(grad_gate, gate_full) + contract_last(grad_up, up_full))
    feed_out = scatter_z(contract_last(mixed_low, down_full))
    block_output = outward((hidden + feed_out).astype(BF16))[None]
    gain_two_grad = jnp.sum(grad_two * normed_two, axis=0)
    grad_hidden = grad_mine.astype(F32) + norm_back(grad_two * gain_two, normed_two, scale_two)

    grad_hidden_low = grad_hidden.astype(BF16)
    grad_hidden_low = jnp.concatenate([grad_hidden_low, swap(grad_hidden_low, "x")])
    grad_heads = (
        dot(grad_hidden_low, output_full).astype(BF16).reshape(2 * tokens, heads, HEAD_DIM)
    )
    delta = jnp.einsum("thd,htd->ht", grad_heads, output_heads, preferred_element_type=F32)
    scores = (
        jnp.einsum("thd,kd->htk", query_rot, key_all, preferred_element_type=F32) * score_scale
    )
    probs = jnp.where(allowed[None], jnp.exp(scores - log_total), 0.0)
    grad_probs = jnp.einsum("thd,kd->htk", grad_heads, value_all, preferred_element_type=F32)
    grad_scores = (probs * (grad_probs - delta[..., None])).astype(BF16)
    grad_query = jnp.einsum("htk,kd->thd", grad_scores, key_all, preferred_element_type=F32)
    grad_key = jnp.einsum("htk,thd->kd", grad_scores, query_rot, preferred_element_type=F32)
    grad_value = jnp.einsum(
        "htk,thd->kd", probs.astype(BF16), grad_heads, preferred_element_type=F32
    )
    kv_grad = jnp.concatenate([grad_key * score_scale, grad_value], -1)
    half = kv_grad.shape[0] // 2
    kv_grad = kv_grad[:half] + swap(kv_grad[half:].astype(BF16), "c").astype(F32)
    half = half // 2
    kv_grad = kv_grad[:half] + swap(kv_grad[half:].astype(BF16), "x").astype(F32)
    kv_grad = scatter_m(kv_grad.reshape(M, Z, tokens, 2 * HEAD_DIM), 0)
    kv_low = kv_grad.astype(BF16)
    kv_mine = kv_grad[0]
    for k in range(1, Z):
        kv_mine = kv_mine + hop(kv_low[k], k).astype(F32)
    kv_mine = kv_mine + shared_grad[0].astype(F32)
    query_grad_low = (
        rotate(grad_query * score_scale, cosine[:, None, :], -sine_part[:, None, :])
        .reshape(2 * tokens, half_width)
        .astype(BF16)
    )
    keyvalue_grad_low = jnp.concatenate(
        [
            rotate(kv_mine[:, :HEAD_DIM], cosine[:tokens], -sine_part[:tokens]),
            kv_mine[:, HEAD_DIM:],
        ],
        -1,
    ).astype(BF16)
    grad_one = contract_last(query_grad_low, query_full)
    grad_one = grad_one[:tokens] + swap(grad_one[tokens:].astype(BF16), "x").astype(F32)
    grad_one = grad_one + contract_last(keyvalue_grad_low, keyvalue_full)
    normed_mine = normed_one[:tokens]
    gain_one_grad = jnp.sum(grad_one * normed_mine, axis=0)
    input_grad = outward(
        grad_hidden + norm_back(grad_one * gain_one, normed_mine, scale_one[:tokens])
    )[None]

    def scatter_feed(grad):
        grad = grad.astype(BF16)
        half = width // 2
        grad = grad[:half].astype(F32) + swap(grad[half:], "c").astype(F32)
        own, by_x, by_y, by_d = (grad[i * 2 * mid : (i + 1) * 2 * mid] for i in range(4))
        by_d = by_d.astype(BF16)
        from_y = swap(by_d[:mid], "y").astype(F32)
        from_x = swap(by_d[mid:], "x").astype(F32)
        by_x = jnp.concatenate([by_x[:mid] + from_y, by_x[mid:]]).astype(BF16)
        by_y = jnp.concatenate([by_y[:mid], by_y[mid:] + from_x]).astype(BF16)
        own = own + swap(by_x, "x").astype(F32) + swap(by_y, "y").astype(F32)
        own = scatter_m(own.reshape(M, Z, rows, part), 0).astype(BF16)
        got = [pick(own, z)] + [hop(pick(own, z ^ k), k) for k in range(1, Z)]
        return put(got, others, 0).transpose(1, 0, 2).reshape(rows, hidden_units).astype(F32)

    down_weight_grad = scatter_feed(contract_first(grad_low, mixed_low))
    gate_weight_grad = scatter_feed(contract_first(normed_two_low, grad_gate))
    up_weight_grad = scatter_feed(contract_first(normed_two_low, grad_up))
    output_weight_grad = scatter_heads(contract_first(grad_hidden_low, attended_low))
    query_weight_grad = scatter_heads(contract_first(normed_one_low, query_grad_low))

    small_grad = contract_first(normed_one_low[:tokens], keyvalue_grad_low)
    small_gains = jnp.stack([gain_one_grad, gain_two_grad], -1)
    small_gains = jnp.pad(small_gains, ((0, 0), (0, HEAD_DIM - 2)))
    small_grad = jnp.concatenate([small_grad, small_gains], -1)
    half = width // 2
    small_grad = small_grad[:half] + swap(small_grad[half:].astype(BF16), "c").astype(F32)
    half = half // 2
    small_grad = small_grad[:half] + swap(small_grad[half:].astype(BF16), "y").astype(F32)
    small_grad = small_grad.reshape(2, M, Z, rows, 3 * HEAD_DIM)
    small_grad = pick(small_grad, x) + swap(pick(small_grad, 1 - x).astype(BF16), "x").astype(F32)
    small_grad = scatter_m(small_grad, 0)
    small_low = small_grad.astype(BF16)
    small_grad = pick(small_grad, z)
    for k in range(1, Z):
        small_grad = small_grad + hop(pick(small_low, z ^ k), k).astype(F32)
    keyvalue_weight_grad = small_grad[:, : 2 * HEAD_DIM]
    gain_one_mine = small_grad[:, 2 * HEAD_DIM]
    gain_two_mine = small_grad[:, 2 * HEAD_DIM + 1]
    return (
        block_output,
        shared_mine[None],
        input_grad,
        gain_one_mine,
        query_weight_grad,
        keyvalue_weight_grad,
        output_weight_grad,
        gain_two_mine,
        gate_weight_grad,
        up_weight_grad,
        down_weight_grad,
    )


def solution(mesh):
    streams, seq = mesh.shape["dp"], mesh.shape["seq"]
    fine = Mesh(mesh.devices.reshape(streams, Z, seq // (4 * Z), 2, 2), tuple("yzmxc"))
    stream = P("y", ("z", "m", "x", "c"), None)
    vector, matrix = P(tuple("yzmxc")), P(tuple("yzmxc"), None)
    return jax.shard_map(
        on_device,
        mesh=fine,
        in_specs=(
            stream,
            vector,
            matrix,
            matrix,
            matrix,
            vector,
            matrix,
            matrix,
            matrix,
            P("y", None),
            P(),
            stream,
            stream,
        ),
        out_specs=(
            stream,
            stream,
            stream,
            vector,
            matrix,
            matrix,
            matrix,
            vector,
            matrix,
            matrix,
            matrix,
        ),
        check_vma=False,
    )
```

time: 2920 us -> 857 us (0.29)
  waiting for transfers between devices: 2450 us -> 351 us
  starting transfers between devices: 1.06 us -> 151 us
  matrix products: 229 us -> 102 us
  blocking collectives: 89.1 us -> 0 us
  local copies, waits for them, and re-layouts: 86 us -> 149 us
  other arithmetic: 33.2 us -> 90.6 us
    reduce_scatter x7 -> x0, waiting for transfers between devices: 1410 us -> none  [the longest x1 491 us: on_device(): lax.psum_scatter(up_term, ('dp', 'seq'), scatter_dimension=0, tiled=True)]
    all_gather x7 -> x0, waiting for transfers between devices: 546 us -> none  [the longest x1 139 us: on_device(): gate_piece = lax.all_gather(gate_weight, ('dp', 'seq'), axis=0, tiled=True)]
    unnamed x16 -> x0, waiting for transfers between devices: 496 us -> none
    ppermute x0 -> x99, waiting for transfers between devices: none -> 351 us  [the longest x48 180 us: hop(): return lax.ppermute(value, 'z', [(i, i ^ k) for i in range(Z)])]
    ppermute x0 -> x99, starting transfers between devices: none -> 151 us  [the longest x48 112 us: hop(): return lax.ppermute(value, 'z', [(i, i ^ k) for i in range(Z)])]
    unnamed x2 -> x0, blocking collectives: 89.1 us -> none
    dot_general x6, matrix products: 75.6 us -> 17.5 us  [contract_first(): lax.dot_general(left, right, (((0,), (0,)), ((), ())), preferred_element_...]
    dot_general x34 -> x12, matrix products: 101 us -> 61.3 us  [the longest x6 22.4 us: dot(): return jnp.dot(left, right, preferred_element_type=F32)]
  transfers between devices with their start and end apart: 15 -> 99, of which waited for: 14 -> 38; matrix products, arithmetic and copies ran while one was open for 8% -> 37% of each run, Pallas kernels for 0% -> 0%
where the time goes in v1:
time: 857 us; the launch traced here: 848 us
  waiting for transfers between devices  351 us (41%)
  starting transfers between devices  151 us (18%)
  local copies, waits for them, and re-layouts  149 us (17%)
  matrix products  102 us (12%)
  other arithmetic  90.6 us (11%)
    ppermute x48, waiting for transfers between devices, hop(): return lax.ppermute(value, 'z', [(i, i ^ k) for i in range(Z)])  180 us
    ppermute x51, waiting for transfers between devices, swap(): return lax.ppermute(value, axis, [(0, 1), (1, 0)])  171 us
    ppermute x48, starting transfers between devices, hop(): return lax.ppermute(value, 'z', [(i, i ^ k) for i in range(Z)])  112 us
    unnamed x185, local copies, waits for them, and re-layouts  45.4 us
    ppermute x51, starting transfers between devices, swap(): return lax.ppermute(value, axis, [(0, 1), (1, 0)])  39.6 us
    dynamic_update_slice x23, local copies, waits for them, and re-layouts, put(): result = lax.dynamic_update_index_in_dim(result, piece, index, axis)  33.6 us
    dot_general x6, matrix products, contract_last(): lax.dot_general(left, right, (((1,), (1,)), ((), ())), preferred_element_...  23.3 us
    dot_general x6, matrix products, dot(): return jnp.dot(left, right, preferred_element_type=F32)  22.4 us
  transfers between devices with their start and end apart: 99, of which 38 were waited for; matrix products, arithmetic and copies ran while one was open for 37% of the time, Pallas kernels for 0%

profile of v1, /device:TPU:0, one launch (start us, length us, event | category | flops | bytes accessed | tf_op | source)
XLA Modules:
  0.0 847.7 jit_solution(15758094725156806746)
XLA Ops:
  16.4 5.7 constant_dynamic-slice_fusion.2
  24.7 3.5 collective-permute-start.30
  73.2 3.2 collective-permute-start.16
  77.2 13.1 %collective-permute-done.15 = bf16[2,64,1024]{2,1,0:T(8,128)(2,1)S(1)} collective-permute-done((bf16[2,64,1024]{2,1,0:T(8,128)(2,1)S(1)}, bf16[2,64,1024]{2,1,0:T(8,128)(2,1)S(1)}, u32[]{:S(2)}, u32[]{:S(2)}) %collective-permute-start.15) | collective-permute-done | bytes 262176 | tf_op jit(solution)/shard_map/ppermute | solution.py:57
  91.0 4.7 collective-permute-start.21
  96.4 5.1 collective-permute-done.20
  102.3 11.8 %collective-permute-done.21 = bf16[2,64,1024]{2,1,0:T(8,128)(2,1)S(1)} collective-permute-done((bf16[2,64,1024]{2,1,0:T(8,128)(2,1)S(1)}, bf16[2,64,1024]{2,1,0:T(8,128)(2,1)S(1)}, u32[]{:S(2)}, u32[]{:S(2)}) %collective-permute-start.21) | collective-permute-done | bytes 262176 | tf_op jit(solution)/shard_map/ppermute | solution.py:57
  125.4 3.5 collective-permute-done.31
  135.6 3.6 collective-permute-start.10
  140.9 13.3 %collective-permute-start.9 = (bf16[128,256]{1,0:T(8,128)(2,1)S(1)}, bf16[128,256]{1,0:T(8,128)(2,1)S(1)}, u32[]{:S(2)}, u32[]{:S(2)}) collective-permute-start(bf16[128,256]{1,0:T(8,128)(2,1)S(1)} %pad_maximum_fusion.39), channel_id=1, source_target_pairs={{0,8},{4,12},{8,0},{12,4},{1,9},{5,13},{9,1},{13,5},{2,10},{6,14},... | collective-permute-start | bytes 196616 | tf_op jit(solution)/shard_map/ppermute | solution.py:57
  164.7 17.7 %collective-permute-done.11 = bf16[1,4,128,256]{3,2,1,0:T(8,128)(2,1)S(1)} collective-permute-done((bf16[1,4,128,256]{3,2,1,0:T(8,128)(2,1)S(1)}, bf16[1,4,128,256]{3,2,1,0:T(8,128)(2,1)S(1)}, u32[]{:S(2)}, u32[]{:S(2)}) %collective-permute-start.11) | collective-permute-done | bytes 262176 | tf_op jit(solution)/shard_map/ppermute | solution.py:53
  184.2 28.8 %collective-permute-done.23 = bf16[512,1024]{1,0:T(8,128)(2,1)} collective-permute-done((bf16[512,1024]{1,0:T(8,128)(2,1)}, bf16[512,1024]{1,0:T(8,128)(2,1)}, u32[]{:S(2)}, u32[]{:S(2)}) %collective-permute-start.23) | collective-permute-done | bytes 1048608 | tf_op jit(solution)/shard_map/ppermute | solution.py:53
  217.2 14.7 %collective-permute-start.45 = (bf16[128,2048]{0,1:T(8,128)(2,1)}, bf16[128,2048]{0,1:T(8,128)(2,1)}, u32[]{:S(2)}, u32[]{:S(2)}) collective-permute-start(bf16[128,2048]{0,1:T(8,128)(2,1)} %bitcast.542), channel_id=1, source_target_pairs={{0,8},{4,12},{8,0},{12,4},{1,9},{5,13},{9,1},{13,5},{2,10},{6,14},... | collective-permute-start | bytes 1572872 | tf_op jit(solution)/shard_map/ppermute | solution.py:57
  249.6 7.5 fusion.4
  257.2 9.3 %fusion.5 = f32[8,256]{1,0:T(8,128)S(1)} fusion(f32[2048,256,8]{1,0,2:T(8,128)} %get-tuple-element.184, f32[8,256]{1,0:T(8,128)S(1)} %get-tuple-element.183, pred[256,2048]{0,1:T(8,128)(4,1)S(1)} %compare_and_fusion), kind=kLoop, calls=%fused_computation.11 | loop fusion | flops 16775168 | bytes 17317888 | tf_op jit(solution)/shard_map/reduce_sum | solution.py:255
  266.5 9.0 %fusion.45 = (bf16[256,8,128]{0,2,1:T(8,128)(2,1)S(1)}, f32[8,256,128]{1,2,0:T(8,128)}) fusion(f32[256,8]{0,1:T(8,128)S(1)} %bitcast.566, bf16[2048,256]{1,0:T(8,128)(2,1)S(1)} %bitcast.492, f32[2048,256,8]{1,0,2:T(8,128)} %get-tuple-element.184, f32[8,256]{1,0:T(8,128)S(1)} %get-tuple-element.183, pred[256,2048]{0,1:T(8,128)(4,1)S(1)} %compare_and_fusion), kind=kOutput, calls=%fused_computation.105 | convolution fusion | flops 1091043328 | bytes 19415040 | tf_op jit(solution)/shard_map/htk,kd->htd/dot_general | solution.py:258
  275.8 3.5 fusion.20
  281.9 19.5 %collective-permute-done.35 = bf16[3,128,1408]{2,1,0:T(8,128)(2,1)S(1)} collective-permute-done((bf16[3,128,1408]{2,1,0:T(8,128)(2,1)S(1)}, bf16[3,128,1408]{2,1,0:T(8,128)(2,1)S(1)}, u32[]{:S(2)}, u32[]{:S(2)}) %collective-permute-start.35) | collective-permute-done | bytes 1081376 | tf_op jit(solution)/shard_map/ppermute | solution.py:53
  305.7 11.0 %collective-permute-done.25 = bf16[128,2048]{1,0:T(8,128)(2,1)S(1)} collective-permute-done((bf16[128,2048]{1,0:T(8,128)(2,1)S(1)}, bf16[128,2048]{1,0:T(8,128)(2,1)S(1)}, u32[]{:S(2)}, u32[]{:S(2)}) %collective-permute-start.25) | collective-permute-done | bytes 524320 | tf_op jit(solution)/shard_map/ppermute | solution.py:53
  332.2 4.3 collective-permute-done.44
  336.5 6.4 fusion.88
  342.9 5.0 collective-permute-done.28
  347.9 25.0 %collective-permute-done.27 = bf16[128,2048]{0,1:T(8,128)(2,1)S(1)} collective-permute-done((bf16[128,2048]{0,1:T(8,128)(2,1)S(1)}, bf16[128,2048]{0,1:T(8,128)(2,1)S(1)}, u32[]{:S(2)}, u32[]{:S(2)}) %collective-permute-start.27) | collective-permute-done | bytes 524320 | tf_op jit(solution)/shard_map/ppermute | solution.py:57
  373.0 3.5 fusion.134
  376.5 5.5 multiply_convert_fusion.1
  382.1 5.0 fusion.150
  387.1 5.4 fusion.148
  397.2 5.0 fusion.149
  406.0 3.6 convolution_convert_fusion.2
  412.0 5.6 convolution_convert_fusion.1
  417.6 13.8 %collective-permute-start.41 = (bf16[128,2048]{1,0:T(8,128)(2,1)}, bf16[128,2048]{1,0:T(8,128)(2,1)}, u32[]{:S(2)}, u32[]{:S(2)}) collective-permute-start(bf16[128,2048]{1,0:T(8,128)(2,1)} %get-tuple-element.116), channel_id=1, source_target_pairs={{0,4},{4,0},{8,12},{12,8},{1,5},{5,1},{9,13},{13,9},{2,6},{6,2},{1... | collective-permute-start | bytes 1572872 | tf_op jit(solution)/shard_map/ppermute | solution.py:57
  431.5 31.6 %collective-permute-done.48 = bf16[128,2048]{1,0:T(8,128)(2,1)S(1)} collective-permute-done((bf16[128,2048]{1,0:T(8,128)(2,1)S(1)}, bf16[128,2048]{1,0:T(8,128)(2,1)S(1)}, u32[]{:S(2)}, u32[]{:S(2)}) %collective-permute-start.48) | collective-permute-done | bytes 524320 | tf_op jit(solution)/shard_map/ppermute | solution.py:57
  469.3 14.2 %collective-permute-done.42 = bf16[128,2048]{1,0:T(8,128)(2,1)} collective-permute-done((bf16[128,2048]{1,0:T(8,128)(2,1)}, bf16[128,2048]{1,0:T(8,128)(2,1)}, u32[]{:S(2)}, u32[]{:S(2)}) %collective-permute-start.42) | collective-permute-done | bytes 524320 | tf_op jit(solution)/shard_map/ppermute | solution.py:57
  494.0 3.3 fusion.138
  497.7 5.2 convolution_convert_fusion
  509.1 3.7 fusion.35
  515.2 7.4 fusion.16
  522.7 8.9 %fusion.1 = bf16[8,256,2048]{1,2,0:T(8,128)(2,1)S(1)} fusion(f32[2048,256,8]{1,0,2:T(8,128)} %get-tuple-element.184, f32[8,256]{1,0:T(8,128)S(1)} %multiply_reduce_fusion.1, f32[8,256]{1,0:T(8,128)S(1)} %log_add_fusion, pred[256,2048]{0,1:T(8,128)(4,1)S(1)} %compare_and_fusion, bf16[256,8,128]{0,2,1:T(8,128)(2,1)S(1)} %copy.209, ...), kind=kOutput, calls=%fused_computation.4 | convolution fusion | flops 1098907648 | bytes 26755072 | tf_op jit(solution)/shard_map/thd,kd->htk/dot_general | solution.py:306
  534.1 3.5 fusion.33
  539.5 3.5 fusion.21
  547.8 15.3 %collective-permute-done.53 = bf16[512,256]{1,0:T(8,128)(2,1)S(1)} collective-permute-done((bf16[512,256]{1,0:T(8,128)(2,1)S(1)}, bf16[512,256]{1,0:T(8,128)(2,1)S(1)}, u32[]{:S(2)}, u32[]{:S(2)}) %collective-permute-start.53) | collective-permute-done | bytes 262176 | tf_op jit(solution)/shard_map/ppermute | solution.py:53
  589.7 5.8 fusion.131
  597.5 5.4 fusion.132
  605.3 5.2 fusion.133
  613.9 3.7 convert_add_fusion.4
  621.4 3.2 convert_add_fusion.3
  632.7 4.5 collective-permute-done.94
  637.4 4.0 collective-permute-done.59
  652.8 4.0 collective-permute-done.77
  658.7 53.0 %collective-permute-done.87 = bf16[256,1408]{1,0:T(8,128)(2,1)S(1)} collective-permute-done((bf16[256,1408]{1,0:T(8,128)(2,1)S(1)}, bf16[256,1408]{1,0:T(8,128)(2,1)S(1)}, u32[]{:S(2)}, u32[]{:S(2)}) %collective-permute-start.87) | collective-permute-done | bytes 720928 | tf_op jit(solution)/shard_map/ppermute | solution.py:53
  713.0 8.8 %collective-permute-done.95 = bf16[256,1408]{1,0:T(8,128)(2,1)S(1)} collective-permute-done((bf16[256,1408]{1,0:T(8,128)(2,1)S(1)}, bf16[256,1408]{1,0:T(8,128)(2,1)S(1)}, u32[]{:S(2)}, u32[]{:S(2)}) %collective-permute-start.95) | collective-permute-done | bytes 720928 | tf_op jit(solution)/shard_map/ppermute | solution.py:53
  724.3 4.8 collective-permute-done.88
  732.1 8.6 %collective-permute-done.89 = bf16[64,1408]{1,0:T(8,128)(2,1)S(1)} collective-permute-done((bf16[64,1408]{1,0:T(8,128)(2,1)S(1)}, bf16[64,1408]{1,0:T(8,128)(2,1)S(1)}, u32[]{:S(2)}, u32[]{:S(2)}) %collective-permute-start.89) | collective-permute-done | bytes 180256 | tf_op jit(solution)/shard_map/ppermute | solution.py:57
  742.1 5.9 collective-permute-done.90
  748.2 5.6 collective-permute-done.96
  754.0 12.0 %collective-permute-done.97 = bf16[64,1408]{1,0:T(8,128)(2,1)S(1)} collective-permute-done((bf16[64,1408]{1,0:T(8,128)(2,1)S(1)}, bf16[64,1408]{1,0:T(8,128)(2,1)S(1)}, u32[]{:S(2)}, u32[]{:S(2)}) %collective-permute-start.97) | collective-permute-done | bytes 180256 | tf_op jit(solution)/shard_map/ppermute | solution.py:57
  768.3 5.3 collective-permute-done.98
  776.9 4.0 collective-permute-done.82
  781.9 4.9 dynamic_update_slice.105
  786.8 7.0 dynamic_update_slice.106
  793.8 7.0 dynamic_update_slice.107
  816.5 6.1 collective-permute-start.71
  822.6 10.7 %collective-permute-done.66 = bf16[2,64,1024]{2,1,0:T(8,128)(2,1)S(1)} collective-permute-done((bf16[2,64,1024]{2,1,0:T(8,128)(2,1)S(1)}, bf16[2,64,1024]{2,1,0:T(8,128)(2,1)S(1)}, u32[]{:S(2)}, u32[]{:S(2)}) %collective-permute-start.66) | collective-permute-done | bytes 262176 | tf_op jit(solution)/shard_map/ppermute | solution.py:57
  834.8 5.4 collective-permute-done.72
  (579 shorter events, 286.5 us)
Async XLA Ops:
  2.7 52.5 %collective-permute-start.1 = (bf16[80,256]{1,0:T(8,128)(2,1)}, bf16[80,256]{1,0:T(8,128)(2,1)}, u32[]{:S(2)}, u32[]{:S(2)}) collective-permute-start(bf16[80,256]{1,0:T(8,128)(2,1)} %pad_maximum_fusion.41), channel_id=1, source_target_pairs={{0,4},{4,0},{8,12},{12,8},{1,5},{5,1},{9,13},{13,9},{2,6},{6,2},{1... | collective-permute-start | bytes 122888 | tf_op jit(solution)/shard_map/ppermute | solution.py:57
  5.8 52.5 %collective-permute-start.2 = (bf16[80,256]{1,0:T(8,128)(2,1)}, bf16[80,256]{1,0:T(8,128)(2,1)}, u32[]{:S(2)}, u32[]{:S(2)}) collective-permute-start(bf16[80,256]{1,0:T(8,128)(2,1)} %pad_maximum_fusion.41), channel_id=1, source_target_pairs={{0,8},{4,12},{8,0},{12,4},{1,9},{5,13},{9,1},{13,5},{2,10},{6,14},... | collective-permute-start | bytes 122888 | tf_op jit(solution)/shard_map/ppermute | solution.py:57
  8.3 51.8 %collective-permute-start.3 = (bf16[80,256]{1,0:T(8,128)(2,1)}, bf16[80,256]{1,0:T(8,128)(2,1)}, u32[]{:S(2)}, u32[]{:S(2)}) collective-permute-start(bf16[80,256]{1,0:T(8,128)(2,1)} %pad_maximum_fusion.41), channel_id=1, source_target_pairs={{0,12},{4,8},{8,4},{12,0},{1,13},{5,9},{9,5},{13,1},{2,14},{6,10},... | collective-permute-start | bytes 122888 | tf_op jit(solution)/shard_map/ppermute | solution.py:57
  22.9 98.8 %collective-permute-start.29 = (bf16[3,64,1408]{2,1,0:T(8,128)(2,1)}, bf16[3,64,1408]{2,1,0:T(8,128)(2,1)}, u32[]{:S(2)}, u32[]{:S(2)}) collective-permute-start(bf16[3,64,1408]{2,1,0:T(8,128)(2,1)} %bitcast.463), channel_id=1, source_target_pairs={{0,4},{4,0},{8,12},{12,8},{1,5},{5,1},{9,13},{13,9},{2,6},{6,2},{1... | collective-permute-start | bytes 1622024 | tf_op jit(solution)/shard_map/ppermute | solution.py:57
  24.7 98.9 %collective-permute-start.30 = (bf16[3,64,1408]{2,1,0:T(8,128)(2,1)}, bf16[3,64,1408]{2,1,0:T(8,128)(2,1)}, u32[]{:S(2)}, u32[]{:S(2)}) collective-permute-start(bf16[3,64,1408]{2,1,0:T(8,128)(2,1)} %bitcast.462), channel_id=1, source_target_pairs={{0,8},{4,12},{8,0},{12,4},{1,9},{5,13},{9,1},{13,5},{2,10},{6,14},... | collective-permute-start | bytes 1622024 | tf_op jit(solution)/shard_map/ppermute | solution.py:57
  71.5 46.8 %collective-permute-start = (bf16[128,2048]{1,0:T(8,128)(2,1)S(1)}, bf16[128,2048]{1,0:T(8,128)(2,1)S(1)}, u32[]{:S(2)}, u32[]{:S(2)}) collective-permute-start(bf16[128,2048]{1,0:T(8,128)(2,1)S(1)} %copy.169), channel_id=1, source_target_pairs={{0,2},{2,0},{1,3},{3,1},{4,6},{6,4},{5,7},{7,5},{8,10},{10,8},{9,1... | collective-permute-start | bytes 1572872 | tf_op jit(solution)/shard_map/ppermute | solution.py:53
  73.1 17.2 %collective-permute-start.15 = (bf16[2,64,1024]{2,1,0:T(8,128)(2,1)S(1)}, bf16[2,64,1024]{2,1,0:T(8,128)(2,1)S(1)}, u32[]{:S(2)}, u32[]{:S(2)}) collective-permute-start(bf16[2,64,1024]{2,1,0:T(8,128)(2,1)S(1)} %maximum_select_fusion.5), channel_id=1, source_target_pairs={{0,8},{4,12},{8,0},{12,4},{1,9},{5,13},{9,1},{13,5},{2,10},{6,14},... | collective-permute-start | bytes 786440 | tf_op jit(solution)/shard_map/ppermute | solution.py:57
  73.2 17.8 %collective-permute-start.16 = (bf16[2,64,1024]{2,1,0:T(8,128)(2,1)S(1)}, bf16[2,64,1024]{2,1,0:T(8,128)(2,1)S(1)}, u32[]{:S(2)}, u32[]{:S(2)}) collective-permute-start(bf16[2,64,1024]{2,1,0:T(8,128)(2,1)S(1)} %maximum_select_fusion.5), channel_id=1, source_target_pairs={{0,12},{4,8},{8,4},{12,0},{1,13},{5,9},{9,5},{13,1},{2,14},{6,10},... | collective-permute-start | bytes 786440 | tf_op jit(solution)/shard_map/ppermute | solution.py:57
  91.0 23.1 %collective-permute-start.21 = (bf16[2,64,1024]{2,1,0:T(8,128)(2,1)S(1)}, bf16[2,64,1024]{2,1,0:T(8,128)(2,1)S(1)}, u32[]{:S(2)}, u32[]{:S(2)}) collective-permute-start(bf16[2,64,1024]{2,1,0:T(8,128)(2,1)S(1)} %maximum_select_fusion.7), channel_id=1, source_target_pairs={{0,8},{4,12},{8,0},{12,4},{1,9},{5,13},{9,1},{13,5},{2,10},{6,14},... | collective-permute-start | bytes 786440 | tf_op jit(solution)/shard_map/ppermute | solution.py:57
  101.6 16.0 %collective-permute-start.22 = (bf16[2,64,1024]{2,1,0:T(8,128)(2,1)S(1)}, bf16[2,64,1024]{2,1,0:T(8,128)(2,1)S(1)}, u32[]{:S(2)}, u32[]{:S(2)}) collective-permute-start(bf16[2,64,1024]{2,1,0:T(8,128)(2,1)S(1)} %maximum_select_fusion.7), channel_id=1, source_target_pairs={{0,12},{4,8},{8,4},{12,0},{1,13},{5,9},{9,5},{13,1},{2,14},{6,10},... | collective-permute-start | bytes 786440 | tf_op jit(solution)/shard_map/ppermute | solution.py:57
  114.1 14.9 %collective-permute-start.31 = (bf16[3,64,1408]{2,1,0:T(8,128)(2,1)}, bf16[3,64,1408]{2,1,0:T(8,128)(2,1)S(1)}, u32[]{:S(2)}, u32[]{:S(2)}) collective-permute-start(bf16[3,64,1408]{2,1,0:T(8,128)(2,1)} %bitcast.461), channel_id=1, source_target_pairs={{0,12},{4,8},{8,4},{12,0},{1,13},{5,9},{9,5},{13,1},{2,14},{6,10},... | collective-permute-start | bytes 1622024 | tf_op jit(solution)/shard_map/ppermute | solution.py:57
  118.3 42.1 %collective-permute-start.17 = (bf16[512,1024]{1,0:T(8,128)(2,1)}, bf16[512,1024]{1,0:T(8,128)(2,1)}, u32[]{:S(2)}, u32[]{:S(2)}) collective-permute-start(bf16[512,1024]{1,0:T(8,128)(2,1)} %bitcast.62), channel_id=1, source_target_pairs={{0,16},{16,0},{1,17},{17,1},{2,18},{18,2},{3,19},{19,3},{4,20},{20... | collective-permute-start | bytes 3145736 | tf_op jit(solution)/shard_map/ppermute | solution.py:53
  129.8 103.2 %collective-permute-start.32 = (bf16[3,256,1408]{2,1,0:T(8,128)(2,1)}, bf16[3,256,1408]{2,1,0:T(8,128)(2,1)}, u32[]{:S(2)}, u32[]{:S(2)}) collective-permute-start(bf16[3,256,1408]{2,1,0:T(8,128)(2,1)} %bitcast.86), channel_id=1, source_target_pairs={{0,2},{2,0},{1,3},{3,1},{4,6},{6,4},{5,7},{7,5},{8,10},{10,8},{9,1... | collective-permute-start | bytes 6488072 | tf_op jit(solution)/shard_map/ppermute | solution.py:53
  130.7 104.9 %collective-permute-start.33 = (bf16[3,256,1408]{2,1,0:T(8,128)(2,1)}, bf16[3,256,1408]{2,1,0:T(8,128)(2,1)}, u32[]{:S(2)}, u32[]{:S(2)}) collective-permute-start(bf16[3,256,1408]{2,1,0:T(8,128)(2,1)} %bitcast.86), channel_id=1, source_target_pairs={{0,16},{16,0},{1,17},{17,1},{2,18},{18,2},{3,19},{19,3},{4,20},{20... | collective-permute-start | bytes 6488072 | tf_op jit(solution)/shard_map/ppermute | solution.py:53
  135.6 18.6 %collective-permute-start.10 = (bf16[128,256]{1,0:T(8,128)(2,1)S(1)}, bf16[128,256]{1,0:T(8,128)(2,1)S(1)}, u32[]{:S(2)}, u32[]{:S(2)}) collective-permute-start(bf16[128,256]{1,0:T(8,128)(2,1)S(1)} %pad_maximum_fusion.39), channel_id=1, source_target_pairs={{0,12},{4,8},{8,4},{12,0},{1,13},{5,9},{9,5},{13,1},{2,14},{6,10},... | collective-permute-start | bytes 196616 | tf_op jit(solution)/shard_map/ppermute | solution.py:57
  140.9 15.6 %collective-permute-start.9 = (bf16[128,256]{1,0:T(8,128)(2,1)S(1)}, bf16[128,256]{1,0:T(8,128)(2,1)S(1)}, u32[]{:S(2)}, u32[]{:S(2)}) collective-permute-start(bf16[128,256]{1,0:T(8,128)(2,1)S(1)} %pad_maximum_fusion.39), channel_id=1, source_target_pairs={{0,8},{4,12},{8,0},{12,4},{1,9},{5,13},{9,1},{13,5},{2,10},{6,14},... | collective-permute-start | bytes 196616 | tf_op jit(solution)/shard_map/ppermute | solution.py:57
  156.5 56.5 %collective-permute-start.23 = (bf16[512,1024]{1,0:T(8,128)(2,1)}, bf16[512,1024]{1,0:T(8,128)(2,1)}, u32[]{:S(2)}, u32[]{:S(2)}) collective-permute-start(bf16[512,1024]{1,0:T(8,128)(2,1)} %bitcast.76), channel_id=1, source_target_pairs={{0,16},{16,0},{1,17},{17,1},{2,18},{18,2},{3,19},{19,3},{4,20},{20... | collective-permute-start | bytes 3145736 | tf_op jit(solution)/shard_map/ppermute | solution.py:53
  158.6 23.8 %collective-permute-start.11 = (bf16[1,4,128,256]{3,2,1,0:T(8,128)(2,1)S(1)}, bf16[1,4,128,256]{3,2,1,0:T(8,128)(2,1)S(1)}, u32[]{:S(2)}, u32[]{:S(2)}) collective-permute-start(bf16[1,4,128,256]{3,2,1,0:T(8,128)(2,1)S(1)} %get-tuple-element.165), channel_id=1, source_target_pairs={{0,2},{2,0},{1,3},{3,1},{4,6},{6,4},{5,7},{7,5},{8,10},{10,8},{9,1... | collective-permute-start | bytes 786440 | tf_op jit(solution)/shard_map/ppermute | solution.py:53
  163.5 80.6 %collective-permute-start.18 = (bf16[1024,1024]{1,0:T(8,128)(2,1)}, bf16[1024,1024]{1,0:T(8,128)(2,1)}, u32[]{:S(2)}, u32[]{:S(2)}) collective-permute-start(bf16[1024,1024]{1,0:T(8,128)(2,1)} %pad_maximum_fusion.2), channel_id=1, source_target_pairs={{0,1},{1,0},{2,3},{3,2},{4,5},{5,4},{6,7},{7,6},{8,9},{9,8},{10,11... | collective-permute-start | bytes 6291464 | tf_op jit(solution)/shard_map/ppermute | solution.py:53
  182.4 34.7 %collective-permute-start.12 = (bf16[2,1,4,128,256]{4,3,2,1,0:T(8,128)(2,1)S(1)}, bf16[2,1,4,128,256]{4,3,2,1,0:T(8,128)(2,1)}, u32[]{:S(2)}, u32[]{:S(2)}) collective-permute-start(bf16[2,1,4,128,256]{4,3,2,1,0:T(8,128)(2,1)S(1)} %get-tuple-element.159), channel_id=1, source_target_pairs={{0,1},{1,0},{2,3},{3,2},{4,5},{5,4},{6,7},{7,6},{8,9},{9,8},{10,11... | collective-permute-start | bytes 1572872 | tf_op jit(solution)/shard_map/ppermute | solution.py:53
  213.0 118.0 %collective-permute-start.46 = (bf16[128,2048]{0,1:T(8,128)(2,1)}, bf16[128,2048]{0,1:T(8,128)(2,1)}, u32[]{:S(2)}, u32[]{:S(2)}) collective-permute-start(bf16[128,2048]{0,1:T(8,128)(2,1)} %bitcast.541), channel_id=1, source_target_pairs={{0,12},{4,8},{8,4},{12,0},{1,13},{5,9},{9,5},{13,1},{2,14},{6,10},... | collective-permute-start | bytes 1572872 | tf_op jit(solution)/shard_map/ppermute | solution.py:57
  217.2 115.1 %collective-permute-start.45 = (bf16[128,2048]{0,1:T(8,128)(2,1)}, bf16[128,2048]{0,1:T(8,128)(2,1)}, u32[]{:S(2)}, u32[]{:S(2)}) collective-permute-start(bf16[128,2048]{0,1:T(8,128)(2,1)} %bitcast.542), channel_id=1, source_target_pairs={{0,8},{4,12},{8,0},{12,4},{1,9},{5,13},{9,1},{13,5},{2,10},{6,14},... | collective-permute-start | bytes 1572872 | tf_op jit(solution)/shard_map/ppermute | solution.py:57
  233.0 69.4 %collective-permute-start.36 = (bf16[3,256,1408]{2,1,0:T(8,128)(2,1)}, bf16[3,256,1408]{2,1,0:T(8,128)(2,1)}, u32[]{:S(2)}, u32[]{:S(2)}) collective-permute-start(bf16[3,256,1408]{2,1,0:T(8,128)(2,1)} %bitcast.86), channel_id=1, source_target_pairs={{0,1},{1,0},{2,3},{3,2},{4,5},{5,4},{6,7},{7,6},{8,9},{9,8},{10,11... | collective-permute-start | bytes 6488072 | tf_op jit(solution)/shard_map/ppermute | solution.py:53
  235.7 39.8 %collective-permute-start.24 = (bf16[1024,1024]{1,0:T(8,128)(2,1)}, bf16[1024,1024]{1,0:T(8,128)(2,1)}, u32[]{:S(2)}, u32[]{:S(2)}) collective-permute-start(bf16[1024,1024]{1,0:T(8,128)(2,1)} %pad_maximum_fusion.3), channel_id=1, source_target_pairs={{0,1},{1,0},{2,3},{3,2},{4,5},{5,4},{6,7},{7,6},{8,9},{9,8},{10,11... | collective-permute-start | bytes 6291464 | tf_op jit(solution)/shard_map/ppermute | solution.py:53
  244.1 35.3 %collective-permute-start.34 = (bf16[3,128,1408]{2,1,0:T(8,128)(2,1)}, bf16[3,128,1408]{2,1,0:T(8,128)(2,1)}, u32[]{:S(2)}, u32[]{:S(2)}) collective-permute-start(bf16[3,128,1408]{2,1,0:T(8,128)(2,1)} %slice.553), channel_id=1, source_target_pairs={{0,16},{16,0},{1,17},{17,1},{2,18},{18,2},{3,19},{19,3},{4,20},{20... | collective-permute-start | bytes 3244040 | tf_op jit(solution)/shard_map/ppermute | solution.py:53
  275.5 25.9 %collective-permute-start.35 = (bf16[3,128,1408]{2,1,0:T(8,128)(2,1)S(1)}, bf16[3,128,1408]{2,1,0:T(8,128)(2,1)S(1)}, u32[]{:S(2)}, u32[]{:S(2)}) collective-permute-start(bf16[3,128,1408]{2,1,0:T(8,128)(2,1)S(1)} %copy-done.38), channel_id=1, source_target_pairs={{0,2},{2,0},{1,3},{3,1},{4,6},{6,4},{5,7},{7,5},{8,10},{10,8},{9,1... | collective-permute-start | bytes 3244040 | tf_op jit(solution)/shard_map/ppermute | solution.py:53
  279.4 38.2 %collective-permute-start.37 = (bf16[3,256,1408]{2,1,0:T(8,128)(2,1)}, bf16[3,256,1408]{2,1,0:T(8,128)(2,1)}, u32[]{:S(2)}, u32[]{:S(2)}) collective-permute-start(bf16[3,256,1408]{2,1,0:T(8,128)(2,1)} %collective-permute-done.32), channel_id=1, source_target_pairs={{0,1},{1,0},{2,3},{3,2},{4,5},{5,4},{6,7},{7,6},{8,9},{9,8},{10,11... | collective-permute-start | bytes 6488072 | tf_op jit(solution)/shard_map/ppermute | solution.py:53
  301.4 19.8 %collective-permute-start.38 = (bf16[3,256,1408]{2,1,0:T(8,128)(2,1)}, bf16[3,256,1408]{2,1,0:T(8,128)(2,1)}, u32[]{:S(2)}, u32[]{:S(2)}) collective-permute-start(bf16[3,256,1408]{2,1,0:T(8,128)(2,1)} %collective-permute-done.33), channel_id=1, source_target_pairs={{0,1},{1,0},{2,3},{3,2},{4,5},{5,4},{6,7},{7,6},{8,9},{9,8},{10,11... | collective-permute-start | bytes 6488072 | tf_op jit(solution)/shard_map/ppermute | solution.py:53
  321.1 15.4 %collective-permute-start.44 = (bf16[128,2048]{0,1:T(8,128)(2,1)S(1)}, bf16[128,2048]{0,1:T(8,128)(2,1)S(1)}, u32[]{:S(2)}, u32[]{:S(2)}) collective-permute-start(bf16[128,2048]{0,1:T(8,128)(2,1)S(1)} %bitcast.543), channel_id=1, source_target_pairs={{0,4},{4,0},{8,12},{12,8},{1,5},{5,1},{9,13},{13,9},{2,6},{6,2},{1... | collective-permute-start | bytes 1572872 | tf_op jit(solution)/shard_map/ppermute | solution.py:57
  324.5 23.4 %collective-permute-start.28 = (bf16[128,2048]{0,1:T(8,128)(2,1)S(1)}, bf16[128,2048]{0,1:T(8,128)(2,1)S(1)}, u32[]{:S(2)}, u32[]{:S(2)}) collective-permute-start(bf16[128,2048]{0,1:T(8,128)(2,1)S(1)} %bitcast.546), channel_id=1, source_target_pairs={{0,12},{4,8},{8,4},{12,0},{1,13},{5,9},{9,5},{13,1},{2,14},{6,10},... | collective-permute-start | bytes 1572872 | tf_op jit(solution)/shard_map/ppermute | solution.py:57
  329.2 43.8 %collective-permute-start.27 = (bf16[128,2048]{0,1:T(8,128)(2,1)S(1)}, bf16[128,2048]{0,1:T(8,128)(2,1)S(1)}, u32[]{:S(2)}, u32[]{:S(2)}) collective-permute-start(bf16[128,2048]{0,1:T(8,128)(2,1)S(1)} %bitcast.547), channel_id=1, source_target_pairs={{0,8},{4,12},{8,0},{12,4},{1,9},{5,13},{9,1},{13,5},{2,10},{6,14},... | collective-permute-start | bytes 1572872 | tf_op jit(solution)/shard_map/ppermute | solution.py:57
  331.0 42.0 %collective-permute-start.26 = (bf16[128,2048]{0,1:T(8,128)(2,1)S(1)}, bf16[128,2048]{0,1:T(8,128)(2,1)S(1)}, u32[]{:S(2)}, u32[]{:S(2)}) collective-permute-start(bf16[128,2048]{0,1:T(8,128)(2,1)S(1)} %bitcast.548), channel_id=1, source_target_pairs={{0,4},{4,0},{8,12},{12,8},{1,5},{5,1},{9,13},{13,9},{2,6},{6,2},{1... | collective-permute-start | bytes 1572872 | tf_op jit(solution)/shard_map/ppermute | solution.py:57
  392.7 24.9 %collective-permute-start.49 = (bf16[128,2048]{1,0:T(8,128)(2,1)S(1)}, bf16[128,2048]{1,0:T(8,128)(2,1)S(1)}, u32[]{:S(2)}, u32[]{:S(2)}) collective-permute-start(bf16[128,2048]{1,0:T(8,128)(2,1)S(1)} %get-tuple-element.114), channel_id=1, source_target_pairs={{0,12},{4,8},{8,4},{12,0},{1,13},{5,9},{9,5},{13,1},{2,14},{6,10},... | collective-permute-start | bytes 1572872 | tf_op jit(solution)/shard_map/ppermute | solution.py:57
  395.4 67.6 %collective-permute-start.48 = (bf16[128,2048]{1,0:T(8,128)(2,1)S(1)}, bf16[128,2048]{1,0:T(8,128)(2,1)S(1)}, u32[]{:S(2)}, u32[]{:S(2)}) collective-permute-start(bf16[128,2048]{1,0:T(8,128)(2,1)S(1)} %get-tuple-element.115), channel_id=1, source_target_pairs={{0,8},{4,12},{8,0},{12,4},{1,9},{5,13},{9,1},{13,5},{2,10},{6,14},... | collective-permute-start | bytes 1572872 | tf_op jit(solution)/shard_map/ppermute | solution.py:57
  395.4 67.6 %collective-permute-start.47 = (bf16[128,2048]{1,0:T(8,128)(2,1)S(1)}, bf16[128,2048]{1,0:T(8,128)(2,1)S(1)}, u32[]{:S(2)}, u32[]{:S(2)}) collective-permute-start(bf16[128,2048]{1,0:T(8,128)(2,1)S(1)} %get-tuple-element.113), channel_id=1, source_target_pairs={{0,4},{4,0},{8,12},{12,8},{1,5},{5,1},{9,13},{13,9},{2,6},{6,2},{1... | collective-permute-start | bytes 1572872 | tf_op jit(solution)/shard_map/ppermute | solution.py:57
  403.4 65.9 %collective-permute-start.43 = (bf16[128,2048]{1,0:T(8,128)(2,1)}, bf16[128,2048]{1,0:T(8,128)(2,1)S(1)}, u32[]{:S(2)}, u32[]{:S(2)}) collective-permute-start(bf16[128,2048]{1,0:T(8,128)(2,1)} %get-tuple-element.117), channel_id=1, source_target_pairs={{0,12},{4,8},{8,4},{12,0},{1,13},{5,9},{9,5},{13,1},{2,14},{6,10},... | collective-permute-start | bytes 1572872 | tf_op jit(solution)/shard_map/ppermute | solution.py:57
  406.0 77.4 %collective-permute-start.42 = (bf16[128,2048]{1,0:T(8,128)(2,1)}, bf16[128,2048]{1,0:T(8,128)(2,1)}, u32[]{:S(2)}, u32[]{:S(2)}) collective-permute-start(bf16[128,2048]{1,0:T(8,128)(2,1)} %get-tuple-element.118), channel_id=1, source_target_pairs={{0,8},{4,12},{8,0},{12,4},{1,9},{5,13},{9,1},{13,5},{2,10},{6,14},... | collective-permute-start | bytes 1572872 | tf_op jit(solution)/shard_map/ppermute | solution.py:57
  417.6 65.9 %collective-permute-start.41 = (bf16[128,2048]{1,0:T(8,128)(2,1)}, bf16[128,2048]{1,0:T(8,128)(2,1)}, u32[]{:S(2)}, u32[]{:S(2)}) collective-permute-start(bf16[128,2048]{1,0:T(8,128)(2,1)} %get-tuple-element.116), channel_id=1, source_target_pairs={{0,4},{4,0},{8,12},{12,8},{1,5},{5,1},{9,13},{13,9},{2,6},{6,2},{1... | collective-permute-start | bytes 1572872 | tf_op jit(solution)/shard_map/ppermute | solution.py:57
  463.1 125.4 %collective-permute-start.75 = (bf16[1024,1408]{1,0:T(8,128)(2,1)}, bf16[1024,1408]{1,0:T(8,128)(2,1)}, u32[]{:S(2)}, u32[]{:S(2)}) collective-permute-start(bf16[1024,1408]{1,0:T(8,128)(2,1)} %slice.622), channel_id=1, source_target_pairs={{0,1},{1,0},{2,3},{3,2},{4,5},{5,4},{6,7},{7,6},{8,9},{9,8},{10,11... | collective-permute-start | bytes 8650760 | tf_op jit(solution)/shard_map/ppermute | solution.py:53
  543.1 30.6 %collective-permute-start.51 = (bf16[128,2048]{1,0:T(8,128)(2,1)S(1)}, bf16[128,2048]{1,0:T(8,128)(2,1)S(1)}, u32[]{:S(2)}, u32[]{:S(2)}) collective-permute-start(bf16[128,2048]{1,0:T(8,128)(2,1)S(1)} %slice.868), channel_id=1, source_target_pairs={{0,2},{2,0},{1,3},{3,1},{4,6},{6,4},{5,7},{7,5},{8,10},{10,8},{9,1... | collective-permute-start | bytes 1572872 | tf_op jit(solution)/shard_map/ppermute | solution.py:53
  545.5 17.6 %collective-permute-start.53 = (bf16[512,256]{1,0:T(8,128)(2,1)S(1)}, bf16[512,256]{1,0:T(8,128)(2,1)S(1)}, u32[]{:S(2)}, u32[]{:S(2)}) collective-permute-start(bf16[512,256]{1,0:T(8,128)(2,1)S(1)} %slice.871), channel_id=1, source_target_pairs={{0,2},{2,0},{1,3},{3,1},{4,6},{6,4},{5,7},{7,5},{8,10},{10,8},{9,1... | collective-permute-start | bytes 786440 | tf_op jit(solution)/shard_map/ppermute | solution.py:53
  572.9 23.7 %collective-permute-start.83 = (bf16[1024,1408]{1,0:T(8,128)(2,1)}, bf16[1024,1408]{1,0:T(8,128)(2,1)}, u32[]{:S(2)}, u32[]{:S(2)}) collective-permute-start(bf16[1024,1408]{1,0:T(8,128)(2,1)} %slice.631), channel_id=1, source_target_pairs={{0,1},{1,0},{2,3},{3,2},{4,5},{5,4},{6,7},{7,6},{8,9},{9,8},{10,11... | collective-permute-start | bytes 8650760 | tf_op jit(solution)/shard_map/ppermute | solution.py:53
  572.9 31.2 %collective-permute-start.91 = (bf16[1024,1408]{1,0:T(8,128)(2,1)}, bf16[1024,1408]{1,0:T(8,128)(2,1)}, u32[]{:S(2)}, u32[]{:S(2)}) collective-permute-start(bf16[1024,1408]{1,0:T(8,128)(2,1)} %slice.640), channel_id=1, source_target_pairs={{0,1},{1,0},{2,3},{3,2},{4,5},{5,4},{6,7},{7,6},{8,9},{9,8},{10,11... | collective-permute-start | bytes 8650760 | tf_op jit(solution)/shard_map/ppermute | solution.py:53
  573.4 39.5 %collective-permute-start.63 = (bf16[1024,1024]{1,0:T(8,128)(2,1)}, bf16[1024,1024]{1,0:T(8,128)(2,1)}, u32[]{:S(2)}, u32[]{:S(2)}) collective-permute-start(bf16[1024,1024]{1,0:T(8,128)(2,1)} %slice.612), channel_id=1, source_target_pairs={{0,1},{1,0},{2,3},{3,2},{4,5},{5,4},{6,7},{7,6},{8,9},{9,8},{10,11... | collective-permute-start | bytes 6291464 | tf_op jit(solution)/shard_map/ppermute | solution.py:53
  586.8 33.4 %collective-permute-start.69 = (bf16[1024,1024]{1,0:T(8,128)(2,1)}, bf16[1024,1024]{1,0:T(8,128)(2,1)}, u32[]{:S(2)}, u32[]{:S(2)}) collective-permute-start(bf16[1024,1024]{1,0:T(8,128)(2,1)} %slice.617), channel_id=1, source_target_pairs={{0,1},{1,0},{2,3},{3,2},{4,5},{5,4},{6,7},{7,6},{8,9},{9,8},{10,11... | collective-permute-start | bytes 6291464 | tf_op jit(solution)/shard_map/ppermute | solution.py:53
  588.5 23.0 %collective-permute-start.58 = (bf16[512,384]{0,1:T(8,128)(2,1)S(1)}, bf16[512,384]{0,1:T(8,128)(2,1)S(1)}, u32[]{:S(2)}, u32[]{:S(2)}) collective-permute-start(bf16[512,384]{0,1:T(8,128)(2,1)S(1)} %slice.870), channel_id=1, source_target_pairs={{0,16},{16,0},{1,17},{17,1},{2,18},{18,2},{3,19},{19,3},{4,20},{20... | collective-permute-start | bytes 1179656 | tf_op jit(solution)/shard_map/ppermute | solution.py:53
  596.6 29.2 %collective-permute-start.76 = (bf16[128,1408]{1,0:T(8,128)(2,1)}, bf16[128,1408]{1,0:T(8,128)(2,1)}, u32[]{:S(2)}, u32[]{:S(2)}) collective-permute-start(bf16[128,1408]{1,0:T(8,128)(2,1)} %get-tuple-element.85), channel_id=1, source_target_pairs={{0,16},{16,0},{1,17},{17,1},{2,18},{18,2},{3,19},{19,3},{4,20},{20... | collective-permute-start | bytes 1081352 | tf_op jit(solution)/shard_map/ppermute | solution.py:53
  604.1 22.6 %collective-permute-start.78 = (bf16[128,1408]{1,0:T(8,128)(2,1)}, bf16[128,1408]{1,0:T(8,128)(2,1)}, u32[]{:S(2)}, u32[]{:S(2)}) collective-permute-start(bf16[128,1408]{1,0:T(8,128)(2,1)} %get-tuple-element.86), channel_id=1, source_target_pairs={{0,2},{2,0},{1,3},{3,1},{4,6},{6,4},{5,7},{7,5},{8,10},{10,8},{9,1... | collective-permute-start | bytes 1081352 | tf_op jit(solution)/shard_map/ppermute | solution.py:53
  611.5 17.9 %collective-permute-start.84 = (bf16[128,1408]{1,0:T(8,128)(2,1)}, bf16[128,1408]{1,0:T(8,128)(2,1)}, u32[]{:S(2)}, u32[]{:S(2)}) collective-permute-start(bf16[128,1408]{1,0:T(8,128)(2,1)} %get-tuple-element.81), channel_id=1, source_target_pairs={{0,16},{16,0},{1,17},{17,1},{2,18},{18,2},{3,19},{19,3},{4,20},{20... | collective-permute-start | bytes 1081352 | tf_op jit(solution)/shard_map/ppermute | solution.py:53
  612.9 17.5 %collective-permute-start.86 = (bf16[128,1408]{1,0:T(8,128)(2,1)}, bf16[128,1408]{1,0:T(8,128)(2,1)S(1)}, u32[]{:S(2)}, u32[]{:S(2)}) collective-permute-start(bf16[128,1408]{1,0:T(8,128)(2,1)} %get-tuple-element.82), channel_id=1, source_target_pairs={{0,2},{2,0},{1,3},{3,1},{4,6},{6,4},{5,7},{7,5},{8,10},{10,8},{9,1... | collective-permute-start | bytes 1081352 | tf_op jit(solution)/shard_map/ppermute | solution.py:53
  629.5 22.4 %collective-permute-start.79 = (bf16[256,1408]{1,0:T(8,128)(2,1)S(1)}, bf16[256,1408]{1,0:T(8,128)(2,1)S(1)}, u32[]{:S(2)}, u32[]{:S(2)}) collective-permute-start(bf16[256,1408]{1,0:T(8,128)(2,1)S(1)} %pad_maximum_fusion.22), channel_id=1, source_target_pairs={{0,16},{16,0},{1,17},{17,1},{2,18},{18,2},{3,19},{19,3},{4,20},{20... | collective-permute-start | bytes 2162696 | tf_op jit(solution)/shard_map/ppermute | solution.py:53
  630.4 26.4 %collective-permute-start.77 = (bf16[256,1408]{1,0:T(8,128)(2,1)S(1)}, bf16[256,1408]{1,0:T(8,128)(2,1)S(1)}, u32[]{:S(2)}, u32[]{:S(2)}) collective-permute-start(bf16[256,1408]{1,0:T(8,128)(2,1)S(1)} %pad_maximum_fusion.21), channel_id=1, source_target_pairs={{0,2},{2,0},{1,3},{3,1},{4,6},{6,4},{5,7},{7,5},{8,10},{10,8},{9,1... | collective-permute-start | bytes 2162696 | tf_op jit(solution)/shard_map/ppermute | solution.py:53
  647.5 157.2 %collective-permute-start.64 = (bf16[512,1024]{1,0:T(8,128)(2,1)}, bf16[512,1024]{1,0:T(8,128)(2,1)}, u32[]{:S(2)}, u32[]{:S(2)}) collective-permute-start(bf16[512,1024]{1,0:T(8,128)(2,1)} %slice.867), channel_id=1, source_target_pairs={{0,16},{16,0},{1,17},{17,1},{2,18},{18,2},{3,19},{19,3},{4,20},{20... | collective-permute-start | bytes 3145736 | tf_op jit(solution)/shard_map/ppermute | solution.py:53
  648.5 163.5 %collective-permute-start.70 = (bf16[512,1024]{1,0:T(8,128)(2,1)}, bf16[512,1024]{1,0:T(8,128)(2,1)}, u32[]{:S(2)}, u32[]{:S(2)}) collective-permute-start(bf16[512,1024]{1,0:T(8,128)(2,1)} %slice.866), channel_id=1, source_target_pairs={{0,16},{16,0},{1,17},{17,1},{2,18},{18,2},{3,19},{19,3},{4,20},{20... | collective-permute-start | bytes 3145736 | tf_op jit(solution)/shard_map/ppermute | solution.py:53
  649.5 62.2 %collective-permute-start.87 = (bf16[256,1408]{1,0:T(8,128)(2,1)S(1)}, bf16[256,1408]{1,0:T(8,128)(2,1)S(1)}, u32[]{:S(2)}, u32[]{:S(2)}) collective-permute-start(bf16[256,1408]{1,0:T(8,128)(2,1)S(1)} %pad_maximum_fusion.24), channel_id=1, source_target_pairs={{0,16},{16,0},{1,17},{17,1},{2,18},{18,2},{3,19},{19,3},{4,20},{20... | collective-permute-start | bytes 2162696 | tf_op jit(solution)/shard_map/ppermute | solution.py:53
  651.9 60.6 %collective-permute-start.85 = (bf16[256,1408]{1,0:T(8,128)(2,1)S(1)}, bf16[256,1408]{1,0:T(8,128)(2,1)S(1)}, u32[]{:S(2)}, u32[]{:S(2)}) collective-permute-start(bf16[256,1408]{1,0:T(8,128)(2,1)S(1)} %pad_maximum_fusion.23), channel_id=1, source_target_pairs={{0,2},{2,0},{1,3},{3,1},{4,6},{6,4},{5,7},{7,5},{8,10},{10,8},{9,1... | collective-permute-start | bytes 2162696 | tf_op jit(solution)/shard_map/ppermute | solution.py:53
  656.8 64.9 %collective-permute-start.95 = (bf16[256,1408]{1,0:T(8,128)(2,1)S(1)}, bf16[256,1408]{1,0:T(8,128)(2,1)S(1)}, u32[]{:S(2)}, u32[]{:S(2)}) collective-permute-start(bf16[256,1408]{1,0:T(8,128)(2,1)S(1)} %pad_maximum_fusion.26), channel_id=1, source_target_pairs={{0,16},{16,0},{1,17},{17,1},{2,18},{18,2},{3,19},{19,3},{4,20},{20... | collective-permute-start | bytes 2162696 | tf_op jit(solution)/shard_map/ppermute | solution.py:53
  712.5 63.0 %collective-permute-start.80 = (bf16[64,1408]{1,0:T(8,128)(2,1)S(1)}, bf16[64,1408]{1,0:T(8,128)(2,1)S(1)}, u32[]{:S(2)}, u32[]{:S(2)}) collective-permute-start(bf16[64,1408]{1,0:T(8,128)(2,1)S(1)} %get-tuple-element.154), channel_id=1, source_target_pairs={{0,4},{4,0},{8,12},{12,8},{1,5},{5,1},{9,13},{13,9},{2,6},{6,2},{1... | collective-permute-start | bytes 540680 | tf_op jit(solution)/shard_map/ppermute | solution.py:57
  721.7 54.1 %collective-permute-start.81 = (bf16[64,1408]{1,0:T(8,128)(2,1)S(1)}, bf16[64,1408]{1,0:T(8,128)(2,1)S(1)}, u32[]{:S(2)}, u32[]{:S(2)}) collective-permute-start(bf16[64,1408]{1,0:T(8,128)(2,1)S(1)} %get-tuple-element.153), channel_id=1, source_target_pairs={{0,8},{4,12},{8,0},{12,4},{1,9},{5,13},{9,1},{13,5},{2,10},{6,14},... | collective-permute-start | bytes 540680 | tf_op jit(solution)/shard_map/ppermute | solution.py:57
  809.6 23.7 %collective-permute-start.66 = (bf16[2,64,1024]{2,1,0:T(8,128)(2,1)S(1)}, bf16[2,64,1024]{2,1,0:T(8,128)(2,1)S(1)}, u32[]{:S(2)}, u32[]{:S(2)}) collective-permute-start(bf16[2,64,1024]{2,1,0:T(8,128)(2,1)S(1)} %get-tuple-element.140), channel_id=1, source_target_pairs={{0,8},{4,12},{8,0},{12,4},{1,9},{5,13},{9,1},{13,5},{2,10},{6,14},... | collective-permute-start | bytes 786440 | tf_op jit(solution)/shard_map/ppermute | solution.py:57
  809.6 23.7 %collective-permute-start.65 = (bf16[2,64,1024]{2,1,0:T(8,128)(2,1)S(1)}, bf16[2,64,1024]{2,1,0:T(8,128)(2,1)S(1)}, u32[]{:S(2)}, u32[]{:S(2)}) collective-permute-start(bf16[2,64,1024]{2,1,0:T(8,128)(2,1)S(1)} %get-tuple-element.138), channel_id=1, source_target_pairs={{0,4},{4,0},{8,12},{12,8},{1,5},{5,1},{9,13},{13,9},{2,6},{6,2},{1... | collective-permute-start | bytes 786440 | tf_op jit(solution)/shard_map/ppermute | solution.py:57
  813.9 20.8 %collective-permute-start.73 = (bf16[2,64,1024]{2,1,0:T(8,128)(2,1)S(1)}, bf16[2,64,1024]{2,1,0:T(8,128)(2,1)S(1)}, u32[]{:S(2)}, u32[]{:S(2)}) collective-permute-start(bf16[2,64,1024]{2,1,0:T(8,128)(2,1)S(1)} %get-tuple-element.136), channel_id=1, source_target_pairs={{0,12},{4,8},{8,4},{12,0},{1,13},{5,9},{9,5},{13,1},{2,14},{6,10},... | collective-permute-start | bytes 786440 | tf_op jit(solution)/shard_map/ppermute | solution.py:57
  815.9 24.2 %collective-permute-start.72 = (bf16[2,64,1024]{2,1,0:T(8,128)(2,1)S(1)}, bf16[2,64,1024]{2,1,0:T(8,128)(2,1)S(1)}, u32[]{:S(2)}, u32[]{:S(2)}) collective-permute-start(bf16[2,64,1024]{2,1,0:T(8,128)(2,1)S(1)} %get-tuple-element.137), channel_id=1, source_target_pairs={{0,8},{4,12},{8,0},{12,4},{1,9},{5,13},{9,1},{13,5},{2,10},{6,14},... | collective-permute-start | bytes 786440 | tf_op jit(solution)/shard_map/ppermute | solution.py:57
  816.5 23.7 %collective-permute-start.71 = (bf16[2,64,1024]{2,1,0:T(8,128)(2,1)S(1)}, bf16[2,64,1024]{2,1,0:T(8,128)(2,1)S(1)}, u32[]{:S(2)}, u32[]{:S(2)}) collective-permute-start(bf16[2,64,1024]{2,1,0:T(8,128)(2,1)S(1)} %get-tuple-element.135), channel_id=1, source_target_pairs={{0,4},{4,0},{8,12},{12,8},{1,5},{5,1},{9,13},{13,9},{2,6},{6,2},{1... | collective-permute-start | bytes 786440 | tf_op jit(solution)/shard_map/ppermute | solution.py:57
  (114 other events, 1380.2 us)

commit v2 on v1

v2 whole, which is shorter than its diff:
```python
import math

import jax
import jax.numpy as jnp
from jax import lax
from jax.experimental import pallas as pl
from jax.experimental.pallas import tpu as pltpu
from jax.sharding import Mesh
from jax.sharding import PartitionSpec as P

HEAD_DIM = 128
EPSILON = 1e-05
NEGATIVE = -1e30
AXES = "yhlmxc"
BF16 = jnp.bfloat16
F32 = jnp.float32


def angles(offset):
    half_dim = HEAD_DIM // 2
    frequency = jnp.exp(
        jnp.arange(half_dim, dtype=F32) * (-2.0 * math.log(10000.0) / HEAD_DIM)
    )
    phases = offset.astype(F32)[:, None] * frequency[None, :]
    return (jnp.cos(phases), jnp.sin(phases))


def rotate(vectors, cosine, sine_part):
    half_dim = vectors.shape[-1] // 2
    first, second = vectors[..., :half_dim], vectors[..., half_dim:]
    return jnp.concatenate(
        [first * cosine - second * sine_part, second * cosine + first * sine_part], -1
    )


def dot(left, right):
    return jnp.dot(left, right, preferred_element_type=F32)


def contract_last(left, right):
    return lax.dot_general(left, right, (((1,), (1,)), ((), ())), preferred_element_type=F32)


def contract_first(left, right):
    return lax.dot_general(left, right, (((0,), (0,)), ((), ())), preferred_element_type=F32)


def norm_back(grad_normed, normed, scale_rows):
    return scale_rows * (
        grad_normed - normed * jnp.mean(grad_normed * normed, axis=-1, keepdims=True)
    )


def swap(value, axis):
    return lax.ppermute(value, axis, [(0, 1), (1, 0)])


def low(value):
    return value.astype(BF16)


def pick(stacked, index, axis=0):
    return lax.dynamic_index_in_dim(stacked, index, axis, keepdims=False)


def pair(own, other, index, axis=0):
    return jnp.where(
        index == 0, jnp.stack([own, other], axis), jnp.stack([other, own], axis)
    )


def gather_m(value, axis):
    if lax.axis_size("m") > 1:
        return lax.all_gather(value, "m", axis=axis)
    return jnp.expand_dims(value, axis)


def scatter_m(value, axis):
    if lax.axis_size("m") > 1:
        return lax.psum_scatter(value, "m", scatter_dimension=axis)
    return lax.squeeze(value, (axis,))


def fold(total, axis):
    half = total.shape[0] // 2
    return total[:half].astype(F32) + swap(low(total[half:]), axis).astype(F32)


def gather_group(value):
    return lax.all_to_all(jnp.broadcast_to(value, (4, *value.shape)), ("l", "x"), 0, 0)


def scatter_group(value):
    return jnp.sum(lax.all_to_all(low(value), ("l", "x"), 0, 0).astype(F32), axis=0)


LOG2E = math.log2(math.e)
SCALE = 1.0 / math.sqrt(HEAD_DIM)
NT = (((1,), (1,)), ((), ()))
NN = (((1,), (0,)), ((), ()))


def mxu(left, right, dims):
    return lax.dot_general(left, right, dims, preferred_element_type=F32)


def turn(vectors, cosine, sine_part):
    half = HEAD_DIM // 2
    first, second = vectors[:half], vectors[half:]
    return jnp.concatenate(
        [first * cosine - second * sine_part, second * cosine + first * sine_part], 0
    )


def fill_bias(bias, key_place, query_place, query_start):
    keys = bias.shape[0]
    block = 256
    for i in range(keys // block):
        at = key_place[i * block : (i + 1) * block, :]
        fits = (at <= query_place[...]) & (at >= query_start[...])
        bias[i * block : (i + 1) * block, :] = jnp.where(fits, 0.0, NEGATIVE)


def attend_kernel(
    query_sum, key, value_t, cosine, sine_part, key_place, query_place, query_start,
    query_rot, attended, attended_low, lse, bias,
):
    fill_bias(bias, key_place, query_place, query_start)
    for head in range(query_sum.shape[0] // HEAD_DIM):
        at = slice(head * HEAD_DIM, (head + 1) * HEAD_DIM)
        query = turn(query_sum[at, :], cosine[...], sine_part[...]).astype(BF16)
        query_rot[at, :] = query
        scores = mxu(key[...], query, NN) * (SCALE * LOG2E) + bias[...]
        top = jnp.max(scores, axis=0, keepdims=True)
        weights = jnp.exp2(scores - top)
        total = jnp.sum(weights, axis=0, keepdims=True)
        result = mxu(value_t[...], weights.astype(BF16), NN) / total
        attended[at, :] = result
        attended_low[at, :] = result.astype(BF16)
        lse[head : head + 1, :] = top + jnp.log2(total)


def attend_back_kernel(
    query_rot, key, key_t, value, grad, attended, lse, cosine, sine_part, key_place,
    query_place, query_start, query_grad, kv_grad, bias,
):
    fill_bias(bias, key_place, query_place, query_start)
    for head in range(query_rot.shape[0] // HEAD_DIM):
        at = slice(head * HEAD_DIM, (head + 1) * HEAD_DIM)
        query = query_rot[at, :]
        grad_head = grad[at, :]
        delta = jnp.sum(grad_head.astype(F32) * attended[at, :], axis=0, keepdims=True)
        scores = mxu(key[...], query, NN) * (SCALE * LOG2E) + bias[...]
        probs = jnp.exp2(scores - lse[head : head + 1, :])
        grad_probs = mxu(value[...], grad_head, NN)
        grad_scores = (probs * (grad_probs - delta)).astype(BF16)
        key_part = mxu(grad_scores, query, NT) * SCALE
        value_part = mxu(probs.astype(BF16), grad_head, NT)
        if head:
            key_part = key_part + kv_grad[:, :HEAD_DIM]
            value_part = value_part + kv_grad[:, HEAD_DIM:]
        kv_grad[:, :HEAD_DIM] = key_part
        kv_grad[:, HEAD_DIM:] = value_part
        grad_query = mxu(key_t[...], grad_scores, NN) * SCALE
        query_grad[at, :] = turn(grad_query, cosine[...], -sine_part[...]).astype(BF16)


def local_call(kernel, outs, scratch, *args):
    flops = 1 << 32
    return pl.pallas_call(
        kernel,
        out_shape=outs,
        in_specs=[pl.BlockSpec(memory_space=pltpu.VMEM)] * len(args),
        out_specs=[pl.BlockSpec(memory_space=pltpu.VMEM)] * len(outs),
        scratch_shapes=scratch,
        compiler_params=pltpu.CompilerParams(vmem_limit_bytes=48 << 20),
        cost_estimate=pl.CostEstimate(flops=flops, bytes_accessed=1 << 24, transcendentals=1 << 22),
    )(*args)


def on_device(
    block_input,
    attention_gain,
    query_weight,
    keyvalue_weight,
    output_weight,
    feedforward_gain,
    gate_weight,
    up_weight,
    down_weight,
    document_lengths,
    piece_order,
    output_grad,
    shared_grad,
):
    y, h, l, m, x, c = (lax.axis_index(a) for a in AXES)
    M = lax.axis_size("m")
    tokens, width = block_input.shape[1:]
    rows = query_weight.shape[0]
    query_width = query_weight.shape[1]
    half_width = query_width // 2
    heads = half_width // HEAD_DIM
    hidden_units = gate_weight.shape[1]
    part = hidden_units // 4
    piece_len = tokens // 2

    def inward(value):
        value = value.reshape(tokens, 2, 2, 2, M, 2, 2, rows)
        value = value.transpose(0, 6, 1, 2, 4, 3, 5, 7)
        value = jnp.where(c == 0, value, value[:, ::-1])
        value = jnp.where(y == 0, value, value[:, :, ::-1])
        value = jnp.where(h == 0, value, value[:, :, :, ::-1])
        return value.reshape(tokens, width)

    def outward(value):
        value = value.reshape(tokens, 2, 2, 2, M, 2, 2, rows)
        value = jnp.where(h == 0, value, value[:, :, :, ::-1])
        value = jnp.where(y == 0, value, value[:, :, ::-1])
        value = jnp.where(c == 0, value, value[:, ::-1])
        return value.transpose(0, 2, 3, 5, 4, 6, 1, 7).reshape(tokens, width)

    finish = jnp.cumsum(document_lengths[0])
    starts = finish - document_lengths[0]

    def places(slots):
        order = piece_order[(slots[:, None] * 2 + jnp.arange(2)[None, :]).reshape(-1)]
        return (
            order[:, None] * piece_len + jnp.arange(piece_len, dtype=jnp.int32)[None, :]
        ).reshape(-1)

    def slot(h_at, l_at, m_at, x_at, c_at):
        return (((h_at * 2 + l_at) * M + m_at) * 2 + x_at) * 2 + c_at

    position = places(jnp.stack([slot(h, l, m, x, c), slot(h, l, m, 1 - x, c)]))
    begins = jnp.max(
        jnp.where(starts[None, :] <= position[:, None], starts[None, :], 0), axis=1
    )
    key_position = places(
        jnp.stack(
            [
                slot(h ^ i, l ^ j, m_at, x ^ k, c ^ n)
                for n in range(2)
                for k in range(2)
                for j in range(2)
                for m_at in range(M)
                for i in range(2)
            ]
        )
    )[:, None]
    query_place, query_start = position[None, :], begins[None, :]
    cosine, sine_part = angles(position - begins)

    gains = jnp.stack([attention_gain, feedforward_gain])
    gains = jnp.pad(gains, ((0, 14), (0, 2 * HEAD_DIM - rows)))
    small = jnp.concatenate([keyvalue_weight, gains])
    small = jnp.stack([small, swap(small, "h")])
    small = pair(small, swap(small, "l"), l, 1)
    small = pair(small, swap(small, "x"), x, 2)
    small = gather_m(small, 1)
    small = jnp.stack([small, swap(small, "y")])
    small = jnp.stack([small, swap(small, "c")])
    small = small.reshape(width // rows, rows + 16, 2 * HEAD_DIM)
    keyvalue_full = small[:, :rows].reshape(width, 2 * HEAD_DIM)
    gain_one = small[:, rows, :rows].reshape(1, width).astype(F32)
    gain_two = small[:, rows + 1, :rows].reshape(1, width).astype(F32)

    def gather_heads(weight):
        parts = weight.reshape(rows, 2, half_width).transpose(1, 0, 2)
        got = pair(pick(parts, x), swap(pick(parts, 1 - x), "x"), x)
        got = jnp.stack([got, swap(got, "h")])
        got = pair(got, swap(got, "l"), l, 1)
        got = gather_m(got, 1).reshape(-1, half_width)
        got = jnp.concatenate([got, swap(got, "y")])
        return jnp.concatenate([got, swap(got, "c")])

    def scatter_heads(grad):
        grad = fold(fold(low(grad), "c"), "y")
        grad = scatter_m(grad.reshape(2, M, 2, 2, rows, half_width), 1)
        grad = pick(grad, l, 1) + swap(low(pick(grad, 1 - l, 1)), "l").astype(F32)
        grad = grad[0] + swap(low(grad[1]), "h").astype(F32)
        other = swap(low(pick(grad, 1 - x)), "x").astype(F32)
        return pair(pick(grad, x), other, x, 1).reshape(rows, query_width)

    query_full = gather_heads(query_weight)
    output_full = gather_heads(output_weight)

    def gather_feed(weight):
        parts = weight.reshape(rows, 4, part).transpose(1, 0, 2)
        got = lax.all_to_all(parts, ("l", "x"), 0, 0)
        got = gather_m(got, 0).reshape(width // 8, part)
        by_h = swap(got, "h")
        near = jnp.concatenate([got, by_h])
        far = jnp.concatenate([swap(got, "y"), swap(by_h, "y")])
        return jnp.concatenate([near, far, swap(near, "c"), swap(far, "c")])

    def scatter_feed(left, right):
        half, quarter = width // 2, width // 4
        sent = swap(low(contract_first(left[:, half:], right)), "c")
        grad = contract_first(left[:, :half], right) + sent.astype(F32)
        near, far = grad[:quarter], low(grad[quarter:])
        block = width // 8
        by_h = near[block:] + swap(far[block:], "y").astype(F32)
        own = near[:block] + swap(far[:block], "y").astype(F32)
        own = own + swap(low(by_h), "h").astype(F32)
        own = low(scatter_m(own.reshape(M, 4, rows, part), 0))
        got = lax.all_to_all(own, ("l", "x"), 0, 0)
        return got.transpose(1, 0, 2).reshape(rows, hidden_units).astype(F32)

    gate_full = gather_feed(gate_weight)
    up_full = gather_feed(up_weight)
    down_full = gather_feed(down_weight)

    input_mine = inward(block_input[0])
    inputs = jnp.concatenate([input_mine, swap(input_mine, "x")]).astype(F32)
    scale_one = lax.rsqrt(jnp.mean(inputs * inputs, axis=-1, keepdims=True) + EPSILON)
    normed_one = inputs * scale_one
    normed_one_low = low(normed_one * gain_one)
    keyvalue_sum = dot(normed_one_low[:tokens], keyvalue_full)
    shared_mine = low(
        jnp.concatenate(
            [
                rotate(keyvalue_sum[:, :HEAD_DIM], cosine[:tokens], sine_part[:tokens]),
                keyvalue_sum[:, HEAD_DIM:],
            ],
            -1,
        )
    )
    gathered = jnp.stack([shared_mine, swap(shared_mine, "h")])
    gathered = gather_m(gathered, 0)
    for axis in "lxc":
        gathered = jnp.stack([gathered, swap(gathered, axis)])
    gathered = gathered.reshape(-1, 2 * HEAD_DIM)
    stream_len = gathered.shape[0]
    key, value = gathered[:, :HEAD_DIM], gathered[:, HEAD_DIM:]
    query_sum = lax.dot_general(
        query_full, normed_one_low, (((0,), (1,)), ((), ())), preferred_element_type=F32
    )
    cosine_t, sine_t = cosine.T, sine_part.T
    wide = (half_width, 2 * tokens)
    places_used = (key_position, query_place, query_start)
    query_rot, attended, attended_low, lse = local_call(
        attend_kernel,
        [
            jax.ShapeDtypeStruct(wide, BF16),
            jax.ShapeDtypeStruct(wide, F32),
            jax.ShapeDtypeStruct(wide, BF16),
            jax.ShapeDtypeStruct((heads, 2 * tokens), F32),
        ],
        [pltpu.VMEM((stream_len, 2 * tokens), F32)],
        query_sum, key, value.T, cosine_t, sine_t, *places_used,
    )
    branch = lax.dot_general(
        attended_low, output_full, (((0,), (1,)), ((), ())), preferred_element_type=F32
    )
    hidden = inputs[:tokens] + fold(branch, "x")

    scale_two = lax.rsqrt(jnp.mean(hidden * hidden, axis=-1, keepdims=True) + EPSILON)
    normed_two = hidden * scale_two
    grad_mine = inward(output_grad[0])
    grad_low = gather_group(grad_mine).reshape(-1, width)
    normed_two_low = gather_group(low(normed_two * gain_two)).reshape(-1, width)
    gate_sum = dot(normed_two_low, gate_full)
    up_sum = dot(normed_two_low, up_full)
    sigmoid_gate = jax.nn.sigmoid(gate_sum)
    silu_gate = gate_sum * sigmoid_gate
    mixed_low = low(silu_gate * up_sum)
    grad_mixed = dot(grad_low, down_full)
    grad_gate = low(
        grad_mixed * up_sum * sigmoid_gate * (1.0 + gate_sum * (1.0 - sigmoid_gate))
    )
    grad_up = low(grad_mixed * silu_gate)
    blocks = (4, tokens, width)
    grad_two = scatter_group(
        (contract_last(grad_gate, gate_full) + contract_last(grad_up, up_full)).reshape(blocks)
    )
    feed_out = scatter_group(contract_last(mixed_low, down_full).reshape(blocks))
    block_output = outward(low(hidden + feed_out))[None]
    gain_two_grad = jnp.sum(grad_two * normed_two, axis=0)
    grad_hidden = grad_mine.astype(F32) + norm_back(grad_two * gain_two, normed_two, scale_two)

    grad_hidden_low = low(grad_hidden)
    grad_hidden_low = jnp.concatenate([grad_hidden_low, swap(grad_hidden_low, "x")])
    grad_heads = low(
        lax.dot_general(
            output_full, grad_hidden_low, (((0,), (1,)), ((), ())), preferred_element_type=F32
        )
    )
    query_grad_low, kv_grad = local_call(
        attend_back_kernel,
        [
            jax.ShapeDtypeStruct(wide, BF16),
            jax.ShapeDtypeStruct((stream_len, 2 * HEAD_DIM), F32),
        ],
        [pltpu.VMEM((stream_len, 2 * tokens), F32)],
        query_rot, key, key.T, value, grad_heads, attended, lse, cosine_t, sine_t, *places_used,
    )
    for axis in "cxl":
        kv_grad = fold(kv_grad, axis)
    kv_grad = scatter_m(kv_grad.reshape(M, 2 * tokens, 2 * HEAD_DIM), 0)
    kv_mine = fold(kv_grad, "h") + shared_grad[0].astype(F32)
    keyvalue_grad_low = low(
        jnp.concatenate(
            [
                rotate(kv_mine[:, :HEAD_DIM], cosine[:tokens], -sine_part[:tokens]),
                kv_mine[:, HEAD_DIM:],
            ],
            -1,
        )
    )
    grad_one = lax.dot_general(
        query_grad_low, query_full, (((0,), (1,)), ((), ())), preferred_element_type=F32
    )
    grad_one = fold(grad_one, "x") + contract_last(keyvalue_grad_low, keyvalue_full)
    normed_mine = normed_one[:tokens]
    gain_one_grad = jnp.sum(grad_one * normed_mine, axis=0)
    input_grad = outward(
        grad_hidden + norm_back(grad_one * gain_one, normed_mine, scale_one[:tokens])
    )[None]

    down_weight_grad = scatter_feed(grad_low, mixed_low)
    gate_weight_grad = scatter_feed(normed_two_low, grad_gate)
    up_weight_grad = scatter_feed(normed_two_low, grad_up)
    across = (((0,), (1,)), ((), ()))
    output_weight_grad = scatter_heads(
        lax.dot_general(grad_hidden_low, attended_low, across, preferred_element_type=F32)
    )
    query_weight_grad = scatter_heads(
        lax.dot_general(normed_one_low, query_grad_low, across, preferred_element_type=F32)
    )

    small_grad = contract_first(normed_one_low[:tokens], keyvalue_grad_low)
    small_gains = jnp.stack([gain_one_grad, gain_two_grad], -1)
    small_gains = jnp.pad(small_gains, ((0, 0), (0, HEAD_DIM - 2)))
    small_grad = jnp.concatenate([small_grad, small_gains], -1)
    small_grad = fold(fold(small_grad, "c"), "y")
    small_grad = fold(small_grad, "h").reshape(M, 2, 2, rows, 3 * HEAD_DIM)
    small_grad = pick(small_grad, l, 1) + swap(low(pick(small_grad, 1 - l, 1)), "l").astype(F32)
    small_grad = pick(small_grad, x, 1) + swap(low(pick(small_grad, 1 - x, 1)), "x").astype(F32)
    small_grad = scatter_m(small_grad, 0)
    keyvalue_weight_grad = small_grad[:, : 2 * HEAD_DIM]
    gain_one_mine = small_grad[:, 2 * HEAD_DIM]
    gain_two_mine = small_grad[:, 2 * HEAD_DIM + 1]
    return (
        block_output,
        shared_mine[None],
        input_grad,
        gain_one_mine,
        query_weight_grad,
        keyvalue_weight_grad,
        output_weight_grad,
        gain_two_mine,
        gate_weight_grad,
        up_weight_grad,
        down_weight_grad,
    )


def solution(mesh):
    streams, seq = mesh.shape["dp"], mesh.shape["seq"]
    fine = Mesh(mesh.devices.reshape(streams, 2, 2, seq // 16, 2, 2), tuple(AXES))
    stream = P("y", tuple(AXES[1:]), None)
    vector, matrix = P(tuple(AXES)), P(tuple(AXES), None)
    return jax.shard_map(
        on_device,
        mesh=fine,
        in_specs=(
            stream,
            vector,
            matrix,
            matrix,
            matrix,
            vector,
            matrix,
            matrix,
            matrix,
            P("y", None),
            P(),
            stream,
            stream,
        ),
        out_specs=(
            stream,
            stream,
            stream,
            vector,
            matrix,
            matrix,
            matrix,
            vector,
            matrix,
            matrix,
            matrix,
        ),
        check_vma=False,
    )
```

time: 857 us -> 695 us (0.81)
  waiting for transfers between devices: 351 us -> 268 us
  local copies, waits for them, and re-layouts: 149 us -> 98.6 us
  starting transfers between devices: 151 us -> 119 us
  Pallas kernels: 0 us -> 22.4 us
  matrix products: 102 us -> 89.4 us
    ppermute x48 -> x0, waiting for transfers between devices: 180 us -> none  [hop(): return lax.ppermute(value, 'z', [(i, i ^ k) for i in range(Z)])]
    ppermute x48 -> x0, starting transfers between devices: 112 us -> none  [hop(): return lax.ppermute(value, 'z', [(i, i ^ k) for i in range(Z)])]
    ppermute x51 -> x69, waiting for transfers between devices: 171 us -> 263 us  [swap(): return lax.ppermute(value, axis, [(0, 1), (1, 0)])]
    all_to_all x0 -> x10, starting transfers between devices: none -> 55.1 us  [the longest x3 23.7 us: gather_feed(): got = lax.all_to_all(parts, ('l', 'x'), 0, 0)]
    dynamic_update_slice x23 -> x0, local copies, waits for them, and re-layouts: 33.6 us -> none  [put(): result = lax.dynamic_update_index_in_dim(result, piece, index, axis)]
    ppermute x51 -> x69, starting transfers between devices: 39.6 us -> 63.4 us  [swap(): return lax.ppermute(value, axis, [(0, 1), (1, 0)])]
    pallas_call x0 -> x2, Pallas kernels: none -> 22.4 us  [local_call(): pl.pallas_call(kernel, out_shape=outs, in_specs=[pl.BlockSpec(memory_spac...]
    dot_general x6, matrix products: 38.9 us -> 16.5 us  [the longest x1 3.64 us: on_device(): lax.dot_general(output_full, grad_hidden_low, (((0,), (1,)), ((), ())), p...]
  transfers between devices with their start and end apart: 99 -> 79, of which waited for: 38 -> 26; matrix products, arithmetic and copies ran while one was open for 37% -> 34% of each run, Pallas kernels for 0% -> 3%
where the time goes in v2:
time: 695 us; the launch traced here: 687 us
  waiting for transfers between devices  268 us (39%)
  starting transfers between devices  119 us (17%)
  local copies, waits for them, and re-layouts  98.6 us (14%)
  matrix products  89.4 us (13%)
  other arithmetic  87.5 us (13%)
  Pallas kernels  22.4 us (3%)
    ppermute x69, waiting for transfers between devices, swap(): return lax.ppermute(value, axis, [(0, 1), (1, 0)])  263 us
    ppermute x69, starting transfers between devices, swap(): return lax.ppermute(value, axis, [(0, 1), (1, 0)])  63.4 us
    unnamed x209, local copies, waits for them, and re-layouts  44.1 us
    dot_general x7, matrix products, contract_first(): lax.dot_general(left, right, (((0,), (0,)), ((), ())), preferred_element_...  35.5 us
    all_to_all x3, starting transfers between devices, gather_feed(): got = lax.all_to_all(parts, ('l', 'x'), 0, 0)  23.7 us
    pallas_call x2, Pallas kernels, local_call(): pl.pallas_call(kernel, out_shape=outs, in_specs=[pl.BlockSpec(memory_spac...  22.4 us
    dot_general x4, matrix products, dot(): return jnp.dot(left, right, preferred_element_type=F32)  20.9 us
    convert_element_type x8, other arithmetic, low(): return value.astype(BF16)  17.1 us
  transfers between devices with their start and end apart: 79, of which 26 were waited for; matrix products, arithmetic and copies ran while one was open for 34% of the time, Pallas kernels for 3%

profile of v2, /device:TPU:0, one launch (start us, length us, event | category | flops | bytes accessed | tf_op | source)
XLA Modules:
  0.0 686.7 jit_solution(17440753560276382334)
XLA Ops:
  4.3 3.0 collective-permute-start
  18.9 4.2 all-to-all-start.3
  49.0 2.7 collective-permute-start.16
  54.5 11.4 %collective-permute-done.2 = bf16[2,64,1024]{2,1,0:T(8,128)(2,1)S(1)} collective-permute-done((bf16[2,64,1024]{2,1,0:T(8,128)(2,1)S(1)}, bf16[2,64,1024]{2,1,0:T(8,128)(2,1)S(1)}, u32[]{:S(2)}, u32[]{:S(2)}) %collective-permute-start.2) | collective-permute-done | bytes 262176 | tf_op jit(solution)/shard_map/ppermute | solution.py:55
  66.1 5.5 collective-permute-done.16
  75.7 7.1 %collective-permute-done.3 = bf16[2,2,64,1024]{3,2,1,0:T(8,128)(2,1)S(1)} collective-permute-done((bf16[2,2,64,1024]{3,2,1,0:T(8,128)(2,1)S(1)}, bf16[2,2,64,1024]{3,2,1,0:T(8,128)(2,1)S(1)}, u32[]{:S(2)}, u32[]{:S(2)}) %collective-permute-start.3) | collective-permute-done | bytes 524320 | tf_op jit(solution)/shard_map/ppermute | solution.py:55
  85.5 4.2 all-to-all-start.2
  89.7 4.4 collective-permute-done.17
  100.8 2.7 broadcast_multiply_fusion
  104.8 15.4 %all-to-all-start.1 = ((bf16[4,64,1408]{2,1,0:T(8,128)(2,1)}), bf16[4,64,1408]{2,1,0:T(8,128)(2,1)S(1)}, u32[]{:S(2)}, u32[]{:S(2)}) async-start(bf16[4,64,1408]{2,1,0:T(8,128)(2,1)} %copy.151), calls=%async_computation.1 | async-start | bytes 1441792 | tf_op jit(solution)/shard_map/all_to_all | solution.py:289
  120.6 3.0 collective-permute-start.11
  123.6 11.2 %collective-permute-done.11 = bf16[128,256]{1,0:T(8,128)(2,1)S(1)} collective-permute-done((bf16[128,256]{1,0:T(8,128)(2,1)S(1)}, bf16[128,256]{1,0:T(8,128)(2,1)S(1)}, u32[]{:S(2)}, u32[]{:S(2)}) %collective-permute-start.11) | collective-permute-done | bytes 65568 | tf_op jit(solution)/shard_map/ppermute | solution.py:55
  137.0 6.8 collective-permute-done.12
  148.6 4.6 all-to-all-start.5
  161.9 18.5 %collective-permute-done.26 = bf16[256,1408]{1,0:T(8,128)(2,1)S(1)} collective-permute-done((bf16[256,1408]{1,0:T(8,128)(2,1)}, bf16[256,1408]{1,0:T(8,128)(2,1)S(1)}, u32[]{:S(2)}, u32[]{:S(2)}) %collective-permute-start.26) | collective-permute-done | bytes 720928 | tf_op jit(solution)/shard_map/ppermute | solution.py:55
  185.6 3.0 pad_maximum_fusion.2
  188.6 26.3 %collective-permute-done.21 = bf16[256,1408]{1,0:T(8,128)(2,1)S(1)} collective-permute-done((bf16[256,1408]{1,0:T(8,128)(2,1)S(1)}, bf16[256,1408]{1,0:T(8,128)(2,1)S(1)}, u32[]{:S(2)}, u32[]{:S(2)}) %collective-permute-start.21) | collective-permute-done | bytes 720928 | tf_op jit(solution)/shard_map/ppermute | solution.py:55
  219.0 3.1 pad_maximum_fusion.3
  225.0 12.0 %collective-permute-done.33 = bf16[256,1408]{1,0:T(8,128)(2,1)} collective-permute-done((bf16[256,1408]{1,0:T(8,128)(2,1)}, bf16[256,1408]{1,0:T(8,128)(2,1)}, u32[]{:S(2)}, u32[]{:S(2)}) %collective-permute-start.33) | collective-permute-done | bytes 720928 | tf_op jit(solution)/shard_map/ppermute | solution.py:55
  240.1 3.1 fusion.4.query_sum
  243.1 10.1 %shard_map.212 = (bf16[1024,256]{1,0:T(8,128)(2,1)S(1)}, f32[1024,256]{1,0:T(8,128)S(1)}, bf16[1024,256]{1,0:T(8,128)(2,1)S(1)}, f32[8,256]{1,0:T(8,128)S(1)}) custom-call(f32[1024,256]{1,0:T(8,128)S(1)} %fusion.4.query_sum, bf16[2048,128]{1,0:T(8,128)(2,1)S(1)} %get-tuple-element.93.key, bf16[128,2048]{1,0:T(8,128)(2,1)S(1)} %copy.148.value_t, ...), custom_call_target="tpu_custom_call" | custom-call | flops 4294967296 | bytes 16777216 | tf_op jit(solution)/shard_map/pallas_call | solution.py:170
  254.9 3.6 fusion.2
  261.6 12.2 %collective-permute-done.23 = bf16[256,1408]{1,0:T(8,128)(2,1)S(1)} collective-permute-done((bf16[256,1408]{1,0:T(8,128)(2,1)S(1)}, bf16[256,1408]{1,0:T(8,128)(2,1)S(1)}, u32[]{:S(2)}, u32[]{:S(2)}) %collective-permute-start.23) | collective-permute-done | bytes 720928 | tf_op jit(solution)/shard_map/ppermute | solution.py:55
  278.6 5.0 all-to-all-start
  287.8 2.6 constant_dynamic-update-slice_fusion.13
  298.2 2.8 constant_dynamic-update-slice_fusion.6
  302.2 6.6 fusion.93
  309.1 6.6 fusion.92
  315.7 7.4 %multiply_convert_fusion.1 = (bf16[512,1408]{1,0:T(8,128)(2,1)S(1)}, bf16[512,1408]{1,0:T(8,128)(2,1)S(1)}, bf16[512,1408]{1,0:T(8,128)(2,1)}) fusion(f32[512,1408]{1,0:T(8,128)S(1)} %copy-done.90, f32[512,1408]{1,0:T(8,128)S(1)} %fusion.92, bf16[512,2048]{1,0:T(8,128)(2,1)} %bitcast.68, bf16[2048,1408]{1,0:T(8,128)(2,1)S(1)} %copy-done.76), kind=kOutput, calls=%fused_computation.21 | convolution fusion | flops 2963603456 | bytes 17956864 | tf_op jit(solution)/shard_map/dot_general | solution.py:37
  323.2 3.4 fusion.94
  326.6 4.7 convolution_convert_fusion.2
  331.4 4.9 add_convert_fusion
  336.2 4.4 all-to-all-start.6
  340.7 5.2 convolution_convert_fusion.1
  348.4 5.2 convolution_convert_fusion
  353.6 7.5 %convolution_convert_fusion.5 = bf16[512,2048]{1,0:T(8,128)(2,1)} fusion(bf16[512,1408]{1,0:T(8,128)(2,1)S(1)} %copy-done.50, bf16[2048,1408]{1,0:T(8,128)(2,1)} %constant_dynamic-update-slice_fusion.12), kind=kOutput, calls=%fused_computation.19 | convolution fusion | flops 2953838592 | bytes 9306112 | tf_op jit(solution)/shard_map/dot_general | solution.py:41
  361.1 6.4 fusion.89
  370.8 4.7 all-to-all-start.4
  375.5 7.0 %fusion.90 = (bf16[1024,1408]{1,0:T(8,128)(2,1)S(1)}, f32[1024,1408]{1,0:T(8,128)}) fusion(bf16[1024,1408]{1,0:T(8,128)(2,1)} %collective-permute-done.61, bf16[512,1408]{1,0:T(8,128)(2,1)} %copy-done.52, bf16[512,2048]{1,0:T(8,128)(2,1)} %bitcast.68), kind=kOutput, calls=%fused_computation.283 | convolution fusion | flops 1480720384 | bytes 14024704 | tf_op jit(solution)/shard_map/dot_general | solution.py:45
  385.7 6.5 fusion.91
  400.4 3.0 convert_reduce_fusion.1
  406.5 12.4 %collective-permute-done.63 = bf16[256,1408]{1,0:T(8,128)(2,1)} collective-permute-done((bf16[256,1408]{1,0:T(8,128)(2,1)}, bf16[256,1408]{1,0:T(8,128)(2,1)}, u32[]{:S(2)}, u32[]{:S(2)}) %collective-permute-start.63) | collective-permute-done | bytes 720928 | tf_op jit(solution)/shard_map/ppermute | solution.py:55
  423.4 26.3 %collective-permute-done.67 = bf16[256,1408]{1,0:T(8,128)(2,1)} collective-permute-done((bf16[256,1408]{1,0:T(8,128)(2,1)}, bf16[256,1408]{1,0:T(8,128)(2,1)}, u32[]{:S(2)}, u32[]{:S(2)}) %collective-permute-start.67) | collective-permute-done | bytes 720928 | tf_op jit(solution)/shard_map/ppermute | solution.py:55
  453.4 3.6 fusion.17.grad
  457.0 12.3 %shard_map.213 = (bf16[1024,256]{1,0:T(8,128)(2,1)S(1)}, f32[2048,256]{1,0:T(8,128)}) custom-call(bf16[1024,256]{1,0:T(8,128)(2,1)S(1)} %copy-done.5, bf16[2048,128]{1,0:T(8,128)(2,1)S(1)} %get-tuple-element.93.key, bf16[128,2048]{1,0:T(8,128)(2,1)S(1)} %copy.161.key_t, bf16[2048,128]{1,0:T(8,128)(2,1)S(1)} %get-tuple-element.90.value, ...), custom_call_target="tpu_custom_call" | custom-call | flops 4294967296 | bytes 16777216 | tf_op jit(solution)/shard_map/pallas_call | solution.py:170
  470.7 3.6 fusion.3
  488.4 2.7 fusion.16
  491.1 4.3 all-to-all-start.7
  498.6 35.0 %collective-permute-done.64 = bf16[256,1408]{1,0:T(8,128)(2,1)S(1)} collective-permute-done((bf16[256,1408]{1,0:T(8,128)(2,1)}, bf16[256,1408]{1,0:T(8,128)(2,1)S(1)}, u32[]{:S(2)}, u32[]{:S(2)}) %collective-permute-start.64) | collective-permute-done | bytes 720928 | tf_op jit(solution)/shard_map/ppermute | solution.py:55
  533.6 2.9 fusion.13
  536.4 15.0 %collective-permute-done.40 = bf16[256,256]{1,0:T(8,128)(2,1)S(1)} collective-permute-done((bf16[256,256]{1,0:T(8,128)(2,1)S(1)}, bf16[256,256]{1,0:T(8,128)(2,1)S(1)}, u32[]{:S(2)}, u32[]{:S(2)}) %collective-permute-start.40) | collective-permute-done | bytes 131104 | tf_op jit(solution)/shard_map/ppermute | solution.py:55
  552.5 2.7 fusion.10
  555.2 3.2 collective-permute-done.41
  567.5 4.2 all-to-all-start.8
  583.0 4.2 all-to-all-start.9
  588.6 3.3 collective-permute-done.43
  600.0 5.0 collective-permute-done.44
  605.3 3.1 convert_add_fusion.3
  620.5 5.4 collective-permute-done.48
  629.5 17.0 %collective-permute-done.53 = bf16[512,1024]{1,0:T(8,128)(2,1)} collective-permute-done((bf16[512,1024]{1,0:T(8,128)(2,1)}, bf16[512,1024]{1,0:T(8,128)(2,1)}, u32[]{:S(2)}, u32[]{:S(2)}) %collective-permute-start.53) | collective-permute-done | bytes 1048608 | tf_op jit(solution)/shard_map/ppermute | solution.py:55
  651.3 2.7 collective-permute-start.50
  654.0 12.0 %collective-permute-done.54 = bf16[2,2,64,1024]{3,2,1,0:T(8,128)(2,1)S(1)} collective-permute-done((bf16[2,2,64,1024]{3,2,1,0:T(8,128)(2,1)S(1)}, bf16[2,2,64,1024]{3,2,1,0:T(8,128)(2,1)S(1)}, u32[]{:S(2)}, u32[]{:S(2)}) %collective-permute-start.54) | collective-permute-done | bytes 524320 | tf_op jit(solution)/shard_map/ppermute | solution.py:55
  669.6 10.0 %collective-permute-done.55 = bf16[2,64,1024]{2,1,0:T(8,128)(2,1)S(1)} collective-permute-done((bf16[2,64,1024]{2,1,0:T(8,128)(2,1)S(1)}, bf16[2,64,1024]{2,1,0:T(8,128)(2,1)S(1)}, u32[]{:S(2)}, u32[]{:S(2)}) %collective-permute-start.55) | collective-permute-done | bytes 262176 | tf_op jit(solution)/shard_map/ppermute | solution.py:55
  682.9 2.7 collective-permute-done.56
  (512 shorter events, 218.8 us)
Async XLA Ops:
  4.3 68.3 %collective-permute-start = (bf16[128,2048]{1,0:T(8,128)(2,1)S(1)}, bf16[128,2048]{1,0:T(8,128)(2,1)S(1)}, u32[]{:S(2)}, u32[]{:S(2)}) collective-permute-start(bf16[128,2048]{1,0:T(8,128)(2,1)S(1)} %copy.143), channel_id=1, source_target_pairs={{0,2},{2,0},{1,3},{3,1},{4,6},{6,4},{5,7},{7,5},{8,10},{10,8},{9,1... | collective-permute-start | bytes 1572872 | tf_op jit(solution)/shard_map/ppermute | solution.py:55
  8.0 19.0 %collective-permute-start.6 = (bf16[80,256]{1,0:T(8,128)(2,1)}, bf16[80,256]{1,0:T(8,128)(2,1)}, u32[]{:S(2)}, u32[]{:S(2)}) collective-permute-start(bf16[80,256]{1,0:T(8,128)(2,1)} %get-tuple-element.124), channel_id=1, source_target_pairs={{0,8},{8,0},{1,9},{9,1},{2,10},{10,2},{3,11},{11,3},{4,12},{12,4},... | collective-permute-start | bytes 122888 | tf_op jit(solution)/shard_map/ppermute | solution.py:55
  12.0 34.5 %collective-permute-start.1 = (bf16[64,1024]{1,0:T(8,128)(2,1)}, bf16[64,1024]{1,0:T(8,128)(2,1)}, u32[]{:S(2)}, u32[]{:S(2)}) collective-permute-start(bf16[64,1024]{1,0:T(8,128)(2,1)} %bitcast.228), channel_id=1, source_target_pairs={{0,2},{2,0},{1,3},{3,1},{4,6},{6,4},{5,7},{7,5},{8,10},{10,8},{9,1... | collective-permute-start | bytes 393224 | tf_op jit(solution)/shard_map/ppermute | solution.py:55
  14.7 33.3 %collective-permute-start.15 = (bf16[64,1024]{1,0:T(8,128)(2,1)}, bf16[64,1024]{1,0:T(8,128)(2,1)}, u32[]{:S(2)}, u32[]{:S(2)}) collective-permute-start(bf16[64,1024]{1,0:T(8,128)(2,1)} %bitcast.227), channel_id=1, source_target_pairs={{0,2},{2,0},{1,3},{3,1},{4,6},{6,4},{5,7},{7,5},{8,10},{10,8},{9,1... | collective-permute-start | bytes 393224 | tf_op jit(solution)/shard_map/ppermute | solution.py:55
  18.9 66.6 %all-to-all-start.3 = ((bf16[4,64,1408]{2,1,0:T(8,128)(2,1)}), bf16[4,64,1408]{2,1,0:T(8,128)(2,1)}, u32[]{:S(2)}, u32[]{:S(2)}) async-start(bf16[4,64,1408]{2,1,0:T(8,128)(2,1)} %copy.153), calls=%async_computation.3 | async-start | bytes 1441792 | tf_op jit(solution)/shard_map/all_to_all | solution.py:289
  28.4 14.5 %collective-permute-start.7 = (bf16[2,80,256]{2,1,0:T(8,128)(2,1)}, bf16[2,80,256]{2,1,0:T(8,128)(2,1)}, u32[]{:S(2)}, u32[]{:S(2)}) collective-permute-start(bf16[2,80,256]{2,1,0:T(8,128)(2,1)} %get-tuple-element.122), channel_id=1, source_target_pairs={{0,4},{4,0},{1,5},{5,1},{2,6},{6,2},{3,7},{7,3},{8,12},{12,8},{9,1... | collective-permute-start | bytes 245768 | tf_op jit(solution)/shard_map/ppermute | solution.py:55
  47.5 18.4 %collective-permute-start.2 = (bf16[2,64,1024]{2,1,0:T(8,128)(2,1)S(1)}, bf16[2,64,1024]{2,1,0:T(8,128)(2,1)S(1)}, u32[]{:S(2)}, u32[]{:S(2)}) collective-permute-start(bf16[2,64,1024]{2,1,0:T(8,128)(2,1)S(1)} %maximum_select_fusion.7), channel_id=1, source_target_pairs={{0,8},{8,0},{1,9},{9,1},{2,10},{10,2},{3,11},{11,3},{4,12},{12,4},... | collective-permute-start | bytes 786440 | tf_op jit(solution)/shard_map/ppermute | solution.py:55
  49.0 22.6 %collective-permute-start.16 = (bf16[2,64,1024]{2,1,0:T(8,128)(2,1)S(1)}, bf16[2,64,1024]{2,1,0:T(8,128)(2,1)S(1)}, u32[]{:S(2)}, u32[]{:S(2)}) collective-permute-start(bf16[2,64,1024]{2,1,0:T(8,128)(2,1)S(1)} %maximum_select_fusion.9), channel_id=1, source_target_pairs={{0,8},{8,0},{1,9},{9,1},{2,10},{10,2},{3,11},{11,3},{4,12},{12,4},... | collective-permute-start | bytes 786440 | tf_op jit(solution)/shard_map/ppermute | solution.py:55
  51.7 21.2 %collective-permute-start.9 = (bf16[2,1,2,2,80,256]{5,4,3,2,0,1:T(8,128)(2,1)S(1)}, bf16[2,1,2,2,80,256]{5,4,3,2,0,1:T(8,128)(2,1)S(1)}, u32[]{:S(2)}, u32[]{:S(2)}) collective-permute-start(bf16[2,1,2,2,80,256]{5,4,3,2,0,1:T(8,128)(2,1)S(1)} %maximum_select_fusion.5), channel_id=1, source_target_pairs={{0,16},{16,0},{1,17},{17,1},{2,18},{18,2},{3,19},{19,3},{4,20},{20... | collective-permute-start | bytes 983048 | tf_op jit(solution)/shard_map/ppermute | solution.py:55
  66.0 16.8 %collective-permute-start.3 = (bf16[2,2,64,1024]{3,2,1,0:T(8,128)(2,1)S(1)}, bf16[2,2,64,1024]{3,2,1,0:T(8,128)(2,1)S(1)}, u32[]{:S(2)}, u32[]{:S(2)}) collective-permute-start(bf16[2,2,64,1024]{3,2,1,0:T(8,128)(2,1)S(1)} %get-tuple-element.101), channel_id=1, source_target_pairs={{0,4},{4,0},{1,5},{5,1},{2,6},{6,2},{3,7},{7,3},{8,12},{12,8},{9,1... | collective-permute-start | bytes 1572872 | tf_op jit(solution)/shard_map/ppermute | solution.py:55
  72.6 21.5 %collective-permute-start.17 = (bf16[2,2,64,1024]{3,2,1,0:T(8,128)(2,1)}, bf16[2,2,64,1024]{3,2,1,0:T(8,128)(2,1)}, u32[]{:S(2)}, u32[]{:S(2)}) collective-permute-start(bf16[2,2,64,1024]{3,2,1,0:T(8,128)(2,1)} %get-tuple-element.97), channel_id=1, source_target_pairs={{0,4},{4,0},{1,5},{5,1},{2,6},{6,2},{3,7},{7,3},{8,12},{12,8},{9,1... | collective-permute-start | bytes 1572872 | tf_op jit(solution)/shard_map/ppermute | solution.py:55
  74.1 24.5 %collective-permute-start.10 = (bf16[2,2,1,2,2,80,256]{6,5,4,3,1,0,2:T(8,128)(2,1)}, bf16[2,2,1,2,2,80,256]{6,5,4,3,1,0,2:T(8,128)(2,1)}, u32[]{:S(2)}, u32[]{:S(2)}) collective-permute-start(bf16[2,2,1,2,2,80,256]{6,5,4,3,1,0,2:T(8,128)(2,1)} %get-tuple-element.95), channel_id=1, source_target_pairs={{0,1},{1,0},{2,3},{3,2},{4,5},{5,4},{6,7},{7,6},{8,9},{9,8},{10,11... | collective-permute-start | bytes 1966088 | tf_op jit(solution)/shard_map/ppermute | solution.py:55
  84.0 101.5 %collective-permute-start.4 = (bf16[512,1024]{1,0:T(8,128)(2,1)}, bf16[512,1024]{1,0:T(8,128)(2,1)}, u32[]{:S(2)}, u32[]{:S(2)}) collective-permute-start(bf16[512,1024]{1,0:T(8,128)(2,1)} %bitcast.9), channel_id=1, source_target_pairs={{0,16},{16,0},{1,17},{17,1},{2,18},{18,2},{3,19},{19,3},{4,20},{20... | collective-permute-start | bytes 3145736 | tf_op jit(solution)/shard_map/ppermute | solution.py:55
  85.5 19.2 %all-to-all-start.2 = ((bf16[4,64,1408]{2,1,0:T(8,128)(2,1)}), bf16[4,64,1408]{2,1,0:T(8,128)(2,1)}, u32[]{:S(2)}, u32[]{:S(2)}) async-start(bf16[4,64,1408]{2,1,0:T(8,128)(2,1)} %copy.152), calls=%async_computation.2 | async-start | bytes 1441792 | tf_op jit(solution)/shard_map/all_to_all | solution.py:289
  97.1 121.4 %collective-permute-start.18 = (bf16[512,1024]{1,0:T(8,128)(2,1)}, bf16[512,1024]{1,0:T(8,128)(2,1)}, u32[]{:S(2)}, u32[]{:S(2)}) collective-permute-start(bf16[512,1024]{1,0:T(8,128)(2,1)} %bitcast.67), channel_id=1, source_target_pairs={{0,16},{16,0},{1,17},{17,1},{2,18},{18,2},{3,19},{19,3},{4,20},{20... | collective-permute-start | bytes 3145736 | tf_op jit(solution)/shard_map/ppermute | solution.py:55
  98.6 57.1 %collective-permute-start.31 = (bf16[256,1408]{1,0:T(8,128)(2,1)}, bf16[256,1408]{1,0:T(8,128)(2,1)}, u32[]{:S(2)}, u32[]{:S(2)}) collective-permute-start(bf16[256,1408]{1,0:T(8,128)(2,1)} %bitcast.74), channel_id=1, source_target_pairs={{0,8},{8,0},{1,9},{9,1},{2,10},{10,2},{3,11},{11,3},{4,12},{12,4},... | collective-permute-start | bytes 2162696 | tf_op jit(solution)/shard_map/ppermute | solution.py:55
  104.8 42.2 %all-to-all-start.1 = ((bf16[4,64,1408]{2,1,0:T(8,128)(2,1)}), bf16[4,64,1408]{2,1,0:T(8,128)(2,1)S(1)}, u32[]{:S(2)}, u32[]{:S(2)}) async-start(bf16[4,64,1408]{2,1,0:T(8,128)(2,1)} %copy.151), calls=%async_computation.1 | async-start | bytes 1441792 | tf_op jit(solution)/shard_map/all_to_all | solution.py:289
  147.0 33.4 %collective-permute-start.26 = (bf16[256,1408]{1,0:T(8,128)(2,1)}, bf16[256,1408]{1,0:T(8,128)(2,1)S(1)}, u32[]{:S(2)}, u32[]{:S(2)}) collective-permute-start(bf16[256,1408]{1,0:T(8,128)(2,1)} %bitcast.72), channel_id=1, source_target_pairs={{0,8},{8,0},{1,9},{9,1},{2,10},{10,2},{3,11},{11,3},{4,12},{12,4},... | collective-permute-start | bytes 2162696 | tf_op jit(solution)/shard_map/ppermute | solution.py:55
  148.6 128.4 %all-to-all-start.5 = ((bf16[4,128,2048]{2,1,0:T(8,128)(2,1)}), bf16[4,128,2048]{2,1,0:T(8,128)(2,1)}, u32[]{:S(2)}, u32[]{:S(2)}) async-start(bf16[4,128,2048]{2,1,0:T(8,128)(2,1)} %broadcast_in_dim.22), calls=%async_computation.5 | async-start | bytes 4194304 | tf_op jit(solution)/shard_map/all_to_all | solution.py:90
  154.2 29.6 %collective-permute-start.32 = (bf16[256,1408]{1,0:T(8,128)(2,1)}, bf16[256,1408]{1,0:T(8,128)(2,1)S(1)}, u32[]{:S(2)}, u32[]{:S(2)}) collective-permute-start(bf16[256,1408]{1,0:T(8,128)(2,1)} %bitcast.74), channel_id=1, source_target_pairs={{0,16},{16,0},{1,17},{17,1},{2,18},{18,2},{3,19},{19,3},{4,20},{20... | collective-permute-start | bytes 2162696 | tf_op jit(solution)/shard_map/ppermute | solution.py:55
  155.7 61.4 %collective-permute-start.27 = (bf16[256,1408]{1,0:T(8,128)(2,1)}, bf16[256,1408]{1,0:T(8,128)(2,1)S(1)}, u32[]{:S(2)}, u32[]{:S(2)}) collective-permute-start(bf16[256,1408]{1,0:T(8,128)(2,1)} %bitcast.72), channel_id=1, source_target_pairs={{0,16},{16,0},{1,17},{17,1},{2,18},{18,2},{3,19},{19,3},{4,20},{20... | collective-permute-start | bytes 2162696 | tf_op jit(solution)/shard_map/ppermute | solution.py:55
  180.4 34.5 %collective-permute-start.21 = (bf16[256,1408]{1,0:T(8,128)(2,1)S(1)}, bf16[256,1408]{1,0:T(8,128)(2,1)S(1)}, u32[]{:S(2)}, u32[]{:S(2)}) collective-permute-start(bf16[256,1408]{1,0:T(8,128)(2,1)S(1)} %bitcast.236), channel_id=1, source_target_pairs={{0,8},{8,0},{1,9},{9,1},{2,10},{10,2},{3,11},{11,3},{4,12},{12,4},... | collective-permute-start | bytes 2162696 | tf_op jit(solution)/shard_map/ppermute | solution.py:55
  183.7 38.4 %collective-permute-start.22 = (bf16[256,1408]{1,0:T(8,128)(2,1)S(1)}, bf16[256,1408]{1,0:T(8,128)(2,1)S(1)}, u32[]{:S(2)}, u32[]{:S(2)}) collective-permute-start(bf16[256,1408]{1,0:T(8,128)(2,1)S(1)} %bitcast.237), channel_id=1, source_target_pairs={{0,16},{16,0},{1,17},{17,1},{2,18},{18,2},{3,19},{19,3},{4,20},{20... | collective-permute-start | bytes 2162696 | tf_op jit(solution)/shard_map/ppermute | solution.py:55
  185.5 37.7 %collective-permute-start.14 = (bf16[2,2,1,2,128,256]{5,4,3,1,2,0:T(8,128)(2,1)S(1)}, bf16[2,2,1,2,128,256]{5,4,3,1,2,0:T(8,128)(2,1)S(1)}, u32[]{:S(2)}, u32[]{:S(2)}) collective-permute-start(bf16[2,2,1,2,128,256]{5,4,3,1,2,0:T(8,128)(2,1)S(1)} %get-tuple-element.99), channel_id=1, source_target_pairs={{0,1},{1,0},{2,3},{3,2},{4,5},{5,4},{6,7},{7,6},{8,9},{9,8},{10,11... | collective-permute-start | bytes 1572872 | tf_op jit(solution)/shard_map/ppermute | solution.py:55
  214.9 24.7 %collective-permute-start.5 = (bf16[1024,1024]{1,0:T(8,128)(2,1)}, bf16[1024,1024]{1,0:T(8,128)(2,1)}, u32[]{:S(2)}, u32[]{:S(2)}) collective-permute-start(bf16[1024,1024]{1,0:T(8,128)(2,1)} %pad_maximum_fusion.2), channel_id=1, source_target_pairs={{0,1},{1,0},{2,3},{3,2},{4,5},{5,4},{6,7},{7,6},{8,9},{9,8},{10,11... | collective-permute-start | bytes 6291464 | tf_op jit(solution)/shard_map/ppermute | solution.py:55
  217.1 69.7 %collective-permute-start.34 = (bf16[512,1408]{1,0:T(8,128)(2,1)}, bf16[512,1408]{1,0:T(8,128)(2,1)}, u32[]{:S(2)}, u32[]{:S(2)}) collective-permute-start(bf16[512,1408]{1,0:T(8,128)(2,1)} %pad_maximum_fusion.13), channel_id=1, source_target_pairs={{0,1},{1,0},{2,3},{3,2},{4,5},{5,4},{6,7},{7,6},{8,9},{9,8},{10,11... | collective-permute-start | bytes 4325384 | tf_op jit(solution)/shard_map/ppermute | solution.py:55
  218.5 18.5 %collective-permute-start.33 = (bf16[256,1408]{1,0:T(8,128)(2,1)}, bf16[256,1408]{1,0:T(8,128)(2,1)}, u32[]{:S(2)}, u32[]{:S(2)}) collective-permute-start(bf16[256,1408]{1,0:T(8,128)(2,1)} %collective-permute-done.31), channel_id=1, source_target_pairs={{0,16},{16,0},{1,17},{17,1},{2,18},{18,2},{3,19},{19,3},{4,20},{20... | collective-permute-start | bytes 2162696 | tf_op jit(solution)/shard_map/ppermute | solution.py:55
  222.1 31.2 %collective-permute-start.19 = (bf16[1024,1024]{1,0:T(8,128)(2,1)}, bf16[1024,1024]{1,0:T(8,128)(2,1)}, u32[]{:S(2)}, u32[]{:S(2)}) collective-permute-start(bf16[1024,1024]{1,0:T(8,128)(2,1)} %pad_maximum_fusion.3), channel_id=1, source_target_pairs={{0,1},{1,0},{2,3},{3,2},{4,5},{5,4},{6,7},{7,6},{8,9},{9,8},{10,11... | collective-permute-start | bytes 6291464 | tf_op jit(solution)/shard_map/ppermute | solution.py:55
  223.2 67.2 %collective-permute-start.29 = (bf16[512,1408]{1,0:T(8,128)(2,1)}, bf16[512,1408]{1,0:T(8,128)(2,1)}, u32[]{:S(2)}, u32[]{:S(2)}) collective-permute-start(bf16[512,1408]{1,0:T(8,128)(2,1)} %pad_maximum_fusion.11), channel_id=1, source_target_pairs={{0,1},{1,0},{2,3},{3,2},{4,5},{5,4},{6,7},{7,6},{8,9},{9,8},{10,11... | collective-permute-start | bytes 4325384 | tf_op jit(solution)/shard_map/ppermute | solution.py:55
  237.0 56.0 %collective-permute-start.24 = (bf16[512,1408]{1,0:T(8,128)(2,1)}, bf16[512,1408]{1,0:T(8,128)(2,1)}, u32[]{:S(2)}, u32[]{:S(2)}) collective-permute-start(bf16[512,1408]{1,0:T(8,128)(2,1)} %pad_maximum_fusion.9), channel_id=1, source_target_pairs={{0,1},{1,0},{2,3},{3,2},{4,5},{5,4},{6,7},{7,6},{8,9},{9,8},{10,11... | collective-permute-start | bytes 4325384 | tf_op jit(solution)/shard_map/ppermute | solution.py:55
  239.6 19.1 %collective-permute-start.28 = (bf16[256,1408]{1,0:T(8,128)(2,1)}, bf16[256,1408]{1,0:T(8,128)(2,1)S(1)}, u32[]{:S(2)}, u32[]{:S(2)}) collective-permute-start(bf16[256,1408]{1,0:T(8,128)(2,1)} %copy-done.35), channel_id=1, source_target_pairs={{0,16},{16,0},{1,17},{17,1},{2,18},{18,2},{3,19},{19,3},{4,20},{20... | collective-permute-start | bytes 2162696 | tf_op jit(solution)/shard_map/ppermute | solution.py:55
  253.3 20.5 %collective-permute-start.23 = (bf16[256,1408]{1,0:T(8,128)(2,1)S(1)}, bf16[256,1408]{1,0:T(8,128)(2,1)S(1)}, u32[]{:S(2)}, u32[]{:S(2)}) collective-permute-start(bf16[256,1408]{1,0:T(8,128)(2,1)S(1)} %copy-done.39), channel_id=1, source_target_pairs={{0,16},{16,0},{1,17},{17,1},{2,18},{18,2},{3,19},{19,3},{4,20},{20... | collective-permute-start | bytes 2162696 | tf_op jit(solution)/shard_map/ppermute | solution.py:55
  258.7 16.4 %collective-permute-start.20 = (bf16[128,2048]{1,0:T(8,128)(2,1)S(1)}, bf16[128,2048]{1,0:T(8,128)(2,1)S(1)}, u32[]{:S(2)}, u32[]{:S(2)}) collective-permute-start(bf16[128,2048]{1,0:T(8,128)(2,1)S(1)} %slice.519), channel_id=1, source_target_pairs={{0,2},{2,0},{1,3},{3,1},{4,6},{6,4},{5,7},{7,5},{8,10},{10,8},{9,1... | collective-permute-start | bytes 1572872 | tf_op jit(solution)/shard_map/ppermute | solution.py:55
  273.8 21.9 %collective-permute-start.35 = (bf16[512,1408]{1,0:T(8,128)(2,1)}, bf16[512,1408]{1,0:T(8,128)(2,1)}, u32[]{:S(2)}, u32[]{:S(2)}) collective-permute-start(bf16[512,1408]{1,0:T(8,128)(2,1)} %pad_maximum_fusion.14), channel_id=1, source_target_pairs={{0,1},{1,0},{2,3},{3,2},{4,5},{5,4},{6,7},{7,6},{8,9},{9,8},{10,11... | collective-permute-start | bytes 4325384 | tf_op jit(solution)/shard_map/ppermute | solution.py:55
  275.1 23.1 %collective-permute-start.30 = (bf16[512,1408]{1,0:T(8,128)(2,1)}, bf16[512,1408]{1,0:T(8,128)(2,1)}, u32[]{:S(2)}, u32[]{:S(2)}) collective-permute-start(bf16[512,1408]{1,0:T(8,128)(2,1)} %pad_maximum_fusion.12), channel_id=1, source_target_pairs={{0,1},{1,0},{2,3},{3,2},{4,5},{5,4},{6,7},{7,6},{8,9},{9,8},{10,11... | collective-permute-start | bytes 4325384 | tf_op jit(solution)/shard_map/ppermute | solution.py:55
  278.6 30.5 %all-to-all-start = ((bf16[4,128,2048]{2,1,0:T(8,128)(2,1)}), bf16[4,128,2048]{2,1,0:T(8,128)(2,1)}, u32[]{:S(2)}, u32[]{:S(2)}) async-start(bf16[4,128,2048]{2,1,0:T(8,128)(2,1)} %broadcast_in_dim.21), calls=%async_computation | async-start | bytes 4194304 | tf_op jit(solution)/shard_map/all_to_all | solution.py:90
  286.8 14.2 %collective-permute-start.25 = (bf16[512,1408]{1,0:T(8,128)(2,1)S(1)}, bf16[512,1408]{1,0:T(8,128)(2,1)S(1)}, u32[]{:S(2)}, u32[]{:S(2)}) collective-permute-start(bf16[512,1408]{1,0:T(8,128)(2,1)S(1)} %copy-done.49), channel_id=1, source_target_pairs={{0,1},{1,0},{2,3},{3,2},{4,5},{5,4},{6,7},{7,6},{8,9},{9,8},{10,11... | collective-permute-start | bytes 4325384 | tf_op jit(solution)/shard_map/ppermute | solution.py:55
  331.3 29.8 %collective-permute-start.57 = (bf16[1024,1408]{1,0:T(8,128)(2,1)}, bf16[1024,1408]{1,0:T(8,128)(2,1)}, u32[]{:S(2)}, u32[]{:S(2)}) collective-permute-start(bf16[1024,1408]{1,0:T(8,128)(2,1)} %convolution_convert_fusion.2), channel_id=1, source_target_pairs={{0,1},{1,0},{2,3},{3,2},{4,5},{5,4},{6,7},{7,6},{8,9},{9,8},{10,11... | collective-permute-start | bytes 8650760 | tf_op jit(solution)/shard_map/ppermute | solution.py:55
  336.2 34.5 %all-to-all-start.6 = ((bf16[4,128,2048]{2,1,0:T(8,128)(2,1)}), bf16[4,128,2048]{2,1,0:T(8,128)(2,1)}, u32[]{:S(2)}, u32[]{:S(2)}) async-start(bf16[4,128,2048]{2,1,0:T(8,128)(2,1)} %bitcast.256), calls=%async_computation.6 | async-start | bytes 4194304 | tf_op jit(solution)/shard_map/all_to_all | solution.py:94
  345.9 29.5 %collective-permute-start.61 = (bf16[1024,1408]{1,0:T(8,128)(2,1)}, bf16[1024,1408]{1,0:T(8,128)(2,1)}, u32[]{:S(2)}, u32[]{:S(2)}) collective-permute-start(bf16[1024,1408]{1,0:T(8,128)(2,1)} %convolution_convert_fusion.1), channel_id=1, source_target_pairs={{0,1},{1,0},{2,3},{3,2},{4,5},{5,4},{6,7},{7,6},{8,9},{9,8},{10,11... | collective-permute-start | bytes 8650760 | tf_op jit(solution)/shard_map/ppermute | solution.py:55
  353.5 32.2 %collective-permute-start.65 = (bf16[1024,1408]{1,0:T(8,128)(2,1)}, bf16[1024,1408]{1,0:T(8,128)(2,1)}, u32[]{:S(2)}, u32[]{:S(2)}) collective-permute-start(bf16[1024,1408]{1,0:T(8,128)(2,1)} %convolution_convert_fusion), channel_id=1, source_target_pairs={{0,1},{1,0},{2,3},{3,2},{4,5},{5,4},{6,7},{7,6},{8,9},{9,8},{10,11... | collective-permute-start | bytes 8650760 | tf_op jit(solution)/shard_map/ppermute | solution.py:55
  368.7 34.7 %collective-permute-start.59 = (bf16[256,1408]{1,0:T(8,128)(2,1)}, bf16[256,1408]{1,0:T(8,128)(2,1)}, u32[]{:S(2)}, u32[]{:S(2)}) collective-permute-start(bf16[256,1408]{1,0:T(8,128)(2,1)} %get-tuple-element.85), channel_id=1, source_target_pairs={{0,16},{16,0},{1,17},{17,1},{2,18},{18,2},{3,19},{19,3},{4,20},{20... | collective-permute-start | bytes 2162696 | tf_op jit(solution)/shard_map/ppermute | solution.py:55
  369.2 116.1 %collective-permute-start.58 = (bf16[256,1408]{1,0:T(8,128)(2,1)}, bf16[256,1408]{1,0:T(8,128)(2,1)}, u32[]{:S(2)}, u32[]{:S(2)}) collective-permute-start(bf16[256,1408]{1,0:T(8,128)(2,1)} %get-tuple-element.84), channel_id=1, source_target_pairs={{0,16},{16,0},{1,17},{17,1},{2,18},{18,2},{3,19},{19,3},{4,20},{20... | collective-permute-start | bytes 2162696 | tf_op jit(solution)/shard_map/ppermute | solution.py:55
  370.8 29.7 %all-to-all-start.4 = ((bf16[4,128,2048]{2,1,0:T(8,128)(2,1)}), bf16[4,128,2048]{2,1,0:T(8,128)(2,1)}, u32[]{:S(2)}, u32[]{:S(2)}) async-start(bf16[4,128,2048]{2,1,0:T(8,128)(2,1)} %bitcast.255), calls=%async_computation.4 | async-start | bytes 4194304 | tf_op jit(solution)/shard_map/all_to_all | solution.py:94
  383.7 35.2 %collective-permute-start.63 = (bf16[256,1408]{1,0:T(8,128)(2,1)}, bf16[256,1408]{1,0:T(8,128)(2,1)}, u32[]{:S(2)}, u32[]{:S(2)}) collective-permute-start(bf16[256,1408]{1,0:T(8,128)(2,1)} %get-tuple-element.83), channel_id=1, source_target_pairs={{0,16},{16,0},{1,17},{17,1},{2,18},{18,2},{3,19},{19,3},{4,20},{20... | collective-permute-start | bytes 2162696 | tf_op jit(solution)/shard_map/ppermute | solution.py:55
  384.2 114.3 %collective-permute-start.62 = (bf16[256,1408]{1,0:T(8,128)(2,1)}, bf16[256,1408]{1,0:T(8,128)(2,1)}, u32[]{:S(2)}, u32[]{:S(2)}) collective-permute-start(bf16[256,1408]{1,0:T(8,128)(2,1)} %get-tuple-element.82), channel_id=1, source_target_pairs={{0,16},{16,0},{1,17},{17,1},{2,18},{18,2},{3,19},{19,3},{4,20},{20... | collective-permute-start | bytes 2162696 | tf_op jit(solution)/shard_map/ppermute | solution.py:55
  393.4 56.4 %collective-permute-start.67 = (bf16[256,1408]{1,0:T(8,128)(2,1)}, bf16[256,1408]{1,0:T(8,128)(2,1)}, u32[]{:S(2)}, u32[]{:S(2)}) collective-permute-start(bf16[256,1408]{1,0:T(8,128)(2,1)} %get-tuple-element.81), channel_id=1, source_target_pairs={{0,16},{16,0},{1,17},{17,1},{2,18},{18,2},{3,19},{19,3},{4,20},{20... | collective-permute-start | bytes 2162696 | tf_op jit(solution)/shard_map/ppermute | solution.py:55
  403.5 148.1 %collective-permute-start.66 = (bf16[256,1408]{1,0:T(8,128)(2,1)}, bf16[256,1408]{1,0:T(8,128)(2,1)}, u32[]{:S(2)}, u32[]{:S(2)}) collective-permute-start(bf16[256,1408]{1,0:T(8,128)(2,1)} %get-tuple-element.80), channel_id=1, source_target_pairs={{0,16},{16,0},{1,17},{17,1},{2,18},{18,2},{3,19},{19,3},{4,20},{20... | collective-permute-start | bytes 2162696 | tf_op jit(solution)/shard_map/ppermute | solution.py:55
  418.9 34.5 %collective-permute-start.36 = (bf16[128,2048]{1,0:T(8,128)(2,1)S(1)}, bf16[128,2048]{1,0:T(8,128)(2,1)S(1)}, u32[]{:S(2)}, u32[]{:S(2)}) collective-permute-start(bf16[128,2048]{1,0:T(8,128)(2,1)S(1)} %copy-done.48), channel_id=1, source_target_pairs={{0,2},{2,0},{1,3},{3,1},{4,6},{6,4},{5,7},{7,5},{8,10},{10,8},{9,1... | collective-permute-start | bytes 1572872 | tf_op jit(solution)/shard_map/ppermute | solution.py:55
  449.8 36.6 %collective-permute-start.60 = (bf16[256,1408]{1,0:T(8,128)(2,1)}, bf16[256,1408]{1,0:T(8,128)(2,1)S(1)}, u32[]{:S(2)}, u32[]{:S(2)}) collective-permute-start(bf16[256,1408]{1,0:T(8,128)(2,1)} %fusion.14), channel_id=1, source_target_pairs={{0,8},{8,0},{1,9},{9,1},{2,10},{10,2},{3,11},{11,3},{4,12},{12,4},... | collective-permute-start | bytes 2162696 | tf_op jit(solution)/shard_map/ppermute | solution.py:55
  482.6 50.9 %collective-permute-start.64 = (bf16[256,1408]{1,0:T(8,128)(2,1)}, bf16[256,1408]{1,0:T(8,128)(2,1)S(1)}, u32[]{:S(2)}, u32[]{:S(2)}) collective-permute-start(bf16[256,1408]{1,0:T(8,128)(2,1)} %fusion.11), channel_id=1, source_target_pairs={{0,8},{8,0},{1,9},{9,1},{2,10},{10,2},{3,11},{11,3},{4,12},{12,4},... | collective-permute-start | bytes 2162696 | tf_op jit(solution)/shard_map/ppermute | solution.py:55
  485.4 67.1 %collective-permute-start.68 = (bf16[256,1408]{1,0:T(8,128)(2,1)S(1)}, bf16[256,1408]{1,0:T(8,128)(2,1)S(1)}, u32[]{:S(2)}, u32[]{:S(2)}) collective-permute-start(bf16[256,1408]{1,0:T(8,128)(2,1)S(1)} %copy-done.59), channel_id=1, source_target_pairs={{0,8},{8,0},{1,9},{9,1},{2,10},{10,2},{3,11},{11,3},{4,12},{12,4},... | collective-permute-start | bytes 2162696 | tf_op jit(solution)/shard_map/ppermute | solution.py:55
  491.1 76.5 %all-to-all-start.7 = ((bf16[4,64,1408]{2,1,0:T(8,128)(2,1)}), bf16[4,64,1408]{2,1,0:T(8,128)(2,1)}, u32[]{:S(2)}, u32[]{:S(2)}) async-start(bf16[4,64,1408]{2,1,0:T(8,128)(2,1)} %bitcast.116), calls=%async_computation.7 | async-start | bytes 1441792 | tf_op jit(solution)/shard_map/all_to_all | solution.py:306
  495.4 63.3 %collective-permute-start.37 = (bf16[128,2048]{1,0:T(8,128)(2,1)}, bf16[128,2048]{1,0:T(8,128)(2,1)S(1)}, u32[]{:S(2)}, u32[]{:S(2)}) collective-permute-start(bf16[128,2048]{1,0:T(8,128)(2,1)} %slice.518), channel_id=1, source_target_pairs={{0,2},{2,0},{1,3},{3,1},{4,6},{6,4},{5,7},{7,5},{8,10},{10,8},{9,1... | collective-permute-start | bytes 1572872 | tf_op jit(solution)/shard_map/ppermute | solution.py:55
  498.5 95.3 %collective-permute-start.47 = (bf16[1024,1024]{1,0:T(8,128)(2,1)}, bf16[1024,1024]{1,0:T(8,128)(2,1)}, u32[]{:S(2)}, u32[]{:S(2)}) collective-permute-start(bf16[1024,1024]{1,0:T(8,128)(2,1)} %slice.350), channel_id=1, source_target_pairs={{0,1},{1,0},{2,3},{3,2},{4,5},{5,4},{6,7},{7,6},{8,9},{9,8},{10,11... | collective-permute-start | bytes 6291464 | tf_op jit(solution)/shard_map/ppermute | solution.py:55
  533.6 17.9 %collective-permute-start.40 = (bf16[256,256]{1,0:T(8,128)(2,1)S(1)}, bf16[256,256]{1,0:T(8,128)(2,1)S(1)}, u32[]{:S(2)}, u32[]{:S(2)}) collective-permute-start(bf16[256,256]{1,0:T(8,128)(2,1)S(1)} %slice.523), channel_id=1, source_target_pairs={{0,4},{4,0},{1,5},{5,1},{2,6},{6,2},{3,7},{7,3},{8,12},{12,8},{9,1... | collective-permute-start | bytes 393224 | tf_op jit(solution)/shard_map/ppermute | solution.py:55
  551.4 53.8 %collective-permute-start.52 = (bf16[1024,1024]{1,0:T(8,128)(2,1)}, bf16[1024,1024]{1,0:T(8,128)(2,1)}, u32[]{:S(2)}, u32[]{:S(2)}) collective-permute-start(bf16[1024,1024]{1,0:T(8,128)(2,1)} %slice.357), channel_id=1, source_target_pairs={{0,1},{1,0},{2,3},{3,2},{4,5},{5,4},{6,7},{7,6},{8,9},{9,8},{10,11... | collective-permute-start | bytes 6291464 | tf_op jit(solution)/shard_map/ppermute | solution.py:55
  567.5 15.5 %all-to-all-start.8 = ((bf16[4,64,1408]{2,1,0:T(8,128)(2,1)}), bf16[4,64,1408]{2,1,0:T(8,128)(2,1)}, u32[]{:S(2)}, u32[]{:S(2)}) async-start(bf16[4,64,1408]{2,1,0:T(8,128)(2,1)} %bitcast.249), calls=%async_computation.8 | async-start | bytes 1441792 | tf_op jit(solution)/shard_map/all_to_all | solution.py:306
  583.0 31.8 %all-to-all-start.9 = ((bf16[4,64,1408]{2,1,0:T(8,128)(2,1)}), bf16[4,64,1408]{2,1,0:T(8,128)(2,1)}, u32[]{:S(2)}, u32[]{:S(2)}) async-start(bf16[4,64,1408]{2,1,0:T(8,128)(2,1)} %bitcast.248), calls=%async_computation.9 | async-start | bytes 1441792 | tf_op jit(solution)/shard_map/all_to_all | solution.py:306
  599.5 26.4 %collective-permute-start.48 = (bf16[512,1024]{1,0:T(8,128)(2,1)}, bf16[512,1024]{1,0:T(8,128)(2,1)}, u32[]{:S(2)}, u32[]{:S(2)}) collective-permute-start(bf16[512,1024]{1,0:T(8,128)(2,1)} %slice.516), channel_id=1, source_target_pairs={{0,16},{16,0},{1,17},{17,1},{2,18},{18,2},{3,19},{19,3},{4,20},{20... | collective-permute-start | bytes 3145736 | tf_op jit(solution)/shard_map/ppermute | solution.py:55
  611.5 35.0 %collective-permute-start.53 = (bf16[512,1024]{1,0:T(8,128)(2,1)}, bf16[512,1024]{1,0:T(8,128)(2,1)}, u32[]{:S(2)}, u32[]{:S(2)}) collective-permute-start(bf16[512,1024]{1,0:T(8,128)(2,1)} %slice.515), channel_id=1, source_target_pairs={{0,16},{16,0},{1,17},{17,1},{2,18},{18,2},{3,19},{19,3},{4,20},{20... | collective-permute-start | bytes 3145736 | tf_op jit(solution)/shard_map/ppermute | solution.py:55
  627.6 23.5 %collective-permute-start.49 = (bf16[2,2,64,1024]{3,2,1,0:T(8,128)(2,1)S(1)}, bf16[2,2,64,1024]{3,2,1,0:T(8,128)(2,1)S(1)}, u32[]{:S(2)}, u32[]{:S(2)}) collective-permute-start(bf16[2,2,64,1024]{3,2,1,0:T(8,128)(2,1)S(1)} %fusion.35), channel_id=1, source_target_pairs={{0,4},{4,0},{1,5},{5,1},{2,6},{6,2},{3,7},{7,3},{8,12},{12,8},{9,1... | collective-permute-start | bytes 1572872 | tf_op jit(solution)/shard_map/ppermute | solution.py:55
  648.3 17.8 %collective-permute-start.54 = (bf16[2,2,64,1024]{3,2,1,0:T(8,128)(2,1)S(1)}, bf16[2,2,64,1024]{3,2,1,0:T(8,128)(2,1)S(1)}, u32[]{:S(2)}, u32[]{:S(2)}) collective-permute-start(bf16[2,2,64,1024]{3,2,1,0:T(8,128)(2,1)S(1)} %fusion.36), channel_id=1, source_target_pairs={{0,4},{4,0},{1,5},{5,1},{2,6},{6,2},{3,7},{7,3},{8,12},{12,8},{9,1... | collective-permute-start | bytes 1572872 | tf_op jit(solution)/shard_map/ppermute | solution.py:55
  651.3 16.6 %collective-permute-start.50 = (bf16[2,64,1024]{2,1,0:T(8,128)(2,1)S(1)}, bf16[2,64,1024]{2,1,0:T(8,128)(2,1)S(1)}, u32[]{:S(2)}, u32[]{:S(2)}) collective-permute-start(bf16[2,64,1024]{2,1,0:T(8,128)(2,1)S(1)} %fusion.45), channel_id=1, source_target_pairs={{0,8},{8,0},{1,9},{9,1},{2,10},{10,2},{3,11},{11,3},{4,12},{12,4},... | collective-permute-start | bytes 786440 | tf_op jit(solution)/shard_map/ppermute | solution.py:55
  (109 other events, 1004.8 us)

commit v3 on v2

--- a/solution.py
+++ b/solution.py
@@ -1,3 +1,4 @@
+import functools
 import math
 
 import jax
@@ -59,6 +60,10 @@
     return value.astype(BF16)
 
 
+def after(value, *events):
+    return lax.optimization_barrier((value, *events))[0]
+
+
 def pick(stacked, index, axis=0):
     return lax.dynamic_index_in_dim(stacked, index, axis, keepdims=False)
 
@@ -126,8 +131,9 @@
     query_rot, attended, attended_low, lse, bias,
 ):
     fill_bias(bias, key_place, query_place, query_start)
-    for head in range(query_sum.shape[0] // HEAD_DIM):
-        at = slice(head * HEAD_DIM, (head + 1) * HEAD_DIM)
+
+    def one(head, unused):
+        at = pl.ds(pl.multiple_of(head * HEAD_DIM, HEAD_DIM), HEAD_DIM)
         query = turn(query_sum[at, :], cosine[...], sine_part[...]).astype(BF16)
         query_rot[at, :] = query
         scores = mxu(key[...], query, NN) * (SCALE * LOG2E) + bias[...]
@@ -137,7 +143,19 @@
         result = mxu(value_t[...], weights.astype(BF16), NN) / total
         attended[at, :] = result
         attended_low[at, :] = result.astype(BF16)
-        lse[head : head + 1, :] = top + jnp.log2(total)
+        lse[pl.ds(head, 1), :] = top + jnp.log2(total)
+        return unused
+
+    each_head(one, query_sum, key)
+
+
+def each_head(one, heads_ref, key):
+    count = heads_ref.shape[0] // HEAD_DIM
+    if key.shape[0] > 2048:
+        lax.fori_loop(0, count, one, 0)
+    else:
+        for head in range(count):
+            one(head, 0)
 
 
 def attend_back_kernel(
@@ -145,36 +163,191 @@
     query_place, query_start, query_grad, kv_grad, bias,
 ):
     fill_bias(bias, key_place, query_place, query_start)
-    for head in range(query_rot.shape[0] // HEAD_DIM):
-        at = slice(head * HEAD_DIM, (head + 1) * HEAD_DIM)
+    kv_grad[...] = jnp.zeros_like(kv_grad)
+
+    def one(head, unused):
+        at = pl.ds(pl.multiple_of(head * HEAD_DIM, HEAD_DIM), HEAD_DIM)
         query = query_rot[at, :]
         grad_head = grad[at, :]
         delta = jnp.sum(grad_head.astype(F32) * attended[at, :], axis=0, keepdims=True)
         scores = mxu(key[...], query, NN) * (SCALE * LOG2E) + bias[...]
-        probs = jnp.exp2(scores - lse[head : head + 1, :])
+        probs = jnp.exp2(scores - lse[pl.ds(head, 1), :])
         grad_probs = mxu(value[...], grad_head, NN)
         grad_scores = (probs * (grad_probs - delta)).astype(BF16)
-        key_part = mxu(grad_scores, query, NT) * SCALE
-        value_part = mxu(probs.astype(BF16), grad_head, NT)
-        if head:
-            key_part = key_part + kv_grad[:, :HEAD_DIM]
-            value_part = value_part + kv_grad[:, HEAD_DIM:]
-        kv_grad[:, :HEAD_DIM] = key_part
-        kv_grad[:, HEAD_DIM:] = value_part
+        kv_grad[:, :HEAD_DIM] += mxu(grad_scores, query, NT) * SCALE
+        kv_grad[:, HEAD_DIM:] += mxu(probs.astype(BF16), grad_head, NT)
         grad_query = mxu(key_t[...], grad_scores, NN) * SCALE
         query_grad[at, :] = turn(grad_query, cosine[...], -sine_part[...]).astype(BF16)
-
-
-def local_call(kernel, outs, scratch, *args):
-    flops = 1 << 32
+        return unused
+
+    each_head(one, query_rot, key)
+
+
+def columns_of(width):
+    return width // 256, width % 256
+
+
+def each_block(width, body):
+    full, rest = columns_of(width)
+
+    def step(i, unused):
+        body(pl.ds(pl.multiple_of(i * 256, 256), 256))
+        return unused
+
+    lax.fori_loop(0, full, step, 0)
+    if rest:
+        body(pl.ds(full * 256, rest))
+
+
+def load_pieces(pieces, slots, held, sems):
+    waits = []
+    for slot, (arrays, at) in enumerate(slots):
+        copies = [
+            pltpu.make_async_copy(pieces[a].at[:, at], held.at[slot, p], sems.at[slot, p])
+            for p, a in enumerate(arrays)
+        ]
+        for copy in copies:
+            copy.start()
+        waits.append(copies)
+
+    def wait(slot):
+        for copy in waits[slot]:
+            copy.wait()
+
+    return wait
+
+
+def feed_kernel(normed, grad, *refs):
+    pieces = refs[:16]
+    mixed, grad_gate, grad_up, grad_two, held, gate_sum, up_sum, sems = refs[16:]
+    both, down = range(8), range(8, 16)
+    wait = load_pieces(pieces, [(both, 0), (both, 1), (down, 0)], held, sems)
+    width, part = normed.shape[1], mixed.shape[1]
+
+    def block(slot, at):
+        return held[slot, :, :, :, at].reshape(width, at.size)
+
+    wait(0)
+
+    def gate_step(at):
+        gate_sum[:, at] = mxu(normed[...], block(0, at), NN)
+
+    each_block(part, gate_step)
+    wait(1)
+
+    def up_step(at):
+        up_sum[:, at] = mxu(normed[...], block(1, at), NN)
+
+    each_block(part, up_step)
+    wait(2)
+
+    def down_step(at):
+        grad_mixed = mxu(grad[...], block(2, at), NN)
+        gate, up = gate_sum[:, at], up_sum[:, at]
+        sigmoid_gate = jax.nn.sigmoid(gate)
+        silu_gate = gate * sigmoid_gate
+        mixed[:, at] = (silu_gate * up).astype(BF16)
+        grad_up[:, at] = (grad_mixed * silu_gate).astype(BF16)
+        grad_gate[:, at] = (
+            grad_mixed * up * sigmoid_gate * (1.0 + gate * (1.0 - sigmoid_gate))
+        ).astype(BF16)
+
+    each_block(part, down_step)
+
+    def two_step(p, unused):
+        at = pl.ds(pl.multiple_of(p * (width // 8), width // 8), width // 8)
+        grad_two[:, at] = (
+            mxu(grad_gate[...], held[0, p].reshape(width // 8, part), NT)
+            + mxu(grad_up[...], held[1, p].reshape(width // 8, part), NT)
+        ).astype(BF16)
+        return unused
+
+    lax.fori_loop(0, 8, two_step, 0)
+
+
+TN = (((0,), (0,)), ((), ()))
+
+
+def outer(first_block, left, right, result):
+    rows = left.shape[1] // 8
+
+    def step(p, unused):
+        at = pl.ds(pl.multiple_of((first_block + p) * rows, rows), rows)
+        to = pl.ds(pl.multiple_of(p * rows, rows), rows)
+        result[to, :] = mxu(left[:, at], right[...], TN).astype(result.dtype)
+        return unused
+
+    lax.fori_loop(0, 4, step, 0)
+
+
+def outer_far_kernel(normed, grad, mixed, grad_gate, grad_up, down_far, gate_far, up_far):
+    outer(4, grad, mixed, down_far)
+    outer(4, normed, grad_gate, gate_far)
+    outer(4, normed, grad_up, up_far)
+
+
+def outer_near_kernel(normed, grad, mixed, grad_gate, grad_up, *refs):
+    pieces = refs[:8]
+    down_near, gate_near, up_near, feed, held, sems = refs[8:]
+    wait = load_pieces(pieces, [(range(8), 0)], held, sems)
+    outer(0, grad, mixed, down_near)
+    outer(0, normed, grad_gate, gate_near)
+    outer(0, normed, grad_up, up_near)
+    wait(0)
+    width, part = normed.shape[1], mixed.shape[1]
+
+    def feed_step(p, unused):
+        at = pl.ds(pl.multiple_of(p * (width // 8), width // 8), width // 8)
+        feed[:, at] = mxu(
+            mixed[...], held[0, p].reshape(width // 8, part), NT
+        ).astype(BF16)
+        return unused
+
+    lax.fori_loop(0, 8, feed_step, 0)
+
+
+def split_kernel(count, *refs):
+    matrices, result, sems = refs[:count], refs[count], refs[count + 1]
+    part = result.shape[-1]
+    copies = [
+        pltpu.make_async_copy(
+            matrix.at[:, pl.ds(i * part, part)], result.at[i, j], sems.at[i, j]
+        )
+        for i in range(4)
+        for j, matrix in enumerate(matrices)
+    ]
+    for copy in copies:
+        copy.start()
+    for copy in copies:
+        copy.wait()
+
+
+def split(*matrices):
+    rows, columns = matrices[0].shape
+    count = len(matrices)
+    anywhere = pl.BlockSpec(memory_space=pl.ANY)
+    return pl.pallas_call(
+        functools.partial(split_kernel, count),
+        out_shape=jax.ShapeDtypeStruct((4, count, rows, columns // 4), matrices[0].dtype),
+        in_specs=[anywhere] * count,
+        out_specs=anywhere,
+        scratch_shapes=[pltpu.SemaphoreType.DMA((4, count))],
+        cost_estimate=pl.CostEstimate(flops=0, bytes_accessed=1 << 22, transcendentals=0),
+    )(*matrices)
+
+
+def local_call(kernel, outs, scratch, *args, far=0, micros=10):
+    near = [pl.BlockSpec(memory_space=pltpu.VMEM)] * (len(args) - far)
     return pl.pallas_call(
         kernel,
         out_shape=outs,
-        in_specs=[pl.BlockSpec(memory_space=pltpu.VMEM)] * len(args),
+        in_specs=near + [pl.BlockSpec(memory_space=pl.ANY)] * far,
         out_specs=[pl.BlockSpec(memory_space=pltpu.VMEM)] * len(outs),
         scratch_shapes=scratch,
-        compiler_params=pltpu.CompilerParams(vmem_limit_bytes=48 << 20),
-        cost_estimate=pl.CostEstimate(flops=flops, bytes_accessed=1 << 24, transcendentals=1 << 22),
+        compiler_params=pltpu.CompilerParams(vmem_limit_bytes=56 << 20),
+        cost_estimate=pl.CostEstimate(
+            flops=micros * 900_000_000, bytes_accessed=1 << 20, transcendentals=0
+        ),
     )(*args)
 
 
@@ -253,25 +426,40 @@
     gains = jnp.stack([attention_gain, feedforward_gain])
     gains = jnp.pad(gains, ((0, 14), (0, 2 * HEAD_DIM - rows)))
     small = jnp.concatenate([keyvalue_weight, gains])
-    small = jnp.stack([small, swap(small, "h")])
-    small = pair(small, swap(small, "l"), l, 1)
-    small = pair(small, swap(small, "x"), x, 2)
+    small_steps = [swap(small, "h")]
+    small = jnp.stack([small, small_steps[-1]])
+    small_steps.append(swap(small, "l"))
+    small = pair(small, small_steps[-1], l, 1)
+    small_steps.append(swap(small, "x"))
+    small = pair(small, small_steps[-1], x, 2)
     small = gather_m(small, 1)
-    small = jnp.stack([small, swap(small, "y")])
-    small = jnp.stack([small, swap(small, "c")])
+    small_steps.append(swap(small, "y"))
+    small = jnp.stack([small, small_steps[-1]])
+    small_steps.append(swap(small, "c"))
+    small = jnp.stack([small, small_steps[-1]])
     small = small.reshape(width // rows, rows + 16, 2 * HEAD_DIM)
     keyvalue_full = small[:, :rows].reshape(width, 2 * HEAD_DIM)
     gain_one = small[:, rows, :rows].reshape(1, width).astype(F32)
     gain_two = small[:, rows + 1, :rows].reshape(1, width).astype(F32)
 
-    def gather_heads(weight):
+    def halves(weight):
         parts = weight.reshape(rows, 2, half_width).transpose(1, 0, 2)
-        got = pair(pick(parts, x), swap(pick(parts, 1 - x), "x"), x)
-        got = jnp.stack([got, swap(got, "h")])
-        got = pair(got, swap(got, "l"), l, 1)
+        return pick(parts, x), pick(parts, 1 - x)
+
+    def gather_heads(weight, ahead=None):
+        ahead = ahead or [()] * 5
+        mine, sent = halves(weight)
+        steps = [swap(after(sent, *ahead[0]), "x")]
+        got = pair(mine, steps[-1], x)
+        steps.append(swap(after(got, *ahead[1]), "h"))
+        got = jnp.stack([got, steps[-1]])
+        steps.append(swap(after(got, *ahead[2]), "l"))
+        got = pair(got, steps[-1], l, 1)
         got = gather_m(got, 1).reshape(-1, half_width)
-        got = jnp.concatenate([got, swap(got, "y")])
-        return jnp.concatenate([got, swap(got, "c")])
+        steps.append(swap(after(got, *ahead[3]), "y"))
+        got = jnp.concatenate([got, steps[-1]])
+        steps.append(swap(after(got, *ahead[4]), "c"))
+        return jnp.concatenate([got, steps[-1]]), [(step,) for step in steps]
 
     def scatter_heads(grad):
         grad = fold(fold(low(grad), "c"), "y")
@@ -281,34 +469,19 @@
         other = swap(low(pick(grad, 1 - x)), "x").astype(F32)
         return pair(pick(grad, x), other, x, 1).reshape(rows, query_width)
 
-    query_full = gather_heads(query_weight)
-    output_full = gather_heads(output_weight)
-
-    def gather_feed(weight):
-        parts = weight.reshape(rows, 4, part).transpose(1, 0, 2)
+    query_full, query_steps = gather_heads(query_weight)
+    output_full, output_steps = gather_heads(output_weight, query_steps)
+
+    def exchange(parts):
         got = lax.all_to_all(parts, ("l", "x"), 0, 0)
-        got = gather_m(got, 0).reshape(width // 8, part)
-        by_h = swap(got, "h")
-        near = jnp.concatenate([got, by_h])
-        far = jnp.concatenate([swap(got, "y"), swap(by_h, "y")])
-        return jnp.concatenate([near, far, swap(near, "c"), swap(far, "c")])
-
-    def scatter_feed(left, right):
-        half, quarter = width // 2, width // 4
-        sent = swap(low(contract_first(left[:, half:], right)), "c")
-        grad = contract_first(left[:, :half], right) + sent.astype(F32)
-        near, far = grad[:quarter], low(grad[quarter:])
-        block = width // 8
-        by_h = near[block:] + swap(far[block:], "y").astype(F32)
-        own = near[:block] + swap(far[:block], "y").astype(F32)
-        own = own + swap(low(by_h), "h").astype(F32)
-        own = low(scatter_m(own.reshape(M, 4, rows, part), 0))
-        got = lax.all_to_all(own, ("l", "x"), 0, 0)
-        return got.transpose(1, 0, 2).reshape(rows, hidden_units).astype(F32)
-
-    gate_full = gather_feed(gate_weight)
-    up_full = gather_feed(up_weight)
-    down_full = gather_feed(down_weight)
+        got = gather_m(got, 0)
+        return got.reshape(M * 4, -1, rows, part)
+
+    both = exchange(after(split(gate_weight, up_weight), small_steps[0]))
+    both = after(both, small_steps[3])
+    both_h = swap(both, "h")
+    both_y = swap(both, "y")
+    down = exchange(after(split(down_weight), both, small_steps[4]))
 
     input_mine = inward(block_input[0])
     inputs = jnp.concatenate([input_mine, swap(input_mine, "x")]).astype(F32)
@@ -352,28 +525,49 @@
     branch = lax.dot_general(
         attended_low, output_full, (((0,), (1,)), ((), ())), preferred_element_type=F32
     )
-    hidden = inputs[:tokens] + fold(branch, "x")
+    branch_sent = low(branch[tokens:])
+    hidden = inputs[:tokens] + (branch[:tokens] + swap(branch_sent, "x").astype(F32))
+
+    grad_mine = inward(output_grad[0])
+    down = after(down, query_sum)
+    down_y = swap(after(down, both_y), "y")
+    both_h = after(both_h, branch_sent)
+    down_h = swap(after(down, both_h), "h")
+    both_far = swap(both_h, "y")
+    down_far = swap(after(down_h, both_far), "y")
+    both_all = [both, both_h, both_y, both_far]
+    down_all = [down, down_h, down_y, down_far]
+    both_all = both_all + [swap(piece, "c") for piece in both_all]
+    down_all = down_all + [swap(piece, "c") for piece in down_all]
+    grad_low = gather_group(after(grad_mine, down, query_sum)).reshape(-1, width)
 
     scale_two = lax.rsqrt(jnp.mean(hidden * hidden, axis=-1, keepdims=True) + EPSILON)
     normed_two = hidden * scale_two
-    grad_mine = inward(output_grad[0])
-    grad_low = gather_group(grad_mine).reshape(-1, width)
     normed_two_low = gather_group(low(normed_two * gain_two)).reshape(-1, width)
-    gate_sum = dot(normed_two_low, gate_full)
-    up_sum = dot(normed_two_low, up_full)
-    sigmoid_gate = jax.nn.sigmoid(gate_sum)
-    silu_gate = gate_sum * sigmoid_gate
-    mixed_low = low(silu_gate * up_sum)
-    grad_mixed = dot(grad_low, down_full)
-    grad_gate = low(
-        grad_mixed * up_sum * sigmoid_gate * (1.0 + gate_sum * (1.0 - sigmoid_gate))
-    )
-    grad_up = low(grad_mixed * silu_gate)
-    blocks = (4, tokens, width)
-    grad_two = scatter_group(
-        (contract_last(grad_gate, gate_full) + contract_last(grad_up, up_full)).reshape(blocks)
-    )
-    feed_out = scatter_group(contract_last(mixed_low, down_full).reshape(blocks))
+    group = 4 * tokens
+    units = jax.ShapeDtypeStruct((group, part), BF16)
+    features = jax.ShapeDtypeStruct((group, width), BF16)
+    held = pltpu.VMEM((3, 8, M * 4, rows, part), BF16)
+    wide_sum = pltpu.VMEM((group, part), F32)
+    mixed_low, grad_gate, grad_up, grad_two = local_call(
+        feed_kernel,
+        [units, units, units, features],
+        [held, wide_sum, wide_sum, pltpu.SemaphoreType.DMA((3, 8))],
+        normed_two_low, grad_low, *both_all, *down_all,
+        far=16, micros=22,
+    )
+    grad_two = scatter_group(grad_two.reshape(4, tokens, width))
+    outers = (normed_two_low, grad_low, mixed_low, grad_gate, grad_up)
+    half_rows = jax.ShapeDtypeStruct((width // 2, part), BF16)
+    far_parts = local_call(outer_far_kernel, [half_rows] * 3, [], *outers, micros=8)
+    *near_parts, feed_out = local_call(
+        outer_near_kernel,
+        [half_rows] * 3 + [features],
+        [pltpu.VMEM((1, 8, M * 4, rows, part), BF16), pltpu.SemaphoreType.DMA((1, 8))],
+        *(after(o, *far_parts) for o in outers), *down_all,
+        far=8, micros=12,
+    )
+    feed_out = scatter_group(after(feed_out, grad_two).reshape(4, tokens, width))
     block_output = outward(low(hidden + feed_out))[None]
     gain_two_grad = jnp.sum(grad_two * normed_two, axis=0)
     grad_hidden = grad_mine.astype(F32) + norm_back(grad_two * gain_two, normed_two, scale_two)
@@ -394,7 +588,8 @@
         [pltpu.VMEM((stream_len, 2 * tokens), F32)],
         query_rot, key, key.T, value, grad_heads, attended, lse, cosine_t, sine_t, *places_used,
     )
-    for axis in "cxl":
+    kv_grad = kv_first = fold(kv_grad, "c")
+    for axis in "xl":
         kv_grad = fold(kv_grad, axis)
     kv_grad = scatter_m(kv_grad.reshape(M, 2 * tokens, 2 * HEAD_DIM), 0)
     kv_mine = fold(kv_grad, "h") + shared_grad[0].astype(F32)
@@ -417,9 +612,30 @@
         grad_hidden + norm_back(grad_one * gain_one, normed_mine, scale_one[:tokens])
     )[None]
 
-    down_weight_grad = scatter_feed(grad_low, mixed_low)
-    gate_weight_grad = scatter_feed(normed_two_low, grad_gate)
-    up_weight_grad = scatter_feed(normed_two_low, grad_up)
+    block = width // 8
+
+    def fold_y(near, far):
+        got = swap(far, "c")
+
+        def total(i):
+            at = slice(i * block, (i + 1) * block)
+            return near[at].astype(F32) + got[at].astype(F32)
+
+        return total, swap(low(total(3)), "y")
+
+    def finish_feed(total, by_y, event):
+        by_h = swap(low(total(1) + after(by_y, *event).astype(F32)), "h")
+        own = total(0) + swap(low(total(2)), "y").astype(F32)
+        own = own + by_h.astype(F32)
+        own = low(scatter_m(own.reshape(M, 4, rows, part), 0))
+        got = lax.all_to_all(own, ("l", "x"), 0, 0)
+        return got.transpose(1, 0, 2).reshape(rows, hidden_units).astype(F32)
+
+    totals = [fold_y(n, f) for n, f in zip(near_parts, far_parts)]
+    events = [(grad_two,), (grad_heads,), (kv_first,)]
+    down_weight_grad, gate_weight_grad, up_weight_grad = (
+        finish_feed(*total, event) for total, event in zip(totals, events)
+    )
     across = (((0,), (1,)), ((), ()))
     output_weight_grad = scatter_heads(
         lax.dot_general(grad_hidden_low, attended_low, across, preferred_element_type=F32)

time: 695 us -> 763 us (1.098)
  Pallas kernels: 22.4 us -> 156 us
  matrix products: 89.4 us -> 25.2 us
  waiting for transfers between devices: 268 us -> 309 us
  local copies, waits for them, and re-layouts: 98.6 us -> 64.3 us
  starting transfers between devices: 119 us -> 107 us
    pallas_call x2 -> x7, Pallas kernels: 22.4 us -> 156 us  [the longest x5 88.3 us: local_call(): pl.pallas_call(kernel, out_shape=outs, in_specs=near + [pl.BlockSpec(memo...]
    ppermute x69 -> x68, waiting for transfers between devices: 263 us -> 304 us  [swap(): return lax.ppermute(value, axis, [(0, 1), (1, 0)])]
    dot_general x7 -> x1, matrix products: 35.5 us -> 1.97 us  [contract_first(): lax.dot_general(left, right, (((0,), (0,)), ((), ())), preferred_element_...]
    unnamed x209 -> x146, local copies, waits for them, and re-layouts: 44.1 us -> 17.5 us
    dot_general x4 -> x1, matrix products: 20.9 us -> 0.31 us  [dot(): return jnp.dot(left, right, preferred_element_type=F32)]
    all_to_all x6 -> x5, starting transfers between devices: 36.5 us -> 21.2 us  [the longest x3 12.7 us: finish_feed(): got = lax.all_to_all(own, ('l', 'x'), 0, 0)]
    dot_general x4 -> x1, matrix products: 16.5 us -> 2.57 us  [contract_last(): lax.dot_general(left, right, (((1,), (1,)), ((), ())), preferred_element_...]
    concatenate x8 -> x2, other arithmetic: 17.3 us -> 6.11 us  [gather_heads(): got = jnp.concatenate([got, steps[-1]])]
  transfers between devices with their start and end apart: 79 -> 77, of which waited for: 26 -> 28; matrix products, arithmetic and copies ran while one was open for 34% -> 22% of each run, Pallas kernels for 3% -> 15%
where the time goes in v3:
time: 763 us; the launch traced here: 753 us
  waiting for transfers between devices  309 us (40%)
  Pallas kernels  156 us (20%)
  starting transfers between devices  107 us (14%)
  other arithmetic  89 us (12%)
  local copies, waits for them, and re-layouts  64.3 us (8%)
  matrix products  25.2 us (3%)
    ppermute x68, waiting for transfers between devices, swap(): return lax.ppermute(value, axis, [(0, 1), (1, 0)])  304 us
    pallas_call x5, Pallas kernels, local_call(): pl.pallas_call(kernel, out_shape=outs, in_specs=near + [pl.BlockSpec(memo...  88.3 us
    pallas_call x2, Pallas kernels, split(): pl.pallas_call(functools.partial(split_kernel, count), out_shape=jax.Shap...  67.8 us
    ppermute x68, starting transfers between devices, swap(): return lax.ppermute(value, axis, [(0, 1), (1, 0)])  67.3 us
    convert_element_type x11, other arithmetic, low(): return value.astype(BF16)  27.3 us
    unnamed x146, local copies, waits for them, and re-layouts  17.5 us
  transfers between devices with their start and end apart: 77, of which 28 were waited for; matrix products, arithmetic and copies ran while one was open for 22% of the time, Pallas kernels for 15%

profile of v3, /device:TPU:0, one launch (start us, length us, event | category | flops | bytes accessed | tf_op | source)
XLA Modules:
  0.0 752.6 jit_solution(5057945176208761472)
XLA Ops:
  2.2 4.0 collective-permute-start.6
  23.0 6.2 collective-permute-done.8
  31.5 3.4 collective-permute-done.2
  35.8 44.9 %shard_map.214 = bf16[4,2,64,1408]{3,2,1,0:T(8,128)(2,1)} custom-call(bf16[64,5632]{1,0:T(8,128)(2,1)} %refs_0_.3, bf16[64,5632]{1,0:T(8,128)(2,1)} %refs_1_.1), custom_call_target="tpu_custom_call" | custom-call | bytes 4194304 | tf_op jit(solution)/shard_map/pallas_call | solution.py:329
  80.6 4.3 all-to-all-start.1
  93.2 12.4 %collective-permute-done.16 = bf16[2,64,1024]{2,1,0:T(8,128)(2,1)S(1)} collective-permute-done((bf16[2,64,1024]{2,1,0:T(8,128)(2,1)S(1)}, bf16[2,64,1024]{2,1,0:T(8,128)(2,1)S(1)}, u32[]{:S(2)}, u32[]{:S(2)}) %collective-permute-start.16) | collective-permute-done | bytes 262176 | tf_op jit(solution)/shard_map/ppermute | solution.py:56
  106.7 4.6 collective-permute-start.17
  117.3 3.1 pad_maximum_fusion.2
  122.3 4.2 collective-permute-done.11
  137.1 23.0 %shard_map.213 = bf16[4,1,64,1408]{3,2,1,0:T(8,128)(2,1)} custom-call(bf16[64,5632]{1,0:T(8,128)(2,1)} %refs_0_.2), custom_call_target="tpu_custom_call" | custom-call | bytes 4194304 | tf_op jit(solution)/shard_map/pallas_call | solution.py:329
  164.4 4.2 all-to-all-start.2
  168.6 3.0 pad_maximum_fusion.3
  179.0 4.5 fusion.3.query_sum
  185.6 2.6 broadcast_in_dim.22
  188.2 4.7 all-to-all-start.3
  192.8 2.6 fusion.60
  197.5 13.1 %shard_map.212 = (bf16[1024,256]{1,0:T(8,128)(2,1)}, f32[1024,256]{1,0:T(8,128)}, bf16[1024,256]{1,0:T(8,128)(2,1)}, f32[8,256]{1,0:T(8,128)}) custom-call(f32[1024,256]{1,0:T(8,128)} %fusion.3.query_sum, bf16[2048,128]{1,0:T(8,128)(2,1)} %get-tuple-element.147.key, bf16[128,2048]{1,0:T(8,128)(2,1)} %copy.110.value_t, f32[64,256]{1,0:T(8,128)} %get-tuple-element.180.cosine, ...), custom_call_target="tpu_custom_call" | custom-call | flops 8999999488 | bytes 1048576 | tf_op jit(solution)/shard_map/pallas_call | solution.py:341
  210.6 3.7 fusion.1
  221.7 8.0 %collective-permute-done.20 = bf16[128,2048]{1,0:T(8,128)(2,1)} collective-permute-done((bf16[128,2048]{1,0:T(8,128)(2,1)}, bf16[128,2048]{1,0:T(8,128)(2,1)}, u32[]{:S(2)}, u32[]{:S(2)}) %collective-permute-start.20) | collective-permute-done | bytes 524320 | tf_op jit(solution)/shard_map/ppermute | solution.py:56
  233.0 2.6 broadcast_in_dim.21
  235.6 4.5 all-to-all-start
  240.1 42.6 %collective-permute-done.21.refs_1_ = bf16[4,2,64,1408]{3,2,1,0:T(8,128)(2,1)} collective-permute-done((bf16[4,2,64,1408]{3,2,1,0:T(8,128)(2,1)}, bf16[4,2,64,1408]{3,2,1,0:T(8,128)(2,1)}, u32[]{:S(2)}, u32[]{:S(2)}) %collective-permute-start.21) | collective-permute-done | bytes 1441824 | tf_op jit(solution)/shard_map/ppermute | solution.py:56
  285.3 33.5 %collective-permute-done.28.refs_9_.refs_1_ = bf16[4,1,64,1408]{3,2,1,0:T(8,128)(2,1)S(1)} collective-permute-done((bf16[4,1,64,1408]{3,2,1,0:T(8,128)(2,1)}, bf16[4,1,64,1408]{3,2,1,0:T(8,128)(2,1)S(1)}, u32[]{:S(2)}, u32[]{:S(2)}) %collective-permute-start.28) | collective-permute-done | bytes 720928 | tf_op jit(solution)/shard_map/ppermute | solution.py:56
  320.2 12.7 %collective-permute-done.29.refs_10_.refs_2_ = bf16[4,1,64,1408]{3,2,1,0:T(8,128)(2,1)S(1)} collective-permute-done((bf16[4,1,64,1408]{3,2,1,0:T(8,128)(2,1)}, bf16[4,1,64,1408]{3,2,1,0:T(8,128)(2,1)S(1)}, u32[]{:S(2)}, u32[]{:S(2)}) %collective-permute-start.29) | collective-permute-done | bytes 720928 | tf_op jit(solution)/shard_map/ppermute | solution.py:56
  333.5 12.9 %collective-permute-done.30.refs_11_.refs_3_ = bf16[4,1,64,1408]{3,2,1,0:T(8,128)(2,1)S(1)} collective-permute-done((bf16[4,1,64,1408]{3,2,1,0:T(8,128)(2,1)S(1)}, bf16[4,1,64,1408]{3,2,1,0:T(8,128)(2,1)S(1)}, u32[]{:S(2)}, u32[]{:S(2)}) %collective-permute-start.30) | collective-permute-done | bytes 720928 | tf_op jit(solution)/shard_map/ppermute | solution.py:56
  349.3 28.0 %shard_map.215 = (bf16[512,1408]{1,0:T(8,128)(2,1)}, bf16[512,1408]{1,0:T(8,128)(2,1)}, bf16[512,1408]{1,0:T(8,128)(2,1)}, bf16[512,2048]{1,0:T(8,128)(2,1)}) custom-call(bf16[512,2048]{1,0:T(8,128)(2,1)} %bitcast.68.normed, bf16[512,2048]{1,0:T(8,128)(2,1)} %bitcast.73.grad, bf16[4,2,64,1408]{3,2,1,0:T(8,128)(2,1)} %all-to-all-done.1.refs_0_, ...), custom_call_target="tpu_custom_call" | custom-call | flops 19800000512 | bytes 1048576 | tf_op jit(solution)/shard_map/pallas_call | solution.py:341
  377.4 13.7 %shard_map.216 = (bf16[1024,1408]{1,0:T(8,128)(2,1)}, bf16[1024,1408]{1,0:T(8,128)(2,1)}, bf16[1024,1408]{1,0:T(8,128)(2,1)}) custom-call(bf16[512,2048]{1,0:T(8,128)(2,1)} %bitcast.68.normed, bf16[512,2048]{1,0:T(8,128)(2,1)} %bitcast.73.grad, bf16[512,1408]{1,0:T(8,128)(2,1)} %get-tuple-element.74.mixed, bf16[512,1408]{1,0:T(8,128)(2,1)} %get-tuple-element.75.grad_gate, ...), custom_call_target="tpu_custom_call" | custom-call | flops 7200000000 | bytes 1048576 | tf_op jit(solution)/shard_map/pallas_call | solution.py:341
  391.8 4.6 all-to-all-start.4
  401.3 19.2 %shard_map.217 = (bf16[1024,1408]{1,0:T(8,128)(2,1)}, bf16[1024,1408]{1,0:T(8,128)(2,1)}, bf16[1024,1408]{1,0:T(8,128)(2,1)}, bf16[512,2048]{1,0:T(8,128)(2,1)}) custom-call(bf16[512,2048]{1,0:T(8,128)(2,1)} %bitcast.68.normed, bf16[512,2048]{1,0:T(8,128)(2,1)} %bitcast.73.grad, bf16[512,1408]{1,0:T(8,128)(2,1)} %get-tuple-element.74.mixed, ...), custom_call_target="tpu_custom_call" | custom-call | flops 10800000000 | bytes 1048576 | tf_op jit(solution)/shard_map/pallas_call | solution.py:341
  420.5 3.4 add_convert_fusion.3
  425.9 2.9 add_convert_fusion.11
  430.9 2.8 add_convert_fusion.7
  438.6 20.0 %collective-permute-done.66 = bf16[256,1408]{1,0:T(8,128)(2,1)} collective-permute-done((bf16[256,1408]{1,0:T(8,128)(2,1)}, bf16[256,1408]{1,0:T(8,128)(2,1)}, u32[]{:S(2)}, u32[]{:S(2)}) %collective-permute-start.66) | collective-permute-done | bytes 720928 | tf_op jit(solution)/shard_map/ppermute | solution.py:56
  463.1 8.0 %collective-permute-done.35 = bf16[128,2048]{1,0:T(8,128)(2,1)S(1)} collective-permute-done((bf16[128,2048]{1,0:T(8,128)(2,1)S(1)}, bf16[128,2048]{1,0:T(8,128)(2,1)S(1)}, u32[]{:S(2)}, u32[]{:S(2)}) %collective-permute-start.35) | collective-permute-done | bytes 524320 | tf_op jit(solution)/shard_map/ppermute | solution.py:56
  472.7 4.4 fusion.7.grad
  477.1 14.3 %shard_map.218 = (bf16[1024,256]{1,0:T(8,128)(2,1)}, f32[2048,256]{1,0:T(8,128)}) custom-call(bf16[1024,256]{1,0:T(8,128)(2,1)} %get-tuple-element.80.query_rot, bf16[2048,128]{1,0:T(8,128)(2,1)} %get-tuple-element.147.key, bf16[128,2048]{1,0:T(8,128)(2,1)} %copy.120.key_t, bf16[2048,128]{1,0:T(8,128)(2,1)} %get-tuple-element.144.value, ...), custom_call_target="tpu_custom_call" | custom-call | flops 8999999488 | bytes 1048576 | tf_op jit(solution)/shard_map/pallas_call | solution.py:341
  491.4 3.8 fusion.2
  500.8 2.7 add_convert_fusion.9
  503.7 16.0 %collective-permute-done.62 = bf16[256,1408]{1,0:T(8,128)(2,1)} collective-permute-done((bf16[256,1408]{1,0:T(8,128)(2,1)}, bf16[256,1408]{1,0:T(8,128)(2,1)}, u32[]{:S(2)}, u32[]{:S(2)}) %collective-permute-start.62) | collective-permute-done | bytes 720928 | tf_op jit(solution)/shard_map/ppermute | solution.py:56
  521.4 2.7 add_convert_fusion.5
  524.1 3.2 collective-permute-done.38
  528.9 25.3 %collective-permute-done.67 = bf16[256,1408]{1,0:T(8,128)(2,1)S(1)} collective-permute-done((bf16[256,1408]{1,0:T(8,128)(2,1)S(1)}, bf16[256,1408]{1,0:T(8,128)(2,1)S(1)}, u32[]{:S(2)}, u32[]{:S(2)}) %collective-permute-start.67) | collective-permute-done | bytes 720928 | tf_op jit(solution)/shard_map/ppermute | solution.py:56
  554.2 2.6 add_convert_fusion
  556.9 4.1 all-to-all-start.8
  560.9 11.2 %collective-permute-done.39 = bf16[256,256]{1,0:T(8,128)(2,1)S(1)} collective-permute-done((bf16[256,256]{1,0:T(8,128)(2,1)S(1)}, bf16[256,256]{1,0:T(8,128)(2,1)S(1)}, u32[]{:S(2)}, u32[]{:S(2)}) %collective-permute-start.39) | collective-permute-done | bytes 131104 | tf_op jit(solution)/shard_map/ppermute | solution.py:56
  573.3 2.9 collective-permute-start.40
  576.2 3.0 add_convert_fusion.8
  579.1 31.0 %collective-permute-done.40 = bf16[128,256]{1,0:T(8,128)(2,1)S(1)} collective-permute-done((bf16[128,256]{1,0:T(8,128)(2,1)S(1)}, bf16[128,256]{1,0:T(8,128)(2,1)S(1)}, u32[]{:S(2)}, u32[]{:S(2)}) %collective-permute-start.40) | collective-permute-done | bytes 65568 | tf_op jit(solution)/shard_map/ppermute | solution.py:56
  610.5 2.6 multiply_reduce_fusion.2
  613.1 4.2 all-to-all-start.6
  620.5 3.1 add_convert_fusion.4
  623.5 4.5 all-to-all-done.6
  628.0 4.4 all-to-all-start.7
  632.4 2.7 convolution_convert_fusion
  642.8 4.4 all-to-all-start.5
  649.8 3.6 collective-permute-done.42
  660.8 13.6 %collective-permute-done.43 = bf16[256,384]{0,1:T(8,128)(2,1)S(1)} collective-permute-done((bf16[256,384]{0,1:T(8,128)(2,1)S(1)}, bf16[256,384]{0,1:T(8,128)(2,1)S(1)}, u32[]{:S(2)}, u32[]{:S(2)}) %collective-permute-start.43) | collective-permute-done | bytes 196640 | tf_op jit(solution)/shard_map/ppermute | solution.py:56
  674.7 3.5 collective-permute-start.44
  678.1 3.1 convert_add_fusion
  691.9 2.9 multiply_add_fusion
  702.3 5.5 collective-permute-done.52
  720.1 11.9 %collective-permute-done.53 = bf16[2,2,64,1024]{3,2,1,0:T(8,128)(2,1)} collective-permute-done((bf16[2,2,64,1024]{3,2,1,0:T(8,128)(2,1)}, bf16[2,2,64,1024]{3,2,1,0:T(8,128)(2,1)}, u32[]{:S(2)}, u32[]{:S(2)}) %collective-permute-start.53) | collective-permute-done | bytes 524320 | tf_op jit(solution)/shard_map/ppermute | solution.py:56
  734.7 11.0 %collective-permute-done.54 = bf16[2,64,1024]{2,1,0:T(8,128)(2,1)S(1)} collective-permute-done((bf16[2,64,1024]{2,1,0:T(8,128)(2,1)S(1)}, bf16[2,64,1024]{2,1,0:T(8,128)(2,1)S(1)}, u32[]{:S(2)}, u32[]{:S(2)}) %collective-permute-start.54) | collective-permute-done | bytes 262176 | tf_op jit(solution)/shard_map/ppermute | solution.py:56
  748.3 3.0 collective-permute-done.55
  (425 shorter events, 171.0 us)
Async XLA Ops:
  2.2 13.9 %collective-permute-start.6 = (bf16[80,256]{1,0:T(8,128)(2,1)S(1)}, bf16[80,256]{1,0:T(8,128)(2,1)S(1)}, u32[]{:S(2)}, u32[]{:S(2)}) collective-permute-start(bf16[80,256]{1,0:T(8,128)(2,1)S(1)} %get-tuple-element.178), channel_id=1, source_target_pairs={{0,8},{8,0},{1,9},{9,1},{2,10},{10,2},{3,11},{11,3},{4,12},{12,4},... | collective-permute-start | bytes 122888 | tf_op jit(solution)/shard_map/ppermute | solution.py:56
  8.0 14.2 %collective-permute-start.1 = (bf16[64,1024]{1,0:T(8,128)(2,1)S(1)}, bf16[64,1024]{1,0:T(8,128)(2,1)S(1)}, u32[]{:S(2)}, u32[]{:S(2)}) collective-permute-start(bf16[64,1024]{1,0:T(8,128)(2,1)S(1)} %bitcast.253), channel_id=1, source_target_pairs={{0,2},{2,0},{1,3},{3,1},{4,6},{6,4},{5,7},{7,5},{8,10},{10,8},{9,1... | collective-permute-start | bytes 393224 | tf_op jit(solution)/shard_map/ppermute | solution.py:56
  11.1 79.0 %collective-permute-start = (bf16[128,2048]{1,0:T(8,128)(2,1)S(1)}, bf16[128,2048]{1,0:T(8,128)(2,1)S(1)}, u32[]{:S(2)}, u32[]{:S(2)}) collective-permute-start(bf16[128,2048]{1,0:T(8,128)(2,1)S(1)} %copy.105), channel_id=1, source_target_pairs={{0,2},{2,0},{1,3},{3,1},{4,6},{6,4},{5,7},{7,5},{8,10},{10,8},{9,1... | collective-permute-start | bytes 1572872 | tf_op jit(solution)/shard_map/ppermute | solution.py:56
  22.2 12.7 %collective-permute-start.2 = (bf16[2,64,1024]{2,1,0:T(8,128)(2,1)S(1)}, bf16[2,64,1024]{2,1,0:T(8,128)(2,1)S(1)}, u32[]{:S(2)}, u32[]{:S(2)}) collective-permute-start(bf16[2,64,1024]{2,1,0:T(8,128)(2,1)S(1)} %maximum_select_fusion.7), channel_id=1, source_target_pairs={{0,8},{8,0},{1,9},{9,1},{2,10},{10,2},{3,11},{11,3},{4,12},{12,4},... | collective-permute-start | bytes 786440 | tf_op jit(solution)/shard_map/ppermute | solution.py:56
  22.7 62.3 %collective-permute-start.15 = (bf16[64,1024]{1,0:T(8,128)(2,1)}, bf16[64,1024]{1,0:T(8,128)(2,1)}, u32[]{:S(2)}, u32[]{:S(2)}) collective-permute-start(bf16[64,1024]{1,0:T(8,128)(2,1)} %bitcast.203), channel_id=1, source_target_pairs={{0,2},{2,0},{1,3},{3,1},{4,6},{6,4},{5,7},{7,5},{8,10},{10,8},{9,1... | collective-permute-start | bytes 393224 | tf_op jit(solution)/shard_map/ppermute | solution.py:56
  29.9 56.1 %collective-permute-start.9 = (bf16[2,1,2,2,80,256]{5,4,3,2,0,1:T(8,128)(2,1)}, bf16[2,1,2,2,80,256]{5,4,3,2,0,1:T(8,128)(2,1)}, u32[]{:S(2)}, u32[]{:S(2)}) collective-permute-start(bf16[2,1,2,2,80,256]{5,4,3,2,0,1:T(8,128)(2,1)} %maximum_select_fusion.5), channel_id=1, source_target_pairs={{0,16},{16,0},{1,17},{17,1},{2,18},{18,2},{3,19},{19,3},{4,20},{20... | collective-permute-start | bytes 983048 | tf_op jit(solution)/shard_map/ppermute | solution.py:56
  35.0 55.4 %collective-permute-start.3 = (bf16[2,2,64,1024]{3,2,1,0:T(8,128)(2,1)S(1)}, bf16[2,2,64,1024]{3,2,1,0:T(8,128)(2,1)S(1)}, u32[]{:S(2)}, u32[]{:S(2)}) collective-permute-start(bf16[2,2,64,1024]{3,2,1,0:T(8,128)(2,1)S(1)} %get-tuple-element.155), channel_id=1, source_target_pairs={{0,4},{4,0},{1,5},{5,1},{2,6},{6,2},{3,7},{7,3},{8,12},{12,8},{9,1... | collective-permute-start | bytes 1572872 | tf_op jit(solution)/shard_map/ppermute | solution.py:56
  80.6 83.7 %all-to-all-start.1 = ((bf16[4,2,64,1408]{3,2,1,0:T(8,128)(2,1)}), bf16[4,2,64,1408]{3,2,1,0:T(8,128)(2,1)}, u32[]{:S(2)}, u32[]{:S(2)}) async-start(bf16[4,2,64,1408]{3,2,1,0:T(8,128)(2,1)} %shard_map.214), calls=%async_computation.1 | async-start | bytes 2883584 | tf_op jit(solution)/shard_map/all_to_all | solution.py:476
  87.1 24.1 %collective-permute-start.10 = (bf16[2,2,1,2,2,80,256]{6,5,4,3,1,0,2:T(8,128)(2,1)S(1)}, bf16[2,2,1,2,2,80,256]{6,5,4,3,1,0,2:T(8,128)(2,1)S(1)}, u32[]{:S(2)}, u32[]{:S(2)}) collective-permute-start(bf16[2,2,1,2,2,80,256]{6,5,4,3,1,0,2:T(8,128)(2,1)S(1)} %get-tuple-element.149), channel_id=1, source_target_pairs={{0,1},{1,0},{2,3},{3,2},{4,5},{5,4},{6,7},{7,6},{8,9},{9,8},{10,11... | collective-permute-start | bytes 1966088 | tf_op jit(solution)/shard_map/ppermute | solution.py:56
  88.2 17.4 %collective-permute-start.16 = (bf16[2,64,1024]{2,1,0:T(8,128)(2,1)S(1)}, bf16[2,64,1024]{2,1,0:T(8,128)(2,1)S(1)}, u32[]{:S(2)}, u32[]{:S(2)}) collective-permute-start(bf16[2,64,1024]{2,1,0:T(8,128)(2,1)S(1)} %maximum_select_fusion.9), channel_id=1, source_target_pairs={{0,8},{8,0},{1,9},{9,1},{2,10},{10,2},{3,11},{11,3},{4,12},{12,4},... | collective-permute-start | bytes 786440 | tf_op jit(solution)/shard_map/ppermute | solution.py:56
  91.7 25.6 %collective-permute-start.4 = (bf16[512,1024]{1,0:T(8,128)(2,1)}, bf16[512,1024]{1,0:T(8,128)(2,1)}, u32[]{:S(2)}, u32[]{:S(2)}) collective-permute-start(bf16[512,1024]{1,0:T(8,128)(2,1)} %bitcast.9), channel_id=1, source_target_pairs={{0,16},{16,0},{1,17},{17,1},{2,18},{18,2},{3,19},{19,3},{4,20},{20... | collective-permute-start | bytes 3145736 | tf_op jit(solution)/shard_map/ppermute | solution.py:56
  106.7 22.0 %collective-permute-start.17 = (bf16[2,2,64,1024]{3,2,1,0:T(8,128)(2,1)}, bf16[2,2,64,1024]{3,2,1,0:T(8,128)(2,1)}, u32[]{:S(2)}, u32[]{:S(2)}) collective-permute-start(bf16[2,2,64,1024]{3,2,1,0:T(8,128)(2,1)} %get-tuple-element.54), channel_id=1, source_target_pairs={{0,4},{4,0},{1,5},{5,1},{2,6},{6,2},{3,7},{7,3},{8,12},{12,8},{9,1... | collective-permute-start | bytes 1572872 | tf_op jit(solution)/shard_map/ppermute | solution.py:56
  120.3 51.3 %collective-permute-start.5 = (bf16[1024,1024]{1,0:T(8,128)(2,1)}, bf16[1024,1024]{1,0:T(8,128)(2,1)}, u32[]{:S(2)}, u32[]{:S(2)}) collective-permute-start(bf16[1024,1024]{1,0:T(8,128)(2,1)} %pad_maximum_fusion.2), channel_id=1, source_target_pairs={{0,1},{1,0},{2,3},{3,2},{4,5},{5,4},{6,7},{7,6},{8,9},{9,8},{10,11... | collective-permute-start | bytes 6291464 | tf_op jit(solution)/shard_map/ppermute | solution.py:56
  131.2 37.4 %collective-permute-start.18 = (bf16[512,1024]{1,0:T(8,128)(2,1)}, bf16[512,1024]{1,0:T(8,128)(2,1)}, u32[]{:S(2)}, u32[]{:S(2)}) collective-permute-start(bf16[512,1024]{1,0:T(8,128)(2,1)} %bitcast.67), channel_id=1, source_target_pairs={{0,16},{16,0},{1,17},{17,1},{2,18},{18,2},{3,19},{19,3},{4,20},{20... | collective-permute-start | bytes 3145736 | tf_op jit(solution)/shard_map/ppermute | solution.py:56
  133.5 28.9 %collective-permute-start.13 = (bf16[2,1,2,128,256]{4,3,2,1,0:T(8,128)(2,1)}, bf16[2,1,2,128,256]{4,3,2,1,0:T(8,128)(2,1)}, u32[]{:S(2)}, u32[]{:S(2)}) collective-permute-start(bf16[2,1,2,128,256]{4,3,2,1,0:T(8,128)(2,1)} %get-tuple-element.163), channel_id=1, source_target_pairs={{0,2},{2,0},{1,3},{3,1},{4,6},{6,4},{5,7},{7,5},{8,10},{10,8},{9,1... | collective-permute-start | bytes 786440 | tf_op jit(solution)/shard_map/ppermute | solution.py:56
  164.4 19.2 %all-to-all-start.2 = ((bf16[4,1,64,1408]{3,2,1,0:T(8,128)(2,1)}), bf16[4,1,64,1408]{3,2,1,0:T(8,128)(2,1)}, u32[]{:S(2)}, u32[]{:S(2)}) async-start(bf16[4,1,64,1408]{3,2,1,0:T(8,128)(2,1)} %shard_map.213), calls=%async_computation.2 | async-start | bytes 1441792 | tf_op jit(solution)/shard_map/all_to_all | solution.py:476
  171.6 39.0 %collective-permute-start.19 = (bf16[1024,1024]{1,0:T(8,128)(2,1)}, bf16[1024,1024]{1,0:T(8,128)(2,1)}, u32[]{:S(2)}, u32[]{:S(2)}) collective-permute-start(bf16[1024,1024]{1,0:T(8,128)(2,1)} %pad_maximum_fusion.3), channel_id=1, source_target_pairs={{0,1},{1,0},{2,3},{3,2},{4,5},{5,4},{6,7},{7,6},{8,9},{9,8},{10,11... | collective-permute-start | bytes 6291464 | tf_op jit(solution)/shard_map/ppermute | solution.py:56
  188.2 44.9 %all-to-all-start.3 = ((bf16[4,128,2048]{2,1,0:T(8,128)(2,1)}), bf16[4,128,2048]{2,1,0:T(8,128)(2,1)}, u32[]{:S(2)}, u32[]{:S(2)}) async-start(bf16[4,128,2048]{2,1,0:T(8,128)(2,1)} %broadcast_in_dim.22), calls=%async_computation.3 | async-start | bytes 4194304 | tf_op jit(solution)/shard_map/all_to_all | solution.py:95
  215.3 14.4 %collective-permute-start.20 = (bf16[128,2048]{1,0:T(8,128)(2,1)}, bf16[128,2048]{1,0:T(8,128)(2,1)}, u32[]{:S(2)}, u32[]{:S(2)}) collective-permute-start(bf16[128,2048]{1,0:T(8,128)(2,1)} %slice.506), channel_id=1, source_target_pairs={{0,2},{2,0},{1,3},{3,1},{4,6},{6,4},{5,7},{7,5},{8,10},{10,8},{9,1... | collective-permute-start | bytes 1572872 | tf_op jit(solution)/shard_map/ppermute | solution.py:56
  217.2 65.5 %collective-permute-start.21 = (bf16[4,2,64,1408]{3,2,1,0:T(8,128)(2,1)}, bf16[4,2,64,1408]{3,2,1,0:T(8,128)(2,1)}, u32[]{:S(2)}, u32[]{:S(2)}) collective-permute-start(bf16[4,2,64,1408]{3,2,1,0:T(8,128)(2,1)} %all-to-all-done.1.refs_0_), channel_id=1, source_target_pairs={{0,8},{8,0},{1,9},{9,1},{2,10},{10,2},{3,11},{11,3},{4,12},{12,4},... | collective-permute-start | bytes 4325384 | tf_op jit(solution)/shard_map/ppermute | solution.py:56
  220.5 63.7 %collective-permute-start.22 = (bf16[4,2,64,1408]{3,2,1,0:T(8,128)(2,1)}, bf16[4,2,64,1408]{3,2,1,0:T(8,128)(2,1)}, u32[]{:S(2)}, u32[]{:S(2)}) collective-permute-start(bf16[4,2,64,1408]{3,2,1,0:T(8,128)(2,1)} %all-to-all-done.1.refs_0_), channel_id=1, source_target_pairs={{0,16},{16,0},{1,17},{17,1},{2,18},{18,2},{3,19},{19,3},{4,20},{20... | collective-permute-start | bytes 4325384 | tf_op jit(solution)/shard_map/ppermute | solution.py:56
  235.6 113.7 %all-to-all-start = ((bf16[4,128,2048]{2,1,0:T(8,128)(2,1)}), bf16[4,128,2048]{2,1,0:T(8,128)(2,1)}, u32[]{:S(2)}, u32[]{:S(2)}) async-start(bf16[4,128,2048]{2,1,0:T(8,128)(2,1)} %broadcast_in_dim.21), calls=%async_computation | async-start | bytes 4194304 | tf_op jit(solution)/shard_map/all_to_all | solution.py:95
  282.7 36.1 %collective-permute-start.23 = (bf16[4,2,64,1408]{3,2,1,0:T(8,128)(2,1)}, bf16[4,2,64,1408]{3,2,1,0:T(8,128)(2,1)S(1)}, u32[]{:S(2)}, u32[]{:S(2)}) collective-permute-start(bf16[4,2,64,1408]{3,2,1,0:T(8,128)(2,1)} %collective-permute-done.21.refs_1_), channel_id=1, source_target_pairs={{0,16},{16,0},{1,17},{17,1},{2,18},{18,2},{3,19},{19,3},{4,20},{20... | collective-permute-start | bytes 4325384 | tf_op jit(solution)/shard_map/ppermute | solution.py:56
  284.2 35.1 %collective-permute-start.24 = (bf16[4,2,64,1408]{3,2,1,0:T(8,128)(2,1)}, bf16[4,2,64,1408]{3,2,1,0:T(8,128)(2,1)S(1)}, u32[]{:S(2)}, u32[]{:S(2)}) collective-permute-start(bf16[4,2,64,1408]{3,2,1,0:T(8,128)(2,1)} %all-to-all-done.1.refs_0_), channel_id=1, source_target_pairs={{0,1},{1,0},{2,3},{3,2},{4,5},{5,4},{6,7},{7,6},{8,9},{9,8},{10,11... | collective-permute-start | bytes 4325384 | tf_op jit(solution)/shard_map/ppermute | solution.py:56
  284.2 34.5 %collective-permute-start.28 = (bf16[4,1,64,1408]{3,2,1,0:T(8,128)(2,1)}, bf16[4,1,64,1408]{3,2,1,0:T(8,128)(2,1)S(1)}, u32[]{:S(2)}, u32[]{:S(2)}) collective-permute-start(bf16[4,1,64,1408]{3,2,1,0:T(8,128)(2,1)} %all-to-all-done.2.refs_8_.refs_0_), channel_id=1, source_target_pairs={{0,8},{8,0},{1,9},{9,1},{2,10},{10,2},{3,11},{11,3},{4,12},{12,4},... | collective-permute-start | bytes 2162696 | tf_op jit(solution)/shard_map/ppermute | solution.py:56
  284.2 49.2 %collective-permute-start.26 = (bf16[4,2,64,1408]{3,2,1,0:T(8,128)(2,1)}, bf16[4,2,64,1408]{3,2,1,0:T(8,128)(2,1)S(1)}, u32[]{:S(2)}, u32[]{:S(2)}) collective-permute-start(bf16[4,2,64,1408]{3,2,1,0:T(8,128)(2,1)} %collective-permute-done.22.refs_2_), channel_id=1, source_target_pairs={{0,1},{1,0},{2,3},{3,2},{4,5},{5,4},{6,7},{7,6},{8,9},{9,8},{10,11... | collective-permute-start | bytes 4325384 | tf_op jit(solution)/shard_map/ppermute | solution.py:56
  284.7 48.1 %collective-permute-start.29 = (bf16[4,1,64,1408]{3,2,1,0:T(8,128)(2,1)}, bf16[4,1,64,1408]{3,2,1,0:T(8,128)(2,1)S(1)}, u32[]{:S(2)}, u32[]{:S(2)}) collective-permute-start(bf16[4,1,64,1408]{3,2,1,0:T(8,128)(2,1)} %all-to-all-done.2.refs_8_.refs_0_), channel_id=1, source_target_pairs={{0,16},{16,0},{1,17},{17,1},{2,18},{18,2},{3,19},{19,3},{4,20},{20... | collective-permute-start | bytes 2162696 | tf_op jit(solution)/shard_map/ppermute | solution.py:56
  318.8 14.1 %collective-permute-start.31 = (bf16[4,1,64,1408]{3,2,1,0:T(8,128)(2,1)}, bf16[4,1,64,1408]{3,2,1,0:T(8,128)(2,1)S(1)}, u32[]{:S(2)}, u32[]{:S(2)}) collective-permute-start(bf16[4,1,64,1408]{3,2,1,0:T(8,128)(2,1)} %all-to-all-done.2.refs_8_.refs_0_), channel_id=1, source_target_pairs={{0,1},{1,0},{2,3},{3,2},{4,5},{5,4},{6,7},{7,6},{8,9},{9,8},{10,11... | collective-permute-start | bytes 2162696 | tf_op jit(solution)/shard_map/ppermute | solution.py:56
  318.8 27.6 %collective-permute-start.25 = (bf16[4,2,64,1408]{3,2,1,0:T(8,128)(2,1)}, bf16[4,2,64,1408]{3,2,1,0:T(8,128)(2,1)S(1)}, u32[]{:S(2)}, u32[]{:S(2)}) collective-permute-start(bf16[4,2,64,1408]{3,2,1,0:T(8,128)(2,1)} %collective-permute-done.21.refs_1_), channel_id=1, source_target_pairs={{0,1},{1,0},{2,3},{3,2},{4,5},{5,4},{6,7},{7,6},{8,9},{9,8},{10,11... | collective-permute-start | bytes 4325384 | tf_op jit(solution)/shard_map/ppermute | solution.py:56
  319.3 27.1 %collective-permute-start.30 = (bf16[4,1,64,1408]{3,2,1,0:T(8,128)(2,1)S(1)}, bf16[4,1,64,1408]{3,2,1,0:T(8,128)(2,1)S(1)}, u32[]{:S(2)}, u32[]{:S(2)}) collective-permute-start(bf16[4,1,64,1408]{3,2,1,0:T(8,128)(2,1)S(1)} %collective-permute-done.28.refs_9_.refs_1_), channel_id=1, source_target_pairs={{0,16},{16,0},{1,17},{17,1},{2,18},{18,2},{3,19},{19,3},{4,20},{20... | collective-permute-start | bytes 2162696 | tf_op jit(solution)/shard_map/ppermute | solution.py:56
  332.9 13.6 %collective-permute-start.27 = (bf16[4,2,64,1408]{3,2,1,0:T(8,128)(2,1)S(1)}, bf16[4,2,64,1408]{3,2,1,0:T(8,128)(2,1)S(1)}, u32[]{:S(2)}, u32[]{:S(2)}) collective-permute-start(bf16[4,2,64,1408]{3,2,1,0:T(8,128)(2,1)S(1)} %collective-permute-done.23.refs_3_), channel_id=1, source_target_pairs={{0,1},{1,0},{2,3},{3,2},{4,5},{5,4},{6,7},{7,6},{8,9},{9,8},{10,11... | collective-permute-start | bytes 4325384 | tf_op jit(solution)/shard_map/ppermute | solution.py:56
  332.9 13.5 %collective-permute-start.33 = (bf16[4,1,64,1408]{3,2,1,0:T(8,128)(2,1)S(1)}, bf16[4,1,64,1408]{3,2,1,0:T(8,128)(2,1)S(1)}, u32[]{:S(2)}, u32[]{:S(2)}) collective-permute-start(bf16[4,1,64,1408]{3,2,1,0:T(8,128)(2,1)S(1)} %collective-permute-done.29.refs_10_.refs_2_), channel_id=1, source_target_pairs={{0,1},{1,0},{2,3},{3,2},{4,5},{5,4},{6,7},{7,6},{8,9},{9,8},{10,11... | collective-permute-start | bytes 2162696 | tf_op jit(solution)/shard_map/ppermute | solution.py:56
  333.4 13.0 %collective-permute-start.32 = (bf16[4,1,64,1408]{3,2,1,0:T(8,128)(2,1)S(1)}, bf16[4,1,64,1408]{3,2,1,0:T(8,128)(2,1)S(1)}, u32[]{:S(2)}, u32[]{:S(2)}) collective-permute-start(bf16[4,1,64,1408]{3,2,1,0:T(8,128)(2,1)S(1)} %collective-permute-done.28.refs_9_.refs_1_), channel_id=1, source_target_pairs={{0,1},{1,0},{2,3},{3,2},{4,5},{5,4},{6,7},{7,6},{8,9},{9,8},{10,11... | collective-permute-start | bytes 2162696 | tf_op jit(solution)/shard_map/ppermute | solution.py:56
  391.0 29.4 %collective-permute-start.64 = (bf16[1024,1408]{1,0:T(8,128)(2,1)}, bf16[1024,1408]{1,0:T(8,128)(2,1)}, u32[]{:S(2)}, u32[]{:S(2)}) collective-permute-start(bf16[1024,1408]{1,0:T(8,128)(2,1)} %get-tuple-element.69), channel_id=1, source_target_pairs={{0,1},{1,0},{2,3},{3,2},{4,5},{5,4},{6,7},{7,6},{8,9},{9,8},{10,11... | collective-permute-start | bytes 8650760 | tf_op jit(solution)/shard_map/ppermute | solution.py:56
  391.3 34.6 %collective-permute-start.56 = (bf16[1024,1408]{1,0:T(8,128)(2,1)}, bf16[1024,1408]{1,0:T(8,128)(2,1)}, u32[]{:S(2)}, u32[]{:S(2)}) collective-permute-start(bf16[1024,1408]{1,0:T(8,128)(2,1)} %get-tuple-element.70), channel_id=1, source_target_pairs={{0,1},{1,0},{2,3},{3,2},{4,5},{5,4},{6,7},{7,6},{8,9},{9,8},{10,11... | collective-permute-start | bytes 8650760 | tf_op jit(solution)/shard_map/ppermute | solution.py:56
  391.6 39.3 %collective-permute-start.60 = (bf16[1024,1408]{1,0:T(8,128)(2,1)}, bf16[1024,1408]{1,0:T(8,128)(2,1)}, u32[]{:S(2)}, u32[]{:S(2)}) collective-permute-start(bf16[1024,1408]{1,0:T(8,128)(2,1)} %get-tuple-element.71), channel_id=1, source_target_pairs={{0,1},{1,0},{2,3},{3,2},{4,5},{5,4},{6,7},{7,6},{8,9},{9,8},{10,11... | collective-permute-start | bytes 8650760 | tf_op jit(solution)/shard_map/ppermute | solution.py:56
  391.8 43.3 %all-to-all-start.4 = ((bf16[4,128,2048]{2,1,0:T(8,128)(2,1)}), bf16[4,128,2048]{2,1,0:T(8,128)(2,1)}, u32[]{:S(2)}, u32[]{:S(2)}) async-start(bf16[4,128,2048]{2,1,0:T(8,128)(2,1)} %bitcast.224), calls=%async_computation.4 | async-start | bytes 4194304 | tf_op jit(solution)/shard_map/all_to_all | solution.py:99
  423.9 104.9 %collective-permute-start.65 = (bf16[256,1408]{1,0:T(8,128)(2,1)}, bf16[256,1408]{1,0:T(8,128)(2,1)}, u32[]{:S(2)}, u32[]{:S(2)}) collective-permute-start(bf16[256,1408]{1,0:T(8,128)(2,1)} %get-tuple-element.134), channel_id=1, source_target_pairs={{0,16},{16,0},{1,17},{17,1},{2,18},{18,2},{3,19},{19,3},{4,20},{20... | collective-permute-start | bytes 2162696 | tf_op jit(solution)/shard_map/ppermute | solution.py:56
  425.4 33.2 %collective-permute-start.66 = (bf16[256,1408]{1,0:T(8,128)(2,1)}, bf16[256,1408]{1,0:T(8,128)(2,1)}, u32[]{:S(2)}, u32[]{:S(2)}) collective-permute-start(bf16[256,1408]{1,0:T(8,128)(2,1)} %get-tuple-element.135), channel_id=1, source_target_pairs={{0,16},{16,0},{1,17},{17,1},{2,18},{18,2},{3,19},{19,3},{4,20},{20... | collective-permute-start | bytes 2162696 | tf_op jit(solution)/shard_map/ppermute | solution.py:56
  428.8 144.3 %collective-permute-start.57 = (bf16[256,1408]{1,0:T(8,128)(2,1)}, bf16[256,1408]{1,0:T(8,128)(2,1)}, u32[]{:S(2)}, u32[]{:S(2)}) collective-permute-start(bf16[256,1408]{1,0:T(8,128)(2,1)} %get-tuple-element.138), channel_id=1, source_target_pairs={{0,16},{16,0},{1,17},{17,1},{2,18},{18,2},{3,19},{19,3},{4,20},{20... | collective-permute-start | bytes 2162696 | tf_op jit(solution)/shard_map/ppermute | solution.py:56
  430.3 70.4 %collective-permute-start.58 = (bf16[256,1408]{1,0:T(8,128)(2,1)}, bf16[256,1408]{1,0:T(8,128)(2,1)}, u32[]{:S(2)}, u32[]{:S(2)}) collective-permute-start(bf16[256,1408]{1,0:T(8,128)(2,1)} %get-tuple-element.139), channel_id=1, source_target_pairs={{0,16},{16,0},{1,17},{17,1},{2,18},{18,2},{3,19},{19,3},{4,20},{20... | collective-permute-start | bytes 2162696 | tf_op jit(solution)/shard_map/ppermute | solution.py:56
  433.6 186.9 %collective-permute-start.61 = (bf16[256,1408]{1,0:T(8,128)(2,1)}, bf16[256,1408]{1,0:T(8,128)(2,1)}, u32[]{:S(2)}, u32[]{:S(2)}) collective-permute-start(bf16[256,1408]{1,0:T(8,128)(2,1)} %get-tuple-element.136), channel_id=1, source_target_pairs={{0,16},{16,0},{1,17},{17,1},{2,18},{18,2},{3,19},{19,3},{4,20},{20... | collective-permute-start | bytes 2162696 | tf_op jit(solution)/shard_map/ppermute | solution.py:56
  458.6 12.6 %collective-permute-start.35 = (bf16[128,2048]{1,0:T(8,128)(2,1)S(1)}, bf16[128,2048]{1,0:T(8,128)(2,1)S(1)}, u32[]{:S(2)}, u32[]{:S(2)}) collective-permute-start(bf16[128,2048]{1,0:T(8,128)(2,1)S(1)} %fusion.58), channel_id=1, source_target_pairs={{0,2},{2,0},{1,3},{3,1},{4,6},{6,4},{5,7},{7,5},{8,10},{10,8},{9,1... | collective-permute-start | bytes 1572872 | tf_op jit(solution)/shard_map/ppermute | solution.py:56
  471.2 48.5 %collective-permute-start.62 = (bf16[256,1408]{1,0:T(8,128)(2,1)}, bf16[256,1408]{1,0:T(8,128)(2,1)}, u32[]{:S(2)}, u32[]{:S(2)}) collective-permute-start(bf16[256,1408]{1,0:T(8,128)(2,1)} %get-tuple-element.137), channel_id=1, source_target_pairs={{0,16},{16,0},{1,17},{17,1},{2,18},{18,2},{3,19},{19,3},{4,20},{20... | collective-permute-start | bytes 2162696 | tf_op jit(solution)/shard_map/ppermute | solution.py:56
  503.5 50.7 %collective-permute-start.67 = (bf16[256,1408]{1,0:T(8,128)(2,1)S(1)}, bf16[256,1408]{1,0:T(8,128)(2,1)S(1)}, u32[]{:S(2)}, u32[]{:S(2)}) collective-permute-start(bf16[256,1408]{1,0:T(8,128)(2,1)S(1)} %copy-done.35), channel_id=1, source_target_pairs={{0,8},{8,0},{1,9},{9,1},{2,10},{10,2},{3,11},{11,3},{4,12},{12,4},... | collective-permute-start | bytes 2162696 | tf_op jit(solution)/shard_map/ppermute | solution.py:56
  527.3 83.1 %collective-permute-start.36 = (bf16[128,2048]{1,0:T(8,128)(2,1)}, bf16[128,2048]{1,0:T(8,128)(2,1)}, u32[]{:S(2)}, u32[]{:S(2)}) collective-permute-start(bf16[128,2048]{1,0:T(8,128)(2,1)} %slice.505), channel_id=1, source_target_pairs={{0,2},{2,0},{1,3},{3,1},{4,6},{6,4},{5,7},{7,5},{8,10},{10,8},{9,1... | collective-permute-start | bytes 1572872 | tf_op jit(solution)/shard_map/ppermute | solution.py:56
  528.8 44.4 %collective-permute-start.59 = (bf16[256,1408]{1,0:T(8,128)(2,1)}, bf16[256,1408]{1,0:T(8,128)(2,1)}, u32[]{:S(2)}, u32[]{:S(2)}) collective-permute-start(bf16[256,1408]{1,0:T(8,128)(2,1)} %add_convert_fusion.9), channel_id=1, source_target_pairs={{0,8},{8,0},{1,9},{9,1},{2,10},{10,2},{3,11},{11,3},{4,12},{12,4},... | collective-permute-start | bytes 2162696 | tf_op jit(solution)/shard_map/ppermute | solution.py:56
  554.2 17.9 %collective-permute-start.39 = (bf16[256,256]{1,0:T(8,128)(2,1)S(1)}, bf16[256,256]{1,0:T(8,128)(2,1)S(1)}, u32[]{:S(2)}, u32[]{:S(2)}) collective-permute-start(bf16[256,256]{1,0:T(8,128)(2,1)S(1)} %slice.510), channel_id=1, source_target_pairs={{0,4},{4,0},{1,5},{5,1},{2,6},{6,2},{3,7},{7,3},{8,12},{12,8},{9,1... | collective-permute-start | bytes 393224 | tf_op jit(solution)/shard_map/ppermute | solution.py:56
  556.9 56.2 %all-to-all-start.8 = ((bf16[4,64,1408]{2,1,0:T(8,128)(2,1)}), bf16[4,64,1408]{2,1,0:T(8,128)(2,1)S(1)}, u32[]{:S(2)}, u32[]{:S(2)}) async-start(bf16[4,64,1408]{2,1,0:T(8,128)(2,1)} %bitcast.114), calls=%async_computation.8 | async-start | bytes 1441792 | tf_op jit(solution)/shard_map/all_to_all | solution.py:631
  572.1 82.5 %collective-permute-start.46 = (bf16[1024,1024]{1,0:T(8,128)(2,1)}, bf16[1024,1024]{1,0:T(8,128)(2,1)}, u32[]{:S(2)}, u32[]{:S(2)}) collective-permute-start(bf16[1024,1024]{1,0:T(8,128)(2,1)} %slice.359), channel_id=1, source_target_pairs={{0,1},{1,0},{2,3},{3,2},{4,5},{5,4},{6,7},{7,6},{8,9},{9,8},{10,11... | collective-permute-start | bytes 6291464 | tf_op jit(solution)/shard_map/ppermute | solution.py:56
  573.2 47.3 %collective-permute-start.63 = (bf16[256,1408]{1,0:T(8,128)(2,1)}, bf16[256,1408]{1,0:T(8,128)(2,1)}, u32[]{:S(2)}, u32[]{:S(2)}) collective-permute-start(bf16[256,1408]{1,0:T(8,128)(2,1)} %add_convert_fusion.5), channel_id=1, source_target_pairs={{0,8},{8,0},{1,9},{9,1},{2,10},{10,2},{3,11},{11,3},{4,12},{12,4},... | collective-permute-start | bytes 2162696 | tf_op jit(solution)/shard_map/ppermute | solution.py:56
  573.3 36.9 %collective-permute-start.40 = (bf16[128,256]{1,0:T(8,128)(2,1)S(1)}, bf16[128,256]{1,0:T(8,128)(2,1)S(1)}, u32[]{:S(2)}, u32[]{:S(2)}) collective-permute-start(bf16[128,256]{1,0:T(8,128)(2,1)S(1)} %slice.511), channel_id=1, source_target_pairs={{0,8},{8,0},{1,9},{9,1},{2,10},{10,2},{3,11},{11,3},{4,12},{12,4},... | collective-permute-start | bytes 196616 | tf_op jit(solution)/shard_map/ppermute | solution.py:56
  613.1 14.9 %all-to-all-start.6 = ((bf16[4,64,1408]{2,1,0:T(8,128)(2,1)}), bf16[4,64,1408]{2,1,0:T(8,128)(2,1)}, u32[]{:S(2)}, u32[]{:S(2)}) async-start(bf16[4,64,1408]{2,1,0:T(8,128)(2,1)} %bitcast.110), calls=%async_computation.6 | async-start | bytes 1441792 | tf_op jit(solution)/shard_map/all_to_all | solution.py:631
  620.4 18.7 %collective-permute-start.41 = (bf16[1024,384]{0,1:T(8,128)(2,1)}, bf16[1024,384]{0,1:T(8,128)(2,1)}, u32[]{:S(2)}, u32[]{:S(2)}) collective-permute-start(bf16[1024,384]{0,1:T(8,128)(2,1)} %fusion.6), channel_id=1, source_target_pairs={{0,1},{1,0},{2,3},{3,2},{4,5},{5,4},{6,7},{7,6},{8,9},{9,8},{10,11... | collective-permute-start | bytes 2359304 | tf_op jit(solution)/shard_map/ppermute | solution.py:56
  628.0 14.8 %all-to-all-start.7 = ((bf16[4,64,1408]{2,1,0:T(8,128)(2,1)}), bf16[4,64,1408]{2,1,0:T(8,128)(2,1)}, u32[]{:S(2)}, u32[]{:S(2)}) async-start(bf16[4,64,1408]{2,1,0:T(8,128)(2,1)} %bitcast.220), calls=%async_computation.7 | async-start | bytes 1441792 | tf_op jit(solution)/shard_map/all_to_all | solution.py:631
  637.8 40.3 %collective-permute-start.51 = (bf16[1024,1024]{1,0:T(8,128)(2,1)}, bf16[1024,1024]{1,0:T(8,128)(2,1)}, u32[]{:S(2)}, u32[]{:S(2)}) collective-permute-start(bf16[1024,1024]{1,0:T(8,128)(2,1)} %slice.366), channel_id=1, source_target_pairs={{0,1},{1,0},{2,3},{3,2},{4,5},{5,4},{6,7},{7,6},{8,9},{9,8},{10,11... | collective-permute-start | bytes 6291464 | tf_op jit(solution)/shard_map/ppermute | solution.py:56
  642.8 46.9 %all-to-all-start.5 = ((bf16[4,128,2048]{2,1,0:T(8,128)(2,1)}), bf16[4,128,2048]{2,1,0:T(8,128)(2,1)}, u32[]{:S(2)}, u32[]{:S(2)}) async-start(bf16[4,128,2048]{2,1,0:T(8,128)(2,1)} %bitcast.223), calls=%async_computation.5 | async-start | bytes 4194304 | tf_op jit(solution)/shard_map/all_to_all | solution.py:99
  653.6 20.8 %collective-permute-start.43 = (bf16[256,384]{0,1:T(8,128)(2,1)S(1)}, bf16[256,384]{0,1:T(8,128)(2,1)S(1)}, u32[]{:S(2)}, u32[]{:S(2)}) collective-permute-start(bf16[256,384]{0,1:T(8,128)(2,1)S(1)} %slice.509), channel_id=1, source_target_pairs={{0,8},{8,0},{1,9},{9,1},{2,10},{10,2},{3,11},{11,3},{4,12},{12,4},... | collective-permute-start | bytes 589832 | tf_op jit(solution)/shard_map/ppermute | solution.py:56
  660.3 37.0 %collective-permute-start.47 = (bf16[512,1024]{1,0:T(8,128)(2,1)}, bf16[512,1024]{1,0:T(8,128)(2,1)}, u32[]{:S(2)}, u32[]{:S(2)}) collective-permute-start(bf16[512,1024]{1,0:T(8,128)(2,1)} %slice.503), channel_id=1, source_target_pairs={{0,16},{16,0},{1,17},{17,1},{2,18},{18,2},{3,19},{19,3},{4,20},{20... | collective-permute-start | bytes 3145736 | tf_op jit(solution)/shard_map/ppermute | solution.py:56
  682.5 25.2 %collective-permute-start.52 = (bf16[512,1024]{1,0:T(8,128)(2,1)}, bf16[512,1024]{1,0:T(8,128)(2,1)}, u32[]{:S(2)}, u32[]{:S(2)}) collective-permute-start(bf16[512,1024]{1,0:T(8,128)(2,1)} %slice.502), channel_id=1, source_target_pairs={{0,16},{16,0},{1,17},{17,1},{2,18},{18,2},{3,19},{19,3},{4,20},{20... | collective-permute-start | bytes 3145736 | tf_op jit(solution)/shard_map/ppermute | solution.py:56
  702.2 15.2 %collective-permute-start.48 = (bf16[2,2,64,1024]{3,2,1,0:T(8,128)(2,1)}, bf16[2,2,64,1024]{3,2,1,0:T(8,128)(2,1)}, u32[]{:S(2)}, u32[]{:S(2)}) collective-permute-start(bf16[2,2,64,1024]{3,2,1,0:T(8,128)(2,1)} %fusion.10), channel_id=1, source_target_pairs={{0,4},{4,0},{1,5},{5,1},{2,6},{6,2},{3,7},{7,3},{8,12},{12,8},{9,1... | collective-permute-start | bytes 1572872 | tf_op jit(solution)/shard_map/ppermute | solution.py:56
  710.2 21.7 %collective-permute-start.53 = (bf16[2,2,64,1024]{3,2,1,0:T(8,128)(2,1)}, bf16[2,2,64,1024]{3,2,1,0:T(8,128)(2,1)}, u32[]{:S(2)}, u32[]{:S(2)}) collective-permute-start(bf16[2,2,64,1024]{3,2,1,0:T(8,128)(2,1)} %fusion.11), channel_id=1, source_target_pairs={{0,4},{4,0},{1,5},{5,1},{2,6},{6,2},{3,7},{7,3},{8,12},{12,8},{9,1... | collective-permute-start | bytes 1572872 | tf_op jit(solution)/shard_map/ppermute | solution.py:56
  719.0 14.3 %collective-permute-start.49 = (bf16[2,64,1024]{2,1,0:T(8,128)(2,1)S(1)}, bf16[2,64,1024]{2,1,0:T(8,128)(2,1)S(1)}, u32[]{:S(2)}, u32[]{:S(2)}) collective-permute-start(bf16[2,64,1024]{2,1,0:T(8,128)(2,1)S(1)} %fusion.20), channel_id=1, source_target_pairs={{0,8},{8,0},{1,9},{9,1},{2,10},{10,2},{3,11},{11,3},{4,12},{12,4},... | collective-permute-start | bytes 786440 | tf_op jit(solution)/shard_map/ppermute | solution.py:56
  733.4 13.9 %collective-permute-start.50 = (bf16[64,1024]{1,0:T(8,128)(2,1)S(1)}, bf16[64,1024]{1,0:T(8,128)(2,1)S(1)}, u32[]{:S(2)}, u32[]{:S(2)}) collective-permute-start(bf16[64,1024]{1,0:T(8,128)(2,1)S(1)} %fusion.22), channel_id=1, source_target_pairs={{0,2},{2,0},{1,3},{3,1},{4,6},{6,4},{5,7},{7,5},{8,10},{10,8},{9,1... | collective-permute-start | bytes 393224 | tf_op jit(solution)/shard_map/ppermute | solution.py:56
  (83 other events, 1396.6 us)

commit v4 on v3

--- a/solution.py
+++ b/solution.py
@@ -56,12 +56,18 @@
     return lax.ppermute(value, axis, [(0, 1), (1, 0)])
 
 
+def swap_core(value):
+    size = value.shape[0] // 4
+    parts = [value[i * size : (i + 1) * size] for i in range(4)]
+    return jnp.concatenate([swap(part, "c") for part in parts])
+
+
 def low(value):
     return value.astype(BF16)
 
 
-def after(value, *events):
-    return lax.optimization_barrier((value, *events))[0]
+def sync(*values):
+    return lax.optimization_barrier(values)
 
 
 def pick(stacked, index, axis=0):
@@ -199,13 +205,22 @@
         body(pl.ds(full * 256, rest))
 
 
-def load_pieces(pieces, slots, held, sems):
+def load_pieces(pieces, parts, held, sems):
     waits = []
-    for slot, (arrays, at) in enumerate(slots):
-        copies = [
-            pltpu.make_async_copy(pieces[a].at[:, at], held.at[slot, p], sems.at[slot, p])
-            for p, a in enumerate(arrays)
-        ]
+    half = held.shape[2] // 2
+    for slot, matrix in enumerate(parts):
+        copies = []
+        for core in range(2):
+            for i, (p, first, count) in enumerate(
+                ((0, 0, 2), (1, 0, 1), (1, 1, 1), (2, 0, 1), (2, 1, 1), (3, 0, 1), (3, 1, 1))
+            ):
+                copies.append(
+                    pltpu.make_async_copy(
+                        pieces[core * 7 + i].at[:, matrix],
+                        held.at[slot, core * 4 + p, pl.ds(first * half, count * half)],
+                        sems.at[slot, core * 7 + i],
+                    )
+                )
         for copy in copies:
             copy.start()
         waits.append(copies)
@@ -218,27 +233,21 @@
 
 
 def feed_kernel(normed, grad, *refs):
-    pieces = refs[:16]
-    mixed, grad_gate, grad_up, grad_two, held, gate_sum, up_sum, sems = refs[16:]
-    both, down = range(8), range(8, 16)
-    wait = load_pieces(pieces, [(both, 0), (both, 1), (down, 0)], held, sems)
+    pieces = refs[:14]
+    mixed, grad_gate, grad_up, grad_two, held, gate_sum, up_sum, sems = refs[14:]
+    wait = load_pieces(pieces, range(3), held, sems)
     width, part = normed.shape[1], mixed.shape[1]
 
     def block(slot, at):
         return held[slot, :, :, :, at].reshape(width, at.size)
 
-    wait(0)
-
-    def gate_step(at):
-        gate_sum[:, at] = mxu(normed[...], block(0, at), NN)
-
-    each_block(part, gate_step)
-    wait(1)
-
-    def up_step(at):
-        up_sum[:, at] = mxu(normed[...], block(1, at), NN)
-
-    each_block(part, up_step)
+    for slot, result in enumerate((gate_sum, up_sum)):
+        wait(slot)
+
+        def step(at):
+            result[:, at] = mxu(normed[...], block(slot, at), NN)
+
+        each_block(part, step)
     wait(2)
 
     def down_step(at):
@@ -265,36 +274,45 @@
     lax.fori_loop(0, 8, two_step, 0)
 
 
-TN = (((0,), (0,)), ((), ()))
-
-
-def outer(first_block, left, right, result):
+def outer_kernel(left, *refs):
+    count = len(refs) // 3
+    rights, results = refs[:count], refs[count:]
     rows = left.shape[1] // 8
 
     def step(p, unused):
-        at = pl.ds(pl.multiple_of((first_block + p) * rows, rows), rows)
         to = pl.ds(pl.multiple_of(p * rows, rows), rows)
-        result[to, :] = mxu(left[:, at], right[...], TN).astype(result.dtype)
+        for part in range(2):
+            first = 4 * (1 - part)
+            at = pl.ds(pl.multiple_of((first + p) * rows, rows), rows)
+            turned = left[:, at].T
+            for i, right in enumerate(rights):
+                result = results[2 * i + part]
+                result[to, :] = mxu(turned, right[...], NN).astype(result.dtype)
         return unused
 
     lax.fori_loop(0, 4, step, 0)
 
 
-def outer_far_kernel(normed, grad, mixed, grad_gate, grad_up, down_far, gate_far, up_far):
-    outer(4, grad, mixed, down_far)
-    outer(4, normed, grad_gate, gate_far)
-    outer(4, normed, grad_up, up_far)
-
-
-def outer_near_kernel(normed, grad, mixed, grad_gate, grad_up, *refs):
-    pieces = refs[:8]
-    down_near, gate_near, up_near, feed, held, sems = refs[8:]
-    wait = load_pieces(pieces, [(range(8), 0)], held, sems)
-    outer(0, grad, mixed, down_near)
-    outer(0, normed, grad_gate, gate_near)
-    outer(0, normed, grad_up, up_near)
+def outer_all_kernel(order, left, *refs):
+    *rights, result = refs
+    rows = left.shape[1] // 8
+
+    def step(p, unused):
+        at = pl.ds(pl.multiple_of(p * rows, rows), rows)
+        turned = left[:, at].T
+        for i, right in enumerate(rights):
+            result[order[p], i] = mxu(turned, right[...], NN).astype(result.dtype)
+        return unused
+
+    lax.fori_loop(0, 8, step, 0)
+
+
+def feed_out_kernel(mixed, *refs):
+    pieces = refs[:14]
+    feed, held, sems = refs[14:]
+    wait = load_pieces(pieces, [2], held, sems)
     wait(0)
-    width, part = normed.shape[1], mixed.shape[1]
+    width, part = feed.shape[1], mixed.shape[1]
 
     def feed_step(p, unused):
         at = pl.ds(pl.multiple_of(p * (width // 8), width // 8), width // 8)
@@ -306,38 +324,47 @@
     lax.fori_loop(0, 8, feed_step, 0)
 
 
-def split_kernel(count, *refs):
-    matrices, result, sems = refs[:count], refs[count], refs[count + 1]
-    part = result.shape[-1]
-    copies = [
-        pltpu.make_async_copy(
-            matrix.at[:, pl.ds(i * part, part)], result.at[i, j], sems.at[i, j]
-        )
-        for i in range(4)
-        for j, matrix in enumerate(matrices)
-    ]
-    for copy in copies:
-        copy.start()
-    for copy in copies:
-        copy.wait()
+def split_kernel(*refs):
+    result = refs[-1]
+    for i, matrix in enumerate(refs[:-1]):
+        result[0, i] = matrix[...]
 
 
 def split(*matrices):
     rows, columns = matrices[0].shape
-    count = len(matrices)
-    anywhere = pl.BlockSpec(memory_space=pl.ANY)
+    count, part = len(matrices), columns // 4
     return pl.pallas_call(
-        functools.partial(split_kernel, count),
-        out_shape=jax.ShapeDtypeStruct((4, count, rows, columns // 4), matrices[0].dtype),
-        in_specs=[anywhere] * count,
-        out_specs=anywhere,
-        scratch_shapes=[pltpu.SemaphoreType.DMA((4, count))],
-        cost_estimate=pl.CostEstimate(flops=0, bytes_accessed=1 << 22, transcendentals=0),
+        split_kernel,
+        out_shape=jax.ShapeDtypeStruct((4, count, rows, part), matrices[0].dtype),
+        grid=(4,),
+        in_specs=[pl.BlockSpec((rows, part), lambda i: (0, i))] * count,
+        out_specs=pl.BlockSpec((1, count, rows, part), lambda i: (i, 0, 0, 0)),
+        cost_estimate=NO_COST,
     )(*matrices)
 
 
-def local_call(kernel, outs, scratch, *args, far=0, micros=10):
-    near = [pl.BlockSpec(memory_space=pltpu.VMEM)] * (len(args) - far)
+def merge_kernel(parts, result):
+    result[...] = parts[0].astype(F32)
+
+
+def merge(parts):
+    _, rows, part = parts.shape
+    return pl.pallas_call(
+        merge_kernel,
+        out_shape=jax.ShapeDtypeStruct((rows, 4 * part), F32),
+        grid=(4,),
+        in_specs=[pl.BlockSpec((1, rows, part), lambda i: (i, 0, 0))],
+        out_specs=pl.BlockSpec((rows, part), lambda i: (0, i)),
+        cost_estimate=NO_COST,
+    )(parts)
+
+
+NO_COST = pl.CostEstimate(flops=1, bytes_accessed=1, transcendentals=0)
+
+
+def local_call(kernel, outs, scratch, *args, far=0, scalars=0):
+    near = [pl.BlockSpec(memory_space=pltpu.SMEM)] * scalars
+    near = near + [pl.BlockSpec(memory_space=pltpu.VMEM)] * (len(args) - far - scalars)
     return pl.pallas_call(
         kernel,
         out_shape=outs,
@@ -345,9 +372,7 @@
         out_specs=[pl.BlockSpec(memory_space=pltpu.VMEM)] * len(outs),
         scratch_shapes=scratch,
         compiler_params=pltpu.CompilerParams(vmem_limit_bytes=56 << 20),
-        cost_estimate=pl.CostEstimate(
-            flops=micros * 900_000_000, bytes_accessed=1 << 20, transcendentals=0
-        ),
+        cost_estimate=NO_COST,
     )(*args)
 
 
@@ -426,69 +451,51 @@
     gains = jnp.stack([attention_gain, feedforward_gain])
     gains = jnp.pad(gains, ((0, 14), (0, 2 * HEAD_DIM - rows)))
     small = jnp.concatenate([keyvalue_weight, gains])
-    small_steps = [swap(small, "h")]
-    small = jnp.stack([small, small_steps[-1]])
-    small_steps.append(swap(small, "l"))
-    small = pair(small, small_steps[-1], l, 1)
-    small_steps.append(swap(small, "x"))
-    small = pair(small, small_steps[-1], x, 2)
-    small = gather_m(small, 1)
-    small_steps.append(swap(small, "y"))
-    small = jnp.stack([small, small_steps[-1]])
-    small_steps.append(swap(small, "c"))
-    small = jnp.stack([small, small_steps[-1]])
+
+    def halves(weight):
+        parts = weight.reshape(rows, 2, half_width).transpose(1, 0, 2)
+        return pick(parts, x), pick(parts, 1 - x)
+
+    query_mine, query_sent = halves(query_weight)
+    output_mine, output_sent = halves(output_weight)
+
+    small_x, query_x, output_x = sync(
+        swap(small, "x"), swap(query_sent, "x"), swap(output_sent, "x")
+    )
+    small = pair(small, small_x, x)
+    query_part, output_part = pair(query_mine, query_x, x), pair(output_mine, output_x, x)
+    input_mine, small, gate_weight, up_weight, down_weight = sync(
+        inward(block_input[0]), small, gate_weight, up_weight, down_weight
+    )
+    feed_parts = split(gate_weight, up_weight, down_weight)
+    small_l, query_l, output_l, input_other = sync(
+        swap(small, "l"), swap(query_part, "l"), swap(output_part, "l"), swap(input_mine, "x")
+    )
+    small = gather_m(pair(small, small_l, l), 0)
+    query_part = gather_m(pair(query_part, query_l, l), 0)
+    output_part = gather_m(pair(output_part, output_l, l), 0)
+    small, query_part, feed_parts = sync(small, query_part, feed_parts)
+    feed = gather_m(lax.all_to_all(feed_parts, ("l", "x"), 0, 0), 0)
+    feed = feed.reshape(M * 4, 3, rows, part)
+    query_h = swap(query_part, "h")
+    small_h = sync(swap(small, "h"))[0]
+    small = jnp.stack([small, small_h])
+    small_y = sync(swap(small, "y"))[0]
+    small = jnp.stack([small, small_y])
+    small_c = sync(swap(small, "c"), input_other)[0]
+    small = jnp.stack([small, small_c])
     small = small.reshape(width // rows, rows + 16, 2 * HEAD_DIM)
     keyvalue_full = small[:, :rows].reshape(width, 2 * HEAD_DIM)
     gain_one = small[:, rows, :rows].reshape(1, width).astype(F32)
     gain_two = small[:, rows + 1, :rows].reshape(1, width).astype(F32)
-
-    def halves(weight):
-        parts = weight.reshape(rows, 2, half_width).transpose(1, 0, 2)
-        return pick(parts, x), pick(parts, 1 - x)
-
-    def gather_heads(weight, ahead=None):
-        ahead = ahead or [()] * 5
-        mine, sent = halves(weight)
-        steps = [swap(after(sent, *ahead[0]), "x")]
-        got = pair(mine, steps[-1], x)
-        steps.append(swap(after(got, *ahead[1]), "h"))
-        got = jnp.stack([got, steps[-1]])
-        steps.append(swap(after(got, *ahead[2]), "l"))
-        got = pair(got, steps[-1], l, 1)
-        got = gather_m(got, 1).reshape(-1, half_width)
-        steps.append(swap(after(got, *ahead[3]), "y"))
-        got = jnp.concatenate([got, steps[-1]])
-        steps.append(swap(after(got, *ahead[4]), "c"))
-        return jnp.concatenate([got, steps[-1]]), [(step,) for step in steps]
-
-    def scatter_heads(grad):
-        grad = fold(fold(low(grad), "c"), "y")
-        grad = scatter_m(grad.reshape(2, M, 2, 2, rows, half_width), 1)
-        grad = pick(grad, l, 1) + swap(low(pick(grad, 1 - l, 1)), "l").astype(F32)
-        grad = grad[0] + swap(low(grad[1]), "h").astype(F32)
-        other = swap(low(pick(grad, 1 - x)), "x").astype(F32)
-        return pair(pick(grad, x), other, x, 1).reshape(rows, query_width)
-
-    query_full, query_steps = gather_heads(query_weight)
-    output_full, output_steps = gather_heads(output_weight, query_steps)
-
-    def exchange(parts):
-        got = lax.all_to_all(parts, ("l", "x"), 0, 0)
-        got = gather_m(got, 0)
-        return got.reshape(M * 4, -1, rows, part)
-
-    both = exchange(after(split(gate_weight, up_weight), small_steps[0]))
-    both = after(both, small_steps[3])
-    both_h = swap(both, "h")
-    both_y = swap(both, "y")
-    down = exchange(after(split(down_weight), both, small_steps[4]))
-
-    input_mine = inward(block_input[0])
-    inputs = jnp.concatenate([input_mine, swap(input_mine, "x")]).astype(F32)
-    scale_one = lax.rsqrt(jnp.mean(inputs * inputs, axis=-1, keepdims=True) + EPSILON)
-    normed_one = inputs * scale_one
-    normed_one_low = low(normed_one * gain_one)
-    keyvalue_sum = dot(normed_one_low[:tokens], keyvalue_full)
+    def normalize(value):
+        value = value.astype(F32)
+        scale = lax.rsqrt(jnp.mean(value * value, axis=-1, keepdims=True) + EPSILON)
+        normed = value * scale
+        return value, scale, normed, low(normed * gain_one)
+
+    inputs, scale_one, normed_one, normed_mine_low = normalize(input_mine)
+    keyvalue_sum = dot(normed_mine_low, keyvalue_full)
     shared_mine = low(
         jnp.concatenate(
             [
@@ -498,12 +505,34 @@
             -1,
         )
     )
-    gathered = jnp.stack([shared_mine, swap(shared_mine, "h")])
-    gathered = gather_m(gathered, 0)
-    for axis in "lxc":
-        gathered = jnp.stack([gathered, swap(gathered, axis)])
-    gathered = gathered.reshape(-1, 2 * HEAD_DIM)
+    shared_h, feed, input_other, query_h = sync(
+        swap(shared_mine, "h"), feed, input_other, query_h
+    )
+    gathered = gather_m(jnp.stack([shared_mine, shared_h]), 0)
+    gathered, input_other, output_part = sync(gathered, input_other, output_part)
+    query_y = swap(jnp.stack([query_part, query_h]), "y")
+    output_h = swap(output_part, "h")
+    normed_one_low = jnp.concatenate([normed_mine_low, normalize(input_other)[3]])
+    shared_l, normed_one_low = sync(swap(gathered, "l"), normed_one_low)
+    gathered = jnp.stack([gathered, shared_l])
+    shared_x, output_h, query_y = sync(swap(gathered, "x"), output_h, query_y)
+    gathered = jnp.stack([gathered, shared_x])
+    query_part = jnp.stack([query_part, query_h])
+    query_part = jnp.stack([query_part, query_y]).reshape(-1, half_width)
+    query_part, gathered = sync(query_part, gathered)
+    query_c = swap_core(query_part)
+    output_part = jnp.stack([output_part, output_h])
+    output_part, gathered, feed = sync(output_part, gathered, feed)
+    output_y = swap(output_part, "y")
+    quarters = [feed[i * M : (i + 1) * M] for i in range(4)]
+    middle = 2 * M
+    feed_h = [swap(quarters[0], "h")]
+    shared_c, query_c = sync(swap(gathered, "c"), query_c)
+    query_full = jnp.concatenate([query_part, query_c])
+    gathered = jnp.stack([gathered, shared_c]).reshape(-1, 2 * HEAD_DIM)
     stream_len = gathered.shape[0]
+    grad_mine, gathered = sync(inward(output_grad[0]), gathered)
+    grad_low = gather_group(grad_mine).reshape(-1, width)
     key, value = gathered[:, :HEAD_DIM], gathered[:, HEAD_DIM:]
     query_sum = lax.dot_general(
         query_full, normed_one_low, (((0,), (1,)), ((), ())), preferred_element_type=F32
@@ -522,63 +551,118 @@
         [pltpu.VMEM((stream_len, 2 * tokens), F32)],
         query_sum, key, value.T, cosine_t, sine_t, *places_used,
     )
+    attended_low, output_y, output_part, feed_h[0] = sync(
+        attended_low, output_y, output_part, feed_h[0]
+    )
+    output_part = jnp.stack([output_part, output_y]).reshape(-1, half_width)
+    output_c = swap_core(output_part)
+    sent, feed_sent = sync(quarters[1], feed[:middle], attended_low)[:2]
+    feed_h.append(swap(sent, "h"))
+    feed_y = [swap(feed_sent, "y")]
+    output_part, output_c, attended_low = sync(output_part, output_c, attended_low)
+    output_full = jnp.concatenate([output_part, output_c])
     branch = lax.dot_general(
         attended_low, output_full, (((0,), (1,)), ((), ())), preferred_element_type=F32
     )
-    branch_sent = low(branch[tokens:])
-    hidden = inputs[:tokens] + (branch[:tokens] + swap(branch_sent, "x").astype(F32))
-
-    grad_mine = inward(output_grad[0])
-    down = after(down, query_sum)
-    down_y = swap(after(down, both_y), "y")
-    both_h = after(both_h, branch_sent)
-    down_h = swap(after(down, both_h), "h")
-    both_far = swap(both_h, "y")
-    down_far = swap(after(down_h, both_far), "y")
-    both_all = [both, both_h, both_y, both_far]
-    down_all = [down, down_h, down_y, down_far]
-    both_all = both_all + [swap(piece, "c") for piece in both_all]
-    down_all = down_all + [swap(piece, "c") for piece in down_all]
-    grad_low = gather_group(after(grad_mine, down, query_sum)).reshape(-1, width)
-
+    branch_x, feed_h[1], feed_y[0], grad_low = sync(
+        swap(low(branch[tokens:]), "x"), feed_h[1], feed_y[0], grad_low
+    )
+    hidden = inputs + (branch[:tokens] + branch_x.astype(F32))
+
+    feed_h = [jnp.concatenate(feed_h)]
+    sent2, sent3, feed_sent, branch_x = sync(quarters[2], quarters[3], feed[middle:], branch_x)
+    sent2, sent3 = swap(sent2, "h"), swap(sent3, "h")
+    feed_far = [swap(feed_h[0], "y")]
     scale_two = lax.rsqrt(jnp.mean(hidden * hidden, axis=-1, keepdims=True) + EPSILON)
     normed_two = hidden * scale_two
-    normed_two_low = gather_group(low(normed_two * gain_two)).reshape(-1, width)
+    normed_two_low = low(normed_two * gain_two)
+    normed_two_low = gather_group(normed_two_low).reshape(-1, width)
+    normed_two_low, sent2, sent3, feed_far[0] = sync(normed_two_low, sent2, sent3, feed_far[0])
+    feed_h.append(jnp.concatenate([sent2, sent3]))
+    feed_far.append(swap(feed_h[1], "y"))
+    feed_y.append(swap(feed_sent, "y"))
+    early = [feed, *feed_h, feed_y[0], feed_far[0]]
+    early_c = [swap(piece, "c") for piece in early]
+    feed_y[1], feed_far[1], *early_c = sync(feed_y[1], feed_far[1], *early_c)
+    feed_all = [feed, *feed_h, *feed_y, *feed_far]
+    feed_all = feed_all + [*early_c[:4], swap(feed_y[1], "c"), early_c[4]]
+    feed_all = feed_all + [swap(feed_far[1], "c")]
+    order = jnp.stack(
+        [
+            ((y ^ j) * 2 + (h ^ k)) * 2 + (c ^ i)
+            for i in range(2)
+            for j in range(2)
+            for k in range(2)
+        ]
+    )
     group = 4 * tokens
     units = jax.ShapeDtypeStruct((group, part), BF16)
     features = jax.ShapeDtypeStruct((group, width), BF16)
-    held = pltpu.VMEM((3, 8, M * 4, rows, part), BF16)
+
+    def held(count):
+        return pltpu.VMEM((count, 8, M * 4, rows, part), BF16)
+
     wide_sum = pltpu.VMEM((group, part), F32)
     mixed_low, grad_gate, grad_up, grad_two = local_call(
         feed_kernel,
         [units, units, units, features],
-        [held, wide_sum, wide_sum, pltpu.SemaphoreType.DMA((3, 8))],
-        normed_two_low, grad_low, *both_all, *down_all,
-        far=16, micros=22,
-    )
+        [held(3), wide_sum, wide_sum, pltpu.SemaphoreType.DMA((3, 14))],
+        normed_two_low, grad_low, *feed_all,
+        far=14,
+    )
+
+    half, block = width // 2, width // 8
+    half_rows = jax.ShapeDtypeStruct((half, part), BF16)
+    mixed_low, grad_gate, grad_up, grad_two = sync(mixed_low, grad_gate, grad_up, grad_two)
     grad_two = scatter_group(grad_two.reshape(4, tokens, width))
-    outers = (normed_two_low, grad_low, mixed_low, grad_gate, grad_up)
-    half_rows = jax.ShapeDtypeStruct((width // 2, part), BF16)
-    far_parts = local_call(outer_far_kernel, [half_rows] * 3, [], *outers, micros=8)
-    *near_parts, feed_out = local_call(
-        outer_near_kernel,
-        [half_rows] * 3 + [features],
-        [pltpu.VMEM((1, 8, M * 4, rows, part), BF16), pltpu.SemaphoreType.DMA((1, 8))],
-        *(after(o, *far_parts) for o in outers), *down_all,
-        far=8, micros=12,
-    )
-    feed_out = scatter_group(after(feed_out, grad_two).reshape(4, tokens, width))
-    block_output = outward(low(hidden + feed_out))[None]
-    gain_two_grad = jnp.sum(grad_two * normed_two, axis=0)
+    both_grad = local_call(
+        outer_all_kernel,
+        [jax.ShapeDtypeStruct((8, 2, block, part), BF16)],
+        [],
+        order, normed_two_low, grad_gate, grad_up,
+        scalars=1,
+    )[0]
+    mixed_low, both_grad = sync(mixed_low, both_grad)
+    both_grad = lax.psum_scatter(both_grad, ("y", "h", "c"), scatter_dimension=0)
+    down_far_half, down_near = local_call(
+        outer_kernel, [half_rows] * 2, [], grad_low, mixed_low
+    )
+    mixed_low, down_far_half = sync(mixed_low, down_far_half)
+    down_got = swap(down_far_half, "c")
+    feed_out = local_call(
+        feed_out_kernel,
+        [features],
+        [held(1), pltpu.SemaphoreType.DMA((1, 14))],
+        mixed_low, *feed_all,
+        far=14,
+    )[0]
+
+    def quarter(i, *more):
+        at = slice(i * block, (i + 1) * block)
+        total = down_near[at].astype(F32) + down_got[at].astype(F32)
+        for other in more:
+            total = total + other.astype(F32)
+        return low(total)
+
+    grad_two, down_got, feed_out = sync(grad_two, down_got, feed_out)
+    across = (((0,), (1,)), ((), ()))
     grad_hidden = grad_mine.astype(F32) + norm_back(grad_two * gain_two, normed_two, scale_two)
-
-    grad_hidden_low = low(grad_hidden)
-    grad_hidden_low = jnp.concatenate([grad_hidden_low, swap(grad_hidden_low, "x")])
+    grad_hidden_low, grad_two = sync(low(grad_hidden), grad_two)
+    hidden_x = swap(grad_hidden_low, "x")
+    down_y3, down_y2 = swap(quarter(3), "y"), swap(quarter(2), "y")
+    hidden_x, feed_out = sync(hidden_x, feed_out)
+    feed_out = scatter_group(feed_out.reshape(4, tokens, width))
+    grad_hidden_low = jnp.concatenate([grad_hidden_low, hidden_x])
+    output_term = low(
+        lax.dot_general(grad_hidden_low, attended_low, across, preferred_element_type=F32)
+    )
+    output_got = swap(output_term[half:], "c")
     grad_heads = low(
         lax.dot_general(
             output_full, grad_hidden_low, (((0,), (1,)), ((), ())), preferred_element_type=F32
         )
     )
+    grad_heads, output_got, output_term = sync(grad_heads, output_got, output_term)
     query_grad_low, kv_grad = local_call(
         attend_back_kernel,
         [
@@ -588,11 +672,48 @@
         [pltpu.VMEM((stream_len, 2 * tokens), F32)],
         query_rot, key, key.T, value, grad_heads, attended, lse, cosine_t, sine_t, *places_used,
     )
-    kv_grad = kv_first = fold(kv_grad, "c")
-    for axis in "xl":
-        kv_grad = fold(kv_grad, axis)
-    kv_grad = scatter_m(kv_grad.reshape(M, 2 * tokens, 2 * HEAD_DIM), 0)
-    kv_mine = fold(kv_grad, "h") + shared_grad[0].astype(F32)
+    query_grad_low, kv_grad, down_y3 = sync(query_grad_low, kv_grad, down_y3)
+
+    def fold_l(total):
+        total = total.reshape(2, 2, M, 2, 2, rows, -1)
+        return pick(total, l, 3), swap(low(pick(total, 1 - l, 3)), "l")
+
+    def give_x(total, got):
+        total = total + got.astype(F32)
+        return pick(total, x, 3), swap(low(pick(total, 1 - x, 3)), "x")
+
+    def take_x(total, got):
+        got = got.astype(F32)
+        both = pair(total[..., :half_width], got[..., :half_width], x, 4)
+        both = both.reshape(2, 2, M, rows, query_width)
+        return jnp.concatenate([both, (total + got)[..., half_width:]], -1)
+
+    def next_fold(total, axis):
+        return total[0], swap(low(total[1]), axis)
+
+    kv_half = kv_grad.shape[0] // 2
+    kv_sent = low(kv_grad[kv_half:])
+    kv_got, feed_out, query_grad_low = sync(swap(kv_sent, "c"), feed_out, query_grad_low)
+    kv_grad = (kv_grad[:kv_half] + kv_got.astype(F32)).reshape(4, M, 2, tokens, 2 * HEAD_DIM)
+    kv_got = swap(low(kv_grad[2:]), "x")
+    query_term = low(
+        lax.dot_general(normed_one_low, query_grad_low, across, preferred_element_type=F32)
+    )
+    kv_got, query_term = sync(kv_got, query_term)
+    kv_grad = kv_grad[:2] + kv_got.astype(F32)
+    kv_got = swap(low(kv_grad[1]), "l")
+    grad_one = lax.dot_general(
+        query_grad_low, query_full, (((0,), (1,)), ((), ())), preferred_element_type=F32
+    )
+    kv_got, grad_one = sync(kv_got, grad_one)
+    grad_one_x = swap(low(grad_one[tokens:]), "x")
+    output_total, output_got = fold_l(
+        output_term[:half].astype(F32) + output_got.astype(F32)
+    )
+    kv_grad = kv_grad[0] + kv_got.astype(F32)
+    kv_got, grad_one_x = sync(swap(low(kv_grad[:, 1]), "h"), grad_one_x)
+    down_h1 = swap(quarter(1, down_y3), "h")
+    kv_mine = scatter_m(kv_grad[:, 0] + kv_got.astype(F32), 0) + shared_grad[0].astype(F32)
     keyvalue_grad_low = low(
         jnp.concatenate(
             [
@@ -602,60 +723,48 @@
             -1,
         )
     )
-    grad_one = lax.dot_general(
-        query_grad_low, query_full, (((0,), (1,)), ((), ())), preferred_element_type=F32
-    )
-    grad_one = fold(grad_one, "x") + contract_last(keyvalue_grad_low, keyvalue_full)
-    normed_mine = normed_one[:tokens]
-    gain_one_grad = jnp.sum(grad_one * normed_mine, axis=0)
-    input_grad = outward(
-        grad_hidden + norm_back(grad_one * gain_one, normed_mine, scale_one[:tokens])
-    )[None]
-
-    block = width // 8
-
-    def fold_y(near, far):
-        got = swap(far, "c")
-
-        def total(i):
-            at = slice(i * block, (i + 1) * block)
-            return near[at].astype(F32) + got[at].astype(F32)
-
-        return total, swap(low(total(3)), "y")
-
-    def finish_feed(total, by_y, event):
-        by_h = swap(low(total(1) + after(by_y, *event).astype(F32)), "h")
-        own = total(0) + swap(low(total(2)), "y").astype(F32)
-        own = own + by_h.astype(F32)
-        own = low(scatter_m(own.reshape(M, 4, rows, part), 0))
-        got = lax.all_to_all(own, ("l", "x"), 0, 0)
-        return got.transpose(1, 0, 2).reshape(rows, hidden_units).astype(F32)
-
-    totals = [fold_y(n, f) for n, f in zip(near_parts, far_parts)]
-    events = [(grad_two,), (grad_heads,), (kv_first,)]
-    down_weight_grad, gate_weight_grad, up_weight_grad = (
-        finish_feed(*total, event) for total, event in zip(totals, events)
-    )
-    across = (((0,), (1,)), ((), ()))
-    output_weight_grad = scatter_heads(
-        lax.dot_general(grad_hidden_low, attended_low, across, preferred_element_type=F32)
-    )
-    query_weight_grad = scatter_heads(
-        lax.dot_general(normed_one_low, query_grad_low, across, preferred_element_type=F32)
-    )
-
-    small_grad = contract_first(normed_one_low[:tokens], keyvalue_grad_low)
+    grad_one = grad_one[:tokens] + grad_one_x.astype(F32)
+    grad_one = grad_one + contract_last(keyvalue_grad_low, keyvalue_full)
+    gain_one_grad = jnp.sum(grad_one * normed_one, axis=0)
+    gain_two_grad = jnp.sum(grad_two * normed_two, axis=0)
+    small_grad = contract_first(normed_mine_low, keyvalue_grad_low)
     small_gains = jnp.stack([gain_one_grad, gain_two_grad], -1)
     small_gains = jnp.pad(small_gains, ((0, 0), (0, HEAD_DIM - 2)))
-    small_grad = jnp.concatenate([small_grad, small_gains], -1)
-    small_grad = fold(fold(small_grad, "c"), "y")
-    small_grad = fold(small_grad, "h").reshape(M, 2, 2, rows, 3 * HEAD_DIM)
-    small_grad = pick(small_grad, l, 1) + swap(low(pick(small_grad, 1 - l, 1)), "l").astype(F32)
-    small_grad = pick(small_grad, x, 1) + swap(low(pick(small_grad, 1 - x, 1)), "x").astype(F32)
-    small_grad = scatter_m(small_grad, 0)
-    keyvalue_weight_grad = small_grad[:, : 2 * HEAD_DIM]
-    gain_one_mine = small_grad[:, 2 * HEAD_DIM]
-    gain_two_mine = small_grad[:, 2 * HEAD_DIM + 1]
+    query_total = jnp.concatenate([query_term, low(small_grad), low(small_gains)], -1)
+    query_got = swap_core(query_total[half:])
+    query_got, output_got, query_total = sync(query_got, output_got, query_total)
+    query_total, query_got = fold_l(query_total[:half].astype(F32) + query_got.astype(F32))
+    output_total, output_got = give_x(output_total, output_got)
+    input_grad = outward(
+        grad_hidden + norm_back(grad_one * gain_one, normed_one, scale_one)
+    )[None]
+    block_output = outward(low(hidden + feed_out))[None]
+    output_got, down_y2 = sync(output_got, down_y2)
+    output_total, output_got = next_fold(take_x(output_total, output_got), "y")
+    query_got, output_got = sync(query_got, output_got)
+    query_total, query_got = give_x(query_total, query_got)
+    output_total, output_got = next_fold(output_total + output_got.astype(F32), "h")
+    query_got, output_got, down_h1, both_grad = sync(query_got, output_got, down_h1, both_grad)
+    query_total, query_got = next_fold(take_x(query_total, query_got), "y")
+    output_weight_grad = scatter_m(output_total + output_got.astype(F32), 0)
+
+    def finish_feed(own):
+        own = low(scatter_m(own, 0))
+        got = lax.all_to_all(own, ("l", "x"), 0, 0)
+        return [merge(got[:, i]) for i in range(own.shape[1])]
+
+    (down_weight_grad,) = finish_feed(
+        quarter(0, down_h1, down_y2).reshape(M, 4, 1, rows, part)
+    )
+    query_got, down_weight_grad = sync(query_got, down_weight_grad)
+    query_total, query_got = next_fold(query_total + query_got.astype(F32), "h")
+    both_grad = both_grad.reshape(2, M, 4, rows, part).transpose(1, 2, 0, 3, 4)
+    gate_weight_grad, up_weight_grad = finish_feed(both_grad)
+    query_total = scatter_m(query_total + query_got.astype(F32), 0)
+    query_weight_grad = query_total[:, :query_width]
+    keyvalue_weight_grad = query_total[:, query_width : query_width + 2 * HEAD_DIM]
+    gain_one_mine = query_total[:, query_width + 2 * HEAD_DIM]
+    gain_two_mine = query_total[:, query_width + 2 * HEAD_DIM + 1]
     return (
         block_output,
         shared_mine[None],

time: 763 us -> 649 us (0.85)
  waiting for transfers between devices: 309 us -> 242 us
  Pallas kernels: 156 us -> 104 us
  local copies, waits for them, and re-layouts: 64.3 us -> 85.5 us
  starting transfers between devices: 107 us -> 92.4 us
  between operations: 2.68 us -> 16.3 us
  other arithmetic: 89 us -> 80.3 us
    ppermute x68 -> x65, waiting for transfers between devices: 304 us -> 241 us  [swap(): return lax.ppermute(value, axis, [(0, 1), (1, 0)])]
    pallas_call x2 -> x4, Pallas kernels: 67.8 us -> 14 us  [the longest x3 10.2 us: merge(): pl.pallas_call(merge_kernel, out_shape=jax.ShapeDtypeStruct((rows, 4 * pa...]
    convert_element_type x11 -> x8, other arithmetic: 27.3 us -> 10.3 us  [low(): return value.astype(BF16)]
    unnamed x146 -> x157, local copies, waits for them, and re-layouts: 17.5 us -> 26.7 us
    ppermute x68 -> x65, starting transfers between devices: 67.3 us -> 60.5 us  [swap(): return lax.ppermute(value, axis, [(0, 1), (1, 0)])]
    add x17 -> x11, other arithmetic: 17.6 us -> 13.3 us  [the longest x1 4.48 us: on_device(): output_term[:half].astype(F32) + output_got.astype(F32)]
    pallas_call x5 -> x6, Pallas kernels: 88.3 us -> 89.5 us  [local_call(): pl.pallas_call(kernel, out_shape=outs, in_specs=near + [pl.BlockSpec(memo...]
  transfers between devices with their start and end apart: 77 -> 73, of which waited for: 28 -> 32; matrix products, arithmetic and copies ran while one was open for 22% -> 23% of each run, Pallas kernels for 15% -> 11%
where the time goes in v4:
time: 649 us; the launch traced here: 639 us
  waiting for transfers between devices  242 us (37%)
  Pallas kernels  104 us (16%)
  starting transfers between devices  92.4 us (14%)
  local copies, waits for them, and re-layouts  85.5 us (13%)
  other arithmetic  80.3 us (12%)
  matrix products  18.8 us (3%)
  between operations  16.3 us (3%)
    ppermute x65, waiting for transfers between devices, swap(): return lax.ppermute(value, axis, [(0, 1), (1, 0)])  241 us
    pallas_call x6, Pallas kernels, local_call(): pl.pallas_call(kernel, out_shape=outs, in_specs=near + [pl.BlockSpec(memo...  89.5 us
    ppermute x65, starting transfers between devices, swap(): return lax.ppermute(value, axis, [(0, 1), (1, 0)])  60.5 us
    unnamed x157, local copies, waits for them, and re-layouts  26.7 us
  transfers between devices with their start and end apart: 73, of which 32 were waited for; matrix products, arithmetic and copies ran while one was open for 23% of the time, Pallas kernels for 11%

profile of v4, /device:TPU:0, one launch (start us, length us, event | category | flops | bytes accessed | tf_op | source)
XLA Modules:
  0.0 638.6 jit_solution(5366324915887797394)
XLA Ops:
  9.3 2.9 collective-permute-start
  29.2 3.9 shard_map.212
  33.1 5.8 collective-permute-done.3
  41.2 2.6 collective-permute-start.7
  43.9 3.6 all-to-all-start
  55.9 3.3 collective-permute-done.8
  69.5 20.4 %collective-permute-done.11 = bf16[1,2,2,64,1024]{4,3,2,1,0:T(8,128)(2,1)} collective-permute-done((bf16[1,2,2,64,1024]{4,3,2,1,0:T(8,128)(2,1)}, bf16[1,2,2,64,1024]{4,3,2,1,0:T(8,128)(2,1)}, u32[]{:S(2)}, u32[]{:S(2)}) %collective-permute-start.11) | collective-permute-done | bytes 524320 | tf_op jit(solution)/shard_map/ppermute | solution.py:56
  92.5 2.7 fusion.58
  98.0 3.4 collective-permute-start.14
  103.9 2.8 collective-permute-start.13
  109.1 2.7 add.534.key_place
  113.4 10.7 %collective-permute-done.14 = bf16[1,2,2,64,1024]{4,3,2,1,0:T(8,128)(2,1)S(1)} collective-permute-done((bf16[1,2,2,64,1024]{4,3,2,1,0:T(8,128)(2,1)}, bf16[1,2,2,64,1024]{4,3,2,1,0:T(8,128)(2,1)S(1)}, u32[]{:S(2)}, u32[]{:S(2)}) %collective-permute-start.14) | collective-permute-done | bytes 524320 | tf_op jit(solution)/shard_map/ppermute | solution.py:56
  127.0 2.3 pad_maximum_fusion.9
  138.8 6.5 %all-to-all-start.1 = ((bf16[4,128,2048]{2,1,0:T(8,128)(2,1)}), bf16[4,128,2048]{2,1,0:T(8,128)(2,1)}, u32[]{:S(2)}, u32[]{:S(2)}) async-start(bf16[4,128,2048]{2,1,0:T(8,128)(2,1)} %broadcast_in_dim.21), calls=%async_computation.1 | async-start | bytes 4194304 | tf_op jit(solution)/shard_map/all_to_all | solution.py:101
  145.2 2.5 fusion.65
  148.7 3.3 constant_dynamic-update-slice_fusion
  152.0 4.5 fusion.67.query_sum
  156.5 13.1 %shard_map.213 = (bf16[1024,256]{1,0:T(8,128)(2,1)}, f32[1024,256]{1,0:T(8,128)}, bf16[1024,256]{1,0:T(8,128)(2,1)}, f32[8,256]{1,0:T(8,128)}) custom-call(f32[1024,256]{1,0:T(8,128)} %fusion.67.query_sum, bf16[2048,128]{1,0:T(8,128)(2,1)} %get-tuple-element.322.key, bf16[128,2048]{1,0:T(8,128)(2,1)} %copy.165.value_t, f32[64,256]{1,0:T(8,128)} %get-tuple-element.346.cosine, ...), custom_call_target="tpu_custom_call" | custom-call | flops 1 | bytes 1 | tf_op jit(solution)/shard_map/pallas_call | solution.py:368
  182.4 2.8 collective-permute-start.27
  185.2 16.1 %collective-permute-done.28 = bf16[1,3,64,1408]{3,2,1,0:T(8,128)(2,1)} collective-permute-done((bf16[1,3,64,1408]{3,2,1,0:T(8,128)(2,1)}, bf16[1,3,64,1408]{3,2,1,0:T(8,128)(2,1)}, u32[]{:S(2)}, u32[]{:S(2)}) %collective-permute-start.28) | collective-permute-done | bytes 540704 | tf_op jit(solution)/shard_map/ppermute | solution.py:56
  205.0 4.5 all-to-all-start.2
  218.4 26.5 %collective-permute-done.30 = bf16[1,3,64,1408]{3,2,1,0:T(8,128)(2,1)S(1)} collective-permute-done((bf16[1,3,64,1408]{3,2,1,0:T(8,128)(2,1)S(1)}, bf16[1,3,64,1408]{3,2,1,0:T(8,128)(2,1)S(1)}, u32[]{:S(2)}, u32[]{:S(2)}) %collective-permute-start.30) | collective-permute-done | bytes 540704 | tf_op jit(solution)/shard_map/ppermute | solution.py:56
  245.0 20.3 %collective-permute-done.31 = bf16[1,3,64,1408]{3,2,1,0:T(8,128)(2,1)S(1)} collective-permute-done((bf16[1,3,64,1408]{3,2,1,0:T(8,128)(2,1)S(1)}, bf16[1,3,64,1408]{3,2,1,0:T(8,128)(2,1)S(1)}, u32[]{:S(2)}, u32[]{:S(2)}) %collective-permute-start.31) | collective-permute-done | bytes 540704 | tf_op jit(solution)/shard_map/ppermute | solution.py:56
  271.1 23.6 %collective-permute-done.34.refs_6_ = bf16[2,3,64,1408]{3,2,1,0:T(8,128)(2,1)S(1)} collective-permute-done((bf16[2,3,64,1408]{3,2,1,0:T(8,128)(2,1)S(1)}, bf16[2,3,64,1408]{3,2,1,0:T(8,128)(2,1)S(1)}, u32[]{:S(2)}, u32[]{:S(2)}) %collective-permute-start.34) | collective-permute-done | bytes 1081376 | tf_op jit(solution)/shard_map/ppermute | solution.py:56
  295.2 3.2 collective-permute-done.40.refs_11_
  300.4 28.3 %shard_map.214 = (bf16[512,1408]{1,0:T(8,128)(2,1)}, bf16[512,1408]{1,0:T(8,128)(2,1)}, bf16[512,1408]{1,0:T(8,128)(2,1)}, bf16[512,2048]{1,0:T(8,128)(2,1)}) custom-call(bf16[512,2048]{1,0:T(8,128)(2,1)} %bitcast.79.normed.left, bf16[512,2048]{1,0:T(8,128)(2,1)} %bitcast.77.grad.left, bf16[4,3,64,1408]{3,2,1,0:T(8,128)(2,1)} %copy-done.2, ...), custom_call_target="tpu_custom_call" | custom-call | flops 1 | bytes 1 | tf_op jit(solution)/shard_map/pallas_call | solution.py:368
  328.7 4.5 all-to-all-start.3
  333.9 14.8 %shard_map.215 = bf16[8,2,256,1408]{3,2,1,0:T(8,128)(2,1)} custom-call(s32[8]{0:T(128)} %stack.424.order, bf16[512,2048]{1,0:T(8,128)(2,1)} %bitcast.79.normed.left, bf16[512,1408]{1,0:T(8,128)(2,1)} %get-tuple-element.194.refs_0_, bf16[512,1408]{1,0:T(8,128)(2,1)} %get-tuple-element.195.refs_1_), custom_call_target="tpu_custom_call" | custom-call | flops 1 | bytes 1 | tf_op jit(solution)/shard_map/pallas_call | solution.py:368
  348.7 8.2 %shard_map.216 = (bf16[1024,1408]{1,0:T(8,128)(2,1)}, bf16[1024,1408]{1,0:T(8,128)(2,1)}) custom-call(bf16[512,2048]{1,0:T(8,128)(2,1)} %bitcast.77.grad.left, bf16[512,1408]{1,0:T(8,128)(2,1)} %get-tuple-element.199.refs_0_.mixed), custom_call_target="tpu_custom_call" | custom-call | flops 1 | bytes 1 | tf_op jit(solution)/shard_map/pallas_call | solution.py:368
  357.1 10.3 %shard_map.217 = bf16[512,2048]{1,0:T(8,128)(2,1)} custom-call(bf16[512,1408]{1,0:T(8,128)(2,1)} %get-tuple-element.199.refs_0_.mixed, bf16[4,3,64,1408]{3,2,1,0:T(8,128)(2,1)} %copy-done.2, bf16[2,3,64,1408]{3,2,1,0:T(8,128)(2,1)} %constant_dynamic-update-slice_fusion.4.refs_1_, bf16[2,3,64,1408]{3,2,1,0:T(8,128)(2,1)} %copy-done.18, ...), custom_call_target="tpu_custom_call" | custom-call | flops 1 | bytes 1 | tf_op jit(solution)/shard_map/pallas_call | solution.py:368
  367.4 2.7 convert_reduce_fusion.1
  370.8 2.3 collective-permute-start.43
  373.2 12.4 %collective-permute-done.43 = bf16[128,2048]{1,0:T(8,128)(2,1)S(1)} collective-permute-done((bf16[128,2048]{1,0:T(8,128)(2,1)S(1)}, bf16[128,2048]{1,0:T(8,128)(2,1)S(1)}, u32[]{:S(2)}, u32[]{:S(2)}) %collective-permute-start.43) | collective-permute-done | bytes 524320 | tf_op jit(solution)/shard_map/ppermute | solution.py:56
  386.3 4.7 all-to-all-start.4
  397.2 2.4 add_convert_fusion.3
  404.0 4.3 convolution_convert_fusion.3.grad
  408.3 14.8 %shard_map.218 = (bf16[1024,256]{1,0:T(8,128)(2,1)}, f32[2048,256]{1,0:T(8,128)}) custom-call(bf16[1024,256]{1,0:T(8,128)(2,1)} %get-tuple-element.173.query_rot, bf16[2048,128]{1,0:T(8,128)(2,1)} %get-tuple-element.322.key, bf16[128,2048]{1,0:T(8,128)(2,1)} %copy.170.key_t, bf16[2048,128]{1,0:T(8,128)(2,1)} %get-tuple-element.319.value, ...), custom_call_target="tpu_custom_call" | custom-call | flops 1 | bytes 1 | tf_op jit(solution)/shard_map/pallas_call | solution.py:368
  423.1 10.3 %collective-permute-done.45 = bf16[256,1408]{1,0:T(8,128)(2,1)} collective-permute-done((bf16[256,1408]{1,0:T(8,128)(2,1)}, bf16[256,1408]{1,0:T(8,128)(2,1)}, u32[]{:S(2)}, u32[]{:S(2)}) %collective-permute-start.45) | collective-permute-done | bytes 720928 | tf_op jit(solution)/shard_map/ppermute | solution.py:56
  435.6 4.5 convert_add_fusion.1
  440.1 2.4 convert_reduce_fusion
  445.8 3.3 convolution_convert_fusion
  449.1 3.6 collective-permute-done.47
  456.0 3.6 collective-permute-done.48
  461.9 2.8 fusion.22
  466.3 7.2 %collective-permute-done.49 = bf16[1,128,256]{2,1,0:T(8,128)(2,1)S(1)} collective-permute-done((bf16[1,128,256]{2,1,0:T(8,128)(2,1)S(1)}, bf16[1,128,256]{2,1,0:T(8,128)(2,1)S(1)}, u32[]{:S(2)}, u32[]{:S(2)}) %collective-permute-start.49) | collective-permute-done | bytes 65568 | tf_op jit(solution)/shard_map/ppermute | solution.py:56
  478.1 3.4 fusion.1
  486.2 3.1 add_convert_fusion.1
  490.9 2.3 pad_maximum_fusion.1
  493.1 16.6 %collective-permute-done.55 = bf16[2,2,1,2,64,1024]{5,4,1,0,3,2:T(8,128)(2,1)} collective-permute-done((bf16[2,2,1,2,64,1024]{5,4,1,0,3,2:T(8,128)(2,1)}, bf16[2,2,1,2,64,1024]{5,4,1,0,3,2:T(8,128)(2,1)}, u32[]{:S(2)}, u32[]{:S(2)}) %collective-permute-start.55) | collective-permute-done | bytes 1048608 | tf_op jit(solution)/shard_map/ppermute | solution.py:56
  514.5 2.4 copy-done.8
  529.4 2.6 collective-permute-start.59
  534.1 7.8 %collective-permute-done.59 = bf16[2,1,64,2048]{3,2,0,1:T(8,128)(2,1)} collective-permute-done((bf16[2,1,64,2048]{3,2,0,1:T(8,128)(2,1)}, bf16[2,1,64,2048]{3,2,0,1:T(8,128)(2,1)}, u32[]{:S(2)}, u32[]{:S(2)}) %collective-permute-start.59) | collective-permute-done | bytes 524320 | tf_op jit(solution)/shard_map/ppermute | solution.py:56
  541.8 14.0 %collective-permute-done.56 = bf16[2,2,1,2,64,1408]{5,4,1,0,3,2:T(8,128)(2,1)} collective-permute-done((bf16[2,2,1,2,64,1408]{5,4,1,0,3,2:T(8,128)(2,1)}, bf16[2,2,1,2,64,1408]{5,4,1,0,3,2:T(8,128)(2,1)}, u32[]{:S(2)}, u32[]{:S(2)}) %collective-permute-start.56) | collective-permute-done | bytes 1441824 | tf_op jit(solution)/shard_map/ppermute | solution.py:56
  555.8 2.5 bitcast_add_fusion
  562.7 12.6 %collective-permute-done.61 = bf16[1,64,2048]{2,1,0:T(8,128)(2,1)} collective-permute-done((bf16[1,64,2048]{2,1,0:T(8,128)(2,1)S(1)}, bf16[1,64,2048]{2,1,0:T(8,128)(2,1)}, u32[]{:S(2)}, u32[]{:S(2)}) %collective-permute-start.61) | collective-permute-done | bytes 262176 | tf_op jit(solution)/shard_map/ppermute | solution.py:56
  578.1 3.1 add_convert_fusion
  581.1 4.2 all-to-all-start.5
  588.1 2.5 copy.197
  590.7 2.6 copy.225
  595.1 4.0 all-to-all-start.6
  599.1 3.4 shard_map.219
  606.7 13.7 %collective-permute-done.64 = bf16[1,64,2432]{2,1,0:T(8,128)(2,1)S(1)} collective-permute-done((bf16[1,64,2432]{2,1,0:T(8,128)(2,1)S(1)}, bf16[1,64,2432]{2,1,0:T(8,128)(2,1)S(1)}, u32[]{:S(2)}, u32[]{:S(2)}) %collective-permute-start.64) | collective-permute-done | bytes 311328 | tf_op jit(solution)/shard_map/ppermute | solution.py:56
  624.5 3.4 shard_map.221
  627.9 3.4 shard_map.220
  (434 shorter events, 173.9 us)
Async XLA Ops:
  9.3 13.6 %collective-permute-start = (bf16[80,256]{1,0:T(8,128)(2,1)}, bf16[80,256]{1,0:T(8,128)(2,1)S(1)}, u32[]{:S(2)}, u32[]{:S(2)}) collective-permute-start(bf16[80,256]{1,0:T(8,128)(2,1)} %get-tuple-element.344), channel_id=1, source_target_pairs={{0,2},{2,0},{1,3},{3,1},{4,6},{6,4},{5,7},{7,5},{8,10},{10,8},{9,1... | collective-permute-start | bytes 122888 | tf_op jit(solution)/shard_map/ppermute | solution.py:56
  16.4 6.6 %collective-permute-start.1 = (bf16[64,1024]{1,0:T(8,128)(2,1)}, bf16[64,1024]{1,0:T(8,128)(2,1)S(1)}, u32[]{:S(2)}, u32[]{:S(2)}) collective-permute-start(bf16[64,1024]{1,0:T(8,128)(2,1)} %bitcast.247), channel_id=1, source_target_pairs={{0,2},{2,0},{1,3},{3,1},{4,6},{6,4},{5,7},{7,5},{8,10},{10,8},{9,1... | collective-permute-start | bytes 393224 | tf_op jit(solution)/shard_map/ppermute | solution.py:56
  17.1 7.3 %collective-permute-start.2 = (bf16[64,1024]{1,0:T(8,128)(2,1)}, bf16[64,1024]{1,0:T(8,128)(2,1)S(1)}, u32[]{:S(2)}, u32[]{:S(2)}) collective-permute-start(bf16[64,1024]{1,0:T(8,128)(2,1)} %bitcast.246), channel_id=1, source_target_pairs={{0,2},{2,0},{1,3},{3,1},{4,6},{6,4},{5,7},{7,5},{8,10},{10,8},{9,1... | collective-permute-start | bytes 393224 | tf_op jit(solution)/shard_map/ppermute | solution.py:56
  24.6 14.3 %collective-permute-start.4 = (bf16[2,64,1024]{2,1,0:T(8,128)(2,1)S(1)}, bf16[2,64,1024]{2,1,0:T(8,128)(2,1)}, u32[]{:S(2)}, u32[]{:S(2)}) collective-permute-start(bf16[2,64,1024]{2,1,0:T(8,128)(2,1)S(1)} %maximum_select_fusion.4), channel_id=1, source_target_pairs={{0,4},{4,0},{1,5},{5,1},{2,6},{6,2},{3,7},{7,3},{8,12},{12,8},{9,1... | collective-permute-start | bytes 786440 | tf_op jit(solution)/shard_map/ppermute | solution.py:56
  26.3 12.7 %collective-permute-start.6 = (bf16[128,2048]{1,0:T(8,128)(2,1)S(1)}, bf16[128,2048]{1,0:T(8,128)(2,1)S(1)}, u32[]{:S(2)}, u32[]{:S(2)}) collective-permute-start(bf16[128,2048]{1,0:T(8,128)(2,1)S(1)} %copy.159), channel_id=1, source_target_pairs={{0,2},{2,0},{1,3},{3,1},{4,6},{6,4},{5,7},{7,5},{8,10},{10,8},{9,1... | collective-permute-start | bytes 1572872 | tf_op jit(solution)/shard_map/ppermute | solution.py:56
  26.9 12.1 %collective-permute-start.5 = (bf16[2,64,1024]{2,1,0:T(8,128)(2,1)S(1)}, bf16[2,64,1024]{2,1,0:T(8,128)(2,1)S(1)}, u32[]{:S(2)}, u32[]{:S(2)}) collective-permute-start(bf16[2,64,1024]{2,1,0:T(8,128)(2,1)S(1)} %maximum_select_fusion.5), channel_id=1, source_target_pairs={{0,4},{4,0},{1,5},{5,1},{2,6},{6,2},{3,7},{7,3},{8,12},{12,8},{9,1... | collective-permute-start | bytes 786440 | tf_op jit(solution)/shard_map/ppermute | solution.py:56
  27.3 11.6 %collective-permute-start.3 = (bf16[2,80,256]{2,1,0:T(8,128)(2,1)S(1)}, bf16[2,80,256]{2,1,0:T(8,128)(2,1)S(1)}, u32[]{:S(2)}, u32[]{:S(2)}) collective-permute-start(bf16[2,80,256]{2,1,0:T(8,128)(2,1)S(1)} %maximum_select_fusion.9), channel_id=1, source_target_pairs={{0,4},{4,0},{1,5},{5,1},{2,6},{6,2},{3,7},{7,3},{8,12},{12,8},{9,1... | collective-permute-start | bytes 245768 | tf_op jit(solution)/shard_map/ppermute | solution.py:56
  41.2 8.2 %collective-permute-start.7 = (bf16[1,2,2,80,256]{4,3,2,1,0:T(8,128)(2,1)S(1)}, bf16[1,2,2,80,256]{4,3,2,1,0:T(8,128)(2,1)S(1)}, u32[]{:S(2)}, u32[]{:S(2)}) collective-permute-start(bf16[1,2,2,80,256]{4,3,2,1,0:T(8,128)(2,1)S(1)} %maximum_select_fusion.8), channel_id=1, source_target_pairs={{0,8},{8,0},{1,9},{9,1},{2,10},{10,2},{3,11},{11,3},{4,12},{12,4},... | collective-permute-start | bytes 491528 | tf_op jit(solution)/shard_map/ppermute | solution.py:56
  43.9 46.9 %all-to-all-start = ((bf16[4,3,64,1408]{3,2,1,0:T(8,128)(2,1)}), bf16[4,3,64,1408]{3,2,1,0:T(8,128)(2,1)S(1)}, u32[]{:S(2)}, u32[]{:S(2)}) async-start(bf16[4,3,64,1408]{3,2,1,0:T(8,128)(2,1)} %shard_map.212), calls=%async_computation | async-start | bytes 4325376 | tf_op jit(solution)/shard_map/all_to_all | solution.py:478
  51.9 7.4 %collective-permute-start.8 = (bf16[2,1,2,2,80,256]{5,4,3,2,1,0:T(8,128)(2,1)}, bf16[2,1,2,2,80,256]{5,4,3,2,1,0:T(8,128)(2,1)}, u32[]{:S(2)}, u32[]{:S(2)}) collective-permute-start(bf16[2,1,2,2,80,256]{5,4,3,2,1,0:T(8,128)(2,1)} %get-tuple-element.328), channel_id=1, source_target_pairs={{0,16},{16,0},{1,17},{17,1},{2,18},{18,2},{3,19},{19,3},{4,20},{20... | collective-permute-start | bytes 983048 | tf_op jit(solution)/shard_map/ppermute | solution.py:56
  61.2 28.7 %collective-permute-start.11 = (bf16[1,2,2,64,1024]{4,3,2,1,0:T(8,128)(2,1)}, bf16[1,2,2,64,1024]{4,3,2,1,0:T(8,128)(2,1)}, u32[]{:S(2)}, u32[]{:S(2)}) collective-permute-start(bf16[1,2,2,64,1024]{4,3,2,1,0:T(8,128)(2,1)} %maximum_select_fusion.2), channel_id=1, source_target_pairs={{0,8},{8,0},{1,9},{9,1},{2,10},{10,2},{3,11},{11,3},{4,12},{12,4},... | collective-permute-start | bytes 1572872 | tf_op jit(solution)/shard_map/ppermute | solution.py:56
  68.2 22.5 %collective-permute-start.10 = (bf16[128,256]{1,0:T(8,128)(2,1)S(1)}, bf16[128,256]{1,0:T(8,128)(2,1)S(1)}, u32[]{:S(2)}, u32[]{:S(2)}) collective-permute-start(bf16[128,256]{1,0:T(8,128)(2,1)S(1)} %pad_maximum_fusion.15), channel_id=1, source_target_pairs={{0,8},{8,0},{1,9},{9,1},{2,10},{10,2},{3,11},{11,3},{4,12},{12,4},... | collective-permute-start | bytes 196616 | tf_op jit(solution)/shard_map/ppermute | solution.py:56
  95.2 29.0 %collective-permute-start.15 = (bf16[2,1,2,2,64,1024]{5,4,3,2,1,0:T(8,128)(2,1)}, bf16[2,1,2,2,64,1024]{5,4,3,2,1,0:T(8,128)(2,1)}, u32[]{:S(2)}, u32[]{:S(2)}) collective-permute-start(bf16[2,1,2,2,64,1024]{5,4,3,2,1,0:T(8,128)(2,1)} %get-tuple-element.324), channel_id=1, source_target_pairs={{0,16},{16,0},{1,17},{17,1},{2,18},{18,2},{3,19},{19,3},{4,20},{20... | collective-permute-start | bytes 3145736 | tf_op jit(solution)/shard_map/ppermute | solution.py:56
  96.9 6.3 collective-permute-start.12
  98.0 26.1 %collective-permute-start.14 = (bf16[1,2,2,64,1024]{4,3,2,1,0:T(8,128)(2,1)}, bf16[1,2,2,64,1024]{4,3,2,1,0:T(8,128)(2,1)S(1)}, u32[]{:S(2)}, u32[]{:S(2)}) collective-permute-start(bf16[1,2,2,64,1024]{4,3,2,1,0:T(8,128)(2,1)} %maximum_select_fusion.3), channel_id=1, source_target_pairs={{0,8},{8,0},{1,9},{9,1},{2,10},{10,2},{3,11},{11,3},{4,12},{12,4},... | collective-permute-start | bytes 1572872 | tf_op jit(solution)/shard_map/ppermute | solution.py:56
  103.9 9.5 %collective-permute-start.13 = (bf16[2,1,2,128,256]{4,3,2,0,1:T(8,128)(2,1)}, bf16[2,1,2,128,256]{4,3,2,0,1:T(8,128)(2,1)}, u32[]{:S(2)}, u32[]{:S(2)}) collective-permute-start(bf16[2,1,2,128,256]{4,3,2,0,1:T(8,128)(2,1)} %get-tuple-element.332), channel_id=1, source_target_pairs={{0,2},{2,0},{1,3},{3,1},{4,6},{6,4},{5,7},{7,5},{8,10},{10,8},{9,1... | collective-permute-start | bytes 786440 | tf_op jit(solution)/shard_map/ppermute | solution.py:56
  129.3 6.4 %collective-permute-start.16 = (bf16[2,2,1,2,128,256]{5,4,3,1,0,2:T(8,128)(2,1)S(1)}, bf16[2,2,1,2,128,256]{5,4,3,1,0,2:T(8,128)(2,1)S(1)}, u32[]{:S(2)}, u32[]{:S(2)}) collective-permute-start(bf16[2,2,1,2,128,256]{5,4,3,1,0,2:T(8,128)(2,1)S(1)} %bitcast.281), channel_id=1, source_target_pairs={{0,1},{1,0},{2,3},{3,2},{4,5},{5,4},{6,7},{7,6},{8,9},{9,8},{10,11... | collective-permute-start | bytes 1572872 | tf_op jit(solution)/shard_map/ppermute | solution.py:56
  133.5 36.0 %collective-permute-start.21 = (bf16[2,1,2,2,64,1024]{5,4,3,2,0,1:T(8,128)(2,1)}, bf16[2,1,2,2,64,1024]{5,4,3,2,0,1:T(8,128)(2,1)}, u32[]{:S(2)}, u32[]{:S(2)}) collective-permute-start(bf16[2,1,2,2,64,1024]{5,4,3,2,0,1:T(8,128)(2,1)} %bitcast.73), channel_id=1, source_target_pairs={{0,16},{16,0},{1,17},{17,1},{2,18},{18,2},{3,19},{19,3},{4,20},{20... | collective-permute-start | bytes 3145736 | tf_op jit(solution)/shard_map/ppermute | solution.py:56
  134.0 35.5 %collective-permute-start.22 = (bf16[1,3,64,1408]{3,2,1,0:T(8,128)(2,1)}, bf16[1,3,64,1408]{3,2,1,0:T(8,128)(2,1)}, u32[]{:S(2)}, u32[]{:S(2)}) collective-permute-start(bf16[1,3,64,1408]{3,2,1,0:T(8,128)(2,1)} %get-tuple-element.305), channel_id=1, source_target_pairs={{0,8},{8,0},{1,9},{9,1},{2,10},{10,2},{3,11},{11,3},{4,12},{12,4},... | collective-permute-start | bytes 1622024 | tf_op jit(solution)/shard_map/ppermute | solution.py:56
  138.8 62.5 %all-to-all-start.1 = ((bf16[4,128,2048]{2,1,0:T(8,128)(2,1)}), bf16[4,128,2048]{2,1,0:T(8,128)(2,1)}, u32[]{:S(2)}, u32[]{:S(2)}) async-start(bf16[4,128,2048]{2,1,0:T(8,128)(2,1)} %broadcast_in_dim.21), calls=%async_computation.1 | async-start | bytes 4194304 | tf_op jit(solution)/shard_map/all_to_all | solution.py:101
  171.6 5.1 collective-permute-start.26
  172.4 4.2 collective-permute-start.25
  174.2 27.1 %collective-permute-start.28 = (bf16[1,3,64,1408]{3,2,1,0:T(8,128)(2,1)}, bf16[1,3,64,1408]{3,2,1,0:T(8,128)(2,1)}, u32[]{:S(2)}, u32[]{:S(2)}) collective-permute-start(bf16[1,3,64,1408]{3,2,1,0:T(8,128)(2,1)} %get-tuple-element.169), channel_id=1, source_target_pairs={{0,8},{8,0},{1,9},{9,1},{2,10},{10,2},{3,11},{11,3},{4,12},{12,4},... | collective-permute-start | bytes 1622024 | tf_op jit(solution)/shard_map/ppermute | solution.py:56
  175.2 26.1 %collective-permute-start.29 = (bf16[2,3,64,1408]{3,2,1,0:T(8,128)(2,1)S(1)}, bf16[2,3,64,1408]{3,2,1,0:T(8,128)(2,1)}, u32[]{:S(2)}, u32[]{:S(2)}) collective-permute-start(bf16[2,3,64,1408]{3,2,1,0:T(8,128)(2,1)S(1)} %get-tuple-element.170), channel_id=1, source_target_pairs={{0,16},{16,0},{1,17},{17,1},{2,18},{18,2},{3,19},{19,3},{4,20},{20... | collective-permute-start | bytes 3244040 | tf_op jit(solution)/shard_map/ppermute | solution.py:56
  182.4 18.9 %collective-permute-start.27 = (bf16[128,2048]{1,0:T(8,128)(2,1)}, bf16[128,2048]{1,0:T(8,128)(2,1)}, u32[]{:S(2)}, u32[]{:S(2)}) collective-permute-start(bf16[128,2048]{1,0:T(8,128)(2,1)} %slice.482), channel_id=1, source_target_pairs={{0,2},{2,0},{1,3},{3,1},{4,6},{6,4},{5,7},{7,5},{8,10},{10,8},{9,1... | collective-permute-start | bytes 1572872 | tf_op jit(solution)/shard_map/ppermute | solution.py:56
  205.0 61.1 %all-to-all-start.2 = ((bf16[4,128,2048]{2,1,0:T(8,128)(2,1)}), bf16[4,128,2048]{2,1,0:T(8,128)(2,1)}, u32[]{:S(2)}, u32[]{:S(2)}) async-start(bf16[4,128,2048]{2,1,0:T(8,128)(2,1)} %broadcast_in_dim.22), calls=%async_computation.2 | async-start | bytes 4194304 | tf_op jit(solution)/shard_map/all_to_all | solution.py:101
  209.5 58.9 %collective-permute-start.35 = (bf16[4,3,64,1408]{3,2,1,0:T(8,128)(2,1)S(1)}, bf16[4,3,64,1408]{3,2,1,0:T(8,128)(2,1)}, u32[]{:S(2)}, u32[]{:S(2)}) collective-permute-start(bf16[4,3,64,1408]{3,2,1,0:T(8,128)(2,1)S(1)} %all-to-all-done.refs_0_), channel_id=1, source_target_pairs={{0,1},{1,0},{2,3},{3,2},{4,5},{5,4},{6,7},{7,6},{8,9},{9,8},{10,11... | collective-permute-start | bytes 6488072 | tf_op jit(solution)/shard_map/ppermute | solution.py:56
  213.5 52.6 %collective-permute-start.32 = (bf16[2,3,64,1408]{3,2,1,0:T(8,128)(2,1)}, bf16[2,3,64,1408]{3,2,1,0:T(8,128)(2,1)}, u32[]{:S(2)}, u32[]{:S(2)}) collective-permute-start(bf16[2,3,64,1408]{3,2,1,0:T(8,128)(2,1)} %constant_dynamic-update-slice_fusion.4.refs_1_), channel_id=1, source_target_pairs={{0,16},{16,0},{1,17},{17,1},{2,18},{18,2},{3,19},{19,3},{4,20},{20... | collective-permute-start | bytes 3244040 | tf_op jit(solution)/shard_map/ppermute | solution.py:56
  215.0 55.0 %collective-permute-start.33 = (bf16[2,3,64,1408]{3,2,1,0:T(8,128)(2,1)}, bf16[2,3,64,1408]{3,2,1,0:T(8,128)(2,1)}, u32[]{:S(2)}, u32[]{:S(2)}) collective-permute-start(bf16[2,3,64,1408]{3,2,1,0:T(8,128)(2,1)} %get-tuple-element.183), channel_id=1, source_target_pairs={{0,16},{16,0},{1,17},{17,1},{2,18},{18,2},{3,19},{19,3},{4,20},{20... | collective-permute-start | bytes 3244040 | tf_op jit(solution)/shard_map/ppermute | solution.py:56
  215.5 29.4 %collective-permute-start.30 = (bf16[1,3,64,1408]{3,2,1,0:T(8,128)(2,1)S(1)}, bf16[1,3,64,1408]{3,2,1,0:T(8,128)(2,1)S(1)}, u32[]{:S(2)}, u32[]{:S(2)}) collective-permute-start(bf16[1,3,64,1408]{3,2,1,0:T(8,128)(2,1)S(1)} %copy-done.41), channel_id=1, source_target_pairs={{0,8},{8,0},{1,9},{9,1},{2,10},{10,2},{3,11},{11,3},{4,12},{12,4},... | collective-permute-start | bytes 1622024 | tf_op jit(solution)/shard_map/ppermute | solution.py:56
  217.0 48.3 %collective-permute-start.31 = (bf16[1,3,64,1408]{3,2,1,0:T(8,128)(2,1)S(1)}, bf16[1,3,64,1408]{3,2,1,0:T(8,128)(2,1)S(1)}, u32[]{:S(2)}, u32[]{:S(2)}) collective-permute-start(bf16[1,3,64,1408]{3,2,1,0:T(8,128)(2,1)S(1)} %copy-done.40), channel_id=1, source_target_pairs={{0,8},{8,0},{1,9},{9,1},{2,10},{10,2},{3,11},{11,3},{4,12},{12,4},... | collective-permute-start | bytes 1622024 | tf_op jit(solution)/shard_map/ppermute | solution.py:56
  245.0 25.2 %collective-permute-start.36 = (bf16[2,3,64,1408]{3,2,1,0:T(8,128)(2,1)}, bf16[2,3,64,1408]{3,2,1,0:T(8,128)(2,1)}, u32[]{:S(2)}, u32[]{:S(2)}) collective-permute-start(bf16[2,3,64,1408]{3,2,1,0:T(8,128)(2,1)} %constant_dynamic-update-slice_fusion.4.refs_1_), channel_id=1, source_target_pairs={{0,1},{1,0},{2,3},{3,2},{4,5},{5,4},{6,7},{7,6},{8,9},{9,8},{10,11... | collective-permute-start | bytes 3244040 | tf_op jit(solution)/shard_map/ppermute | solution.py:56
  265.3 4.9 collective-permute-start.38
  268.4 26.3 %collective-permute-start.34 = (bf16[2,3,64,1408]{3,2,1,0:T(8,128)(2,1)S(1)}, bf16[2,3,64,1408]{3,2,1,0:T(8,128)(2,1)S(1)}, u32[]{:S(2)}, u32[]{:S(2)}) collective-permute-start(bf16[2,3,64,1408]{3,2,1,0:T(8,128)(2,1)S(1)} %constant_dynamic-update-slice_fusion.6.refs_2_), channel_id=1, source_target_pairs={{0,16},{16,0},{1,17},{17,1},{2,18},{18,2},{3,19},{19,3},{4,20},{20... | collective-permute-start | bytes 3244040 | tf_op jit(solution)/shard_map/ppermute | solution.py:56
  270.0 24.7 %collective-permute-start.39 = (bf16[2,3,64,1408]{3,2,1,0:T(8,128)(2,1)}, bf16[2,3,64,1408]{3,2,1,0:T(8,128)(2,1)S(1)}, u32[]{:S(2)}, u32[]{:S(2)}) collective-permute-start(bf16[2,3,64,1408]{3,2,1,0:T(8,128)(2,1)} %collective-permute-done.32.refs_5_), channel_id=1, source_target_pairs={{0,1},{1,0},{2,3},{3,2},{4,5},{5,4},{6,7},{7,6},{8,9},{9,8},{10,11... | collective-permute-start | bytes 3244040 | tf_op jit(solution)/shard_map/ppermute | solution.py:56
  294.7 4.2 collective-permute-start.41
  328.7 38.7 %all-to-all-start.3 = ((bf16[4,128,2048]{2,1,0:T(8,128)(2,1)}), bf16[4,128,2048]{2,1,0:T(8,128)(2,1)}, u32[]{:S(2)}, u32[]{:S(2)}) async-start(bf16[4,128,2048]{2,1,0:T(8,128)(2,1)} %bitcast.275), calls=%async_computation.3 | async-start | bytes 4194304 | tf_op jit(solution)/shard_map/all_to_all | solution.py:105
  333.2 243.5 %reduce-scatter.2.cloned.1.call-start = ((), (), s32[]{:S(2)}) async-start(), calls=%async_computation.8 | async-start | bytes 12976128 | tf_op jit(solution)/shard_map/reduce_scatter | solution.py:626
  356.9 13.2 %collective-permute-start.42 = (bf16[1024,1408]{1,0:T(8,128)(2,1)}, bf16[1024,1408]{1,0:T(8,128)(2,1)}, u32[]{:S(2)}, u32[]{:S(2)}) collective-permute-start(bf16[1024,1408]{1,0:T(8,128)(2,1)} %get-tuple-element.198), channel_id=1, source_target_pairs={{0,1},{1,0},{2,3},{3,2},{4,5},{5,4},{6,7},{7,6},{8,9},{9,8},{10,11... | collective-permute-start | bytes 8650760 | tf_op jit(solution)/shard_map/ppermute | solution.py:56
  370.8 14.7 %collective-permute-start.43 = (bf16[128,2048]{1,0:T(8,128)(2,1)S(1)}, bf16[128,2048]{1,0:T(8,128)(2,1)S(1)}, u32[]{:S(2)}, u32[]{:S(2)}) collective-permute-start(bf16[128,2048]{1,0:T(8,128)(2,1)S(1)} %fusion.59), channel_id=1, source_target_pairs={{0,2},{2,0},{1,3},{3,1},{4,6},{6,4},{5,7},{7,5},{8,10},{10,8},{9,1... | collective-permute-start | bytes 1572872 | tf_op jit(solution)/shard_map/ppermute | solution.py:56
  386.3 53.7 %all-to-all-start.4 = ((bf16[4,128,2048]{2,1,0:T(8,128)(2,1)}), bf16[4,128,2048]{2,1,0:T(8,128)(2,1)}, u32[]{:S(2)}, u32[]{:S(2)}) async-start(bf16[4,128,2048]{2,1,0:T(8,128)(2,1)} %bitcast.264), calls=%async_computation.4 | async-start | bytes 4194304 | tf_op jit(solution)/shard_map/all_to_all | solution.py:105
  397.2 11.1 %collective-permute-start.44 = (bf16[1024,1024]{1,0:T(8,128)(2,1)}, bf16[1024,1024]{1,0:T(8,128)(2,1)}, u32[]{:S(2)}, u32[]{:S(2)}) collective-permute-start(bf16[1024,1024]{1,0:T(8,128)(2,1)} %slice.333), channel_id=1, source_target_pairs={{0,1},{1,0},{2,3},{3,2},{4,5},{5,4},{6,7},{7,6},{8,9},{9,8},{10,11... | collective-permute-start | bytes 6291464 | tf_op jit(solution)/shard_map/ppermute | solution.py:56
  399.6 33.9 %collective-permute-start.45 = (bf16[256,1408]{1,0:T(8,128)(2,1)}, bf16[256,1408]{1,0:T(8,128)(2,1)}, u32[]{:S(2)}, u32[]{:S(2)}) collective-permute-start(bf16[256,1408]{1,0:T(8,128)(2,1)} %add_convert_fusion.3), channel_id=1, source_target_pairs={{0,16},{16,0},{1,17},{17,1},{2,18},{18,2},{3,19},{19,3},{4,20},{20... | collective-permute-start | bytes 2162696 | tf_op jit(solution)/shard_map/ppermute | solution.py:56
  435.6 6.9 %collective-permute-start.46 = (bf16[1024,256]{1,0:T(8,128)(2,1)}, bf16[1024,256]{1,0:T(8,128)(2,1)}, u32[]{:S(2)}, u32[]{:S(2)}) collective-permute-start(bf16[1024,256]{1,0:T(8,128)(2,1)} %slice.481), channel_id=1, source_target_pairs={{0,1},{1,0},{2,3},{3,2},{4,5},{5,4},{6,7},{7,6},{8,9},{9,8},{10,11... | collective-permute-start | bytes 1572872 | tf_op jit(solution)/shard_map/ppermute | solution.py:56
  443.8 8.9 %collective-permute-start.47 = (bf16[2,1,2,128,256]{4,3,2,1,0:T(8,128)(2,1)S(1)}, bf16[2,1,2,128,256]{4,3,2,1,0:T(8,128)(2,1)S(1)}, u32[]{:S(2)}, u32[]{:S(2)}) collective-permute-start(bf16[2,1,2,128,256]{4,3,2,1,0:T(8,128)(2,1)S(1)} %bitcast.302), channel_id=1, source_target_pairs={{0,2},{2,0},{1,3},{3,1},{4,6},{6,4},{5,7},{7,5},{8,10},{10,8},{9,1... | collective-permute-start | bytes 786440 | tf_op jit(solution)/shard_map/ppermute | solution.py:56
  452.8 6.8 %collective-permute-start.48 = (bf16[1,2,128,256]{3,2,1,0:T(8,128)(2,1)S(1)}, bf16[1,2,128,256]{3,2,1,0:T(8,128)(2,1)S(1)}, u32[]{:S(2)}, u32[]{:S(2)}) collective-permute-start(bf16[1,2,128,256]{3,2,1,0:T(8,128)(2,1)S(1)} %fusion.37), channel_id=1, source_target_pairs={{0,4},{4,0},{1,5},{5,1},{2,6},{6,2},{3,7},{7,3},{8,12},{12,8},{9,1... | collective-permute-start | bytes 393224 | tf_op jit(solution)/shard_map/ppermute | solution.py:56
  459.7 13.8 %collective-permute-start.50 = (bf16[128,2048]{1,0:T(8,128)(2,1)S(1)}, bf16[128,2048]{1,0:T(8,128)(2,1)S(1)}, u32[]{:S(2)}, u32[]{:S(2)}) collective-permute-start(bf16[128,2048]{1,0:T(8,128)(2,1)S(1)} %slice.480), channel_id=1, source_target_pairs={{0,2},{2,0},{1,3},{3,1},{4,6},{6,4},{5,7},{7,5},{8,10},{10,8},{9,1... | collective-permute-start | bytes 1572872 | tf_op jit(solution)/shard_map/ppermute | solution.py:56
  460.8 12.7 %collective-permute-start.49 = (bf16[1,128,256]{2,1,0:T(8,128)(2,1)S(1)}, bf16[1,128,256]{2,1,0:T(8,128)(2,1)S(1)}, u32[]{:S(2)}, u32[]{:S(2)}) collective-permute-start(bf16[1,128,256]{2,1,0:T(8,128)(2,1)S(1)} %fusion.41), channel_id=1, source_target_pairs={{0,8},{8,0},{1,9},{9,1},{2,10},{10,2},{3,11},{11,3},{4,12},{12,4},... | collective-permute-start | bytes 196616 | tf_op jit(solution)/shard_map/ppermute | solution.py:56
  464.7 45.0 %collective-permute-start.55 = (bf16[2,2,1,2,64,1024]{5,4,1,0,3,2:T(8,128)(2,1)}, bf16[2,2,1,2,64,1024]{5,4,1,0,3,2:T(8,128)(2,1)}, u32[]{:S(2)}, u32[]{:S(2)}) collective-permute-start(bf16[2,2,1,2,64,1024]{5,4,1,0,3,2:T(8,128)(2,1)} %fusion.22), channel_id=1, source_target_pairs={{0,4},{4,0},{1,5},{5,1},{2,6},{6,2},{3,7},{7,3},{8,12},{12,8},{9,1... | collective-permute-start | bytes 3145736 | tf_op jit(solution)/shard_map/ppermute | solution.py:56
  485.2 4.6 collective-permute-start.51
  485.5 5.2 collective-permute-start.54
  485.7 5.2 collective-permute-start.53
  486.0 4.9 collective-permute-start.52
  489.8 72.9 %collective-permute-start.62 = (bf16[256,1408]{1,0:T(8,128)(2,1)}, bf16[256,1408]{1,0:T(8,128)(2,1)}, u32[]{:S(2)}, u32[]{:S(2)}) collective-permute-start(bf16[256,1408]{1,0:T(8,128)(2,1)} %get-tuple-element.294), channel_id=1, source_target_pairs={{0,8},{8,0},{1,9},{9,1},{2,10},{10,2},{3,11},{11,3},{4,12},{12,4},... | collective-permute-start | bytes 2162696 | tf_op jit(solution)/shard_map/ppermute | solution.py:56
  490.7 33.4 %collective-permute-start.58 = (bf16[256,1408]{1,0:T(8,128)(2,1)}, bf16[256,1408]{1,0:T(8,128)(2,1)}, u32[]{:S(2)}, u32[]{:S(2)}) collective-permute-start(bf16[256,1408]{1,0:T(8,128)(2,1)} %get-tuple-element.295), channel_id=1, source_target_pairs={{0,16},{16,0},{1,17},{17,1},{2,18},{18,2},{3,19},{19,3},{4,20},{20... | collective-permute-start | bytes 2162696 | tf_op jit(solution)/shard_map/ppermute | solution.py:56
  512.1 12.4 %collective-permute-start.57 = (bf16[2,2,1,64,1024]{4,3,1,0,2:T(8,128)(2,1)}, bf16[2,2,1,64,1024]{4,3,1,0,2:T(8,128)(2,1)}, u32[]{:S(2)}, u32[]{:S(2)}) collective-permute-start(bf16[2,2,1,64,1024]{4,3,1,0,2:T(8,128)(2,1)} %fusion.27), channel_id=1, source_target_pairs={{0,2},{2,0},{1,3},{3,1},{4,6},{6,4},{5,7},{7,5},{8,10},{10,8},{9,1... | collective-permute-start | bytes 1572872 | tf_op jit(solution)/shard_map/ppermute | solution.py:56
  518.2 37.6 %collective-permute-start.56 = (bf16[2,2,1,2,64,1408]{5,4,1,0,3,2:T(8,128)(2,1)}, bf16[2,2,1,2,64,1408]{5,4,1,0,3,2:T(8,128)(2,1)}, u32[]{:S(2)}, u32[]{:S(2)}) collective-permute-start(bf16[2,2,1,2,64,1408]{5,4,1,0,3,2:T(8,128)(2,1)} %fusion.8), channel_id=1, source_target_pairs={{0,4},{4,0},{1,5},{5,1},{2,6},{6,2},{3,7},{7,3},{8,12},{12,8},{9,1... | collective-permute-start | bytes 4325384 | tf_op jit(solution)/shard_map/ppermute | solution.py:56
  529.4 12.4 %collective-permute-start.59 = (bf16[2,1,64,2048]{3,2,0,1:T(8,128)(2,1)}, bf16[2,1,64,2048]{3,2,0,1:T(8,128)(2,1)}, u32[]{:S(2)}, u32[]{:S(2)}) collective-permute-start(bf16[2,1,64,2048]{3,2,0,1:T(8,128)(2,1)} %convert_element_type.375), channel_id=1, source_target_pairs={{0,16},{16,0},{1,17},{17,1},{2,18},{18,2},{3,19},{19,3},{4,20},{20... | collective-permute-start | bytes 1572872 | tf_op jit(solution)/shard_map/ppermute | solution.py:56
  558.4 18.2 %collective-permute-start.60 = (bf16[2,2,1,64,1408]{4,3,1,0,2:T(8,128)(2,1)S(1)}, bf16[2,2,1,64,1408]{4,3,1,0,2:T(8,128)(2,1)}, u32[]{:S(2)}, u32[]{:S(2)}) collective-permute-start(bf16[2,2,1,64,1408]{4,3,1,0,2:T(8,128)(2,1)S(1)} %fusion.23), channel_id=1, source_target_pairs={{0,2},{2,0},{1,3},{3,1},{4,6},{6,4},{5,7},{7,5},{8,10},{10,8},{9,1... | collective-permute-start | bytes 2162696 | tf_op jit(solution)/shard_map/ppermute | solution.py:56
  561.2 14.1 %collective-permute-start.61 = (bf16[1,64,2048]{2,1,0:T(8,128)(2,1)S(1)}, bf16[1,64,2048]{2,1,0:T(8,128)(2,1)}, u32[]{:S(2)}, u32[]{:S(2)}) collective-permute-start(bf16[1,64,2048]{2,1,0:T(8,128)(2,1)S(1)} %fusion.31), channel_id=1, source_target_pairs={{0,8},{8,0},{1,9},{9,1},{2,10},{10,2},{3,11},{11,3},{4,12},{12,4},... | collective-permute-start | bytes 786440 | tf_op jit(solution)/shard_map/ppermute | solution.py:56
  581.1 14.0 %all-to-all-start.5 = ((bf16[4,1,64,1408]{3,2,1,0:T(8,128)(2,1)}), bf16[4,1,64,1408]{3,2,1,0:T(8,128)(2,1)}, u32[]{:S(2)}, u32[]{:S(2)}) async-start(bf16[4,1,64,1408]{3,2,1,0:T(8,128)(2,1)} %bitcast.272), calls=%async_computation.6 | async-start | bytes 1441792 | tf_op jit(solution)/shard_map/all_to_all | solution.py:753
  586.5 16.0 %collective-permute-start.63 = (bf16[2,1,64,2432]{3,2,0,1:T(8,128)(2,1)}, bf16[2,1,64,2432]{3,2,0,1:T(8,128)(2,1)}, u32[]{:S(2)}, u32[]{:S(2)}) collective-permute-start(bf16[2,1,64,2432]{3,2,0,1:T(8,128)(2,1)} %fusion.24), channel_id=1, source_target_pairs={{0,16},{16,0},{1,17},{17,1},{2,18},{18,2},{3,19},{19,3},{4,20},{20... | collective-permute-start | bytes 1867784 | tf_op jit(solution)/shard_map/ppermute | solution.py:56
  595.1 28.2 %all-to-all-start.6 = ((bf16[4,2,64,1408]{3,2,1,0:T(8,128)(2,1)}), bf16[4,2,64,1408]{3,2,1,0:T(8,128)(2,1)S(1)}, u32[]{:S(2)}, u32[]{:S(2)}) async-start(bf16[4,2,64,1408]{3,2,1,0:T(8,128)(2,1)} %bitcast.245), calls=%async_computation.7 | async-start | bytes 2883584 | tf_op jit(solution)/shard_map/all_to_all | solution.py:753
  604.2 16.2 %collective-permute-start.64 = (bf16[1,64,2432]{2,1,0:T(8,128)(2,1)S(1)}, bf16[1,64,2432]{2,1,0:T(8,128)(2,1)S(1)}, u32[]{:S(2)}, u32[]{:S(2)}) collective-permute-start(bf16[1,64,2432]{2,1,0:T(8,128)(2,1)S(1)} %fusion.30), channel_id=1, source_target_pairs={{0,8},{8,0},{1,9},{9,1},{2,10},{10,2},{3,11},{11,3},{4,12},{12,4},... | collective-permute-start | bytes 933896 | tf_op jit(solution)/shard_map/ppermute | solution.py:56
  (81 other events, 821.0 us)
Sparse Core Ops, SparseCore 0:
  357.2 137.4 reduce-scatter.1

commit v5 on v4

--- a/solution.py
+++ b/solution.py
@@ -57,9 +57,12 @@
 
 
 def swap_core(value):
+    return jnp.concatenate(core_parts(value))
+
+
+def core_parts(value):
     size = value.shape[0] // 4
-    parts = [value[i * size : (i + 1) * size] for i in range(4)]
-    return jnp.concatenate([swap(part, "c") for part in parts])
+    return [swap(value[i * size : (i + 1) * size], "c") for i in range(4)]
 
 
 def low(value):
@@ -132,61 +135,80 @@
         bias[i * block : (i + 1) * block, :] = jnp.where(fits, 0.0, NEGATIVE)
 
 
+def each_pair(one, count, keys):
+    def step(pair, unused):
+        one(pair * 2, pl.ds(pl.multiple_of(pair * 2 * HEAD_DIM, 2 * HEAD_DIM), 2 * HEAD_DIM))
+        return unused
+
+    if keys > 2048:
+        lax.fori_loop(0, count // 2, step, 0)
+    else:
+        for pair in range(count // 2):
+            step(pair, 0)
+
+
+def rows_of(head):
+    return pl.ds(pl.multiple_of(head * HEAD_DIM, HEAD_DIM), HEAD_DIM)
+
+
 def attend_kernel(
-    query_sum, key, value_t, cosine, sine_part, key_place, query_place, query_start,
-    query_rot, attended, attended_low, lse, bias,
+    normed, near, far_0, far_1, far_2, far_3, keyvalue, cosine, sine_part, key_place,
+    query_place, query_start, query_rot, attended, attended_low, lse, bias, value_t,
 ):
     fill_bias(bias, key_place, query_place, query_start)
-
-    def one(head, unused):
-        at = pl.ds(pl.multiple_of(head * HEAD_DIM, HEAD_DIM), HEAD_DIM)
-        query = turn(query_sum[at, :], cosine[...], sine_part[...]).astype(BF16)
-        query_rot[at, :] = query
-        scores = mxu(key[...], query, NN) * (SCALE * LOG2E) + bias[...]
-        top = jnp.max(scores, axis=0, keepdims=True)
-        weights = jnp.exp2(scores - top)
-        total = jnp.sum(weights, axis=0, keepdims=True)
-        result = mxu(value_t[...], weights.astype(BF16), NN) / total
-        attended[at, :] = result
-        attended_low[at, :] = result.astype(BF16)
-        lse[pl.ds(head, 1), :] = top + jnp.log2(total)
-        return unused
-
-    each_head(one, query_sum, key)
-
-
-def each_head(one, heads_ref, key):
-    count = heads_ref.shape[0] // HEAD_DIM
-    if key.shape[0] > 2048:
-        lax.fori_loop(0, count, one, 0)
-    else:
-        for head in range(count):
-            one(head, 0)
+    value_t[...] = keyvalue[:, HEAD_DIM:].T
+    parts = [(0, near)]
+    for part in (far_0, far_1, far_2, far_3):
+        parts.append((parts[-1][0] + parts[-1][1].shape[0], part))
+
+    def one(first, columns):
+        total = sum(
+            mxu(normed[:, at : at + part.shape[0]], part[:, columns], NN) for at, part in parts
+        )
+        turned = total.T
+        for i in range(2):
+            at = rows_of(first + i)
+            query = turn(
+                turned[i * HEAD_DIM : (i + 1) * HEAD_DIM], cosine[...], sine_part[...]
+            ).astype(BF16)
+            query_rot[at, :] = query
+            scores = mxu(keyvalue[:, :HEAD_DIM], query, NN) * (SCALE * LOG2E) + bias[...]
+            top = jnp.max(scores, axis=0, keepdims=True)
+            weights = jnp.exp2(scores - top)
+            total = jnp.sum(weights, axis=0, keepdims=True)
+            result = mxu(value_t[...], weights.astype(BF16), NN) / total
+            attended[at, :] = result
+            attended_low[at, :] = result.astype(BF16)
+            lse[pl.ds(first + i, 1), :] = top + jnp.log2(total)
+
+    each_pair(one, query_rot.shape[0] // HEAD_DIM, keyvalue.shape[0])
 
 
 def attend_back_kernel(
-    query_rot, key, key_t, value, grad, attended, lse, cosine, sine_part, key_place,
-    query_place, query_start, query_grad, kv_grad, bias,
+    query_rot, keyvalue, grad_hidden, output_weight, attended, lse, cosine, sine_part,
+    key_place, query_place, query_start, query_grad, kv_grad, bias, key_t,
 ):
     fill_bias(bias, key_place, query_place, query_start)
     kv_grad[...] = jnp.zeros_like(kv_grad)
-
-    def one(head, unused):
-        at = pl.ds(pl.multiple_of(head * HEAD_DIM, HEAD_DIM), HEAD_DIM)
-        query = query_rot[at, :]
-        grad_head = grad[at, :]
-        delta = jnp.sum(grad_head.astype(F32) * attended[at, :], axis=0, keepdims=True)
-        scores = mxu(key[...], query, NN) * (SCALE * LOG2E) + bias[...]
-        probs = jnp.exp2(scores - lse[pl.ds(head, 1), :])
-        grad_probs = mxu(value[...], grad_head, NN)
-        grad_scores = (probs * (grad_probs - delta)).astype(BF16)
-        kv_grad[:, :HEAD_DIM] += mxu(grad_scores, query, NT) * SCALE
-        kv_grad[:, HEAD_DIM:] += mxu(probs.astype(BF16), grad_head, NT)
-        grad_query = mxu(key_t[...], grad_scores, NN) * SCALE
-        query_grad[at, :] = turn(grad_query, cosine[...], -sine_part[...]).astype(BF16)
-        return unused
-
-    each_head(one, query_rot, key)
+    key_t[...] = keyvalue[:, :HEAD_DIM].T
+
+    def one(first, columns):
+        turned = mxu(grad_hidden[...], output_weight[:, columns], NN).T.astype(BF16)
+        for i in range(2):
+            at = rows_of(first + i)
+            query = query_rot[at, :]
+            grad_head = turned[i * HEAD_DIM : (i + 1) * HEAD_DIM]
+            delta = jnp.sum(grad_head.astype(F32) * attended[at, :], axis=0, keepdims=True)
+            scores = mxu(keyvalue[:, :HEAD_DIM], query, NN) * (SCALE * LOG2E) + bias[...]
+            probs = jnp.exp2(scores - lse[pl.ds(first + i, 1), :])
+            grad_probs = mxu(keyvalue[:, HEAD_DIM:], grad_head, NN)
+            grad_scores = (probs * (grad_probs - delta)).astype(BF16)
+            kv_grad[:, :HEAD_DIM] += mxu(grad_scores, query, NT) * SCALE
+            kv_grad[:, HEAD_DIM:] += mxu(probs.astype(BF16), grad_head, NT)
+            grad_query = mxu(key_t[...], grad_scores, NN) * SCALE
+            query_grad[at, :] = turn(grad_query, cosine[...], -sine_part[...]).astype(BF16)
+
+    each_pair(one, query_rot.shape[0] // HEAD_DIM, keyvalue.shape[0])
 
 
 def columns_of(width):
@@ -205,53 +227,44 @@
         body(pl.ds(full * 256, rest))
 
 
-def load_pieces(pieces, parts, held, sems):
-    waits = []
-    half = held.shape[2] // 2
-    for slot, matrix in enumerate(parts):
-        copies = []
-        for core in range(2):
-            for i, (p, first, count) in enumerate(
-                ((0, 0, 2), (1, 0, 1), (1, 1, 1), (2, 0, 1), (2, 1, 1), (3, 0, 1), (3, 1, 1))
-            ):
-                copies.append(
-                    pltpu.make_async_copy(
-                        pieces[core * 7 + i].at[:, matrix],
-                        held.at[slot, core * 4 + p, pl.ds(first * half, count * half)],
-                        sems.at[slot, core * 7 + i],
-                    )
-                )
+def load_pieces(pieces, held, slot, sems):
+    copies = [
+        pltpu.make_async_copy(piece, held.at[slot, p], sems.at[slot, p])
+        for p, piece in enumerate(pieces)
+    ]
+    for copy in copies:
+        copy.start()
+
+    def wait():
         for copy in copies:
-            copy.start()
-        waits.append(copies)
-
-    def wait(slot):
-        for copy in waits[slot]:
             copy.wait()
 
     return wait
 
 
-def feed_kernel(normed, grad, *refs):
-    pieces = refs[:14]
-    mixed, grad_gate, grad_up, grad_two, held, gate_sum, up_sum, sems = refs[14:]
-    wait = load_pieces(pieces, range(3), held, sems)
-    width, part = normed.shape[1], mixed.shape[1]
-
-    def block(slot, at):
-        return held[slot, :, :, :, at].reshape(width, at.size)
-
+def gate_up_kernel(normed, *refs):
+    gate_sum, up_sum, held, sems = refs[16:]
+    waits = [load_pieces(refs[8 * i : 8 * i + 8], held, i, sems) for i in range(2)]
+    width, part = normed.shape[1], gate_sum.shape[1]
     for slot, result in enumerate((gate_sum, up_sum)):
-        wait(slot)
+        waits[slot]()
 
         def step(at):
-            result[:, at] = mxu(normed[...], block(slot, at), NN)
+            result[:, at] = mxu(
+                normed[...], held[slot, :, :, :, at].reshape(width, at.size), NN
+            )
 
         each_block(part, step)
-    wait(2)
+
+
+def feed_kernel(grad, gate_sum, up_sum, *refs):
+    mixed, grad_gate, grad_up, grad_two, held, sems = refs[24:]
+    waits = [load_pieces(refs[8 * i : 8 * i + 8], held, i, sems) for i in range(3)]
+    width, part = grad.shape[1], mixed.shape[1]
+    waits[0]()
 
     def down_step(at):
-        grad_mixed = mxu(grad[...], block(2, at), NN)
+        grad_mixed = mxu(grad[...], held[0, :, :, :, at].reshape(width, at.size), NN)
         gate, up = gate_sum[:, at], up_sum[:, at]
         sigmoid_gate = jax.nn.sigmoid(gate)
         silu_gate = gate * sigmoid_gate
@@ -262,12 +275,14 @@
         ).astype(BF16)
 
     each_block(part, down_step)
+    waits[1]()
+    waits[2]()
 
     def two_step(p, unused):
         at = pl.ds(pl.multiple_of(p * (width // 8), width // 8), width // 8)
         grad_two[:, at] = (
-            mxu(grad_gate[...], held[0, p].reshape(width // 8, part), NT)
-            + mxu(grad_up[...], held[1, p].reshape(width // 8, part), NT)
+            mxu(grad_gate[...], held[1, p].reshape(width // 8, part), NT)
+            + mxu(grad_up[...], held[2, p].reshape(width // 8, part), NT)
         ).astype(BF16)
         return unused
 
@@ -308,10 +323,8 @@
 
 
 def feed_out_kernel(mixed, *refs):
-    pieces = refs[:14]
-    feed, held, sems = refs[14:]
-    wait = load_pieces(pieces, [2], held, sems)
-    wait(0)
+    feed, held, sems = refs[8:]
+    load_pieces(refs[:8], held, 0, sems)()
     width, part = feed.shape[1], mixed.shape[1]
 
     def feed_step(p, unused):
@@ -475,14 +488,14 @@
     query_part = gather_m(pair(query_part, query_l, l), 0)
     output_part = gather_m(pair(output_part, output_l, l), 0)
     small, query_part, feed_parts = sync(small, query_part, feed_parts)
+    query_h = swap(query_part, "h")
+    small_h = sync(swap(small, "h"))[0]
+    small, feed_parts = sync(jnp.stack([small, small_h]), feed_parts)
     feed = gather_m(lax.all_to_all(feed_parts, ("l", "x"), 0, 0), 0)
     feed = feed.reshape(M * 4, 3, rows, part)
-    query_h = swap(query_part, "h")
-    small_h = sync(swap(small, "h"))[0]
-    small = jnp.stack([small, small_h])
     small_y = sync(swap(small, "y"))[0]
-    small = jnp.stack([small, small_y])
-    small_c = sync(swap(small, "c"), input_other)[0]
+    small = jnp.stack([small, small_y]).reshape(4, M * 4, rows + 16, 2 * HEAD_DIM)
+    small_c, input_other, query_h = sync(swap_core(small), input_other, query_h)
     small = jnp.stack([small, small_c])
     small = small.reshape(width // rows, rows + 16, 2 * HEAD_DIM)
     keyvalue_full = small[:, :rows].reshape(width, 2 * HEAD_DIM)
@@ -505,39 +518,40 @@
             -1,
         )
     )
-    shared_h, feed, input_other, query_h = sync(
-        swap(shared_mine, "h"), feed, input_other, query_h
-    )
+    query_part, keyvalue_sum, key_position, query_place, query_start, cosine_t, sine_t = sync(
+        jnp.stack([query_part, query_h]),
+        keyvalue_sum,
+        key_position,
+        query_place,
+        query_start,
+        cosine.T,
+        sine_part.T,
+    )
+    query_y = swap(query_part, "y")
+    shared_h, input_other = sync(swap(shared_mine, "h"), input_other)
     gathered = gather_m(jnp.stack([shared_mine, shared_h]), 0)
     gathered, input_other, output_part = sync(gathered, input_other, output_part)
-    query_y = swap(jnp.stack([query_part, query_h]), "y")
     output_h = swap(output_part, "h")
     normed_one_low = jnp.concatenate([normed_mine_low, normalize(input_other)[3]])
-    shared_l, normed_one_low = sync(swap(gathered, "l"), normed_one_low)
-    gathered = jnp.stack([gathered, shared_l])
-    shared_x, output_h, query_y = sync(swap(gathered, "x"), output_h, query_y)
-    gathered = jnp.stack([gathered, shared_x])
-    query_part = jnp.stack([query_part, query_h])
+    shared_l, normed_one_low, feed = sync(swap(gathered, "l"), normed_one_low, feed)
+    gate, up, down, gathered = sync(
+        *(feed[:, i] for i in range(3)), jnp.stack([gathered, shared_l])
+    )
+    shared_x, query_y, output_h = sync(swap(gathered, "x"), query_y, output_h)
+    gathered = jnp.stack([gathered, shared_x]).reshape(4, -1, 2 * HEAD_DIM)
     query_part = jnp.stack([query_part, query_y]).reshape(-1, half_width)
     query_part, gathered = sync(query_part, gathered)
-    query_c = swap_core(query_part)
+    query_c = core_parts(query_part)
+    shared_c, *query_c = sync(swap_core(gathered), *query_c)
     output_part = jnp.stack([output_part, output_h])
-    output_part, gathered, feed = sync(output_part, gathered, feed)
+    output_part, gate, shared_c = sync(output_part, gate, shared_c)
     output_y = swap(output_part, "y")
-    quarters = [feed[i * M : (i + 1) * M] for i in range(4)]
-    middle = 2 * M
-    feed_h = [swap(quarters[0], "h")]
-    shared_c, query_c = sync(swap(gathered, "c"), query_c)
-    query_full = jnp.concatenate([query_part, query_c])
+    gate_h = swap(gate, "h")
+    gate_sent, query_place = sync(gate, query_place, *query_c)[:2]
+    gate_y = swap(gate_sent, "y")
     gathered = jnp.stack([gathered, shared_c]).reshape(-1, 2 * HEAD_DIM)
     stream_len = gathered.shape[0]
-    grad_mine, gathered = sync(inward(output_grad[0]), gathered)
-    grad_low = gather_group(grad_mine).reshape(-1, width)
-    key, value = gathered[:, :HEAD_DIM], gathered[:, HEAD_DIM:]
-    query_sum = lax.dot_general(
-        query_full, normed_one_low, (((0,), (1,)), ((), ())), preferred_element_type=F32
-    )
-    cosine_t, sine_t = cosine.T, sine_part.T
+    grad_mine = inward(output_grad[0])
     wide = (half_width, 2 * tokens)
     places_used = (key_position, query_place, query_start)
     query_rot, attended, attended_low, lse = local_call(
@@ -548,45 +562,65 @@
             jax.ShapeDtypeStruct(wide, BF16),
             jax.ShapeDtypeStruct((heads, 2 * tokens), F32),
         ],
-        [pltpu.VMEM((stream_len, 2 * tokens), F32)],
-        query_sum, key, value.T, cosine_t, sine_t, *places_used,
-    )
-    attended_low, output_y, output_part, feed_h[0] = sync(
-        attended_low, output_y, output_part, feed_h[0]
+        [
+            pltpu.VMEM((stream_len, 2 * tokens), F32),
+            pltpu.VMEM((HEAD_DIM, stream_len), BF16),
+        ],
+        normed_one_low, query_part, *query_c, gathered, cosine_t, sine_t, *places_used,
+    )
+    attended_low, output_y, output_part, gate_h, gate_y = sync(
+        attended_low, output_y, output_part, gate_h, gate_y
     )
     output_part = jnp.stack([output_part, output_y]).reshape(-1, half_width)
     output_c = swap_core(output_part)
-    sent, feed_sent = sync(quarters[1], feed[:middle], attended_low)[:2]
-    feed_h.append(swap(sent, "h"))
-    feed_y = [swap(feed_sent, "y")]
+    up_sent, attended_low = sync(up, attended_low)
+    up_h, up_y = swap(up_sent, "h"), swap(up_sent, "y")
     output_part, output_c, attended_low = sync(output_part, output_c, attended_low)
     output_full = jnp.concatenate([output_part, output_c])
     branch = lax.dot_general(
         attended_low, output_full, (((0,), (1,)), ((), ())), preferred_element_type=F32
     )
-    branch_x, feed_h[1], feed_y[0], grad_low = sync(
-        swap(low(branch[tokens:]), "x"), feed_h[1], feed_y[0], grad_low
+    branch, gate_h = sync(branch, gate_h)
+    gate_far = swap(gate_h, "y")
+    branch_x, up_h, up_y, gate_far, grad_mine = sync(
+        swap(low(branch[tokens:]), "x"), up_h, up_y, gate_far, grad_mine
     )
     hidden = inputs + (branch[:tokens] + branch_x.astype(F32))
 
-    feed_h = [jnp.concatenate(feed_h)]
-    sent2, sent3, feed_sent, branch_x = sync(quarters[2], quarters[3], feed[middle:], branch_x)
-    sent2, sent3 = swap(sent2, "h"), swap(sent3, "h")
-    feed_far = [swap(feed_h[0], "y")]
+    down_sent, branch_x = sync(down, branch_x)
+    down_h, up_far, down_y = swap(down_sent, "h"), swap(up_h, "y"), swap(down_sent, "y")
     scale_two = lax.rsqrt(jnp.mean(hidden * hidden, axis=-1, keepdims=True) + EPSILON)
     normed_two = hidden * scale_two
     normed_two_low = low(normed_two * gain_two)
     normed_two_low = gather_group(normed_two_low).reshape(-1, width)
-    normed_two_low, sent2, sent3, feed_far[0] = sync(normed_two_low, sent2, sent3, feed_far[0])
-    feed_h.append(jnp.concatenate([sent2, sent3]))
-    feed_far.append(swap(feed_h[1], "y"))
-    feed_y.append(swap(feed_sent, "y"))
-    early = [feed, *feed_h, feed_y[0], feed_far[0]]
-    early_c = [swap(piece, "c") for piece in early]
-    feed_y[1], feed_far[1], *early_c = sync(feed_y[1], feed_far[1], *early_c)
-    feed_all = [feed, *feed_h, *feed_y, *feed_far]
-    feed_all = feed_all + [*early_c[:4], swap(feed_y[1], "c"), early_c[4]]
-    feed_all = feed_all + [swap(feed_far[1], "c")]
+    up_far, *sent = sync(up_far, gate, gate_h, gate_y, gate_far, up, up_h, up_y)
+    near_c = [swap(piece, "c") for piece in sent]
+    normed_two_low, down_h, down_y, *near_c = sync(normed_two_low, down_h, down_y, *near_c)
+    down_far = swap(down_h, "y")
+    gate_c = near_c[:4]
+    up_sent, grad_sent = sync(up_far, grad_mine, normed_two_low)[:2]
+    late_c = [swap(up_sent, "c")]
+    up_c = near_c[4:] + late_c
+    grad_low = gather_group(grad_sent).reshape(-1, width)
+    gate_all = [gate, gate_h, gate_y, gate_far, *gate_c]
+    up_all = [up, up_h, up_y, up_far, *up_c]
+    group = 4 * tokens
+    units = jax.ShapeDtypeStruct((group, part), BF16)
+    unit_sums = jax.ShapeDtypeStruct((group, part), F32)
+    features = jax.ShapeDtypeStruct((group, width), BF16)
+
+    def held(count):
+        return [
+            pltpu.VMEM((count, 8, M * 4, rows, part), BF16),
+            pltpu.SemaphoreType.DMA((count, 8)),
+        ]
+
+    down_c = [swap(piece, "c") for piece in (down, down_h, down_y)]
+    gate_sum, up_sum = local_call(
+        gate_up_kernel, [unit_sums] * 2, held(2), normed_two_low, *gate_all, *up_all, far=16
+    )
+    down_far, gate_sum, *down_c = sync(down_far, gate_sum, *down_c)
+    down_all = [down, down_h, down_y, down_far, *down_c, swap(down_far, "c")]
     order = jnp.stack(
         [
             ((y ^ j) * 2 + (h ^ k)) * 2 + (c ^ i)
@@ -595,20 +629,12 @@
             for k in range(2)
         ]
     )
-    group = 4 * tokens
-    units = jax.ShapeDtypeStruct((group, part), BF16)
-    features = jax.ShapeDtypeStruct((group, width), BF16)
-
-    def held(count):
-        return pltpu.VMEM((count, 8, M * 4, rows, part), BF16)
-
-    wide_sum = pltpu.VMEM((group, part), F32)
     mixed_low, grad_gate, grad_up, grad_two = local_call(
         feed_kernel,
         [units, units, units, features],
-        [held(3), wide_sum, wide_sum, pltpu.SemaphoreType.DMA((3, 14))],
-        normed_two_low, grad_low, *feed_all,
-        far=14,
+        held(3),
+        grad_low, gate_sum, up_sum, *down_all, *gate_all, *up_all,
+        far=24,
     )
 
     half, block = width // 2, width // 8
@@ -629,14 +655,6 @@
     )
     mixed_low, down_far_half = sync(mixed_low, down_far_half)
     down_got = swap(down_far_half, "c")
-    feed_out = local_call(
-        feed_out_kernel,
-        [features],
-        [held(1), pltpu.SemaphoreType.DMA((1, 14))],
-        mixed_low, *feed_all,
-        far=14,
-    )[0]
-
     def quarter(i, *more):
         at = slice(i * block, (i + 1) * block)
         total = down_near[at].astype(F32) + down_got[at].astype(F32)
@@ -644,35 +662,37 @@
             total = total + other.astype(F32)
         return low(total)
 
-    grad_two, down_got, feed_out = sync(grad_two, down_got, feed_out)
+    grad_two, down_got = sync(grad_two, down_got)
     across = (((0,), (1,)), ((), ()))
     grad_hidden = grad_mine.astype(F32) + norm_back(grad_two * gain_two, normed_two, scale_two)
     grad_hidden_low, grad_two = sync(low(grad_hidden), grad_two)
     hidden_x = swap(grad_hidden_low, "x")
     down_y3, down_y2 = swap(quarter(3), "y"), swap(quarter(2), "y")
+    mixed_low = sync(mixed_low, grad_hidden_low)[0]
+    feed_out = local_call(
+        feed_out_kernel,
+        [features],
+        held(1),
+        mixed_low, *down_all,
+        far=8,
+    )[0]
     hidden_x, feed_out = sync(hidden_x, feed_out)
     feed_out = scatter_group(feed_out.reshape(4, tokens, width))
     grad_hidden_low = jnp.concatenate([grad_hidden_low, hidden_x])
-    output_term = low(
-        lax.dot_general(grad_hidden_low, attended_low, across, preferred_element_type=F32)
-    )
-    output_got = swap(output_term[half:], "c")
-    grad_heads = low(
-        lax.dot_general(
-            output_full, grad_hidden_low, (((0,), (1,)), ((), ())), preferred_element_type=F32
-        )
-    )
-    grad_heads, output_got, output_term = sync(grad_heads, output_got, output_term)
     query_grad_low, kv_grad = local_call(
         attend_back_kernel,
         [
             jax.ShapeDtypeStruct(wide, BF16),
             jax.ShapeDtypeStruct((stream_len, 2 * HEAD_DIM), F32),
         ],
-        [pltpu.VMEM((stream_len, 2 * tokens), F32)],
-        query_rot, key, key.T, value, grad_heads, attended, lse, cosine_t, sine_t, *places_used,
-    )
-    query_grad_low, kv_grad, down_y3 = sync(query_grad_low, kv_grad, down_y3)
+        [
+            pltpu.VMEM((stream_len, 2 * tokens), F32),
+            pltpu.VMEM((HEAD_DIM, stream_len), BF16),
+        ],
+        query_rot, gathered, grad_hidden_low, output_full, attended, lse, cosine_t, sine_t,
+        *places_used,
+    )
+    query_grad_low, kv_grad, grad_hidden_low = sync(query_grad_low, kv_grad, grad_hidden_low)
 
     def fold_l(total):
         total = total.reshape(2, 2, M, 2, 2, rows, -1)
@@ -692,16 +712,25 @@
         return total[0], swap(low(total[1]), axis)
 
     kv_half = kv_grad.shape[0] // 2
-    kv_sent = low(kv_grad[kv_half:])
-    kv_got, feed_out, query_grad_low = sync(swap(kv_sent, "c"), feed_out, query_grad_low)
-    kv_grad = (kv_grad[:kv_half] + kv_got.astype(F32)).reshape(4, M, 2, tokens, 2 * HEAD_DIM)
+    kv_sent = low(kv_grad[kv_half:]).reshape(4, -1, 2 * HEAD_DIM)
+    output_term = low(
+        lax.dot_general(grad_hidden_low, attended_low, across, preferred_element_type=F32)
+    )
+    kv_got, query_grad_low, output_term, feed_out, down_y3 = sync(
+        swap_core(kv_sent), query_grad_low, output_term, feed_out, down_y3
+    )
+    output_got = swap_core(output_term[half:])
+    kv_grad = kv_grad[:kv_half].reshape(4, M, 2, tokens, 2 * HEAD_DIM)
+    kv_grad = kv_grad + kv_got.astype(F32).reshape(kv_grad.shape)
     kv_got = swap(low(kv_grad[2:]), "x")
     query_term = low(
         lax.dot_general(normed_one_low, query_grad_low, across, preferred_element_type=F32)
     )
-    kv_got, query_term = sync(kv_got, query_term)
+    down_h1 = swap(quarter(1, down_y3), "h")
+    kv_got, query_term, output_got = sync(kv_got, query_term, output_got)
     kv_grad = kv_grad[:2] + kv_got.astype(F32)
     kv_got = swap(low(kv_grad[1]), "l")
+    query_full = jnp.concatenate([query_part, *query_c])
     grad_one = lax.dot_general(
         query_grad_low, query_full, (((0,), (1,)), ((), ())), preferred_element_type=F32
     )
@@ -712,7 +741,6 @@
     )
     kv_grad = kv_grad[0] + kv_got.astype(F32)
     kv_got, grad_one_x = sync(swap(low(kv_grad[:, 1]), "h"), grad_one_x)
-    down_h1 = swap(quarter(1, down_y3), "h")
     kv_mine = scatter_m(kv_grad[:, 0] + kv_got.astype(F32), 0) + shared_grad[0].astype(F32)
     keyvalue_grad_low = low(
         jnp.concatenate(
@@ -747,7 +775,6 @@
     query_got, output_got, down_h1, both_grad = sync(query_got, output_got, down_h1, both_grad)
     query_total, query_got = next_fold(take_x(query_total, query_got), "y")
     output_weight_grad = scatter_m(output_total + output_got.astype(F32), 0)
-
     def finish_feed(own):
         own = low(scatter_m(own, 0))
         got = lax.all_to_all(own, ("l", "x"), 0, 0)

time: 649 us -> 621 us (0.957)
  local copies, waits for them, and re-layouts: 85.5 us -> 67.9 us
  starting transfers between devices: 92.4 us -> 109 us
  other arithmetic: 80.3 us -> 64.2 us
  Pallas kernels: 104 us -> 116 us
  waiting for transfers between devices: 242 us -> 231 us
  matrix products: 18.8 us -> 10.6 us
    ppermute x65 -> x83, waiting for transfers between devices: 241 us -> 222 us  [swap(): return lax.ppermute(value, axis, [(0, 1), (1, 0)])]
    all_to_all x1, starting transfers between devices: 3.63 us -> 17 us  [on_device(): feed = gather_m(lax.all_to_all(feed_parts, ('l', 'x'), 0, 0), 0)]
    pallas_call x6 -> x7, Pallas kernels: 89.5 us -> 102 us  [local_call(): pl.pallas_call(kernel, out_shape=outs, in_specs=near + [pl.BlockSpec(memo...]
    dot_general x2 -> x0, matrix products: 8.81 us -> none  [the longest x1 4.48 us: on_device(): lax.dot_general(query_full, normed_one_low, (((0,), (1,)), ((), ())), pre...]
    slice x9 -> x8, local copies, waits for them, and re-layouts: 10.4 us -> 2.35 us  [the longest x7 2.28 us: core_parts(): return [swap(value[i * size:(i + 1) * size], 'c') for i in range(4)]]
    ppermute x65 -> x83, starting transfers between devices: 60.5 us -> 65.2 us  [swap(): return lax.ppermute(value, axis, [(0, 1), (1, 0)])]
    unnamed x157 -> x206, local copies, waits for them, and re-layouts: 26.7 us -> 23.8 us
  transfers between devices with their start and end apart: 73 -> 91, of which waited for: 32 -> 35; matrix products, arithmetic and copies ran while one was open for 23% -> 17% of each run, Pallas kernels for 11% -> 14%
where the time goes in v5:
time: 621 us; the launch traced here: 614 us
  waiting for transfers between devices  231 us (37%)
  Pallas kernels  116 us (19%)
  starting transfers between devices  109 us (18%)
  local copies, waits for them, and re-layouts  67.9 us (11%)
  other arithmetic  64.2 us (10%)
  between operations  16.4 us (3%)
  matrix products  10.6 us (2%)
    ppermute x83, waiting for transfers between devices, swap(): return lax.ppermute(value, axis, [(0, 1), (1, 0)])  222 us
    pallas_call x7, Pallas kernels, local_call(): pl.pallas_call(kernel, out_shape=outs, in_specs=near + [pl.BlockSpec(memo...  102 us
    ppermute x83, starting transfers between devices, swap(): return lax.ppermute(value, axis, [(0, 1), (1, 0)])  65.2 us
    unnamed x206, local copies, waits for them, and re-layouts  23.8 us
    all_to_all x1, starting transfers between devices, on_device(): feed = gather_m(lax.all_to_all(feed_parts, ('l', 'x'), 0, 0), 0)  17 us
  transfers between devices with their start and end apart: 91, of which 35 were waited for; matrix products, arithmetic and copies ran while one was open for 17% of the time, Pallas kernels for 14%

profile of v5, /device:TPU:0, one launch (start us, length us, event | category | flops | bytes accessed | tf_op | source)
XLA Modules:
  0.0 613.8 jit_solution(14663717781863158512)
XLA Ops:
  8.7 2.9 collective-permute-start
  28.1 3.8 shard_map.212
  32.0 6.4 %collective-permute-done.3 = bf16[2,80,256]{2,1,0:T(8,128)(2,1)S(1)} collective-permute-done((bf16[2,80,256]{2,1,0:T(8,128)(2,1)S(1)}, bf16[2,80,256]{2,1,0:T(8,128)(2,1)S(1)}, u32[]{:S(2)}, u32[]{:S(2)}) %collective-permute-start.3) | collective-permute-done | bytes 81952 | tf_op jit(solution)/shard_map/ppermute | solution.py:56
  39.2 2.8 collective-permute-start.7
  43.0 4.9 collective-permute-done.7
  50.2 17.0 %all-to-all-start = ((bf16[4,3,64,1408]{3,2,1,0:T(8,128)(2,1)}), bf16[4,3,64,1408]{3,2,1,0:T(8,128)(2,1)}, u32[]{:S(2)}, u32[]{:S(2)}) async-start(bf16[4,3,64,1408]{3,2,1,0:T(8,128)(2,1)} %shard_map.212), calls=%async_computation | async-start | bytes 4325376 | tf_op jit(solution)/shard_map/all_to_all | solution.py:494
  74.5 10.8 %collective-permute-done.14 = bf16[128,256]{1,0:T(8,128)(2,1)S(1)} collective-permute-done((bf16[128,256]{1,0:T(8,128)(2,1)S(1)}, bf16[128,256]{1,0:T(8,128)(2,1)S(1)}, u32[]{:S(2)}, u32[]{:S(2)}) %collective-permute-start.14) | collective-permute-done | bytes 65568 | tf_op jit(solution)/shard_map/ppermute | solution.py:56
  85.3 9.9 %collective-permute-start.15 = (bf16[1,2,128,256]{3,2,1,0:T(8,128)(2,1)S(1)}, bf16[1,2,128,256]{3,2,1,0:T(8,128)(2,1)S(1)}, u32[]{:S(2)}, u32[]{:S(2)}) collective-permute-start(bf16[1,2,128,256]{3,2,1,0:T(8,128)(2,1)S(1)} %maximum_bitcast_fusion), channel_id=1, source_target_pairs={{0,4},{4,0},{1,5},{5,1},{2,6},{6,2},{3,7},{7,3},{8,12},{12,8},{9,1... | collective-permute-start | bytes 393224 | tf_op jit(solution)/shard_map/ppermute | solution.py:56
  98.9 2.6 slice_bitcast_fusion.5
  104.1 8.1 %collective-permute-done.18 = bf16[1,2,2,64,1024]{4,3,2,1,0:T(8,128)(2,1)} collective-permute-done((bf16[1,2,2,64,1024]{4,3,2,1,0:T(8,128)(2,1)}, bf16[1,2,2,64,1024]{4,3,2,1,0:T(8,128)(2,1)}, u32[]{:S(2)}, u32[]{:S(2)}) %collective-permute-start.18) | collective-permute-done | bytes 524320 | tf_op jit(solution)/shard_map/ppermute | solution.py:56
  116.0 3.2 collective-permute-done.21
  119.4 2.3 pad_maximum_fusion.9
  128.3 15.9 %shard_map.213 = (bf16[1024,256]{1,0:T(8,128)(2,1)}, f32[1024,256]{1,0:T(8,128)}, bf16[1024,256]{1,0:T(8,128)(2,1)}, f32[8,256]{1,0:T(8,128)}) custom-call(bf16[256,2048]{1,0:T(8,128)(2,1)} %pad_maximum_fusion.7.normed, bf16[1024,1024]{1,0:T(8,128)(2,1)} %bitcast.255, bf16[256,1024]{1,0:T(8,128)(2,1)} %copy-done.55, bf16[256,1024]{1,0:T(8,128)(2,1)} %copy-done.53, ...), custom_call_target="tpu_custom_call" | custom-call | flops 1 | bytes 1 | tf_op jit(solution)/shard_map/pallas_call | solution.py:381
  144.1 19.6 %collective-permute-done.29.refs_2_.refs_10_ = bf16[4,64,1408]{2,1,0:T(8,128)(2,1)S(1)} collective-permute-done((bf16[4,64,1408]{2,1,0:T(8,128)(2,1)S(1)}, bf16[4,64,1408]{2,1,0:T(8,128)(2,1)S(1)}, u32[]{:S(2)}, u32[]{:S(2)}) %collective-permute-start.29) | collective-permute-done | bytes 720928 | tf_op jit(solution)/shard_map/ppermute | solution.py:56
  178.0 8.1 %collective-permute-done.36.refs_10_.refs_18_ = bf16[4,64,1408]{2,1,0:T(8,128)(2,1)S(1)} collective-permute-done((bf16[4,64,1408]{2,1,0:T(8,128)(2,1)S(1)}, bf16[4,64,1408]{2,1,0:T(8,128)(2,1)S(1)}, u32[]{:S(2)}, u32[]{:S(2)}) %collective-permute-start.36) | collective-permute-done | bytes 720928 | tf_op jit(solution)/shard_map/ppermute | solution.py:56
  186.1 14.1 %collective-permute-done.35.refs_9_.refs_17_ = bf16[4,64,1408]{2,1,0:T(8,128)(2,1)S(1)} collective-permute-done((bf16[4,64,1408]{2,1,0:T(8,128)(2,1)S(1)}, bf16[4,64,1408]{2,1,0:T(8,128)(2,1)S(1)}, u32[]{:S(2)}, u32[]{:S(2)}) %collective-permute-start.35) | collective-permute-done | bytes 720928 | tf_op jit(solution)/shard_map/ppermute | solution.py:56
  204.3 3.6 all-to-all-start.1
  211.9 15.3 %collective-permute-done.38.refs_11_.refs_19_ = bf16[4,64,1408]{2,1,0:T(8,128)(2,1)S(1)} collective-permute-done((bf16[4,64,1408]{2,1,0:T(8,128)(2,1)}, bf16[4,64,1408]{2,1,0:T(8,128)(2,1)S(1)}, u32[]{:S(2)}, u32[]{:S(2)}) %collective-permute-start.38) | collective-permute-done | bytes 720928 | tf_op jit(solution)/shard_map/ppermute | solution.py:56
  227.7 13.6 %collective-permute-done.40.refs_2_ = bf16[4,64,1408]{2,1,0:T(8,128)(2,1)S(1)} collective-permute-done((bf16[4,64,1408]{2,1,0:T(8,128)(2,1)}, bf16[4,64,1408]{2,1,0:T(8,128)(2,1)S(1)}, u32[]{:S(2)}, u32[]{:S(2)}) %collective-permute-start.40) | collective-permute-done | bytes 720928 | tf_op jit(solution)/shard_map/ppermute | solution.py:56
  241.3 4.9 collective-permute-done.39.refs_1_
  251.7 2.4 copy.166
  254.1 2.7 broadcast_in_dim.22
  256.7 5.8 all-to-all-start.2
  266.0 14.5 %shard_map.214 = (f32[512,1408]{1,0:T(8,128)}, f32[512,1408]{1,0:T(8,128)}) custom-call(bf16[512,2048]{1,0:T(8,128)(2,1)} %bitcast.261, bf16[4,64,1408]{2,1,0:T(8,128)(2,1)} %copy-done.24, bf16[4,64,1408]{2,1,0:T(8,128)(2,1)} %collective-permute-done.28.refs_1_.refs_9_, bf16[4,64,1408]{2,1,0:T(8,128)(2,1)} %copy-done.38, ...), custom_call_target="tpu_custom_call" | custom-call | flops 1 | bytes 1 | tf_op jit(solution)/shard_map/pallas_call | solution.py:381
  284.1 3.6 all-to-all-done.2
  288.9 20.7 %shard_map.215 = (bf16[512,1408]{1,0:T(8,128)(2,1)}, bf16[512,1408]{1,0:T(8,128)(2,1)}, bf16[512,1408]{1,0:T(8,128)(2,1)}, bf16[512,2048]{1,0:T(8,128)(2,1)}) custom-call(bf16[512,2048]{1,0:T(8,128)(2,1)} %bitcast.259, f32[512,1408]{1,0:T(8,128)} %get-tuple-element.254.gate_sum, f32[512,1408]{1,0:T(8,128)} %get-tuple-element.255.up_sum, ...), custom_call_target="tpu_custom_call" | custom-call | flops 1 | bytes 1 | tf_op jit(solution)/shard_map/pallas_call | solution.py:381
  309.7 3.6 all-to-all-start.3
  314.0 14.8 %shard_map.216 = bf16[8,2,256,1408]{3,2,1,0:T(8,128)(2,1)} custom-call(s32[8]{0:T(128)} %stack.417.order, bf16[512,2048]{1,0:T(8,128)(2,1)} %bitcast.262, bf16[512,1408]{1,0:T(8,128)(2,1)} %get-tuple-element.262.refs_0_, bf16[512,1408]{1,0:T(8,128)(2,1)} %get-tuple-element.263.refs_1_), custom_call_target="tpu_custom_call" | custom-call | flops 1 | bytes 1 | tf_op jit(solution)/shard_map/pallas_call | solution.py:381
  328.8 8.2 %shard_map.217 = (bf16[1024,1408]{1,0:T(8,128)(2,1)}, bf16[1024,1408]{1,0:T(8,128)(2,1)}) custom-call(bf16[512,2048]{1,0:T(8,128)(2,1)} %bitcast.260, bf16[512,1408]{1,0:T(8,128)(2,1)} %get-tuple-element.270.refs_0_.mixed), custom_call_target="tpu_custom_call" | custom-call | flops 1 | bytes 1 | tf_op jit(solution)/shard_map/pallas_call | solution.py:381
  339.5 3.2 collective-permute-done.54
  345.4 10.3 %shard_map.218 = bf16[512,2048]{1,0:T(8,128)(2,1)} custom-call(bf16[512,1408]{1,0:T(8,128)(2,1)} %get-tuple-element.270.refs_0_.mixed, bf16[4,64,1408]{2,1,0:T(8,128)(2,1)} %get-tuple-element.233.refs_0_, bf16[4,64,1408]{2,1,0:T(8,128)(2,1)} %copy-done.32, bf16[4,64,1408]{2,1,0:T(8,128)(2,1)} %copy-done.31, bf16[4,64,1408]{2,1,0:T(8,128)(2,1)} %copy-done.36, ...), custom_call_target="tpu_custom_call" | custom-call | flops 1 | bytes 1 | tf_op jit(solution)/shard_map/pallas_call | solution.py:381
  358.3 5.1 all-to-all-start.4
  366.5 3.5 add_convert_fusion.3
  372.6 17.3 %shard_map.219 = (bf16[1024,256]{1,0:T(8,128)(2,1)}, f32[2048,256]{1,0:T(8,128)}) custom-call(bf16[1024,256]{1,0:T(8,128)(2,1)} %get-tuple-element.225.query_rot, bf16[2048,256]{1,0:T(8,128)(2,1)} %bitcast.272, bf16[256,2048]{1,0:T(8,128)(2,1)} %copy-done.16, bf16[2048,1024]{1,0:T(8,128)(2,1)} %copy-done.18, f32[1024,256]{1,0:T(8,128)} %get-tuple-element.272.attended, ...), custom_call_target="tpu_custom_call" | custom-call | flops 1 | bytes 1 | tf_op jit(solution)/shard_map/pallas_call | solution.py:381
  393.0 3.3 convolution_convert_fusion.1
  396.5 4.9 all-to-all-done.4
  401.5 2.3 convert_reduce_fusion
  408.3 3.4 convolution_convert_fusion
  412.0 2.5 collective-permute-start.66
  415.5 7.4 %collective-permute-done.66 = bf16[1,2,128,256]{3,2,1,0:T(8,128)(2,1)S(1)} collective-permute-done((bf16[1,2,128,256]{3,2,1,0:T(8,128)(2,1)S(1)}, bf16[1,2,128,256]{3,2,1,0:T(8,128)(2,1)S(1)}, u32[]{:S(2)}, u32[]{:S(2)}) %collective-permute-start.66) | collective-permute-done | bytes 131104 | tf_op jit(solution)/shard_map/ppermute | solution.py:56
  425.1 2.5 collective-permute-start.73
  427.6 3.3 collective-permute-done.67
  430.9 5.6 collective-permute-done.68
  441.0 3.4 fusion.1
  446.1 2.6 copy-done.5
  449.7 2.9 add_convert_fusion.1
  455.3 2.4 pad_maximum_fusion.1
  457.8 6.9 %collective-permute-done.73 = bf16[2,2,1,2,64,1024]{5,4,1,0,3,2:T(8,128)(2,1)} collective-permute-done((bf16[2,2,1,2,64,1024]{5,4,1,0,3,2:T(8,128)(2,1)}, bf16[2,2,1,2,64,1024]{5,4,1,0,3,2:T(8,128)(2,1)}, u32[]{:S(2)}, u32[]{:S(2)}) %collective-permute-start.73) | collective-permute-done | bytes 1048608 | tf_op jit(solution)/shard_map/ppermute | solution.py:56
  469.4 2.5 copy-done.10
  479.0 2.2 collective-permute-done.75
  483.9 2.2 convert_element_type.356
  489.1 10.1 %collective-permute-done.77 = bf16[2,1,64,2048]{3,2,0,1:T(8,128)(2,1)} collective-permute-done((bf16[2,1,64,2048]{3,2,0,1:T(8,128)(2,1)}, bf16[2,1,64,2048]{3,2,0,1:T(8,128)(2,1)}, u32[]{:S(2)}, u32[]{:S(2)}) %collective-permute-start.77) | collective-permute-done | bytes 524320 | tf_op jit(solution)/shard_map/ppermute | solution.py:56
  499.3 35.4 %collective-permute-done.74 = bf16[2,2,1,2,64,1408]{5,4,1,0,3,2:T(8,128)(2,1)} collective-permute-done((bf16[2,2,1,2,64,1408]{5,4,1,0,3,2:T(8,128)(2,1)}, bf16[2,2,1,2,64,1408]{5,4,1,0,3,2:T(8,128)(2,1)}, u32[]{:S(2)}, u32[]{:S(2)}) %collective-permute-start.74) | collective-permute-done | bytes 1441824 | tf_op jit(solution)/shard_map/ppermute | solution.py:56
  534.7 2.5 bitcast_add_fusion
  540.9 11.1 %collective-permute-done.79 = bf16[1,64,2048]{2,1,0:T(8,128)(2,1)} collective-permute-done((bf16[1,64,2048]{2,1,0:T(8,128)(2,1)S(1)}, bf16[1,64,2048]{2,1,0:T(8,128)(2,1)}, u32[]{:S(2)}, u32[]{:S(2)}) %collective-permute-start.79) | collective-permute-done | bytes 262176 | tf_op jit(solution)/shard_map/ppermute | solution.py:56
  555.6 3.1 add_convert_fusion
  558.6 4.2 all-to-all-start.5
  565.2 2.5 copy.193
  567.7 2.6 copy.223
  572.0 4.1 all-to-all-start.6
  576.1 3.4 shard_map.220
  584.2 12.1 %collective-permute-done.82 = bf16[1,64,2432]{2,1,0:T(8,128)(2,1)S(1)} collective-permute-done((bf16[1,64,2432]{2,1,0:T(8,128)(2,1)S(1)}, bf16[1,64,2432]{2,1,0:T(8,128)(2,1)S(1)}, u32[]{:S(2)}, u32[]{:S(2)}) %collective-permute-start.82) | collective-permute-done | bytes 311328 | tf_op jit(solution)/shard_map/ppermute | solution.py:56
  599.7 3.4 shard_map.222
  603.1 3.4 shard_map.221
  (520 shorter events, 153.7 us)
Async XLA Ops:
  8.7 14.6 %collective-permute-start = (bf16[80,256]{1,0:T(8,128)(2,1)S(1)}, bf16[80,256]{1,0:T(8,128)(2,1)S(1)}, u32[]{:S(2)}, u32[]{:S(2)}) collective-permute-start(bf16[80,256]{1,0:T(8,128)(2,1)S(1)} %get-tuple-element.413), channel_id=1, source_target_pairs={{0,2},{2,0},{1,3},{3,1},{4,6},{6,4},{5,7},{7,5},{8,10},{10,8},{9,1... | collective-permute-start | bytes 122888 | tf_op jit(solution)/shard_map/ppermute | solution.py:56
  15.1 8.2 %collective-permute-start.1 = (bf16[64,1024]{1,0:T(8,128)(2,1)S(1)}, bf16[64,1024]{1,0:T(8,128)(2,1)S(1)}, u32[]{:S(2)}, u32[]{:S(2)}) collective-permute-start(bf16[64,1024]{1,0:T(8,128)(2,1)S(1)} %bitcast.326), channel_id=1, source_target_pairs={{0,2},{2,0},{1,3},{3,1},{4,6},{6,4},{5,7},{7,5},{8,10},{10,8},{9,1... | collective-permute-start | bytes 393224 | tf_op jit(solution)/shard_map/ppermute | solution.py:56
  15.2 8.1 %collective-permute-start.2 = (bf16[64,1024]{1,0:T(8,128)(2,1)S(1)}, bf16[64,1024]{1,0:T(8,128)(2,1)S(1)}, u32[]{:S(2)}, u32[]{:S(2)}) collective-permute-start(bf16[64,1024]{1,0:T(8,128)(2,1)S(1)} %bitcast.327), channel_id=1, source_target_pairs={{0,2},{2,0},{1,3},{3,1},{4,6},{6,4},{5,7},{7,5},{8,10},{10,8},{9,1... | collective-permute-start | bytes 393224 | tf_op jit(solution)/shard_map/ppermute | solution.py:56
  23.6 14.8 %collective-permute-start.6 = (bf16[128,2048]{1,0:T(8,128)(2,1)S(1)}, bf16[128,2048]{1,0:T(8,128)(2,1)S(1)}, u32[]{:S(2)}, u32[]{:S(2)}) collective-permute-start(bf16[128,2048]{1,0:T(8,128)(2,1)S(1)} %copy.155), channel_id=1, source_target_pairs={{0,2},{2,0},{1,3},{3,1},{4,6},{6,4},{5,7},{7,5},{8,10},{10,8},{9,1... | collective-permute-start | bytes 1572872 | tf_op jit(solution)/shard_map/ppermute | solution.py:56
  23.7 14.7 %collective-permute-start.4 = (bf16[2,64,1024]{2,1,0:T(8,128)(2,1)S(1)}, bf16[2,64,1024]{2,1,0:T(8,128)(2,1)S(1)}, u32[]{:S(2)}, u32[]{:S(2)}) collective-permute-start(bf16[2,64,1024]{2,1,0:T(8,128)(2,1)S(1)} %maximum_select_fusion.4), channel_id=1, source_target_pairs={{0,4},{4,0},{1,5},{5,1},{2,6},{6,2},{3,7},{7,3},{8,12},{12,8},{9,1... | collective-permute-start | bytes 786440 | tf_op jit(solution)/shard_map/ppermute | solution.py:56
  25.9 12.5 %collective-permute-start.5 = (bf16[2,64,1024]{2,1,0:T(8,128)(2,1)S(1)}, bf16[2,64,1024]{2,1,0:T(8,128)(2,1)S(1)}, u32[]{:S(2)}, u32[]{:S(2)}) collective-permute-start(bf16[2,64,1024]{2,1,0:T(8,128)(2,1)S(1)} %maximum_select_fusion.5), channel_id=1, source_target_pairs={{0,4},{4,0},{1,5},{5,1},{2,6},{6,2},{3,7},{7,3},{8,12},{12,8},{9,1... | collective-permute-start | bytes 786440 | tf_op jit(solution)/shard_map/ppermute | solution.py:56
  26.1 12.3 %collective-permute-start.3 = (bf16[2,80,256]{2,1,0:T(8,128)(2,1)S(1)}, bf16[2,80,256]{2,1,0:T(8,128)(2,1)S(1)}, u32[]{:S(2)}, u32[]{:S(2)}) collective-permute-start(bf16[2,80,256]{2,1,0:T(8,128)(2,1)S(1)} %maximum_select_fusion.9), channel_id=1, source_target_pairs={{0,4},{4,0},{1,5},{5,1},{2,6},{6,2},{3,7},{7,3},{8,12},{12,8},{9,1... | collective-permute-start | bytes 245768 | tf_op jit(solution)/shard_map/ppermute | solution.py:56
  39.2 8.6 %collective-permute-start.7 = (bf16[1,2,2,80,256]{4,3,2,1,0:T(8,128)(2,1)S(1)}, bf16[1,2,2,80,256]{4,3,2,1,0:T(8,128)(2,1)S(1)}, u32[]{:S(2)}, u32[]{:S(2)}) collective-permute-start(bf16[1,2,2,80,256]{4,3,2,1,0:T(8,128)(2,1)S(1)} %maximum_select_fusion.8), channel_id=1, source_target_pairs={{0,8},{8,0},{1,9},{9,1},{2,10},{10,2},{3,11},{11,3},{4,12},{12,4},... | collective-permute-start | bytes 491528 | tf_op jit(solution)/shard_map/ppermute | solution.py:56
  47.9 19.4 %collective-permute-start.8 = (bf16[2,1,2,2,80,256]{5,4,3,2,1,0:T(8,128)(2,1)S(1)}, bf16[2,1,2,2,80,256]{5,4,3,2,1,0:T(8,128)(2,1)S(1)}, u32[]{:S(2)}, u32[]{:S(2)}) collective-permute-start(bf16[2,1,2,2,80,256]{5,4,3,2,1,0:T(8,128)(2,1)S(1)} %pad_maximum_fusion.16), channel_id=1, source_target_pairs={{0,16},{16,0},{1,17},{17,1},{2,18},{18,2},{3,19},{19,3},{4,20},{20... | collective-permute-start | bytes 983048 | tf_op jit(solution)/shard_map/ppermute | solution.py:56
  49.6 20.1 %collective-permute-start.13 = (bf16[1,2,2,64,1024]{4,3,2,1,0:T(8,128)(2,1)S(1)}, bf16[1,2,2,64,1024]{4,3,2,1,0:T(8,128)(2,1)S(1)}, u32[]{:S(2)}, u32[]{:S(2)}) collective-permute-start(bf16[1,2,2,64,1024]{4,3,2,1,0:T(8,128)(2,1)S(1)} %maximum_select_fusion.2), channel_id=1, source_target_pairs={{0,8},{8,0},{1,9},{9,1},{2,10},{10,2},{3,11},{11,3},{4,12},{12,4},... | collective-permute-start | bytes 1572872 | tf_op jit(solution)/shard_map/ppermute | solution.py:56
  50.2 48.6 %all-to-all-start = ((bf16[4,3,64,1408]{3,2,1,0:T(8,128)(2,1)}), bf16[4,3,64,1408]{3,2,1,0:T(8,128)(2,1)}, u32[]{:S(2)}, u32[]{:S(2)}) async-start(bf16[4,3,64,1408]{3,2,1,0:T(8,128)(2,1)} %shard_map.212), calls=%async_computation | async-start | bytes 4325376 | tf_op jit(solution)/shard_map/all_to_all | solution.py:494
  72.3 13.0 %collective-permute-start.14 = (bf16[128,256]{1,0:T(8,128)(2,1)S(1)}, bf16[128,256]{1,0:T(8,128)(2,1)S(1)}, u32[]{:S(2)}, u32[]{:S(2)}) collective-permute-start(bf16[128,256]{1,0:T(8,128)(2,1)S(1)} %pad_maximum_fusion.19), channel_id=1, source_target_pairs={{0,8},{8,0},{1,9},{9,1},{2,10},{10,2},{3,11},{11,3},{4,12},{12,4},... | collective-permute-start | bytes 196616 | tf_op jit(solution)/shard_map/ppermute | solution.py:56
  73.5 38.7 %collective-permute-start.17 = (bf16[2,1,2,2,64,1024]{5,4,3,2,1,0:T(8,128)(2,1)S(1)}, bf16[2,1,2,2,64,1024]{5,4,3,2,1,0:T(8,128)(2,1)}, u32[]{:S(2)}, u32[]{:S(2)}) collective-permute-start(bf16[2,1,2,2,64,1024]{5,4,3,2,1,0:T(8,128)(2,1)S(1)} %pad_maximum_fusion.8), channel_id=1, source_target_pairs={{0,16},{16,0},{1,17},{17,1},{2,18},{18,2},{3,19},{19,3},{4,20},{20... | collective-permute-start | bytes 3145736 | tf_op jit(solution)/shard_map/ppermute | solution.py:56
  85.3 13.5 %collective-permute-start.15 = (bf16[1,2,128,256]{3,2,1,0:T(8,128)(2,1)S(1)}, bf16[1,2,128,256]{3,2,1,0:T(8,128)(2,1)S(1)}, u32[]{:S(2)}, u32[]{:S(2)}) collective-permute-start(bf16[1,2,128,256]{3,2,1,0:T(8,128)(2,1)S(1)} %maximum_bitcast_fusion), channel_id=1, source_target_pairs={{0,4},{4,0},{1,5},{5,1},{2,6},{6,2},{3,7},{7,3},{8,12},{12,8},{9,1... | collective-permute-start | bytes 393224 | tf_op jit(solution)/shard_map/ppermute | solution.py:56
  96.7 15.5 %collective-permute-start.18 = (bf16[1,2,2,64,1024]{4,3,2,1,0:T(8,128)(2,1)}, bf16[1,2,2,64,1024]{4,3,2,1,0:T(8,128)(2,1)}, u32[]{:S(2)}, u32[]{:S(2)}) collective-permute-start(bf16[1,2,2,64,1024]{4,3,2,1,0:T(8,128)(2,1)} %maximum_select_fusion.3), channel_id=1, source_target_pairs={{0,8},{8,0},{1,9},{9,1},{2,10},{10,2},{3,11},{11,3},{4,12},{12,4},... | collective-permute-start | bytes 1572872 | tf_op jit(solution)/shard_map/ppermute | solution.py:56
  102.5 9.6 %collective-permute-start.16 = (bf16[2,1,2,128,256]{4,3,2,0,1:T(8,128)(2,1)S(1)}, bf16[2,1,2,128,256]{4,3,2,0,1:T(8,128)(2,1)S(1)}, u32[]{:S(2)}, u32[]{:S(2)}) collective-permute-start(bf16[2,1,2,128,256]{4,3,2,0,1:T(8,128)(2,1)S(1)} %bitcast.307), channel_id=1, source_target_pairs={{0,2},{2,0},{1,3},{3,1},{4,6},{6,4},{5,7},{7,5},{8,10},{10,8},{9,1... | collective-permute-start | bytes 786440 | tf_op jit(solution)/shard_map/ppermute | solution.py:56
  114.9 7.6 %collective-permute-start.26 = (bf16[256,1024]{1,0:T(8,128)(2,1)S(1)}, bf16[256,1024]{1,0:T(8,128)(2,1)S(1)}, u32[]{:S(2)}, u32[]{:S(2)}) collective-permute-start(bf16[256,1024]{1,0:T(8,128)(2,1)S(1)} %get-tuple-element.379), channel_id=1, source_target_pairs={{0,1},{1,0},{2,3},{3,2},{4,5},{5,4},{6,7},{7,6},{8,9},{9,8},{10,11... | collective-permute-start | bytes 1572872 | tf_op jit(solution)/shard_map/ppermute | solution.py:56
  114.9 7.6 %collective-permute-start.25 = (bf16[256,1024]{1,0:T(8,128)(2,1)S(1)}, bf16[256,1024]{1,0:T(8,128)(2,1)S(1)}, u32[]{:S(2)}, u32[]{:S(2)}) collective-permute-start(bf16[256,1024]{1,0:T(8,128)(2,1)S(1)} %get-tuple-element.380), channel_id=1, source_target_pairs={{0,1},{1,0},{2,3},{3,2},{4,5},{5,4},{6,7},{7,6},{8,9},{9,8},{10,11... | collective-permute-start | bytes 1572872 | tf_op jit(solution)/shard_map/ppermute | solution.py:56
  115.4 7.1 %collective-permute-start.24 = (bf16[256,1024]{1,0:T(8,128)(2,1)S(1)}, bf16[256,1024]{1,0:T(8,128)(2,1)S(1)}, u32[]{:S(2)}, u32[]{:S(2)}) collective-permute-start(bf16[256,1024]{1,0:T(8,128)(2,1)S(1)} %get-tuple-element.381), channel_id=1, source_target_pairs={{0,1},{1,0},{2,3},{3,2},{4,5},{5,4},{6,7},{7,6},{8,9},{9,8},{10,11... | collective-permute-start | bytes 1572872 | tf_op jit(solution)/shard_map/ppermute | solution.py:56
  115.5 7.1 %collective-permute-start.23 = (bf16[256,1024]{1,0:T(8,128)(2,1)S(1)}, bf16[256,1024]{1,0:T(8,128)(2,1)S(1)}, u32[]{:S(2)}, u32[]{:S(2)}) collective-permute-start(bf16[256,1024]{1,0:T(8,128)(2,1)S(1)} %get-tuple-element.382), channel_id=1, source_target_pairs={{0,1},{1,0},{2,3},{3,2},{4,5},{5,4},{6,7},{7,6},{8,9},{9,8},{10,11... | collective-permute-start | bytes 1572872 | tf_op jit(solution)/shard_map/ppermute | solution.py:56
  122.6 41.2 %collective-permute-start.27 = (bf16[2,1,2,2,64,1024]{5,4,3,2,0,1:T(8,128)(2,1)}, bf16[2,1,2,2,64,1024]{5,4,3,2,0,1:T(8,128)(2,1)}, u32[]{:S(2)}, u32[]{:S(2)}) collective-permute-start(bf16[2,1,2,2,64,1024]{5,4,3,2,0,1:T(8,128)(2,1)} %bitcast.72), channel_id=1, source_target_pairs={{0,16},{16,0},{1,17},{17,1},{2,18},{18,2},{3,19},{19,3},{4,20},{20... | collective-permute-start | bytes 3145736 | tf_op jit(solution)/shard_map/ppermute | solution.py:56
  123.7 40.1 %collective-permute-start.29 = (bf16[4,64,1408]{2,1,0:T(8,128)(2,1)S(1)}, bf16[4,64,1408]{2,1,0:T(8,128)(2,1)S(1)}, u32[]{:S(2)}, u32[]{:S(2)}) collective-permute-start(bf16[4,64,1408]{2,1,0:T(8,128)(2,1)S(1)} %get-tuple-element.234.refs_0_.refs_8_), channel_id=1, source_target_pairs={{0,16},{16,0},{1,17},{17,1},{2,18},{18,2},{3,19},{19,3},{4,20},{20... | collective-permute-start | bytes 2162696 | tf_op jit(solution)/shard_map/ppermute | solution.py:56
  124.7 39.0 %collective-permute-start.28 = (bf16[4,64,1408]{2,1,0:T(8,128)(2,1)S(1)}, bf16[4,64,1408]{2,1,0:T(8,128)(2,1)}, u32[]{:S(2)}, u32[]{:S(2)}) collective-permute-start(bf16[4,64,1408]{2,1,0:T(8,128)(2,1)S(1)} %get-tuple-element.234.refs_0_.refs_8_), channel_id=1, source_target_pairs={{0,8},{8,0},{1,9},{9,1},{2,10},{10,2},{3,11},{11,3},{4,12},{12,4},... | collective-permute-start | bytes 2162696 | tf_op jit(solution)/shard_map/ppermute | solution.py:56
  167.1 19.0 %collective-permute-start.36 = (bf16[4,64,1408]{2,1,0:T(8,128)(2,1)S(1)}, bf16[4,64,1408]{2,1,0:T(8,128)(2,1)S(1)}, u32[]{:S(2)}, u32[]{:S(2)}) collective-permute-start(bf16[4,64,1408]{2,1,0:T(8,128)(2,1)S(1)} %get-tuple-element.238.refs_8_.refs_16_), channel_id=1, source_target_pairs={{0,16},{16,0},{1,17},{17,1},{2,18},{18,2},{3,19},{19,3},{4,20},{20... | collective-permute-start | bytes 2162696 | tf_op jit(solution)/shard_map/ppermute | solution.py:56
  168.1 32.0 %collective-permute-start.35 = (bf16[4,64,1408]{2,1,0:T(8,128)(2,1)S(1)}, bf16[4,64,1408]{2,1,0:T(8,128)(2,1)S(1)}, u32[]{:S(2)}, u32[]{:S(2)}) collective-permute-start(bf16[4,64,1408]{2,1,0:T(8,128)(2,1)S(1)} %get-tuple-element.238.refs_8_.refs_16_), channel_id=1, source_target_pairs={{0,8},{8,0},{1,9},{9,1},{2,10},{10,2},{3,11},{11,3},{4,12},{12,4},... | collective-permute-start | bytes 2162696 | tf_op jit(solution)/shard_map/ppermute | solution.py:56
  173.6 27.2 %collective-permute-start.37 = (bf16[4,64,1408]{2,1,0:T(8,128)(2,1)}, bf16[4,64,1408]{2,1,0:T(8,128)(2,1)}, u32[]{:S(2)}, u32[]{:S(2)}) collective-permute-start(bf16[4,64,1408]{2,1,0:T(8,128)(2,1)} %collective-permute-done.28.refs_1_.refs_9_), channel_id=1, source_target_pairs={{0,16},{16,0},{1,17},{17,1},{2,18},{18,2},{3,19},{19,3},{4,20},{20... | collective-permute-start | bytes 2162696 | tf_op jit(solution)/shard_map/ppermute | solution.py:56
  174.7 25.5 %collective-permute-start.34 = (bf16[128,2048]{1,0:T(8,128)(2,1)S(1)}, bf16[128,2048]{1,0:T(8,128)(2,1)}, u32[]{:S(2)}, u32[]{:S(2)}) collective-permute-start(bf16[128,2048]{1,0:T(8,128)(2,1)S(1)} %slice.548), channel_id=1, source_target_pairs={{0,2},{2,0},{1,3},{3,1},{4,6},{6,4},{5,7},{7,5},{8,10},{10,8},{9,1... | collective-permute-start | bytes 1572872 | tf_op jit(solution)/shard_map/ppermute | solution.py:56
  204.3 47.4 %all-to-all-start.1 = ((bf16[4,128,2048]{2,1,0:T(8,128)(2,1)}), bf16[4,128,2048]{2,1,0:T(8,128)(2,1)S(1)}, u32[]{:S(2)}, u32[]{:S(2)}) async-start(bf16[4,128,2048]{2,1,0:T(8,128)(2,1)} %broadcast_in_dim.21), calls=%async_computation.1 | async-start | bytes 4194304 | tf_op jit(solution)/shard_map/all_to_all | solution.py:104
  207.9 19.3 %collective-permute-start.38 = (bf16[4,64,1408]{2,1,0:T(8,128)(2,1)}, bf16[4,64,1408]{2,1,0:T(8,128)(2,1)S(1)}, u32[]{:S(2)}, u32[]{:S(2)}) collective-permute-start(bf16[4,64,1408]{2,1,0:T(8,128)(2,1)} %copy-done.40), channel_id=1, source_target_pairs={{0,16},{16,0},{1,17},{17,1},{2,18},{18,2},{3,19},{19,3},{4,20},{20... | collective-permute-start | bytes 2162696 | tf_op jit(solution)/shard_map/ppermute | solution.py:56
  208.9 32.4 %collective-permute-start.40 = (bf16[4,64,1408]{2,1,0:T(8,128)(2,1)}, bf16[4,64,1408]{2,1,0:T(8,128)(2,1)S(1)}, u32[]{:S(2)}, u32[]{:S(2)}) collective-permute-start(bf16[4,64,1408]{2,1,0:T(8,128)(2,1)} %get-tuple-element.233.refs_0_), channel_id=1, source_target_pairs={{0,16},{16,0},{1,17},{17,1},{2,18},{18,2},{3,19},{19,3},{4,20},{20... | collective-permute-start | bytes 2162696 | tf_op jit(solution)/shard_map/ppermute | solution.py:56
  210.0 36.2 %collective-permute-start.39 = (bf16[4,64,1408]{2,1,0:T(8,128)(2,1)}, bf16[4,64,1408]{2,1,0:T(8,128)(2,1)S(1)}, u32[]{:S(2)}, u32[]{:S(2)}) collective-permute-start(bf16[4,64,1408]{2,1,0:T(8,128)(2,1)} %get-tuple-element.233.refs_0_), channel_id=1, source_target_pairs={{0,8},{8,0},{1,9},{9,1},{2,10},{10,2},{3,11},{11,3},{4,12},{12,4},... | collective-permute-start | bytes 2162696 | tf_op jit(solution)/shard_map/ppermute | solution.py:56
  227.2 19.0 %collective-permute-start.41 = (bf16[4,64,1408]{2,1,0:T(8,128)(2,1)}, bf16[4,64,1408]{2,1,0:T(8,128)(2,1)S(1)}, u32[]{:S(2)}, u32[]{:S(2)}) collective-permute-start(bf16[4,64,1408]{2,1,0:T(8,128)(2,1)} %copy-done.24), channel_id=1, source_target_pairs={{0,1},{1,0},{2,3},{3,2},{4,5},{5,4},{6,7},{7,6},{8,9},{9,8},{10,11... | collective-permute-start | bytes 2162696 | tf_op jit(solution)/shard_map/ppermute | solution.py:56
  227.2 19.5 %collective-permute-start.42 = (bf16[4,64,1408]{2,1,0:T(8,128)(2,1)}, bf16[4,64,1408]{2,1,0:T(8,128)(2,1)S(1)}, u32[]{:S(2)}, u32[]{:S(2)}) collective-permute-start(bf16[4,64,1408]{2,1,0:T(8,128)(2,1)} %collective-permute-done.28.refs_1_.refs_9_), channel_id=1, source_target_pairs={{0,1},{1,0},{2,3},{3,2},{4,5},{5,4},{6,7},{7,6},{8,9},{9,8},{10,11... | collective-permute-start | bytes 2162696 | tf_op jit(solution)/shard_map/ppermute | solution.py:56
  227.7 19.1 %collective-permute-start.43 = (bf16[4,64,1408]{2,1,0:T(8,128)(2,1)}, bf16[4,64,1408]{2,1,0:T(8,128)(2,1)S(1)}, u32[]{:S(2)}, u32[]{:S(2)}) collective-permute-start(bf16[4,64,1408]{2,1,0:T(8,128)(2,1)} %copy-done.38), channel_id=1, source_target_pairs={{0,1},{1,0},{2,3},{3,2},{4,5},{5,4},{6,7},{7,6},{8,9},{9,8},{10,11... | collective-permute-start | bytes 2162696 | tf_op jit(solution)/shard_map/ppermute | solution.py:56
  256.7 30.9 %all-to-all-start.2 = ((bf16[4,128,2048]{2,1,0:T(8,128)(2,1)}), bf16[4,128,2048]{2,1,0:T(8,128)(2,1)S(1)}, u32[]{:S(2)}, u32[]{:S(2)}) async-start(bf16[4,128,2048]{2,1,0:T(8,128)(2,1)} %broadcast_in_dim.22), calls=%async_computation.2 | async-start | bytes 4194304 | tf_op jit(solution)/shard_map/all_to_all | solution.py:104
  262.5 18.1 %collective-permute-start.50 = (bf16[4,64,1408]{2,1,0:T(8,128)(2,1)}, bf16[4,64,1408]{2,1,0:T(8,128)(2,1)S(1)}, u32[]{:S(2)}, u32[]{:S(2)}) collective-permute-start(bf16[4,64,1408]{2,1,0:T(8,128)(2,1)} %get-tuple-element.233.refs_0_), channel_id=1, source_target_pairs={{0,1},{1,0},{2,3},{3,2},{4,5},{5,4},{6,7},{7,6},{8,9},{9,8},{10,11... | collective-permute-start | bytes 2162696 | tf_op jit(solution)/shard_map/ppermute | solution.py:56
  263.0 17.6 %collective-permute-start.52 = (bf16[4,64,1408]{2,1,0:T(8,128)(2,1)}, bf16[4,64,1408]{2,1,0:T(8,128)(2,1)S(1)}, u32[]{:S(2)}, u32[]{:S(2)}) collective-permute-start(bf16[4,64,1408]{2,1,0:T(8,128)(2,1)} %copy-done.31), channel_id=1, source_target_pairs={{0,1},{1,0},{2,3},{3,2},{4,5},{5,4},{6,7},{7,6},{8,9},{9,8},{10,11... | collective-permute-start | bytes 2162696 | tf_op jit(solution)/shard_map/ppermute | solution.py:56
  263.0 17.6 %collective-permute-start.51 = (bf16[4,64,1408]{2,1,0:T(8,128)(2,1)}, bf16[4,64,1408]{2,1,0:T(8,128)(2,1)S(1)}, u32[]{:S(2)}, u32[]{:S(2)}) collective-permute-start(bf16[4,64,1408]{2,1,0:T(8,128)(2,1)} %copy-done.32), channel_id=1, source_target_pairs={{0,1},{1,0},{2,3},{3,2},{4,5},{5,4},{6,7},{7,6},{8,9},{9,8},{10,11... | collective-permute-start | bytes 2162696 | tf_op jit(solution)/shard_map/ppermute | solution.py:56
  263.5 18.3 %collective-permute-start.48 = (bf16[4,64,1408]{2,1,0:T(8,128)(2,1)}, bf16[4,64,1408]{2,1,0:T(8,128)(2,1)S(1)}, u32[]{:S(2)}, u32[]{:S(2)}) collective-permute-start(bf16[4,64,1408]{2,1,0:T(8,128)(2,1)} %copy-done.32), channel_id=1, source_target_pairs={{0,16},{16,0},{1,17},{17,1},{2,18},{18,2},{3,19},{19,3},{4,20},{20... | collective-permute-start | bytes 2162696 | tf_op jit(solution)/shard_map/ppermute | solution.py:56
  309.7 29.4 %all-to-all-start.3 = ((bf16[4,128,2048]{2,1,0:T(8,128)(2,1)}), bf16[4,128,2048]{2,1,0:T(8,128)(2,1)S(1)}, u32[]{:S(2)}, u32[]{:S(2)}) async-start(bf16[4,128,2048]{2,1,0:T(8,128)(2,1)} %bitcast.295), calls=%async_computation.3 | async-start | bytes 4194304 | tf_op jit(solution)/shard_map/all_to_all | solution.py:108
  313.3 240.9 %reduce-scatter.2.cloned.1.call-start = ((), (), s32[]{:S(2)}) async-start(), calls=%async_computation.8 | async-start | bytes 12976128 | tf_op jit(solution)/shard_map/reduce_scatter | solution.py:652
  343.3 14.2 %collective-permute-start.55 = (bf16[128,2048]{1,0:T(8,128)(2,1)S(1)}, bf16[128,2048]{1,0:T(8,128)(2,1)S(1)}, u32[]{:S(2)}, u32[]{:S(2)}) collective-permute-start(bf16[128,2048]{1,0:T(8,128)(2,1)S(1)} %fusion.54), channel_id=1, source_target_pairs={{0,2},{2,0},{1,3},{3,1},{4,6},{6,4},{5,7},{7,5},{8,10},{10,8},{9,1... | collective-permute-start | bytes 1572872 | tf_op jit(solution)/shard_map/ppermute | solution.py:56
  358.3 43.1 %all-to-all-start.4 = ((bf16[4,128,2048]{2,1,0:T(8,128)(2,1)}), bf16[4,128,2048]{2,1,0:T(8,128)(2,1)}, u32[]{:S(2)}, u32[]{:S(2)}) async-start(bf16[4,128,2048]{2,1,0:T(8,128)(2,1)} %bitcast.275), calls=%async_computation.4 | async-start | bytes 4194304 | tf_op jit(solution)/shard_map/all_to_all | solution.py:108
  370.0 33.7 %collective-permute-start.60 = (bf16[256,1408]{1,0:T(8,128)(2,1)}, bf16[256,1408]{1,0:T(8,128)(2,1)S(1)}, u32[]{:S(2)}, u32[]{:S(2)}) collective-permute-start(bf16[256,1408]{1,0:T(8,128)(2,1)} %add_convert_fusion.3), channel_id=1, source_target_pairs={{0,16},{16,0},{1,17},{17,1},{2,18},{18,2},{3,19},{19,3},{4,20},{20... | collective-permute-start | bytes 2162696 | tf_op jit(solution)/shard_map/ppermute | solution.py:56
  404.0 7.9 %collective-permute-start.61 = (bf16[2,1,2,128,256]{4,3,2,1,0:T(8,128)(2,1)S(1)}, bf16[2,1,2,128,256]{4,3,2,1,0:T(8,128)(2,1)S(1)}, u32[]{:S(2)}, u32[]{:S(2)}) collective-permute-start(bf16[2,1,2,128,256]{4,3,2,1,0:T(8,128)(2,1)S(1)} %slice.549), channel_id=1, source_target_pairs={{0,2},{2,0},{1,3},{3,1},{4,6},{6,4},{5,7},{7,5},{8,10},{10,8},{9,1... | collective-permute-start | bytes 786440 | tf_op jit(solution)/shard_map/ppermute | solution.py:56
  405.9 5.8 collective-permute-start.62
  406.0 5.7 collective-permute-start.65
  412.0 10.9 %collective-permute-start.66 = (bf16[1,2,128,256]{3,2,1,0:T(8,128)(2,1)S(1)}, bf16[1,2,128,256]{3,2,1,0:T(8,128)(2,1)S(1)}, u32[]{:S(2)}, u32[]{:S(2)}) collective-permute-start(bf16[1,2,128,256]{3,2,1,0:T(8,128)(2,1)S(1)} %fusion.35), channel_id=1, source_target_pairs={{0,4},{4,0},{1,5},{5,1},{2,6},{6,2},{3,7},{7,3},{8,12},{12,8},{9,1... | collective-permute-start | bytes 393224 | tf_op jit(solution)/shard_map/ppermute | solution.py:56
  423.0 13.6 %collective-permute-start.68 = (bf16[128,2048]{1,0:T(8,128)(2,1)S(1)}, bf16[128,2048]{1,0:T(8,128)(2,1)S(1)}, u32[]{:S(2)}, u32[]{:S(2)}) collective-permute-start(bf16[128,2048]{1,0:T(8,128)(2,1)S(1)} %slice.547), channel_id=1, source_target_pairs={{0,2},{2,0},{1,3},{3,1},{4,6},{6,4},{5,7},{7,5},{8,10},{10,8},{9,1... | collective-permute-start | bytes 1572872 | tf_op jit(solution)/shard_map/ppermute | solution.py:56
  423.5 7.4 %collective-permute-start.67 = (bf16[1,128,256]{2,1,0:T(8,128)(2,1)S(1)}, bf16[1,128,256]{2,1,0:T(8,128)(2,1)S(1)}, u32[]{:S(2)}, u32[]{:S(2)}) collective-permute-start(bf16[1,128,256]{2,1,0:T(8,128)(2,1)S(1)} %fusion.39), channel_id=1, source_target_pairs={{0,8},{8,0},{1,9},{9,1},{2,10},{10,2},{3,11},{11,3},{4,12},{12,4},... | collective-permute-start | bytes 196616 | tf_op jit(solution)/shard_map/ppermute | solution.py:56
  425.1 39.6 %collective-permute-start.73 = (bf16[2,2,1,2,64,1024]{5,4,1,0,3,2:T(8,128)(2,1)}, bf16[2,2,1,2,64,1024]{5,4,1,0,3,2:T(8,128)(2,1)}, u32[]{:S(2)}, u32[]{:S(2)}) collective-permute-start(bf16[2,2,1,2,64,1024]{5,4,1,0,3,2:T(8,128)(2,1)} %fusion.22), channel_id=1, source_target_pairs={{0,4},{4,0},{1,5},{5,1},{2,6},{6,2},{3,7},{7,3},{8,12},{12,8},{9,1... | collective-permute-start | bytes 3145736 | tf_op jit(solution)/shard_map/ppermute | solution.py:56
  449.2 6.1 %collective-permute-start.71 = (bf16[256,1408]{1,0:T(8,128)(2,1)}, bf16[256,1408]{1,0:T(8,128)(2,1)}, u32[]{:S(2)}, u32[]{:S(2)}) collective-permute-start(bf16[256,1408]{1,0:T(8,128)(2,1)} %get-tuple-element.366), channel_id=1, source_target_pairs={{0,1},{1,0},{2,3},{3,2},{4,5},{5,4},{6,7},{7,6},{8,9},{9,8},{10,11... | collective-permute-start | bytes 2162696 | tf_op jit(solution)/shard_map/ppermute | solution.py:56
  449.2 6.1 collective-permute-start.70
  453.1 87.8 %collective-permute-start.80 = (bf16[256,1408]{1,0:T(8,128)(2,1)}, bf16[256,1408]{1,0:T(8,128)(2,1)}, u32[]{:S(2)}, u32[]{:S(2)}) collective-permute-start(bf16[256,1408]{1,0:T(8,128)(2,1)} %get-tuple-element.362), channel_id=1, source_target_pairs={{0,8},{8,0},{1,9},{9,1},{2,10},{10,2},{3,11},{11,3},{4,12},{12,4},... | collective-permute-start | bytes 2162696 | tf_op jit(solution)/shard_map/ppermute | solution.py:56
  454.0 25.0 %collective-permute-start.76 = (bf16[256,1408]{1,0:T(8,128)(2,1)}, bf16[256,1408]{1,0:T(8,128)(2,1)}, u32[]{:S(2)}, u32[]{:S(2)}) collective-permute-start(bf16[256,1408]{1,0:T(8,128)(2,1)} %get-tuple-element.363), channel_id=1, source_target_pairs={{0,16},{16,0},{1,17},{17,1},{2,18},{18,2},{3,19},{19,3},{4,20},{20... | collective-permute-start | bytes 2162696 | tf_op jit(solution)/shard_map/ppermute | solution.py:56
  467.1 14.0 %collective-permute-start.75 = (bf16[2,2,1,64,1024]{4,3,1,0,2:T(8,128)(2,1)}, bf16[2,2,1,64,1024]{4,3,1,0,2:T(8,128)(2,1)}, u32[]{:S(2)}, u32[]{:S(2)}) collective-permute-start(bf16[2,2,1,64,1024]{4,3,1,0,2:T(8,128)(2,1)} %fusion.27), channel_id=1, source_target_pairs={{0,2},{2,0},{1,3},{3,1},{4,6},{6,4},{5,7},{7,5},{8,10},{10,8},{9,1... | collective-permute-start | bytes 1572872 | tf_op jit(solution)/shard_map/ppermute | solution.py:56
  473.2 61.5 %collective-permute-start.74 = (bf16[2,2,1,2,64,1408]{5,4,1,0,3,2:T(8,128)(2,1)}, bf16[2,2,1,2,64,1408]{5,4,1,0,3,2:T(8,128)(2,1)}, u32[]{:S(2)}, u32[]{:S(2)}) collective-permute-start(bf16[2,2,1,2,64,1408]{5,4,1,0,3,2:T(8,128)(2,1)} %fusion.8), channel_id=1, source_target_pairs={{0,4},{4,0},{1,5},{5,1},{2,6},{6,2},{3,7},{7,3},{8,12},{12,8},{9,1... | collective-permute-start | bytes 4325384 | tf_op jit(solution)/shard_map/ppermute | solution.py:56
  486.1 13.1 %collective-permute-start.77 = (bf16[2,1,64,2048]{3,2,0,1:T(8,128)(2,1)}, bf16[2,1,64,2048]{3,2,0,1:T(8,128)(2,1)}, u32[]{:S(2)}, u32[]{:S(2)}) collective-permute-start(bf16[2,1,64,2048]{3,2,0,1:T(8,128)(2,1)} %convert_element_type.356), channel_id=1, source_target_pairs={{0,16},{16,0},{1,17},{17,1},{2,18},{18,2},{3,19},{19,3},{4,20},{20... | collective-permute-start | bytes 1572872 | tf_op jit(solution)/shard_map/ppermute | solution.py:56
  537.3 16.9 %collective-permute-start.78 = (bf16[2,2,1,64,1408]{4,3,1,0,2:T(8,128)(2,1)S(1)}, bf16[2,2,1,64,1408]{4,3,1,0,2:T(8,128)(2,1)}, u32[]{:S(2)}, u32[]{:S(2)}) collective-permute-start(bf16[2,2,1,64,1408]{4,3,1,0,2:T(8,128)(2,1)S(1)} %fusion.23), channel_id=1, source_target_pairs={{0,2},{2,0},{1,3},{3,1},{4,6},{6,4},{5,7},{7,5},{8,10},{10,8},{9,1... | collective-permute-start | bytes 2162696 | tf_op jit(solution)/shard_map/ppermute | solution.py:56
  539.7 12.3 %collective-permute-start.79 = (bf16[1,64,2048]{2,1,0:T(8,128)(2,1)S(1)}, bf16[1,64,2048]{2,1,0:T(8,128)(2,1)}, u32[]{:S(2)}, u32[]{:S(2)}) collective-permute-start(bf16[1,64,2048]{2,1,0:T(8,128)(2,1)S(1)} %fusion.31), channel_id=1, source_target_pairs={{0,8},{8,0},{1,9},{9,1},{2,10},{10,2},{3,11},{11,3},{4,12},{12,4},... | collective-permute-start | bytes 786440 | tf_op jit(solution)/shard_map/ppermute | solution.py:56
  558.6 13.3 %all-to-all-start.5 = ((bf16[4,1,64,1408]{3,2,1,0:T(8,128)(2,1)}), bf16[4,1,64,1408]{3,2,1,0:T(8,128)(2,1)}, u32[]{:S(2)}, u32[]{:S(2)}) async-start(bf16[4,1,64,1408]{3,2,1,0:T(8,128)(2,1)} %bitcast.290), calls=%async_computation.6 | async-start | bytes 1441792 | tf_op jit(solution)/shard_map/all_to_all | solution.py:780
  564.1 15.4 %collective-permute-start.81 = (bf16[2,1,64,2432]{3,2,0,1:T(8,128)(2,1)}, bf16[2,1,64,2432]{3,2,0,1:T(8,128)(2,1)}, u32[]{:S(2)}, u32[]{:S(2)}) collective-permute-start(bf16[2,1,64,2432]{3,2,0,1:T(8,128)(2,1)} %fusion.24), channel_id=1, source_target_pairs={{0,16},{16,0},{1,17},{17,1},{2,18},{18,2},{3,19},{19,3},{4,20},{20... | collective-permute-start | bytes 1867784 | tf_op jit(solution)/shard_map/ppermute | solution.py:56
  572.0 26.6 %all-to-all-start.6 = ((bf16[4,2,64,1408]{3,2,1,0:T(8,128)(2,1)}), bf16[4,2,64,1408]{3,2,1,0:T(8,128)(2,1)S(1)}, u32[]{:S(2)}, u32[]{:S(2)}) async-start(bf16[4,2,64,1408]{3,2,1,0:T(8,128)(2,1)} %bitcast.249), calls=%async_computation.7 | async-start | bytes 2883584 | tf_op jit(solution)/shard_map/all_to_all | solution.py:780
  581.2 15.1 %collective-permute-start.82 = (bf16[1,64,2432]{2,1,0:T(8,128)(2,1)S(1)}, bf16[1,64,2432]{2,1,0:T(8,128)(2,1)S(1)}, u32[]{:S(2)}, u32[]{:S(2)}) collective-permute-start(bf16[1,64,2432]{2,1,0:T(8,128)(2,1)S(1)} %fusion.30), channel_id=1, source_target_pairs={{0,8},{8,0},{1,9},{9,1},{2,10},{10,2},{3,11},{11,3},{4,12},{12,4},... | collective-permute-start | bytes 933896 | tf_op jit(solution)/shard_map/ppermute | solution.py:56
  (123 other events, 968.7 us)
Sparse Core Ops, SparseCore 0:
  345.5 164.1 reduce-scatter.1

commit v6 on v5

--- a/solution.py
+++ b/solution.py
@@ -716,8 +716,8 @@
     output_term = low(
         lax.dot_general(grad_hidden_low, attended_low, across, preferred_element_type=F32)
     )
-    kv_got, query_grad_low, output_term, feed_out, down_y3 = sync(
-        swap_core(kv_sent), query_grad_low, output_term, feed_out, down_y3
+    kv_got, query_grad_low, output_term = sync(
+        swap_core(kv_sent), query_grad_low, output_term
     )
     output_got = swap_core(output_term[half:])
     kv_grad = kv_grad[:kv_half].reshape(4, M, 2, tokens, 2 * HEAD_DIM)
@@ -726,7 +726,6 @@
     query_term = low(
         lax.dot_general(normed_one_low, query_grad_low, across, preferred_element_type=F32)
     )
-    down_h1 = swap(quarter(1, down_y3), "h")
     kv_got, query_term, output_got = sync(kv_got, query_term, output_got)
     kv_grad = kv_grad[:2] + kv_got.astype(F32)
     kv_got = swap(low(kv_grad[1]), "l")
@@ -734,13 +733,14 @@
     grad_one = lax.dot_general(
         query_grad_low, query_full, (((0,), (1,)), ((), ())), preferred_element_type=F32
     )
-    kv_got, grad_one = sync(kv_got, grad_one)
+    kv_got, grad_one, feed_out = sync(kv_got, grad_one, feed_out)
     grad_one_x = swap(low(grad_one[tokens:]), "x")
     output_total, output_got = fold_l(
         output_term[:half].astype(F32) + output_got.astype(F32)
     )
     kv_grad = kv_grad[0] + kv_got.astype(F32)
-    kv_got, grad_one_x = sync(swap(low(kv_grad[:, 1]), "h"), grad_one_x)
+    kv_got, grad_one_x, down_y3 = sync(swap(low(kv_grad[:, 1]), "h"), grad_one_x, down_y3)
+    down_h1 = swap(quarter(1, down_y3), "h")
     kv_mine = scatter_m(kv_grad[:, 0] + kv_got.astype(F32), 0) + shared_grad[0].astype(F32)
     keyvalue_grad_low = low(
         jnp.concatenate(
@@ -780,13 +780,11 @@
         got = lax.all_to_all(own, ("l", "x"), 0, 0)
         return [merge(got[:, i]) for i in range(own.shape[1])]
 
-    (down_weight_grad,) = finish_feed(
-        quarter(0, down_h1, down_y2).reshape(M, 4, 1, rows, part)
-    )
-    query_got, down_weight_grad = sync(query_got, down_weight_grad)
-    query_total, query_got = next_fold(query_total + query_got.astype(F32), "h")
     both_grad = both_grad.reshape(2, M, 4, rows, part).transpose(1, 2, 0, 3, 4)
     gate_weight_grad, up_weight_grad = finish_feed(both_grad)
+    query_total, query_got = next_fold(query_total + query_got.astype(F32), "h")
+    down_own = sync(quarter(0, down_h1, down_y2), gate_weight_grad)[0]
+    (down_weight_grad,) = finish_feed(down_own.reshape(M, 4, 1, rows, part))
     query_total = scatter_m(query_total + query_got.astype(F32), 0)
     query_weight_grad = query_total[:, :query_width]
     keyvalue_weight_grad = query_total[:, query_width : query_width + 2 * HEAD_DIM]

time: 621 us -> 610 us (0.982)
  waiting for transfers between devices: 231 us -> 213 us
    ppermute x83, waiting for transfers between devices: 222 us -> 193 us  [swap(): return lax.ppermute(value, axis, [(0, 1), (1, 0)])]
    all_to_all x2, waiting for transfers between devices: 0.01 us -> 11.4 us  [finish_feed(): got = lax.all_to_all(own, ('l', 'x'), 0, 0)]
    unnamed x206 -> x188, local copies, waits for them, and re-layouts: 23.8 us -> 22.1 us
  transfers between devices with their start and end apart: 91 -> 91, of which waited for: 35 -> 34; matrix products, arithmetic and copies ran while one was open for 17% -> 19% of each run, Pallas kernels for 14% -> 15%
where the time goes in v6:
time: 610 us; the launch traced here: 603 us
  waiting for transfers between devices  213 us (35%)
  Pallas kernels  117 us (19%)
  starting transfers between devices  110 us (18%)
  other arithmetic  69.3 us (11%)
  local copies, waits for them, and re-layouts  64.6 us (11%)
  between operations  16.4 us (3%)
  matrix products  12 us (2%)
    ppermute x83, waiting for transfers between devices, swap(): return lax.ppermute(value, axis, [(0, 1), (1, 0)])  193 us
    pallas_call x7, Pallas kernels, local_call(): pl.pallas_call(kernel, out_shape=outs, in_specs=near + [pl.BlockSpec(memo...  103 us
    ppermute x83, starting transfers between devices, swap(): return lax.ppermute(value, axis, [(0, 1), (1, 0)])  67.4 us
    unnamed x188, local copies, waits for them, and re-layouts  22.1 us
    all_to_all x1, starting transfers between devices, on_device(): feed = gather_m(lax.all_to_all(feed_parts, ('l', 'x'), 0, 0), 0)  17 us
  transfers between devices with their start and end apart: 91, of which 34 were waited for; matrix products, arithmetic and copies ran while one was open for 19% of the time, Pallas kernels for 15%

profile of v6, /device:TPU:0, one launch (start us, length us, event | category | flops | bytes accessed | tf_op | source)
XLA Modules:
  0.0 603.4 jit_solution(1401990520530772000)
XLA Ops:
  8.7 2.9 collective-permute-start
  28.1 3.9 shard_map.212
  32.0 6.4 %collective-permute-done.3 = bf16[2,80,256]{2,1,0:T(8,128)(2,1)S(1)} collective-permute-done((bf16[2,80,256]{2,1,0:T(8,128)(2,1)S(1)}, bf16[2,80,256]{2,1,0:T(8,128)(2,1)S(1)}, u32[]{:S(2)}, u32[]{:S(2)}) %collective-permute-start.3) | collective-permute-done | bytes 81952 | tf_op jit(solution)/shard_map/ppermute | solution.py:56
  39.2 2.8 collective-permute-start.7
  43.0 4.9 collective-permute-done.7
  50.2 17.0 %all-to-all-start = ((bf16[4,3,64,1408]{3,2,1,0:T(8,128)(2,1)}), bf16[4,3,64,1408]{3,2,1,0:T(8,128)(2,1)}, u32[]{:S(2)}, u32[]{:S(2)}) async-start(bf16[4,3,64,1408]{3,2,1,0:T(8,128)(2,1)} %shard_map.212), calls=%async_computation | async-start | bytes 4325376 | tf_op jit(solution)/shard_map/all_to_all | solution.py:494
  74.5 10.7 %collective-permute-done.14 = bf16[128,256]{1,0:T(8,128)(2,1)S(1)} collective-permute-done((bf16[128,256]{1,0:T(8,128)(2,1)S(1)}, bf16[128,256]{1,0:T(8,128)(2,1)S(1)}, u32[]{:S(2)}, u32[]{:S(2)}) %collective-permute-start.14) | collective-permute-done | bytes 65568 | tf_op jit(solution)/shard_map/ppermute | solution.py:56
  85.3 9.9 %collective-permute-start.15 = (bf16[1,2,128,256]{3,2,1,0:T(8,128)(2,1)S(1)}, bf16[1,2,128,256]{3,2,1,0:T(8,128)(2,1)S(1)}, u32[]{:S(2)}, u32[]{:S(2)}) collective-permute-start(bf16[1,2,128,256]{3,2,1,0:T(8,128)(2,1)S(1)} %maximum_bitcast_fusion), channel_id=1, source_target_pairs={{0,4},{4,0},{1,5},{5,1},{2,6},{6,2},{3,7},{7,3},{8,12},{12,8},{9,1... | collective-permute-start | bytes 393224 | tf_op jit(solution)/shard_map/ppermute | solution.py:56
  98.8 2.6 slice_bitcast_fusion.5
  104.1 8.1 %collective-permute-done.18 = bf16[1,2,2,64,1024]{4,3,2,1,0:T(8,128)(2,1)} collective-permute-done((bf16[1,2,2,64,1024]{4,3,2,1,0:T(8,128)(2,1)}, bf16[1,2,2,64,1024]{4,3,2,1,0:T(8,128)(2,1)}, u32[]{:S(2)}, u32[]{:S(2)}) %collective-permute-start.18) | collective-permute-done | bytes 524320 | tf_op jit(solution)/shard_map/ppermute | solution.py:56
  116.0 3.2 collective-permute-done.21
  119.4 2.3 pad_maximum_fusion.9
  128.3 15.6 %shard_map.213 = (bf16[1024,256]{1,0:T(8,128)(2,1)}, f32[1024,256]{1,0:T(8,128)}, bf16[1024,256]{1,0:T(8,128)(2,1)}, f32[8,256]{1,0:T(8,128)}) custom-call(bf16[256,2048]{1,0:T(8,128)(2,1)} %pad_maximum_fusion.7.normed, bf16[1024,1024]{1,0:T(8,128)(2,1)} %bitcast.255, bf16[256,1024]{1,0:T(8,128)(2,1)} %copy-done.52, bf16[256,1024]{1,0:T(8,128)(2,1)} %copy-done.50, ...), custom_call_target="tpu_custom_call" | custom-call | flops 1 | bytes 1 | tf_op jit(solution)/shard_map/pallas_call | solution.py:381
  143.9 19.9 %collective-permute-done.29.refs_2_.refs_10_ = bf16[4,64,1408]{2,1,0:T(8,128)(2,1)S(1)} collective-permute-done((bf16[4,64,1408]{2,1,0:T(8,128)(2,1)S(1)}, bf16[4,64,1408]{2,1,0:T(8,128)(2,1)S(1)}, u32[]{:S(2)}, u32[]{:S(2)}) %collective-permute-start.29) | collective-permute-done | bytes 720928 | tf_op jit(solution)/shard_map/ppermute | solution.py:56
  178.0 8.1 %collective-permute-done.36.refs_10_.refs_18_ = bf16[4,64,1408]{2,1,0:T(8,128)(2,1)S(1)} collective-permute-done((bf16[4,64,1408]{2,1,0:T(8,128)(2,1)S(1)}, bf16[4,64,1408]{2,1,0:T(8,128)(2,1)S(1)}, u32[]{:S(2)}, u32[]{:S(2)}) %collective-permute-start.36) | collective-permute-done | bytes 720928 | tf_op jit(solution)/shard_map/ppermute | solution.py:56
  186.1 14.1 %collective-permute-done.35.refs_9_.refs_17_ = bf16[4,64,1408]{2,1,0:T(8,128)(2,1)S(1)} collective-permute-done((bf16[4,64,1408]{2,1,0:T(8,128)(2,1)S(1)}, bf16[4,64,1408]{2,1,0:T(8,128)(2,1)S(1)}, u32[]{:S(2)}, u32[]{:S(2)}) %collective-permute-start.35) | collective-permute-done | bytes 720928 | tf_op jit(solution)/shard_map/ppermute | solution.py:56
  204.3 3.6 all-to-all-start.1
  211.9 15.3 %collective-permute-done.38.refs_11_.refs_19_ = bf16[4,64,1408]{2,1,0:T(8,128)(2,1)S(1)} collective-permute-done((bf16[4,64,1408]{2,1,0:T(8,128)(2,1)}, bf16[4,64,1408]{2,1,0:T(8,128)(2,1)S(1)}, u32[]{:S(2)}, u32[]{:S(2)}) %collective-permute-start.38) | collective-permute-done | bytes 720928 | tf_op jit(solution)/shard_map/ppermute | solution.py:56
  227.7 13.6 %collective-permute-done.40.refs_2_ = bf16[4,64,1408]{2,1,0:T(8,128)(2,1)S(1)} collective-permute-done((bf16[4,64,1408]{2,1,0:T(8,128)(2,1)}, bf16[4,64,1408]{2,1,0:T(8,128)(2,1)S(1)}, u32[]{:S(2)}, u32[]{:S(2)}) %collective-permute-start.40) | collective-permute-done | bytes 720928 | tf_op jit(solution)/shard_map/ppermute | solution.py:56
  241.3 4.9 collective-permute-done.39.refs_1_
  251.6 2.4 copy.166
  254.0 2.7 broadcast_in_dim.22
  256.7 6.3 %all-to-all-start.2 = ((bf16[4,128,2048]{2,1,0:T(8,128)(2,1)}), bf16[4,128,2048]{2,1,0:T(8,128)(2,1)S(1)}, u32[]{:S(2)}, u32[]{:S(2)}) async-start(bf16[4,128,2048]{2,1,0:T(8,128)(2,1)} %broadcast_in_dim.22), calls=%async_computation.2 | async-start | bytes 4194304 | tf_op jit(solution)/shard_map/all_to_all | solution.py:104
  266.5 14.5 %shard_map.214 = (f32[512,1408]{1,0:T(8,128)}, f32[512,1408]{1,0:T(8,128)}) custom-call(bf16[512,2048]{1,0:T(8,128)(2,1)} %bitcast.259, bf16[4,64,1408]{2,1,0:T(8,128)(2,1)} %copy-done.19, bf16[4,64,1408]{2,1,0:T(8,128)(2,1)} %collective-permute-done.28.refs_1_.refs_9_, bf16[4,64,1408]{2,1,0:T(8,128)(2,1)} %copy-done.35, ...), custom_call_target="tpu_custom_call" | custom-call | flops 1 | bytes 1 | tf_op jit(solution)/shard_map/pallas_call | solution.py:381
  284.7 3.4 all-to-all-done.2
  289.5 20.6 %shard_map.215 = (bf16[512,1408]{1,0:T(8,128)(2,1)}, bf16[512,1408]{1,0:T(8,128)(2,1)}, bf16[512,1408]{1,0:T(8,128)(2,1)}, bf16[512,2048]{1,0:T(8,128)(2,1)}) custom-call(bf16[512,2048]{1,0:T(8,128)(2,1)} %bitcast.257, f32[512,1408]{1,0:T(8,128)} %get-tuple-element.253.gate_sum, f32[512,1408]{1,0:T(8,128)} %get-tuple-element.254.up_sum, ...), custom_call_target="tpu_custom_call" | custom-call | flops 1 | bytes 1 | tf_op jit(solution)/shard_map/pallas_call | solution.py:381
  310.2 4.5 all-to-all-start.3
  315.4 14.9 %shard_map.216 = bf16[8,2,256,1408]{3,2,1,0:T(8,128)(2,1)} custom-call(s32[8]{0:T(128)} %stack.417.order, bf16[512,2048]{1,0:T(8,128)(2,1)} %bitcast.260, bf16[512,1408]{1,0:T(8,128)(2,1)} %get-tuple-element.261.refs_0_, bf16[512,1408]{1,0:T(8,128)(2,1)} %get-tuple-element.262.refs_1_), custom_call_target="tpu_custom_call" | custom-call | flops 1 | bytes 1 | tf_op jit(solution)/shard_map/pallas_call | solution.py:381
  330.3 8.4 %shard_map.217 = (bf16[1024,1408]{1,0:T(8,128)(2,1)}, bf16[1024,1408]{1,0:T(8,128)(2,1)}) custom-call(bf16[512,2048]{1,0:T(8,128)(2,1)} %bitcast.258, bf16[512,1408]{1,0:T(8,128)(2,1)} %get-tuple-element.269.refs_0_.mixed), custom_call_target="tpu_custom_call" | custom-call | flops 1 | bytes 1 | tf_op jit(solution)/shard_map/pallas_call | solution.py:381
  345.5 2.2 convert_reduce_fusion.1
  350.4 12.0 %shard_map.218 = bf16[512,2048]{1,0:T(8,128)(2,1)} custom-call(bf16[512,1408]{1,0:T(8,128)(2,1)} %get-tuple-element.269.refs_0_.mixed, bf16[4,64,1408]{2,1,0:T(8,128)(2,1)} %get-tuple-element.232.refs_0_, bf16[4,64,1408]{2,1,0:T(8,128)(2,1)} %copy-done.28, bf16[4,64,1408]{2,1,0:T(8,128)(2,1)} %copy-done.27, bf16[4,64,1408]{2,1,0:T(8,128)(2,1)} %copy-done.32, ...), custom_call_target="tpu_custom_call" | custom-call | flops 1 | bytes 1 | tf_op jit(solution)/shard_map/pallas_call | solution.py:381
  362.5 2.4 add_convert_fusion.3
  365.6 4.6 all-to-all-start.4
  372.3 17.0 %shard_map.219 = (bf16[1024,256]{1,0:T(8,128)(2,1)}, f32[2048,256]{1,0:T(8,128)}) custom-call(bf16[1024,256]{1,0:T(8,128)(2,1)} %get-tuple-element.224.query_rot, bf16[2048,256]{1,0:T(8,128)(2,1)} %bitcast.270, bf16[256,2048]{1,0:T(8,128)(2,1)} %copy-done.11, bf16[2048,1024]{1,0:T(8,128)(2,1)} %copy-done.13, f32[1024,256]{1,0:T(8,128)} %get-tuple-element.271.attended, ...), custom_call_target="tpu_custom_call" | custom-call | flops 1 | bytes 1 | tf_op jit(solution)/shard_map/pallas_call | solution.py:381
  397.6 4.8 fusion.63
  402.4 3.3 convolution_convert_fusion
  409.8 2.9 convert_add_fusion.1
  412.7 5.6 all-to-all-done.4
  418.3 2.2 convert_reduce_fusion
  420.6 3.2 collective-permute-done.65
  428.2 2.8 fusion.22
  431.0 3.4 collective-permute-done.66
  434.4 3.4 collective-permute-done.67
  443.0 3.6 fusion.1
  448.4 2.9 add_convert_fusion.1
  452.9 5.1 pad_maximum_fusion.1
  458.0 11.9 %collective-permute-done.73 = bf16[2,2,1,2,64,1024]{5,4,1,0,3,2:T(8,128)(2,1)} collective-permute-done((bf16[2,2,1,2,64,1024]{5,4,1,0,3,2:T(8,128)(2,1)}, bf16[2,2,1,2,64,1024]{5,4,1,0,3,2:T(8,128)(2,1)}, u32[]{:S(2)}, u32[]{:S(2)}) %collective-permute-start.73) | collective-permute-done | bytes 1048608 | tf_op jit(solution)/shard_map/ppermute | solution.py:56
  473.4 2.4 copy-done.8
  480.1 6.3 %collective-permute-done.75 = bf16[2,2,1,64,1024]{4,3,1,0,2:T(8,128)(2,1)} collective-permute-done((bf16[2,2,1,64,1024]{4,3,1,0,2:T(8,128)(2,1)}, bf16[2,2,1,64,1024]{4,3,1,0,2:T(8,128)(2,1)}, u32[]{:S(2)}, u32[]{:S(2)}) %collective-permute-start.75) | collective-permute-done | bytes 524320 | tf_op jit(solution)/shard_map/ppermute | solution.py:56
  489.2 2.2 convert_element_type.356
  496.2 8.5 %collective-permute-done.77 = bf16[2,1,64,2048]{3,2,0,1:T(8,128)(2,1)} collective-permute-done((bf16[2,1,64,2048]{3,2,0,1:T(8,128)(2,1)}, bf16[2,1,64,2048]{3,2,0,1:T(8,128)(2,1)}, u32[]{:S(2)}, u32[]{:S(2)}) %collective-permute-start.77) | collective-permute-done | bytes 524320 | tf_op jit(solution)/shard_map/ppermute | solution.py:56
  504.7 18.2 %collective-permute-done.74 = bf16[2,2,1,2,64,1408]{5,4,1,0,3,2:T(8,128)(2,1)} collective-permute-done((bf16[2,2,1,2,64,1408]{5,4,1,0,3,2:T(8,128)(2,1)}, bf16[2,2,1,2,64,1408]{5,4,1,0,3,2:T(8,128)(2,1)}, u32[]{:S(2)}, u32[]{:S(2)}) %collective-permute-start.74) | collective-permute-done | bytes 1441824 | tf_op jit(solution)/shard_map/ppermute | solution.py:56
  522.9 2.5 bitcast_add_fusion
  525.5 2.3 collective-permute-start.78
  530.1 12.2 %collective-permute-done.79 = bf16[1,64,2048]{2,1,0:T(8,128)(2,1)} collective-permute-done((bf16[1,64,2048]{2,1,0:T(8,128)(2,1)S(1)}, bf16[1,64,2048]{2,1,0:T(8,128)(2,1)}, u32[]{:S(2)}, u32[]{:S(2)}) %collective-permute-start.79) | collective-permute-done | bytes 262176 | tf_op jit(solution)/shard_map/ppermute | solution.py:56
  546.0 2.8 collective-permute-start.81
  550.1 3.6 all-to-all-start.5
  554.9 2.8 add_convert_fusion
  557.7 4.2 collective-permute-done.81
  563.9 11.4 %all-to-all-done.5 = bf16[4,2,64,1408]{3,2,1,0:T(8,128)(2,1)S(1)} async-done(((bf16[4,2,64,1408]{3,2,1,0:T(8,128)(2,1)}), bf16[4,2,64,1408]{3,2,1,0:T(8,128)(2,1)S(1)}, u32[]{:S(2)}, u32[]{:S(2)}) %all-to-all-start.5) | async-done | bytes 1441824 | tf_op jit(solution)/shard_map/all_to_all | solution.py:780
  576.5 3.5 shard_map.220
  579.9 3.5 all-to-all-start.6
  588.5 3.4 shard_map.221
  592.7 3.4 shard_map.222
  (501 shorter events, 153.0 us)
Async XLA Ops:
  8.7 14.6 %collective-permute-start = (bf16[80,256]{1,0:T(8,128)(2,1)S(1)}, bf16[80,256]{1,0:T(8,128)(2,1)S(1)}, u32[]{:S(2)}, u32[]{:S(2)}) collective-permute-start(bf16[80,256]{1,0:T(8,128)(2,1)S(1)} %get-tuple-element.411), channel_id=1, source_target_pairs={{0,2},{2,0},{1,3},{3,1},{4,6},{6,4},{5,7},{7,5},{8,10},{10,8},{9,1... | collective-permute-start | bytes 122888 | tf_op jit(solution)/shard_map/ppermute | solution.py:56
  15.1 8.2 %collective-permute-start.1 = (bf16[64,1024]{1,0:T(8,128)(2,1)S(1)}, bf16[64,1024]{1,0:T(8,128)(2,1)S(1)}, u32[]{:S(2)}, u32[]{:S(2)}) collective-permute-start(bf16[64,1024]{1,0:T(8,128)(2,1)S(1)} %bitcast.326), channel_id=1, source_target_pairs={{0,2},{2,0},{1,3},{3,1},{4,6},{6,4},{5,7},{7,5},{8,10},{10,8},{9,1... | collective-permute-start | bytes 393224 | tf_op jit(solution)/shard_map/ppermute | solution.py:56
  15.2 8.1 %collective-permute-start.2 = (bf16[64,1024]{1,0:T(8,128)(2,1)S(1)}, bf16[64,1024]{1,0:T(8,128)(2,1)S(1)}, u32[]{:S(2)}, u32[]{:S(2)}) collective-permute-start(bf16[64,1024]{1,0:T(8,128)(2,1)S(1)} %bitcast.327), channel_id=1, source_target_pairs={{0,2},{2,0},{1,3},{3,1},{4,6},{6,4},{5,7},{7,5},{8,10},{10,8},{9,1... | collective-permute-start | bytes 393224 | tf_op jit(solution)/shard_map/ppermute | solution.py:56
  23.6 14.8 %collective-permute-start.6 = (bf16[128,2048]{1,0:T(8,128)(2,1)S(1)}, bf16[128,2048]{1,0:T(8,128)(2,1)S(1)}, u32[]{:S(2)}, u32[]{:S(2)}) collective-permute-start(bf16[128,2048]{1,0:T(8,128)(2,1)S(1)} %copy.155), channel_id=1, source_target_pairs={{0,2},{2,0},{1,3},{3,1},{4,6},{6,4},{5,7},{7,5},{8,10},{10,8},{9,1... | collective-permute-start | bytes 1572872 | tf_op jit(solution)/shard_map/ppermute | solution.py:56
  23.7 14.7 %collective-permute-start.4 = (bf16[2,64,1024]{2,1,0:T(8,128)(2,1)S(1)}, bf16[2,64,1024]{2,1,0:T(8,128)(2,1)S(1)}, u32[]{:S(2)}, u32[]{:S(2)}) collective-permute-start(bf16[2,64,1024]{2,1,0:T(8,128)(2,1)S(1)} %maximum_select_fusion.4), channel_id=1, source_target_pairs={{0,4},{4,0},{1,5},{5,1},{2,6},{6,2},{3,7},{7,3},{8,12},{12,8},{9,1... | collective-permute-start | bytes 786440 | tf_op jit(solution)/shard_map/ppermute | solution.py:56
  25.9 12.5 %collective-permute-start.5 = (bf16[2,64,1024]{2,1,0:T(8,128)(2,1)S(1)}, bf16[2,64,1024]{2,1,0:T(8,128)(2,1)S(1)}, u32[]{:S(2)}, u32[]{:S(2)}) collective-permute-start(bf16[2,64,1024]{2,1,0:T(8,128)(2,1)S(1)} %maximum_select_fusion.5), channel_id=1, source_target_pairs={{0,4},{4,0},{1,5},{5,1},{2,6},{6,2},{3,7},{7,3},{8,12},{12,8},{9,1... | collective-permute-start | bytes 786440 | tf_op jit(solution)/shard_map/ppermute | solution.py:56
  26.1 12.3 %collective-permute-start.3 = (bf16[2,80,256]{2,1,0:T(8,128)(2,1)S(1)}, bf16[2,80,256]{2,1,0:T(8,128)(2,1)S(1)}, u32[]{:S(2)}, u32[]{:S(2)}) collective-permute-start(bf16[2,80,256]{2,1,0:T(8,128)(2,1)S(1)} %maximum_select_fusion.9), channel_id=1, source_target_pairs={{0,4},{4,0},{1,5},{5,1},{2,6},{6,2},{3,7},{7,3},{8,12},{12,8},{9,1... | collective-permute-start | bytes 245768 | tf_op jit(solution)/shard_map/ppermute | solution.py:56
  39.2 8.6 %collective-permute-start.7 = (bf16[1,2,2,80,256]{4,3,2,1,0:T(8,128)(2,1)S(1)}, bf16[1,2,2,80,256]{4,3,2,1,0:T(8,128)(2,1)S(1)}, u32[]{:S(2)}, u32[]{:S(2)}) collective-permute-start(bf16[1,2,2,80,256]{4,3,2,1,0:T(8,128)(2,1)S(1)} %maximum_select_fusion.8), channel_id=1, source_target_pairs={{0,8},{8,0},{1,9},{9,1},{2,10},{10,2},{3,11},{11,3},{4,12},{12,4},... | collective-permute-start | bytes 491528 | tf_op jit(solution)/shard_map/ppermute | solution.py:56
  47.9 19.4 %collective-permute-start.8 = (bf16[2,1,2,2,80,256]{5,4,3,2,1,0:T(8,128)(2,1)S(1)}, bf16[2,1,2,2,80,256]{5,4,3,2,1,0:T(8,128)(2,1)S(1)}, u32[]{:S(2)}, u32[]{:S(2)}) collective-permute-start(bf16[2,1,2,2,80,256]{5,4,3,2,1,0:T(8,128)(2,1)S(1)} %pad_maximum_fusion.16), channel_id=1, source_target_pairs={{0,16},{16,0},{1,17},{17,1},{2,18},{18,2},{3,19},{19,3},{4,20},{20... | collective-permute-start | bytes 983048 | tf_op jit(solution)/shard_map/ppermute | solution.py:56
  49.6 20.1 %collective-permute-start.13 = (bf16[1,2,2,64,1024]{4,3,2,1,0:T(8,128)(2,1)S(1)}, bf16[1,2,2,64,1024]{4,3,2,1,0:T(8,128)(2,1)S(1)}, u32[]{:S(2)}, u32[]{:S(2)}) collective-permute-start(bf16[1,2,2,64,1024]{4,3,2,1,0:T(8,128)(2,1)S(1)} %maximum_select_fusion.2), channel_id=1, source_target_pairs={{0,8},{8,0},{1,9},{9,1},{2,10},{10,2},{3,11},{11,3},{4,12},{12,4},... | collective-permute-start | bytes 1572872 | tf_op jit(solution)/shard_map/ppermute | solution.py:56
  50.2 48.6 %all-to-all-start = ((bf16[4,3,64,1408]{3,2,1,0:T(8,128)(2,1)}), bf16[4,3,64,1408]{3,2,1,0:T(8,128)(2,1)}, u32[]{:S(2)}, u32[]{:S(2)}) async-start(bf16[4,3,64,1408]{3,2,1,0:T(8,128)(2,1)} %shard_map.212), calls=%async_computation | async-start | bytes 4325376 | tf_op jit(solution)/shard_map/all_to_all | solution.py:494
  72.3 12.9 %collective-permute-start.14 = (bf16[128,256]{1,0:T(8,128)(2,1)S(1)}, bf16[128,256]{1,0:T(8,128)(2,1)S(1)}, u32[]{:S(2)}, u32[]{:S(2)}) collective-permute-start(bf16[128,256]{1,0:T(8,128)(2,1)S(1)} %pad_maximum_fusion.19), channel_id=1, source_target_pairs={{0,8},{8,0},{1,9},{9,1},{2,10},{10,2},{3,11},{11,3},{4,12},{12,4},... | collective-permute-start | bytes 196616 | tf_op jit(solution)/shard_map/ppermute | solution.py:56
  73.6 38.6 %collective-permute-start.17 = (bf16[2,1,2,2,64,1024]{5,4,3,2,1,0:T(8,128)(2,1)S(1)}, bf16[2,1,2,2,64,1024]{5,4,3,2,1,0:T(8,128)(2,1)}, u32[]{:S(2)}, u32[]{:S(2)}) collective-permute-start(bf16[2,1,2,2,64,1024]{5,4,3,2,1,0:T(8,128)(2,1)S(1)} %pad_maximum_fusion.8), channel_id=1, source_target_pairs={{0,16},{16,0},{1,17},{17,1},{2,18},{18,2},{3,19},{19,3},{4,20},{20... | collective-permute-start | bytes 3145736 | tf_op jit(solution)/shard_map/ppermute | solution.py:56
  85.3 13.5 %collective-permute-start.15 = (bf16[1,2,128,256]{3,2,1,0:T(8,128)(2,1)S(1)}, bf16[1,2,128,256]{3,2,1,0:T(8,128)(2,1)S(1)}, u32[]{:S(2)}, u32[]{:S(2)}) collective-permute-start(bf16[1,2,128,256]{3,2,1,0:T(8,128)(2,1)S(1)} %maximum_bitcast_fusion), channel_id=1, source_target_pairs={{0,4},{4,0},{1,5},{5,1},{2,6},{6,2},{3,7},{7,3},{8,12},{12,8},{9,1... | collective-permute-start | bytes 393224 | tf_op jit(solution)/shard_map/ppermute | solution.py:56
  96.7 15.5 %collective-permute-start.18 = (bf16[1,2,2,64,1024]{4,3,2,1,0:T(8,128)(2,1)}, bf16[1,2,2,64,1024]{4,3,2,1,0:T(8,128)(2,1)}, u32[]{:S(2)}, u32[]{:S(2)}) collective-permute-start(bf16[1,2,2,64,1024]{4,3,2,1,0:T(8,128)(2,1)} %maximum_select_fusion.3), channel_id=1, source_target_pairs={{0,8},{8,0},{1,9},{9,1},{2,10},{10,2},{3,11},{11,3},{4,12},{12,4},... | collective-permute-start | bytes 1572872 | tf_op jit(solution)/shard_map/ppermute | solution.py:56
  102.5 9.7 %collective-permute-start.16 = (bf16[2,1,2,128,256]{4,3,2,0,1:T(8,128)(2,1)S(1)}, bf16[2,1,2,128,256]{4,3,2,0,1:T(8,128)(2,1)S(1)}, u32[]{:S(2)}, u32[]{:S(2)}) collective-permute-start(bf16[2,1,2,128,256]{4,3,2,0,1:T(8,128)(2,1)S(1)} %bitcast.307), channel_id=1, source_target_pairs={{0,2},{2,0},{1,3},{3,1},{4,6},{6,4},{5,7},{7,5},{8,10},{10,8},{9,1... | collective-permute-start | bytes 786440 | tf_op jit(solution)/shard_map/ppermute | solution.py:56
  114.9 7.6 %collective-permute-start.26 = (bf16[256,1024]{1,0:T(8,128)(2,1)S(1)}, bf16[256,1024]{1,0:T(8,128)(2,1)S(1)}, u32[]{:S(2)}, u32[]{:S(2)}) collective-permute-start(bf16[256,1024]{1,0:T(8,128)(2,1)S(1)} %get-tuple-element.377), channel_id=1, source_target_pairs={{0,1},{1,0},{2,3},{3,2},{4,5},{5,4},{6,7},{7,6},{8,9},{9,8},{10,11... | collective-permute-start | bytes 1572872 | tf_op jit(solution)/shard_map/ppermute | solution.py:56
  114.9 7.6 %collective-permute-start.25 = (bf16[256,1024]{1,0:T(8,128)(2,1)S(1)}, bf16[256,1024]{1,0:T(8,128)(2,1)S(1)}, u32[]{:S(2)}, u32[]{:S(2)}) collective-permute-start(bf16[256,1024]{1,0:T(8,128)(2,1)S(1)} %get-tuple-element.378), channel_id=1, source_target_pairs={{0,1},{1,0},{2,3},{3,2},{4,5},{5,4},{6,7},{7,6},{8,9},{9,8},{10,11... | collective-permute-start | bytes 1572872 | tf_op jit(solution)/shard_map/ppermute | solution.py:56
  115.4 7.1 %collective-permute-start.23 = (bf16[256,1024]{1,0:T(8,128)(2,1)S(1)}, bf16[256,1024]{1,0:T(8,128)(2,1)S(1)}, u32[]{:S(2)}, u32[]{:S(2)}) collective-permute-start(bf16[256,1024]{1,0:T(8,128)(2,1)S(1)} %get-tuple-element.380), channel_id=1, source_target_pairs={{0,1},{1,0},{2,3},{3,2},{4,5},{5,4},{6,7},{7,6},{8,9},{9,8},{10,11... | collective-permute-start | bytes 1572872 | tf_op jit(solution)/shard_map/ppermute | solution.py:56
  122.6 41.2 %collective-permute-start.27 = (bf16[2,1,2,2,64,1024]{5,4,3,2,0,1:T(8,128)(2,1)}, bf16[2,1,2,2,64,1024]{5,4,3,2,0,1:T(8,128)(2,1)}, u32[]{:S(2)}, u32[]{:S(2)}) collective-permute-start(bf16[2,1,2,2,64,1024]{5,4,3,2,0,1:T(8,128)(2,1)} %bitcast.72), channel_id=1, source_target_pairs={{0,16},{16,0},{1,17},{17,1},{2,18},{18,2},{3,19},{19,3},{4,20},{20... | collective-permute-start | bytes 3145736 | tf_op jit(solution)/shard_map/ppermute | solution.py:56
  123.6 40.1 %collective-permute-start.29 = (bf16[4,64,1408]{2,1,0:T(8,128)(2,1)S(1)}, bf16[4,64,1408]{2,1,0:T(8,128)(2,1)S(1)}, u32[]{:S(2)}, u32[]{:S(2)}) collective-permute-start(bf16[4,64,1408]{2,1,0:T(8,128)(2,1)S(1)} %get-tuple-element.233.refs_0_.refs_8_), channel_id=1, source_target_pairs={{0,16},{16,0},{1,17},{17,1},{2,18},{18,2},{3,19},{19,3},{4,20},{20... | collective-permute-start | bytes 2162696 | tf_op jit(solution)/shard_map/ppermute | solution.py:56
  124.7 39.0 %collective-permute-start.28 = (bf16[4,64,1408]{2,1,0:T(8,128)(2,1)S(1)}, bf16[4,64,1408]{2,1,0:T(8,128)(2,1)}, u32[]{:S(2)}, u32[]{:S(2)}) collective-permute-start(bf16[4,64,1408]{2,1,0:T(8,128)(2,1)S(1)} %get-tuple-element.233.refs_0_.refs_8_), channel_id=1, source_target_pairs={{0,8},{8,0},{1,9},{9,1},{2,10},{10,2},{3,11},{11,3},{4,12},{12,4},... | collective-permute-start | bytes 2162696 | tf_op jit(solution)/shard_map/ppermute | solution.py:56
  167.1 19.0 %collective-permute-start.36 = (bf16[4,64,1408]{2,1,0:T(8,128)(2,1)S(1)}, bf16[4,64,1408]{2,1,0:T(8,128)(2,1)S(1)}, u32[]{:S(2)}, u32[]{:S(2)}) collective-permute-start(bf16[4,64,1408]{2,1,0:T(8,128)(2,1)S(1)} %get-tuple-element.237.refs_8_.refs_16_), channel_id=1, source_target_pairs={{0,16},{16,0},{1,17},{17,1},{2,18},{18,2},{3,19},{19,3},{4,20},{20... | collective-permute-start | bytes 2162696 | tf_op jit(solution)/shard_map/ppermute | solution.py:56
  168.1 32.1 %collective-permute-start.35 = (bf16[4,64,1408]{2,1,0:T(8,128)(2,1)S(1)}, bf16[4,64,1408]{2,1,0:T(8,128)(2,1)S(1)}, u32[]{:S(2)}, u32[]{:S(2)}) collective-permute-start(bf16[4,64,1408]{2,1,0:T(8,128)(2,1)S(1)} %get-tuple-element.237.refs_8_.refs_16_), channel_id=1, source_target_pairs={{0,8},{8,0},{1,9},{9,1},{2,10},{10,2},{3,11},{11,3},{4,12},{12,4},... | collective-permute-start | bytes 2162696 | tf_op jit(solution)/shard_map/ppermute | solution.py:56
  173.6 27.2 %collective-permute-start.37 = (bf16[4,64,1408]{2,1,0:T(8,128)(2,1)}, bf16[4,64,1408]{2,1,0:T(8,128)(2,1)}, u32[]{:S(2)}, u32[]{:S(2)}) collective-permute-start(bf16[4,64,1408]{2,1,0:T(8,128)(2,1)} %collective-permute-done.28.refs_1_.refs_9_), channel_id=1, source_target_pairs={{0,16},{16,0},{1,17},{17,1},{2,18},{18,2},{3,19},{19,3},{4,20},{20... | collective-permute-start | bytes 2162696 | tf_op jit(solution)/shard_map/ppermute | solution.py:56
  174.6 25.5 %collective-permute-start.34 = (bf16[128,2048]{1,0:T(8,128)(2,1)S(1)}, bf16[128,2048]{1,0:T(8,128)(2,1)}, u32[]{:S(2)}, u32[]{:S(2)}) collective-permute-start(bf16[128,2048]{1,0:T(8,128)(2,1)S(1)} %slice.548), channel_id=1, source_target_pairs={{0,2},{2,0},{1,3},{3,1},{4,6},{6,4},{5,7},{7,5},{8,10},{10,8},{9,1... | collective-permute-start | bytes 1572872 | tf_op jit(solution)/shard_map/ppermute | solution.py:56
  204.3 47.3 %all-to-all-start.1 = ((bf16[4,128,2048]{2,1,0:T(8,128)(2,1)}), bf16[4,128,2048]{2,1,0:T(8,128)(2,1)S(1)}, u32[]{:S(2)}, u32[]{:S(2)}) async-start(bf16[4,128,2048]{2,1,0:T(8,128)(2,1)} %broadcast_in_dim.21), calls=%async_computation.1 | async-start | bytes 4194304 | tf_op jit(solution)/shard_map/all_to_all | solution.py:104
  207.9 19.3 %collective-permute-start.38 = (bf16[4,64,1408]{2,1,0:T(8,128)(2,1)}, bf16[4,64,1408]{2,1,0:T(8,128)(2,1)S(1)}, u32[]{:S(2)}, u32[]{:S(2)}) collective-permute-start(bf16[4,64,1408]{2,1,0:T(8,128)(2,1)} %copy-done.37), channel_id=1, source_target_pairs={{0,16},{16,0},{1,17},{17,1},{2,18},{18,2},{3,19},{19,3},{4,20},{20... | collective-permute-start | bytes 2162696 | tf_op jit(solution)/shard_map/ppermute | solution.py:56
  208.9 32.4 %collective-permute-start.40 = (bf16[4,64,1408]{2,1,0:T(8,128)(2,1)}, bf16[4,64,1408]{2,1,0:T(8,128)(2,1)S(1)}, u32[]{:S(2)}, u32[]{:S(2)}) collective-permute-start(bf16[4,64,1408]{2,1,0:T(8,128)(2,1)} %get-tuple-element.232.refs_0_), channel_id=1, source_target_pairs={{0,16},{16,0},{1,17},{17,1},{2,18},{18,2},{3,19},{19,3},{4,20},{20... | collective-permute-start | bytes 2162696 | tf_op jit(solution)/shard_map/ppermute | solution.py:56
  210.0 36.2 %collective-permute-start.39 = (bf16[4,64,1408]{2,1,0:T(8,128)(2,1)}, bf16[4,64,1408]{2,1,0:T(8,128)(2,1)S(1)}, u32[]{:S(2)}, u32[]{:S(2)}) collective-permute-start(bf16[4,64,1408]{2,1,0:T(8,128)(2,1)} %get-tuple-element.232.refs_0_), channel_id=1, source_target_pairs={{0,8},{8,0},{1,9},{9,1},{2,10},{10,2},{3,11},{11,3},{4,12},{12,4},... | collective-permute-start | bytes 2162696 | tf_op jit(solution)/shard_map/ppermute | solution.py:56
  227.2 19.0 %collective-permute-start.41 = (bf16[4,64,1408]{2,1,0:T(8,128)(2,1)}, bf16[4,64,1408]{2,1,0:T(8,128)(2,1)S(1)}, u32[]{:S(2)}, u32[]{:S(2)}) collective-permute-start(bf16[4,64,1408]{2,1,0:T(8,128)(2,1)} %copy-done.19), channel_id=1, source_target_pairs={{0,1},{1,0},{2,3},{3,2},{4,5},{5,4},{6,7},{7,6},{8,9},{9,8},{10,11... | collective-permute-start | bytes 2162696 | tf_op jit(solution)/shard_map/ppermute | solution.py:56
  227.2 19.5 %collective-permute-start.42 = (bf16[4,64,1408]{2,1,0:T(8,128)(2,1)}, bf16[4,64,1408]{2,1,0:T(8,128)(2,1)S(1)}, u32[]{:S(2)}, u32[]{:S(2)}) collective-permute-start(bf16[4,64,1408]{2,1,0:T(8,128)(2,1)} %collective-permute-done.28.refs_1_.refs_9_), channel_id=1, source_target_pairs={{0,1},{1,0},{2,3},{3,2},{4,5},{5,4},{6,7},{7,6},{8,9},{9,8},{10,11... | collective-permute-start | bytes 2162696 | tf_op jit(solution)/shard_map/ppermute | solution.py:56
  227.7 19.1 %collective-permute-start.43 = (bf16[4,64,1408]{2,1,0:T(8,128)(2,1)}, bf16[4,64,1408]{2,1,0:T(8,128)(2,1)S(1)}, u32[]{:S(2)}, u32[]{:S(2)}) collective-permute-start(bf16[4,64,1408]{2,1,0:T(8,128)(2,1)} %copy-done.35), channel_id=1, source_target_pairs={{0,1},{1,0},{2,3},{3,2},{4,5},{5,4},{6,7},{7,6},{8,9},{9,8},{10,11... | collective-permute-start | bytes 2162696 | tf_op jit(solution)/shard_map/ppermute | solution.py:56
  256.7 31.4 %all-to-all-start.2 = ((bf16[4,128,2048]{2,1,0:T(8,128)(2,1)}), bf16[4,128,2048]{2,1,0:T(8,128)(2,1)S(1)}, u32[]{:S(2)}, u32[]{:S(2)}) async-start(bf16[4,128,2048]{2,1,0:T(8,128)(2,1)} %broadcast_in_dim.22), calls=%async_computation.2 | async-start | bytes 4194304 | tf_op jit(solution)/shard_map/all_to_all | solution.py:104
  263.0 18.1 %collective-permute-start.50 = (bf16[4,64,1408]{2,1,0:T(8,128)(2,1)}, bf16[4,64,1408]{2,1,0:T(8,128)(2,1)S(1)}, u32[]{:S(2)}, u32[]{:S(2)}) collective-permute-start(bf16[4,64,1408]{2,1,0:T(8,128)(2,1)} %get-tuple-element.232.refs_0_), channel_id=1, source_target_pairs={{0,1},{1,0},{2,3},{3,2},{4,5},{5,4},{6,7},{7,6},{8,9},{9,8},{10,11... | collective-permute-start | bytes 2162696 | tf_op jit(solution)/shard_map/ppermute | solution.py:56
  263.5 17.6 %collective-permute-start.52 = (bf16[4,64,1408]{2,1,0:T(8,128)(2,1)}, bf16[4,64,1408]{2,1,0:T(8,128)(2,1)S(1)}, u32[]{:S(2)}, u32[]{:S(2)}) collective-permute-start(bf16[4,64,1408]{2,1,0:T(8,128)(2,1)} %copy-done.27), channel_id=1, source_target_pairs={{0,1},{1,0},{2,3},{3,2},{4,5},{5,4},{6,7},{7,6},{8,9},{9,8},{10,11... | collective-permute-start | bytes 2162696 | tf_op jit(solution)/shard_map/ppermute | solution.py:56
  263.6 17.5 %collective-permute-start.51 = (bf16[4,64,1408]{2,1,0:T(8,128)(2,1)}, bf16[4,64,1408]{2,1,0:T(8,128)(2,1)S(1)}, u32[]{:S(2)}, u32[]{:S(2)}) collective-permute-start(bf16[4,64,1408]{2,1,0:T(8,128)(2,1)} %copy-done.28), channel_id=1, source_target_pairs={{0,1},{1,0},{2,3},{3,2},{4,5},{5,4},{6,7},{7,6},{8,9},{9,8},{10,11... | collective-permute-start | bytes 2162696 | tf_op jit(solution)/shard_map/ppermute | solution.py:56
  264.0 18.3 %collective-permute-start.48 = (bf16[4,64,1408]{2,1,0:T(8,128)(2,1)}, bf16[4,64,1408]{2,1,0:T(8,128)(2,1)S(1)}, u32[]{:S(2)}, u32[]{:S(2)}) collective-permute-start(bf16[4,64,1408]{2,1,0:T(8,128)(2,1)} %copy-done.28), channel_id=1, source_target_pairs={{0,16},{16,0},{1,17},{17,1},{2,18},{18,2},{3,19},{19,3},{4,20},{20... | collective-permute-start | bytes 2162696 | tf_op jit(solution)/shard_map/ppermute | solution.py:56
  310.2 35.4 %all-to-all-start.3 = ((bf16[4,128,2048]{2,1,0:T(8,128)(2,1)}), bf16[4,128,2048]{2,1,0:T(8,128)(2,1)}, u32[]{:S(2)}, u32[]{:S(2)}) async-start(bf16[4,128,2048]{2,1,0:T(8,128)(2,1)} %bitcast.295), calls=%async_computation.3 | async-start | bytes 4194304 | tf_op jit(solution)/shard_map/all_to_all | solution.py:108
  314.6 228.5 %reduce-scatter.2.cloned.1.call-start = ((), (), s32[]{:S(2)}) async-start(), calls=%async_computation.8 | async-start | bytes 12976128 | tf_op jit(solution)/shard_map/reduce_scatter | solution.py:652
  338.6 9.1 %collective-permute-start.54 = (bf16[1024,1408]{1,0:T(8,128)(2,1)}, bf16[1024,1408]{1,0:T(8,128)(2,1)}, u32[]{:S(2)}, u32[]{:S(2)}) collective-permute-start(bf16[1024,1408]{1,0:T(8,128)(2,1)} %get-tuple-element.265), channel_id=1, source_target_pairs={{0,1},{1,0},{2,3},{3,2},{4,5},{5,4},{6,7},{7,6},{8,9},{9,8},{10,11... | collective-permute-start | bytes 8650760 | tf_op jit(solution)/shard_map/ppermute | solution.py:56
  348.4 16.4 %collective-permute-start.55 = (bf16[128,2048]{1,0:T(8,128)(2,1)S(1)}, bf16[128,2048]{1,0:T(8,128)(2,1)S(1)}, u32[]{:S(2)}, u32[]{:S(2)}) collective-permute-start(bf16[128,2048]{1,0:T(8,128)(2,1)S(1)} %fusion.54), channel_id=1, source_target_pairs={{0,2},{2,0},{1,3},{3,1},{4,6},{6,4},{5,7},{7,5},{8,10},{10,8},{9,1... | collective-permute-start | bytes 1572872 | tf_op jit(solution)/shard_map/ppermute | solution.py:56
  365.6 52.7 %all-to-all-start.4 = ((bf16[4,128,2048]{2,1,0:T(8,128)(2,1)}), bf16[4,128,2048]{2,1,0:T(8,128)(2,1)}, u32[]{:S(2)}, u32[]{:S(2)}) async-start(bf16[4,128,2048]{2,1,0:T(8,128)(2,1)} %bitcast.273), calls=%async_computation.4 | async-start | bytes 4194304 | tf_op jit(solution)/shard_map/all_to_all | solution.py:108
  394.4 13.2 %collective-permute-start.60 = (bf16[2,1,2,128,256]{4,3,2,1,0:T(8,128)(2,1)S(1)}, bf16[2,1,2,128,256]{4,3,2,1,0:T(8,128)(2,1)S(1)}, u32[]{:S(2)}, u32[]{:S(2)}) collective-permute-start(bf16[2,1,2,128,256]{4,3,2,1,0:T(8,128)(2,1)S(1)} %slice.549), channel_id=1, source_target_pairs={{0,2},{2,0},{1,3},{3,1},{4,6},{6,4},{5,7},{7,5},{8,10},{10,8},{9,1... | collective-permute-start | bytes 786440 | tf_op jit(solution)/shard_map/ppermute | solution.py:56
  396.5 9.2 %collective-permute-start.61 = (bf16[256,1024]{1,0:T(8,128)(2,1)S(1)}, bf16[256,1024]{1,0:T(8,128)(2,1)S(1)}, u32[]{:S(2)}, u32[]{:S(2)}) collective-permute-start(bf16[256,1024]{1,0:T(8,128)(2,1)S(1)} %get-tuple-element.366), channel_id=1, source_target_pairs={{0,1},{1,0},{2,3},{3,2},{4,5},{5,4},{6,7},{7,6},{8,9},{9,8},{10,11... | collective-permute-start | bytes 1572872 | tf_op jit(solution)/shard_map/ppermute | solution.py:56
  396.6 10.8 %collective-permute-start.64 = (bf16[256,1024]{1,0:T(8,128)(2,1)S(1)}, bf16[256,1024]{1,0:T(8,128)(2,1)S(1)}, u32[]{:S(2)}, u32[]{:S(2)}) collective-permute-start(bf16[256,1024]{1,0:T(8,128)(2,1)S(1)} %get-tuple-element.367), channel_id=1, source_target_pairs={{0,1},{1,0},{2,3},{3,2},{4,5},{5,4},{6,7},{7,6},{8,9},{9,8},{10,11... | collective-permute-start | bytes 1572872 | tf_op jit(solution)/shard_map/ppermute | solution.py:56
  397.1 10.3 %collective-permute-start.63 = (bf16[256,1024]{1,0:T(8,128)(2,1)S(1)}, bf16[256,1024]{1,0:T(8,128)(2,1)S(1)}, u32[]{:S(2)}, u32[]{:S(2)}) collective-permute-start(bf16[256,1024]{1,0:T(8,128)(2,1)S(1)} %get-tuple-element.368), channel_id=1, source_target_pairs={{0,1},{1,0},{2,3},{3,2},{4,5},{5,4},{6,7},{7,6},{8,9},{9,8},{10,11... | collective-permute-start | bytes 1572872 | tf_op jit(solution)/shard_map/ppermute | solution.py:56
  397.2 10.3 %collective-permute-start.62 = (bf16[256,1024]{1,0:T(8,128)(2,1)S(1)}, bf16[256,1024]{1,0:T(8,128)(2,1)S(1)}, u32[]{:S(2)}, u32[]{:S(2)}) collective-permute-start(bf16[256,1024]{1,0:T(8,128)(2,1)S(1)} %get-tuple-element.369), channel_id=1, source_target_pairs={{0,1},{1,0},{2,3},{3,2},{4,5},{5,4},{6,7},{7,6},{8,9},{9,8},{10,11... | collective-permute-start | bytes 1572872 | tf_op jit(solution)/shard_map/ppermute | solution.py:56
  405.7 25.3 %collective-permute-start.68 = (bf16[256,1408]{1,0:T(8,128)(2,1)}, bf16[256,1408]{1,0:T(8,128)(2,1)S(1)}, u32[]{:S(2)}, u32[]{:S(2)}) collective-permute-start(bf16[256,1408]{1,0:T(8,128)(2,1)} %add_convert_fusion.3), channel_id=1, source_target_pairs={{0,16},{16,0},{1,17},{17,1},{2,18},{18,2},{3,19},{19,3},{4,20},{20... | collective-permute-start | bytes 2162696 | tf_op jit(solution)/shard_map/ppermute | solution.py:56
  408.3 15.5 %collective-permute-start.65 = (bf16[1,2,128,256]{3,2,1,0:T(8,128)(2,1)}, bf16[1,2,128,256]{3,2,1,0:T(8,128)(2,1)}, u32[]{:S(2)}, u32[]{:S(2)}) collective-permute-start(bf16[1,2,128,256]{3,2,1,0:T(8,128)(2,1)} %fusion.35), channel_id=1, source_target_pairs={{0,4},{4,0},{1,5},{5,1},{2,6},{6,2},{3,7},{7,3},{8,12},{12,8},{9,1... | collective-permute-start | bytes 393224 | tf_op jit(solution)/shard_map/ppermute | solution.py:56
  423.9 13.9 %collective-permute-start.67 = (bf16[128,2048]{1,0:T(8,128)(2,1)S(1)}, bf16[128,2048]{1,0:T(8,128)(2,1)S(1)}, u32[]{:S(2)}, u32[]{:S(2)}) collective-permute-start(bf16[128,2048]{1,0:T(8,128)(2,1)S(1)} %slice.547), channel_id=1, source_target_pairs={{0,2},{2,0},{1,3},{3,1},{4,6},{6,4},{5,7},{7,5},{8,10},{10,8},{9,1... | collective-permute-start | bytes 1572872 | tf_op jit(solution)/shard_map/ppermute | solution.py:56
  426.4 8.0 %collective-permute-start.66 = (bf16[1,128,256]{2,1,0:T(8,128)(2,1)S(1)}, bf16[1,128,256]{2,1,0:T(8,128)(2,1)S(1)}, u32[]{:S(2)}, u32[]{:S(2)}) collective-permute-start(bf16[1,128,256]{2,1,0:T(8,128)(2,1)S(1)} %fusion.39), channel_id=1, source_target_pairs={{0,8},{8,0},{1,9},{9,1},{2,10},{10,2},{3,11},{11,3},{4,12},{12,4},... | collective-permute-start | bytes 196616 | tf_op jit(solution)/shard_map/ppermute | solution.py:56
  431.0 38.9 %collective-permute-start.73 = (bf16[2,2,1,2,64,1024]{5,4,1,0,3,2:T(8,128)(2,1)}, bf16[2,2,1,2,64,1024]{5,4,1,0,3,2:T(8,128)(2,1)}, u32[]{:S(2)}, u32[]{:S(2)}) collective-permute-start(bf16[2,2,1,2,64,1024]{5,4,1,0,3,2:T(8,128)(2,1)} %fusion.22), channel_id=1, source_target_pairs={{0,4},{4,0},{1,5},{5,1},{2,6},{6,2},{3,7},{7,3},{8,12},{12,8},{9,1... | collective-permute-start | bytes 3145736 | tf_op jit(solution)/shard_map/ppermute | solution.py:56
  451.3 28.8 %collective-permute-start.76 = (bf16[256,1408]{1,0:T(8,128)(2,1)}, bf16[256,1408]{1,0:T(8,128)(2,1)}, u32[]{:S(2)}, u32[]{:S(2)}) collective-permute-start(bf16[256,1408]{1,0:T(8,128)(2,1)} %get-tuple-element.361), channel_id=1, source_target_pairs={{0,16},{16,0},{1,17},{17,1},{2,18},{18,2},{3,19},{19,3},{4,20},{20... | collective-permute-start | bytes 2162696 | tf_op jit(solution)/shard_map/ppermute | solution.py:56
  472.3 14.2 %collective-permute-start.75 = (bf16[2,2,1,64,1024]{4,3,1,0,2:T(8,128)(2,1)}, bf16[2,2,1,64,1024]{4,3,1,0,2:T(8,128)(2,1)}, u32[]{:S(2)}, u32[]{:S(2)}) collective-permute-start(bf16[2,2,1,64,1024]{4,3,1,0,2:T(8,128)(2,1)} %fusion.27), channel_id=1, source_target_pairs={{0,2},{2,0},{1,3},{3,1},{4,6},{6,4},{5,7},{7,5},{8,10},{10,8},{9,1... | collective-permute-start | bytes 1572872 | tf_op jit(solution)/shard_map/ppermute | solution.py:56
  477.1 45.9 %collective-permute-start.74 = (bf16[2,2,1,2,64,1408]{5,4,1,0,3,2:T(8,128)(2,1)}, bf16[2,2,1,2,64,1408]{5,4,1,0,3,2:T(8,128)(2,1)}, u32[]{:S(2)}, u32[]{:S(2)}) collective-permute-start(bf16[2,2,1,2,64,1408]{5,4,1,0,3,2:T(8,128)(2,1)} %fusion.8), channel_id=1, source_target_pairs={{0,4},{4,0},{1,5},{5,1},{2,6},{6,2},{3,7},{7,3},{8,12},{12,8},{9,1... | collective-permute-start | bytes 4325384 | tf_op jit(solution)/shard_map/ppermute | solution.py:56
  491.4 13.3 %collective-permute-start.77 = (bf16[2,1,64,2048]{3,2,0,1:T(8,128)(2,1)}, bf16[2,1,64,2048]{3,2,0,1:T(8,128)(2,1)}, u32[]{:S(2)}, u32[]{:S(2)}) collective-permute-start(bf16[2,1,64,2048]{3,2,0,1:T(8,128)(2,1)} %convert_element_type.356), channel_id=1, source_target_pairs={{0,16},{16,0},{1,17},{17,1},{2,18},{18,2},{3,19},{19,3},{4,20},{20... | collective-permute-start | bytes 1572872 | tf_op jit(solution)/shard_map/ppermute | solution.py:56
  494.3 35.8 %collective-permute-start.80 = (bf16[256,1408]{1,0:T(8,128)(2,1)}, bf16[256,1408]{1,0:T(8,128)(2,1)S(1)}, u32[]{:S(2)}, u32[]{:S(2)}) collective-permute-start(bf16[256,1408]{1,0:T(8,128)(2,1)} %get-tuple-element.360), channel_id=1, source_target_pairs={{0,8},{8,0},{1,9},{9,1},{2,10},{10,2},{3,11},{11,3},{4,12},{12,4},... | collective-permute-start | bytes 2162696 | tf_op jit(solution)/shard_map/ppermute | solution.py:56
  525.5 17.6 %collective-permute-start.78 = (bf16[2,2,1,64,1408]{4,3,1,0,2:T(8,128)(2,1)S(1)}, bf16[2,2,1,64,1408]{4,3,1,0,2:T(8,128)(2,1)}, u32[]{:S(2)}, u32[]{:S(2)}) collective-permute-start(bf16[2,2,1,64,1408]{4,3,1,0,2:T(8,128)(2,1)S(1)} %fusion.23), channel_id=1, source_target_pairs={{0,2},{2,0},{1,3},{3,1},{4,6},{6,4},{5,7},{7,5},{8,10},{10,8},{9,1... | collective-permute-start | bytes 2162696 | tf_op jit(solution)/shard_map/ppermute | solution.py:56
  529.1 13.2 %collective-permute-start.79 = (bf16[1,64,2048]{2,1,0:T(8,128)(2,1)S(1)}, bf16[1,64,2048]{2,1,0:T(8,128)(2,1)}, u32[]{:S(2)}, u32[]{:S(2)}) collective-permute-start(bf16[1,64,2048]{2,1,0:T(8,128)(2,1)S(1)} %fusion.31), channel_id=1, source_target_pairs={{0,8},{8,0},{1,9},{9,1},{2,10},{10,2},{3,11},{11,3},{4,12},{12,4},... | collective-permute-start | bytes 786440 | tf_op jit(solution)/shard_map/ppermute | solution.py:56
  546.0 15.9 %collective-permute-start.81 = (bf16[2,1,64,2432]{3,2,0,1:T(8,128)(2,1)}, bf16[2,1,64,2432]{3,2,0,1:T(8,128)(2,1)}, u32[]{:S(2)}, u32[]{:S(2)}) collective-permute-start(bf16[2,1,64,2432]{3,2,0,1:T(8,128)(2,1)} %fusion.24), channel_id=1, source_target_pairs={{0,16},{16,0},{1,17},{17,1},{2,18},{18,2},{3,19},{19,3},{4,20},{20... | collective-permute-start | bytes 1867784 | tf_op jit(solution)/shard_map/ppermute | solution.py:56
  550.1 25.2 %all-to-all-start.5 = ((bf16[4,2,64,1408]{3,2,1,0:T(8,128)(2,1)}), bf16[4,2,64,1408]{3,2,1,0:T(8,128)(2,1)S(1)}, u32[]{:S(2)}, u32[]{:S(2)}) async-start(bf16[4,2,64,1408]{3,2,1,0:T(8,128)(2,1)} %bitcast.276), calls=%async_computation.6 | async-start | bytes 2883584 | tf_op jit(solution)/shard_map/all_to_all | solution.py:780
  563.9 21.3 %collective-permute-start.82 = (bf16[1,64,2432]{2,1,0:T(8,128)(2,1)}, bf16[1,64,2432]{2,1,0:T(8,128)(2,1)}, u32[]{:S(2)}, u32[]{:S(2)}) collective-permute-start(bf16[1,64,2432]{2,1,0:T(8,128)(2,1)} %fusion.30), channel_id=1, source_target_pairs={{0,8},{8,0},{1,9},{9,1},{2,10},{10,2},{3,11},{11,3},{4,12},{12,4},... | collective-permute-start | bytes 933896 | tf_op jit(solution)/shard_map/ppermute | solution.py:56
  579.9 11.9 %all-to-all-start.6 = ((bf16[4,1,64,1408]{3,2,1,0:T(8,128)(2,1)}), bf16[4,1,64,1408]{3,2,1,0:T(8,128)(2,1)S(1)}, u32[]{:S(2)}, u32[]{:S(2)}) async-start(bf16[4,1,64,1408]{3,2,1,0:T(8,128)(2,1)} %bitcast.289), calls=%async_computation.7 | async-start | bytes 1441792 | tf_op jit(solution)/shard_map/all_to_all | solution.py:780
  (114 other events, 892.8 us)
Sparse Core Ops, SparseCore 0:
  341.9 137.0 reduce-scatter.1

commit v7 on v6

--- a/solution.py
+++ b/solution.py
@@ -100,8 +100,12 @@
     return total[:half].astype(F32) + swap(low(total[half:]), axis).astype(F32)
 
 
-def gather_group(value):
-    return lax.all_to_all(jnp.broadcast_to(value, (4, *value.shape)), ("l", "x"), 0, 0)
+def four_of(value):
+    return jnp.broadcast_to(value, (4, *value.shape))
+
+
+def gather_group(copies):
+    return lax.all_to_all(copies, ("l", "x"), 0, 0)
 
 
 def scatter_group(value):
@@ -568,8 +572,8 @@
         ],
         normed_one_low, query_part, *query_c, gathered, cosine_t, sine_t, *places_used,
     )
-    attended_low, output_y, output_part, gate_h, gate_y = sync(
-        attended_low, output_y, output_part, gate_h, gate_y
+    attended_low, output_y, output_part, gate_h, gate_y, grad_mine, grad_copies = sync(
+        attended_low, output_y, output_part, gate_h, gate_y, grad_mine, four_of(grad_mine)
     )
     output_part = jnp.stack([output_part, output_y]).reshape(-1, half_width)
     output_c = swap_core(output_part)
@@ -582,8 +586,8 @@
     )
     branch, gate_h = sync(branch, gate_h)
     gate_far = swap(gate_h, "y")
-    branch_x, up_h, up_y, gate_far, grad_mine = sync(
-        swap(low(branch[tokens:]), "x"), up_h, up_y, gate_far, grad_mine
+    branch_x, up_h, up_y, gate_far = sync(
+        swap(low(branch[tokens:]), "x"), up_h, up_y, gate_far
     )
     hidden = inputs + (branch[:tokens] + branch_x.astype(F32))
 
@@ -592,13 +596,13 @@
     scale_two = lax.rsqrt(jnp.mean(hidden * hidden, axis=-1, keepdims=True) + EPSILON)
     normed_two = hidden * scale_two
     normed_two_low = low(normed_two * gain_two)
-    normed_two_low = gather_group(normed_two_low).reshape(-1, width)
+    normed_two_low = gather_group(four_of(normed_two_low)).reshape(-1, width)
     up_far, *sent = sync(up_far, gate, gate_h, gate_y, gate_far, up, up_h, up_y)
     near_c = [swap(piece, "c") for piece in sent]
     normed_two_low, down_h, down_y, *near_c = sync(normed_two_low, down_h, down_y, *near_c)
     down_far = swap(down_h, "y")
     gate_c = near_c[:4]
-    up_sent, grad_sent = sync(up_far, grad_mine, normed_two_low)[:2]
+    up_sent, grad_sent = sync(up_far, grad_copies, normed_two_low)[:2]
     late_c = [swap(up_sent, "c")]
     up_c = near_c[4:] + late_c
     grad_low = gather_group(grad_sent).reshape(-1, width)

time: 610 us -> 608 us (level)
    unnamed x188 -> x190, local copies, waits for them, and re-layouts: 22.1 us -> 23.8 us
  transfers between devices with their start and end apart: 91 -> 91, of which waited for: 34 -> 34; matrix products, arithmetic and copies ran while one was open for 19% -> 19% of each run, Pallas kernels for 15% -> 16%
where the time goes in v7:
time: 608 us; the launch traced here: 601 us
  waiting for transfers between devices  213 us (35%)
  Pallas kernels  117 us (19%)
  starting transfers between devices  111 us (18%)
  other arithmetic  69 us (11%)
  local copies, waits for them, and re-layouts  63 us (10%)
  between operations  16.4 us (3%)
  matrix products  12 us (2%)
    ppermute x83, waiting for transfers between devices, swap(): return lax.ppermute(value, axis, [(0, 1), (1, 0)])  192 us
    pallas_call x7, Pallas kernels, local_call(): pl.pallas_call(kernel, out_shape=outs, in_specs=near + [pl.BlockSpec(memo...  103 us
    ppermute x83, starting transfers between devices, swap(): return lax.ppermute(value, axis, [(0, 1), (1, 0)])  67.6 us
    unnamed x190, local copies, waits for them, and re-layouts  23.8 us
    all_to_all x1, starting transfers between devices, on_device(): feed = gather_m(lax.all_to_all(feed_parts, ('l', 'x'), 0, 0), 0)  17 us
  transfers between devices with their start and end apart: 91, of which 34 were waited for; matrix products, arithmetic and copies ran while one was open for 19% of the time, Pallas kernels for 16%

profile of v7, /device:TPU:0, one launch (start us, length us, event | category | flops | bytes accessed | tf_op | source)
XLA Modules:
  0.0 601.1 jit_solution(5559342939264917253)
XLA Ops:
  8.7 2.9 collective-permute-start
  28.1 3.8 shard_map.212
  32.0 6.4 %collective-permute-done.3 = bf16[2,80,256]{2,1,0:T(8,128)(2,1)S(1)} collective-permute-done((bf16[2,80,256]{2,1,0:T(8,128)(2,1)S(1)}, bf16[2,80,256]{2,1,0:T(8,128)(2,1)S(1)}, u32[]{:S(2)}, u32[]{:S(2)}) %collective-permute-start.3) | collective-permute-done | bytes 81952 | tf_op jit(solution)/shard_map/ppermute | solution.py:56
  39.2 2.8 collective-permute-start.7
  43.0 4.9 collective-permute-done.7
  50.2 17.0 %all-to-all-start = ((bf16[4,3,64,1408]{3,2,1,0:T(8,128)(2,1)}), bf16[4,3,64,1408]{3,2,1,0:T(8,128)(2,1)}, u32[]{:S(2)}, u32[]{:S(2)}) async-start(bf16[4,3,64,1408]{3,2,1,0:T(8,128)(2,1)} %shard_map.212), calls=%async_computation | async-start | bytes 4325376 | tf_op jit(solution)/shard_map/all_to_all | solution.py:498
  74.5 10.7 %collective-permute-done.14 = bf16[128,256]{1,0:T(8,128)(2,1)S(1)} collective-permute-done((bf16[128,256]{1,0:T(8,128)(2,1)S(1)}, bf16[128,256]{1,0:T(8,128)(2,1)S(1)}, u32[]{:S(2)}, u32[]{:S(2)}) %collective-permute-start.14) | collective-permute-done | bytes 65568 | tf_op jit(solution)/shard_map/ppermute | solution.py:56
  85.3 9.9 %collective-permute-start.15 = (bf16[1,2,128,256]{3,2,1,0:T(8,128)(2,1)S(1)}, bf16[1,2,128,256]{3,2,1,0:T(8,128)(2,1)S(1)}, u32[]{:S(2)}, u32[]{:S(2)}) collective-permute-start(bf16[1,2,128,256]{3,2,1,0:T(8,128)(2,1)S(1)} %maximum_bitcast_fusion), channel_id=1, source_target_pairs={{0,4},{4,0},{1,5},{5,1},{2,6},{6,2},{3,7},{7,3},{8,12},{12,8},{9,1... | collective-permute-start | bytes 393224 | tf_op jit(solution)/shard_map/ppermute | solution.py:56
  98.8 2.6 slice_bitcast_fusion.5
  104.1 8.1 %collective-permute-done.18 = bf16[1,2,2,64,1024]{4,3,2,1,0:T(8,128)(2,1)} collective-permute-done((bf16[1,2,2,64,1024]{4,3,2,1,0:T(8,128)(2,1)}, bf16[1,2,2,64,1024]{4,3,2,1,0:T(8,128)(2,1)}, u32[]{:S(2)}, u32[]{:S(2)}) %collective-permute-start.18) | collective-permute-done | bytes 524320 | tf_op jit(solution)/shard_map/ppermute | solution.py:56
  116.0 3.2 collective-permute-done.21
  119.4 2.3 pad_maximum_fusion.9
  127.5 2.1 pad_maximum_fusion.10
  129.6 15.6 %shard_map.213 = (bf16[1024,256]{1,0:T(8,128)(2,1)}, f32[1024,256]{1,0:T(8,128)}, bf16[1024,256]{1,0:T(8,128)(2,1)}, f32[8,256]{1,0:T(8,128)}) custom-call(bf16[256,2048]{1,0:T(8,128)(2,1)} %pad_maximum_fusion.7.normed, bf16[1024,1024]{1,0:T(8,128)(2,1)} %bitcast.255, bf16[256,1024]{1,0:T(8,128)(2,1)} %copy-done.52, bf16[256,1024]{1,0:T(8,128)(2,1)} %copy-done.50, ...), custom_call_target="tpu_custom_call" | custom-call | flops 1 | bytes 1 | tf_op jit(solution)/shard_map/pallas_call | solution.py:385
  145.2 18.6 %collective-permute-done.29.refs_2_.refs_10_ = bf16[4,64,1408]{2,1,0:T(8,128)(2,1)} collective-permute-done((bf16[4,64,1408]{2,1,0:T(8,128)(2,1)S(1)}, bf16[4,64,1408]{2,1,0:T(8,128)(2,1)}, u32[]{:S(2)}, u32[]{:S(2)}) %collective-permute-start.29) | collective-permute-done | bytes 720928 | tf_op jit(solution)/shard_map/ppermute | solution.py:56
  178.8 8.8 %collective-permute-done.36.refs_10_.refs_18_ = bf16[4,64,1408]{2,1,0:T(8,128)(2,1)S(1)} collective-permute-done((bf16[4,64,1408]{2,1,0:T(8,128)(2,1)S(1)}, bf16[4,64,1408]{2,1,0:T(8,128)(2,1)S(1)}, u32[]{:S(2)}, u32[]{:S(2)}) %collective-permute-start.36) | collective-permute-done | bytes 720928 | tf_op jit(solution)/shard_map/ppermute | solution.py:56
  187.5 14.1 %collective-permute-done.35.refs_9_.refs_17_ = bf16[4,64,1408]{2,1,0:T(8,128)(2,1)S(1)} collective-permute-done((bf16[4,64,1408]{2,1,0:T(8,128)(2,1)S(1)}, bf16[4,64,1408]{2,1,0:T(8,128)(2,1)S(1)}, u32[]{:S(2)}, u32[]{:S(2)}) %collective-permute-start.35) | collective-permute-done | bytes 720928 | tf_op jit(solution)/shard_map/ppermute | solution.py:56
  205.7 3.6 all-to-all-start.1
  213.3 15.3 %collective-permute-done.38.refs_11_.refs_19_ = bf16[4,64,1408]{2,1,0:T(8,128)(2,1)S(1)} collective-permute-done((bf16[4,64,1408]{2,1,0:T(8,128)(2,1)}, bf16[4,64,1408]{2,1,0:T(8,128)(2,1)S(1)}, u32[]{:S(2)}, u32[]{:S(2)}) %collective-permute-start.38) | collective-permute-done | bytes 720928 | tf_op jit(solution)/shard_map/ppermute | solution.py:56
  229.2 13.6 %collective-permute-done.40.refs_2_ = bf16[4,64,1408]{2,1,0:T(8,128)(2,1)S(1)} collective-permute-done((bf16[4,64,1408]{2,1,0:T(8,128)(2,1)}, bf16[4,64,1408]{2,1,0:T(8,128)(2,1)S(1)}, u32[]{:S(2)}, u32[]{:S(2)}) %collective-permute-start.40) | collective-permute-done | bytes 720928 | tf_op jit(solution)/shard_map/ppermute | solution.py:56
  242.8 4.9 collective-permute-done.39.refs_1_
  254.4 6.2 %all-to-all-start.2 = ((bf16[4,128,2048]{2,1,0:T(8,128)(2,1)}), bf16[4,128,2048]{2,1,0:T(8,128)(2,1)S(1)}, u32[]{:S(2)}, u32[]{:S(2)}) async-start(bf16[4,128,2048]{2,1,0:T(8,128)(2,1)} %broadcast_in_dim.21), calls=%async_computation.2 | async-start | bytes 4194304 | tf_op jit(solution)/shard_map/all_to_all | solution.py:108
  264.3 14.6 %shard_map.214 = (f32[512,1408]{1,0:T(8,128)}, f32[512,1408]{1,0:T(8,128)}) custom-call(bf16[512,2048]{1,0:T(8,128)(2,1)} %bitcast.259, bf16[4,64,1408]{2,1,0:T(8,128)(2,1)} %copy-done.19, bf16[4,64,1408]{2,1,0:T(8,128)(2,1)} %collective-permute-done.28.refs_1_.refs_9_, bf16[4,64,1408]{2,1,0:T(8,128)(2,1)} %collective-permute-done.29.refs_2_.refs_10_, ...), custom_call_target="tpu_custom_call" | custom-call | flops 1 | bytes 1 | tf_op jit(solution)/shard_map/pallas_call | solution.py:385
  282.4 3.4 all-to-all-done.2
  287.3 20.7 %shard_map.215 = (bf16[512,1408]{1,0:T(8,128)(2,1)}, bf16[512,1408]{1,0:T(8,128)(2,1)}, bf16[512,1408]{1,0:T(8,128)(2,1)}, bf16[512,2048]{1,0:T(8,128)(2,1)}) custom-call(bf16[512,2048]{1,0:T(8,128)(2,1)} %bitcast.257, f32[512,1408]{1,0:T(8,128)} %get-tuple-element.255.gate_sum, f32[512,1408]{1,0:T(8,128)} %get-tuple-element.256.up_sum, ...), custom_call_target="tpu_custom_call" | custom-call | flops 1 | bytes 1 | tf_op jit(solution)/shard_map/pallas_call | solution.py:385
  307.9 4.5 all-to-all-start.3
  313.1 14.9 %shard_map.216 = bf16[8,2,256,1408]{3,2,1,0:T(8,128)(2,1)} custom-call(s32[8]{0:T(128)} %stack.417.order, bf16[512,2048]{1,0:T(8,128)(2,1)} %bitcast.260, bf16[512,1408]{1,0:T(8,128)(2,1)} %get-tuple-element.263.refs_0_, bf16[512,1408]{1,0:T(8,128)(2,1)} %get-tuple-element.264.refs_1_), custom_call_target="tpu_custom_call" | custom-call | flops 1 | bytes 1 | tf_op jit(solution)/shard_map/pallas_call | solution.py:385
  328.0 8.3 %shard_map.217 = (bf16[1024,1408]{1,0:T(8,128)(2,1)}, bf16[1024,1408]{1,0:T(8,128)(2,1)}) custom-call(bf16[512,2048]{1,0:T(8,128)(2,1)} %bitcast.258, bf16[512,1408]{1,0:T(8,128)(2,1)} %get-tuple-element.271.refs_0_.mixed), custom_call_target="tpu_custom_call" | custom-call | flops 1 | bytes 1 | tf_op jit(solution)/shard_map/pallas_call | solution.py:385
  343.3 2.2 convert_reduce_fusion.1
  348.1 12.0 %shard_map.218 = bf16[512,2048]{1,0:T(8,128)(2,1)} custom-call(bf16[512,1408]{1,0:T(8,128)(2,1)} %get-tuple-element.271.refs_0_.mixed, bf16[4,64,1408]{2,1,0:T(8,128)(2,1)} %get-tuple-element.234.refs_0_, bf16[4,64,1408]{2,1,0:T(8,128)(2,1)} %copy-done.29, bf16[4,64,1408]{2,1,0:T(8,128)(2,1)} %copy-done.28, bf16[4,64,1408]{2,1,0:T(8,128)(2,1)} %copy-done.33, ...), custom_call_target="tpu_custom_call" | custom-call | flops 1 | bytes 1 | tf_op jit(solution)/shard_map/pallas_call | solution.py:385
  360.2 2.4 add_convert_fusion.3
  363.3 4.6 all-to-all-start.4
  370.0 17.0 %shard_map.219 = (bf16[1024,256]{1,0:T(8,128)(2,1)}, f32[2048,256]{1,0:T(8,128)}) custom-call(bf16[1024,256]{1,0:T(8,128)(2,1)} %get-tuple-element.225.query_rot, bf16[2048,256]{1,0:T(8,128)(2,1)} %bitcast.270, bf16[256,2048]{1,0:T(8,128)(2,1)} %copy-done.11, bf16[2048,1024]{1,0:T(8,128)(2,1)} %copy-done.13, f32[1024,256]{1,0:T(8,128)} %get-tuple-element.273.attended, ...), custom_call_target="tpu_custom_call" | custom-call | flops 1 | bytes 1 | tf_op jit(solution)/shard_map/pallas_call | solution.py:385
  387.1 2.1 convert.73
  395.3 4.8 fusion.63
  400.1 3.3 convolution_convert_fusion
  407.5 2.9 convert_add_fusion.1
  410.4 5.6 all-to-all-done.4
  416.1 2.2 convert_reduce_fusion
  418.4 3.2 collective-permute-done.65
  425.9 2.8 fusion.22
  428.7 3.4 collective-permute-done.66
  432.1 3.4 collective-permute-done.67
  440.8 3.6 fusion.1
  446.2 2.9 add_convert_fusion.1
  450.6 5.1 pad_maximum_fusion.1
  455.7 11.8 %collective-permute-done.73 = bf16[2,2,1,2,64,1024]{5,4,1,0,3,2:T(8,128)(2,1)} collective-permute-done((bf16[2,2,1,2,64,1024]{5,4,1,0,3,2:T(8,128)(2,1)}, bf16[2,2,1,2,64,1024]{5,4,1,0,3,2:T(8,128)(2,1)}, u32[]{:S(2)}, u32[]{:S(2)}) %collective-permute-start.73) | collective-permute-done | bytes 1048608 | tf_op jit(solution)/shard_map/ppermute | solution.py:56
  471.1 2.4 copy-done.8
  477.8 6.3 %collective-permute-done.75 = bf16[2,2,1,64,1024]{4,3,1,0,2:T(8,128)(2,1)} collective-permute-done((bf16[2,2,1,64,1024]{4,3,1,0,2:T(8,128)(2,1)}, bf16[2,2,1,64,1024]{4,3,1,0,2:T(8,128)(2,1)}, u32[]{:S(2)}, u32[]{:S(2)}) %collective-permute-start.75) | collective-permute-done | bytes 524320 | tf_op jit(solution)/shard_map/ppermute | solution.py:56
  486.9 2.2 convert_element_type.356
  493.9 8.5 %collective-permute-done.77 = bf16[2,1,64,2048]{3,2,0,1:T(8,128)(2,1)} collective-permute-done((bf16[2,1,64,2048]{3,2,0,1:T(8,128)(2,1)}, bf16[2,1,64,2048]{3,2,0,1:T(8,128)(2,1)}, u32[]{:S(2)}, u32[]{:S(2)}) %collective-permute-start.77) | collective-permute-done | bytes 524320 | tf_op jit(solution)/shard_map/ppermute | solution.py:56
  502.4 18.2 %collective-permute-done.74 = bf16[2,2,1,2,64,1408]{5,4,1,0,3,2:T(8,128)(2,1)} collective-permute-done((bf16[2,2,1,2,64,1408]{5,4,1,0,3,2:T(8,128)(2,1)}, bf16[2,2,1,2,64,1408]{5,4,1,0,3,2:T(8,128)(2,1)}, u32[]{:S(2)}, u32[]{:S(2)}) %collective-permute-start.74) | collective-permute-done | bytes 1441824 | tf_op jit(solution)/shard_map/ppermute | solution.py:56
  520.6 2.5 bitcast_add_fusion
  523.2 2.3 collective-permute-start.78
  527.8 12.2 %collective-permute-done.79 = bf16[1,64,2048]{2,1,0:T(8,128)(2,1)} collective-permute-done((bf16[1,64,2048]{2,1,0:T(8,128)(2,1)S(1)}, bf16[1,64,2048]{2,1,0:T(8,128)(2,1)}, u32[]{:S(2)}, u32[]{:S(2)}) %collective-permute-start.79) | collective-permute-done | bytes 262176 | tf_op jit(solution)/shard_map/ppermute | solution.py:56
  543.7 2.9 collective-permute-start.81
  547.8 3.6 all-to-all-start.5
  552.7 2.8 add_convert_fusion
  555.4 4.2 collective-permute-done.81
  561.7 11.4 %all-to-all-done.5 = bf16[4,2,64,1408]{3,2,1,0:T(8,128)(2,1)S(1)} async-done(((bf16[4,2,64,1408]{3,2,1,0:T(8,128)(2,1)}), bf16[4,2,64,1408]{3,2,1,0:T(8,128)(2,1)S(1)}, u32[]{:S(2)}, u32[]{:S(2)}) %all-to-all-start.5) | async-done | bytes 1441824 | tf_op jit(solution)/shard_map/all_to_all | solution.py:784
  574.2 3.5 shard_map.220
  577.7 3.5 all-to-all-start.6
  586.2 3.4 shard_map.221
  590.5 3.4 shard_map.222
  (503 shorter events, 152.2 us)
Async XLA Ops:
  8.7 14.6 %collective-permute-start = (bf16[80,256]{1,0:T(8,128)(2,1)S(1)}, bf16[80,256]{1,0:T(8,128)(2,1)S(1)}, u32[]{:S(2)}, u32[]{:S(2)}) collective-permute-start(bf16[80,256]{1,0:T(8,128)(2,1)S(1)} %get-tuple-element.413), channel_id=1, source_target_pairs={{0,2},{2,0},{1,3},{3,1},{4,6},{6,4},{5,7},{7,5},{8,10},{10,8},{9,1... | collective-permute-start | bytes 122888 | tf_op jit(solution)/shard_map/ppermute | solution.py:56
  15.1 8.2 %collective-permute-start.1 = (bf16[64,1024]{1,0:T(8,128)(2,1)S(1)}, bf16[64,1024]{1,0:T(8,128)(2,1)S(1)}, u32[]{:S(2)}, u32[]{:S(2)}) collective-permute-start(bf16[64,1024]{1,0:T(8,128)(2,1)S(1)} %bitcast.326), channel_id=1, source_target_pairs={{0,2},{2,0},{1,3},{3,1},{4,6},{6,4},{5,7},{7,5},{8,10},{10,8},{9,1... | collective-permute-start | bytes 393224 | tf_op jit(solution)/shard_map/ppermute | solution.py:56
  15.2 8.1 %collective-permute-start.2 = (bf16[64,1024]{1,0:T(8,128)(2,1)S(1)}, bf16[64,1024]{1,0:T(8,128)(2,1)S(1)}, u32[]{:S(2)}, u32[]{:S(2)}) collective-permute-start(bf16[64,1024]{1,0:T(8,128)(2,1)S(1)} %bitcast.327), channel_id=1, source_target_pairs={{0,2},{2,0},{1,3},{3,1},{4,6},{6,4},{5,7},{7,5},{8,10},{10,8},{9,1... | collective-permute-start | bytes 393224 | tf_op jit(solution)/shard_map/ppermute | solution.py:56
  23.6 14.8 %collective-permute-start.6 = (bf16[128,2048]{1,0:T(8,128)(2,1)S(1)}, bf16[128,2048]{1,0:T(8,128)(2,1)S(1)}, u32[]{:S(2)}, u32[]{:S(2)}) collective-permute-start(bf16[128,2048]{1,0:T(8,128)(2,1)S(1)} %copy.155), channel_id=1, source_target_pairs={{0,2},{2,0},{1,3},{3,1},{4,6},{6,4},{5,7},{7,5},{8,10},{10,8},{9,1... | collective-permute-start | bytes 1572872 | tf_op jit(solution)/shard_map/ppermute | solution.py:56
  23.7 14.7 %collective-permute-start.4 = (bf16[2,64,1024]{2,1,0:T(8,128)(2,1)S(1)}, bf16[2,64,1024]{2,1,0:T(8,128)(2,1)S(1)}, u32[]{:S(2)}, u32[]{:S(2)}) collective-permute-start(bf16[2,64,1024]{2,1,0:T(8,128)(2,1)S(1)} %maximum_select_fusion.4), channel_id=1, source_target_pairs={{0,4},{4,0},{1,5},{5,1},{2,6},{6,2},{3,7},{7,3},{8,12},{12,8},{9,1... | collective-permute-start | bytes 786440 | tf_op jit(solution)/shard_map/ppermute | solution.py:56
  25.9 12.5 %collective-permute-start.5 = (bf16[2,64,1024]{2,1,0:T(8,128)(2,1)S(1)}, bf16[2,64,1024]{2,1,0:T(8,128)(2,1)S(1)}, u32[]{:S(2)}, u32[]{:S(2)}) collective-permute-start(bf16[2,64,1024]{2,1,0:T(8,128)(2,1)S(1)} %maximum_select_fusion.5), channel_id=1, source_target_pairs={{0,4},{4,0},{1,5},{5,1},{2,6},{6,2},{3,7},{7,3},{8,12},{12,8},{9,1... | collective-permute-start | bytes 786440 | tf_op jit(solution)/shard_map/ppermute | solution.py:56
  26.1 12.3 %collective-permute-start.3 = (bf16[2,80,256]{2,1,0:T(8,128)(2,1)S(1)}, bf16[2,80,256]{2,1,0:T(8,128)(2,1)S(1)}, u32[]{:S(2)}, u32[]{:S(2)}) collective-permute-start(bf16[2,80,256]{2,1,0:T(8,128)(2,1)S(1)} %maximum_select_fusion.9), channel_id=1, source_target_pairs={{0,4},{4,0},{1,5},{5,1},{2,6},{6,2},{3,7},{7,3},{8,12},{12,8},{9,1... | collective-permute-start | bytes 245768 | tf_op jit(solution)/shard_map/ppermute | solution.py:56
  39.2 8.6 %collective-permute-start.7 = (bf16[1,2,2,80,256]{4,3,2,1,0:T(8,128)(2,1)S(1)}, bf16[1,2,2,80,256]{4,3,2,1,0:T(8,128)(2,1)S(1)}, u32[]{:S(2)}, u32[]{:S(2)}) collective-permute-start(bf16[1,2,2,80,256]{4,3,2,1,0:T(8,128)(2,1)S(1)} %maximum_select_fusion.8), channel_id=1, source_target_pairs={{0,8},{8,0},{1,9},{9,1},{2,10},{10,2},{3,11},{11,3},{4,12},{12,4},... | collective-permute-start | bytes 491528 | tf_op jit(solution)/shard_map/ppermute | solution.py:56
  47.9 19.4 %collective-permute-start.8 = (bf16[2,1,2,2,80,256]{5,4,3,2,1,0:T(8,128)(2,1)S(1)}, bf16[2,1,2,2,80,256]{5,4,3,2,1,0:T(8,128)(2,1)S(1)}, u32[]{:S(2)}, u32[]{:S(2)}) collective-permute-start(bf16[2,1,2,2,80,256]{5,4,3,2,1,0:T(8,128)(2,1)S(1)} %pad_maximum_fusion.16), channel_id=1, source_target_pairs={{0,16},{16,0},{1,17},{17,1},{2,18},{18,2},{3,19},{19,3},{4,20},{20... | collective-permute-start | bytes 983048 | tf_op jit(solution)/shard_map/ppermute | solution.py:56
  49.6 20.1 %collective-permute-start.13 = (bf16[1,2,2,64,1024]{4,3,2,1,0:T(8,128)(2,1)S(1)}, bf16[1,2,2,64,1024]{4,3,2,1,0:T(8,128)(2,1)S(1)}, u32[]{:S(2)}, u32[]{:S(2)}) collective-permute-start(bf16[1,2,2,64,1024]{4,3,2,1,0:T(8,128)(2,1)S(1)} %maximum_select_fusion.2), channel_id=1, source_target_pairs={{0,8},{8,0},{1,9},{9,1},{2,10},{10,2},{3,11},{11,3},{4,12},{12,4},... | collective-permute-start | bytes 1572872 | tf_op jit(solution)/shard_map/ppermute | solution.py:56
  50.2 48.6 %all-to-all-start = ((bf16[4,3,64,1408]{3,2,1,0:T(8,128)(2,1)}), bf16[4,3,64,1408]{3,2,1,0:T(8,128)(2,1)}, u32[]{:S(2)}, u32[]{:S(2)}) async-start(bf16[4,3,64,1408]{3,2,1,0:T(8,128)(2,1)} %shard_map.212), calls=%async_computation | async-start | bytes 4325376 | tf_op jit(solution)/shard_map/all_to_all | solution.py:498
  72.3 12.9 %collective-permute-start.14 = (bf16[128,256]{1,0:T(8,128)(2,1)S(1)}, bf16[128,256]{1,0:T(8,128)(2,1)S(1)}, u32[]{:S(2)}, u32[]{:S(2)}) collective-permute-start(bf16[128,256]{1,0:T(8,128)(2,1)S(1)} %pad_maximum_fusion.19), channel_id=1, source_target_pairs={{0,8},{8,0},{1,9},{9,1},{2,10},{10,2},{3,11},{11,3},{4,12},{12,4},... | collective-permute-start | bytes 196616 | tf_op jit(solution)/shard_map/ppermute | solution.py:56
  73.5 38.6 %collective-permute-start.17 = (bf16[2,1,2,2,64,1024]{5,4,3,2,1,0:T(8,128)(2,1)S(1)}, bf16[2,1,2,2,64,1024]{5,4,3,2,1,0:T(8,128)(2,1)}, u32[]{:S(2)}, u32[]{:S(2)}) collective-permute-start(bf16[2,1,2,2,64,1024]{5,4,3,2,1,0:T(8,128)(2,1)S(1)} %pad_maximum_fusion.8), channel_id=1, source_target_pairs={{0,16},{16,0},{1,17},{17,1},{2,18},{18,2},{3,19},{19,3},{4,20},{20... | collective-permute-start | bytes 3145736 | tf_op jit(solution)/shard_map/ppermute | solution.py:56
  85.3 13.5 %collective-permute-start.15 = (bf16[1,2,128,256]{3,2,1,0:T(8,128)(2,1)S(1)}, bf16[1,2,128,256]{3,2,1,0:T(8,128)(2,1)S(1)}, u32[]{:S(2)}, u32[]{:S(2)}) collective-permute-start(bf16[1,2,128,256]{3,2,1,0:T(8,128)(2,1)S(1)} %maximum_bitcast_fusion), channel_id=1, source_target_pairs={{0,4},{4,0},{1,5},{5,1},{2,6},{6,2},{3,7},{7,3},{8,12},{12,8},{9,1... | collective-permute-start | bytes 393224 | tf_op jit(solution)/shard_map/ppermute | solution.py:56
  96.7 15.5 %collective-permute-start.18 = (bf16[1,2,2,64,1024]{4,3,2,1,0:T(8,128)(2,1)}, bf16[1,2,2,64,1024]{4,3,2,1,0:T(8,128)(2,1)}, u32[]{:S(2)}, u32[]{:S(2)}) collective-permute-start(bf16[1,2,2,64,1024]{4,3,2,1,0:T(8,128)(2,1)} %maximum_select_fusion.3), channel_id=1, source_target_pairs={{0,8},{8,0},{1,9},{9,1},{2,10},{10,2},{3,11},{11,3},{4,12},{12,4},... | collective-permute-start | bytes 1572872 | tf_op jit(solution)/shard_map/ppermute | solution.py:56
  102.5 9.7 %collective-permute-start.16 = (bf16[2,1,2,128,256]{4,3,2,0,1:T(8,128)(2,1)S(1)}, bf16[2,1,2,128,256]{4,3,2,0,1:T(8,128)(2,1)S(1)}, u32[]{:S(2)}, u32[]{:S(2)}) collective-permute-start(bf16[2,1,2,128,256]{4,3,2,0,1:T(8,128)(2,1)S(1)} %bitcast.307), channel_id=1, source_target_pairs={{0,2},{2,0},{1,3},{3,1},{4,6},{6,4},{5,7},{7,5},{8,10},{10,8},{9,1... | collective-permute-start | bytes 786440 | tf_op jit(solution)/shard_map/ppermute | solution.py:56
  114.9 7.6 %collective-permute-start.26 = (bf16[256,1024]{1,0:T(8,128)(2,1)S(1)}, bf16[256,1024]{1,0:T(8,128)(2,1)S(1)}, u32[]{:S(2)}, u32[]{:S(2)}) collective-permute-start(bf16[256,1024]{1,0:T(8,128)(2,1)S(1)} %get-tuple-element.379), channel_id=1, source_target_pairs={{0,1},{1,0},{2,3},{3,2},{4,5},{5,4},{6,7},{7,6},{8,9},{9,8},{10,11... | collective-permute-start | bytes 1572872 | tf_op jit(solution)/shard_map/ppermute | solution.py:56
  114.9 7.6 %collective-permute-start.25 = (bf16[256,1024]{1,0:T(8,128)(2,1)S(1)}, bf16[256,1024]{1,0:T(8,128)(2,1)S(1)}, u32[]{:S(2)}, u32[]{:S(2)}) collective-permute-start(bf16[256,1024]{1,0:T(8,128)(2,1)S(1)} %get-tuple-element.380), channel_id=1, source_target_pairs={{0,1},{1,0},{2,3},{3,2},{4,5},{5,4},{6,7},{7,6},{8,9},{9,8},{10,11... | collective-permute-start | bytes 1572872 | tf_op jit(solution)/shard_map/ppermute | solution.py:56
  115.4 7.1 %collective-permute-start.23 = (bf16[256,1024]{1,0:T(8,128)(2,1)S(1)}, bf16[256,1024]{1,0:T(8,128)(2,1)S(1)}, u32[]{:S(2)}, u32[]{:S(2)}) collective-permute-start(bf16[256,1024]{1,0:T(8,128)(2,1)S(1)} %get-tuple-element.382), channel_id=1, source_target_pairs={{0,1},{1,0},{2,3},{3,2},{4,5},{5,4},{6,7},{7,6},{8,9},{9,8},{10,11... | collective-permute-start | bytes 1572872 | tf_op jit(solution)/shard_map/ppermute | solution.py:56
  122.6 41.3 %collective-permute-start.27 = (bf16[2,1,2,2,64,1024]{5,4,3,2,0,1:T(8,128)(2,1)}, bf16[2,1,2,2,64,1024]{5,4,3,2,0,1:T(8,128)(2,1)}, u32[]{:S(2)}, u32[]{:S(2)}) collective-permute-start(bf16[2,1,2,2,64,1024]{5,4,3,2,0,1:T(8,128)(2,1)} %bitcast.72), channel_id=1, source_target_pairs={{0,16},{16,0},{1,17},{17,1},{2,18},{18,2},{3,19},{19,3},{4,20},{20... | collective-permute-start | bytes 3145736 | tf_op jit(solution)/shard_map/ppermute | solution.py:56
  123.6 40.2 %collective-permute-start.29 = (bf16[4,64,1408]{2,1,0:T(8,128)(2,1)S(1)}, bf16[4,64,1408]{2,1,0:T(8,128)(2,1)}, u32[]{:S(2)}, u32[]{:S(2)}) collective-permute-start(bf16[4,64,1408]{2,1,0:T(8,128)(2,1)S(1)} %get-tuple-element.235.refs_0_.refs_8_), channel_id=1, source_target_pairs={{0,16},{16,0},{1,17},{17,1},{2,18},{18,2},{3,19},{19,3},{4,20},{20... | collective-permute-start | bytes 2162696 | tf_op jit(solution)/shard_map/ppermute | solution.py:56
  124.7 39.2 %collective-permute-start.28 = (bf16[4,64,1408]{2,1,0:T(8,128)(2,1)S(1)}, bf16[4,64,1408]{2,1,0:T(8,128)(2,1)}, u32[]{:S(2)}, u32[]{:S(2)}) collective-permute-start(bf16[4,64,1408]{2,1,0:T(8,128)(2,1)S(1)} %get-tuple-element.235.refs_0_.refs_8_), channel_id=1, source_target_pairs={{0,8},{8,0},{1,9},{9,1},{2,10},{10,2},{3,11},{11,3},{4,12},{12,4},... | collective-permute-start | bytes 2162696 | tf_op jit(solution)/shard_map/ppermute | solution.py:56
  168.5 19.0 %collective-permute-start.36 = (bf16[4,64,1408]{2,1,0:T(8,128)(2,1)S(1)}, bf16[4,64,1408]{2,1,0:T(8,128)(2,1)S(1)}, u32[]{:S(2)}, u32[]{:S(2)}) collective-permute-start(bf16[4,64,1408]{2,1,0:T(8,128)(2,1)S(1)} %get-tuple-element.239.refs_8_.refs_16_), channel_id=1, source_target_pairs={{0,16},{16,0},{1,17},{17,1},{2,18},{18,2},{3,19},{19,3},{4,20},{20... | collective-permute-start | bytes 2162696 | tf_op jit(solution)/shard_map/ppermute | solution.py:56
  169.5 32.1 %collective-permute-start.35 = (bf16[4,64,1408]{2,1,0:T(8,128)(2,1)S(1)}, bf16[4,64,1408]{2,1,0:T(8,128)(2,1)S(1)}, u32[]{:S(2)}, u32[]{:S(2)}) collective-permute-start(bf16[4,64,1408]{2,1,0:T(8,128)(2,1)S(1)} %get-tuple-element.239.refs_8_.refs_16_), channel_id=1, source_target_pairs={{0,8},{8,0},{1,9},{9,1},{2,10},{10,2},{3,11},{11,3},{4,12},{12,4},... | collective-permute-start | bytes 2162696 | tf_op jit(solution)/shard_map/ppermute | solution.py:56
  175.0 27.2 %collective-permute-start.37 = (bf16[4,64,1408]{2,1,0:T(8,128)(2,1)}, bf16[4,64,1408]{2,1,0:T(8,128)(2,1)}, u32[]{:S(2)}, u32[]{:S(2)}) collective-permute-start(bf16[4,64,1408]{2,1,0:T(8,128)(2,1)} %collective-permute-done.28.refs_1_.refs_9_), channel_id=1, source_target_pairs={{0,16},{16,0},{1,17},{17,1},{2,18},{18,2},{3,19},{19,3},{4,20},{20... | collective-permute-start | bytes 2162696 | tf_op jit(solution)/shard_map/ppermute | solution.py:56
  176.4 25.2 %collective-permute-start.34 = (bf16[128,2048]{1,0:T(8,128)(2,1)S(1)}, bf16[128,2048]{1,0:T(8,128)(2,1)}, u32[]{:S(2)}, u32[]{:S(2)}) collective-permute-start(bf16[128,2048]{1,0:T(8,128)(2,1)S(1)} %slice.548), channel_id=1, source_target_pairs={{0,2},{2,0},{1,3},{3,1},{4,6},{6,4},{5,7},{7,5},{8,10},{10,8},{9,1... | collective-permute-start | bytes 1572872 | tf_op jit(solution)/shard_map/ppermute | solution.py:56
  205.7 47.4 %all-to-all-start.1 = ((bf16[4,128,2048]{2,1,0:T(8,128)(2,1)}), bf16[4,128,2048]{2,1,0:T(8,128)(2,1)S(1)}, u32[]{:S(2)}, u32[]{:S(2)}) async-start(bf16[4,128,2048]{2,1,0:T(8,128)(2,1)} %broadcast_in_dim.22), calls=%async_computation.1 | async-start | bytes 4194304 | tf_op jit(solution)/shard_map/all_to_all | solution.py:108
  209.3 19.3 %collective-permute-start.38 = (bf16[4,64,1408]{2,1,0:T(8,128)(2,1)}, bf16[4,64,1408]{2,1,0:T(8,128)(2,1)S(1)}, u32[]{:S(2)}, u32[]{:S(2)}) collective-permute-start(bf16[4,64,1408]{2,1,0:T(8,128)(2,1)} %copy-done.37), channel_id=1, source_target_pairs={{0,16},{16,0},{1,17},{17,1},{2,18},{18,2},{3,19},{19,3},{4,20},{20... | collective-permute-start | bytes 2162696 | tf_op jit(solution)/shard_map/ppermute | solution.py:56
  210.4 32.4 %collective-permute-start.40 = (bf16[4,64,1408]{2,1,0:T(8,128)(2,1)}, bf16[4,64,1408]{2,1,0:T(8,128)(2,1)S(1)}, u32[]{:S(2)}, u32[]{:S(2)}) collective-permute-start(bf16[4,64,1408]{2,1,0:T(8,128)(2,1)} %get-tuple-element.234.refs_0_), channel_id=1, source_target_pairs={{0,16},{16,0},{1,17},{17,1},{2,18},{18,2},{3,19},{19,3},{4,20},{20... | collective-permute-start | bytes 2162696 | tf_op jit(solution)/shard_map/ppermute | solution.py:56
  211.4 36.2 %collective-permute-start.39 = (bf16[4,64,1408]{2,1,0:T(8,128)(2,1)}, bf16[4,64,1408]{2,1,0:T(8,128)(2,1)S(1)}, u32[]{:S(2)}, u32[]{:S(2)}) collective-permute-start(bf16[4,64,1408]{2,1,0:T(8,128)(2,1)} %get-tuple-element.234.refs_0_), channel_id=1, source_target_pairs={{0,8},{8,0},{1,9},{9,1},{2,10},{10,2},{3,11},{11,3},{4,12},{12,4},... | collective-permute-start | bytes 2162696 | tf_op jit(solution)/shard_map/ppermute | solution.py:56
  228.7 19.0 %collective-permute-start.41 = (bf16[4,64,1408]{2,1,0:T(8,128)(2,1)}, bf16[4,64,1408]{2,1,0:T(8,128)(2,1)S(1)}, u32[]{:S(2)}, u32[]{:S(2)}) collective-permute-start(bf16[4,64,1408]{2,1,0:T(8,128)(2,1)} %copy-done.19), channel_id=1, source_target_pairs={{0,1},{1,0},{2,3},{3,2},{4,5},{5,4},{6,7},{7,6},{8,9},{9,8},{10,11... | collective-permute-start | bytes 2162696 | tf_op jit(solution)/shard_map/ppermute | solution.py:56
  228.7 19.5 %collective-permute-start.42 = (bf16[4,64,1408]{2,1,0:T(8,128)(2,1)}, bf16[4,64,1408]{2,1,0:T(8,128)(2,1)S(1)}, u32[]{:S(2)}, u32[]{:S(2)}) collective-permute-start(bf16[4,64,1408]{2,1,0:T(8,128)(2,1)} %collective-permute-done.28.refs_1_.refs_9_), channel_id=1, source_target_pairs={{0,1},{1,0},{2,3},{3,2},{4,5},{5,4},{6,7},{7,6},{8,9},{9,8},{10,11... | collective-permute-start | bytes 2162696 | tf_op jit(solution)/shard_map/ppermute | solution.py:56
  229.2 19.1 %collective-permute-start.43 = (bf16[4,64,1408]{2,1,0:T(8,128)(2,1)}, bf16[4,64,1408]{2,1,0:T(8,128)(2,1)S(1)}, u32[]{:S(2)}, u32[]{:S(2)}) collective-permute-start(bf16[4,64,1408]{2,1,0:T(8,128)(2,1)} %collective-permute-done.29.refs_2_.refs_10_), channel_id=1, source_target_pairs={{0,1},{1,0},{2,3},{3,2},{4,5},{5,4},{6,7},{7,6},{8,9},{9,8},{10,11... | collective-permute-start | bytes 2162696 | tf_op jit(solution)/shard_map/ppermute | solution.py:56
  254.4 31.4 %all-to-all-start.2 = ((bf16[4,128,2048]{2,1,0:T(8,128)(2,1)}), bf16[4,128,2048]{2,1,0:T(8,128)(2,1)S(1)}, u32[]{:S(2)}, u32[]{:S(2)}) async-start(bf16[4,128,2048]{2,1,0:T(8,128)(2,1)} %broadcast_in_dim.21), calls=%async_computation.2 | async-start | bytes 4194304 | tf_op jit(solution)/shard_map/all_to_all | solution.py:108
  260.8 18.1 %collective-permute-start.50 = (bf16[4,64,1408]{2,1,0:T(8,128)(2,1)}, bf16[4,64,1408]{2,1,0:T(8,128)(2,1)S(1)}, u32[]{:S(2)}, u32[]{:S(2)}) collective-permute-start(bf16[4,64,1408]{2,1,0:T(8,128)(2,1)} %get-tuple-element.234.refs_0_), channel_id=1, source_target_pairs={{0,1},{1,0},{2,3},{3,2},{4,5},{5,4},{6,7},{7,6},{8,9},{9,8},{10,11... | collective-permute-start | bytes 2162696 | tf_op jit(solution)/shard_map/ppermute | solution.py:56
  261.3 17.6 %collective-permute-start.52 = (bf16[4,64,1408]{2,1,0:T(8,128)(2,1)}, bf16[4,64,1408]{2,1,0:T(8,128)(2,1)S(1)}, u32[]{:S(2)}, u32[]{:S(2)}) collective-permute-start(bf16[4,64,1408]{2,1,0:T(8,128)(2,1)} %copy-done.28), channel_id=1, source_target_pairs={{0,1},{1,0},{2,3},{3,2},{4,5},{5,4},{6,7},{7,6},{8,9},{9,8},{10,11... | collective-permute-start | bytes 2162696 | tf_op jit(solution)/shard_map/ppermute | solution.py:56
  261.4 17.5 %collective-permute-start.51 = (bf16[4,64,1408]{2,1,0:T(8,128)(2,1)}, bf16[4,64,1408]{2,1,0:T(8,128)(2,1)S(1)}, u32[]{:S(2)}, u32[]{:S(2)}) collective-permute-start(bf16[4,64,1408]{2,1,0:T(8,128)(2,1)} %copy-done.29), channel_id=1, source_target_pairs={{0,1},{1,0},{2,3},{3,2},{4,5},{5,4},{6,7},{7,6},{8,9},{9,8},{10,11... | collective-permute-start | bytes 2162696 | tf_op jit(solution)/shard_map/ppermute | solution.py:56
  261.8 18.3 %collective-permute-start.48 = (bf16[4,64,1408]{2,1,0:T(8,128)(2,1)}, bf16[4,64,1408]{2,1,0:T(8,128)(2,1)S(1)}, u32[]{:S(2)}, u32[]{:S(2)}) collective-permute-start(bf16[4,64,1408]{2,1,0:T(8,128)(2,1)} %copy-done.29), channel_id=1, source_target_pairs={{0,16},{16,0},{1,17},{17,1},{2,18},{18,2},{3,19},{19,3},{4,20},{20... | collective-permute-start | bytes 2162696 | tf_op jit(solution)/shard_map/ppermute | solution.py:56
  307.9 35.3 %all-to-all-start.3 = ((bf16[4,128,2048]{2,1,0:T(8,128)(2,1)}), bf16[4,128,2048]{2,1,0:T(8,128)(2,1)}, u32[]{:S(2)}, u32[]{:S(2)}) async-start(bf16[4,128,2048]{2,1,0:T(8,128)(2,1)} %bitcast.295), calls=%async_computation.3 | async-start | bytes 4194304 | tf_op jit(solution)/shard_map/all_to_all | solution.py:112
  312.4 228.4 %reduce-scatter.2.cloned.1.call-start = ((), (), s32[]{:S(2)}) async-start(), calls=%async_computation.8 | async-start | bytes 12976128 | tf_op jit(solution)/shard_map/reduce_scatter | solution.py:656
  336.4 9.1 %collective-permute-start.54 = (bf16[1024,1408]{1,0:T(8,128)(2,1)}, bf16[1024,1408]{1,0:T(8,128)(2,1)}, u32[]{:S(2)}, u32[]{:S(2)}) collective-permute-start(bf16[1024,1408]{1,0:T(8,128)(2,1)} %get-tuple-element.267), channel_id=1, source_target_pairs={{0,1},{1,0},{2,3},{3,2},{4,5},{5,4},{6,7},{7,6},{8,9},{9,8},{10,11... | collective-permute-start | bytes 8650760 | tf_op jit(solution)/shard_map/ppermute | solution.py:56
  346.1 16.4 %collective-permute-start.55 = (bf16[128,2048]{1,0:T(8,128)(2,1)S(1)}, bf16[128,2048]{1,0:T(8,128)(2,1)S(1)}, u32[]{:S(2)}, u32[]{:S(2)}) collective-permute-start(bf16[128,2048]{1,0:T(8,128)(2,1)S(1)} %fusion.54), channel_id=1, source_target_pairs={{0,2},{2,0},{1,3},{3,1},{4,6},{6,4},{5,7},{7,5},{8,10},{10,8},{9,1... | collective-permute-start | bytes 1572872 | tf_op jit(solution)/shard_map/ppermute | solution.py:56
  363.3 52.7 %all-to-all-start.4 = ((bf16[4,128,2048]{2,1,0:T(8,128)(2,1)}), bf16[4,128,2048]{2,1,0:T(8,128)(2,1)}, u32[]{:S(2)}, u32[]{:S(2)}) async-start(bf16[4,128,2048]{2,1,0:T(8,128)(2,1)} %bitcast.273), calls=%async_computation.4 | async-start | bytes 4194304 | tf_op jit(solution)/shard_map/all_to_all | solution.py:112
  392.1 13.2 %collective-permute-start.60 = (bf16[2,1,2,128,256]{4,3,2,1,0:T(8,128)(2,1)S(1)}, bf16[2,1,2,128,256]{4,3,2,1,0:T(8,128)(2,1)S(1)}, u32[]{:S(2)}, u32[]{:S(2)}) collective-permute-start(bf16[2,1,2,128,256]{4,3,2,1,0:T(8,128)(2,1)S(1)} %slice.549), channel_id=1, source_target_pairs={{0,2},{2,0},{1,3},{3,1},{4,6},{6,4},{5,7},{7,5},{8,10},{10,8},{9,1... | collective-permute-start | bytes 786440 | tf_op jit(solution)/shard_map/ppermute | solution.py:56
  394.2 9.2 %collective-permute-start.61 = (bf16[256,1024]{1,0:T(8,128)(2,1)S(1)}, bf16[256,1024]{1,0:T(8,128)(2,1)S(1)}, u32[]{:S(2)}, u32[]{:S(2)}) collective-permute-start(bf16[256,1024]{1,0:T(8,128)(2,1)S(1)} %get-tuple-element.368), channel_id=1, source_target_pairs={{0,1},{1,0},{2,3},{3,2},{4,5},{5,4},{6,7},{7,6},{8,9},{9,8},{10,11... | collective-permute-start | bytes 1572872 | tf_op jit(solution)/shard_map/ppermute | solution.py:56
  394.3 10.8 %collective-permute-start.64 = (bf16[256,1024]{1,0:T(8,128)(2,1)S(1)}, bf16[256,1024]{1,0:T(8,128)(2,1)S(1)}, u32[]{:S(2)}, u32[]{:S(2)}) collective-permute-start(bf16[256,1024]{1,0:T(8,128)(2,1)S(1)} %get-tuple-element.369), channel_id=1, source_target_pairs={{0,1},{1,0},{2,3},{3,2},{4,5},{5,4},{6,7},{7,6},{8,9},{9,8},{10,11... | collective-permute-start | bytes 1572872 | tf_op jit(solution)/shard_map/ppermute | solution.py:56
  394.8 10.3 %collective-permute-start.63 = (bf16[256,1024]{1,0:T(8,128)(2,1)S(1)}, bf16[256,1024]{1,0:T(8,128)(2,1)S(1)}, u32[]{:S(2)}, u32[]{:S(2)}) collective-permute-start(bf16[256,1024]{1,0:T(8,128)(2,1)S(1)} %get-tuple-element.370), channel_id=1, source_target_pairs={{0,1},{1,0},{2,3},{3,2},{4,5},{5,4},{6,7},{7,6},{8,9},{9,8},{10,11... | collective-permute-start | bytes 1572872 | tf_op jit(solution)/shard_map/ppermute | solution.py:56
  394.9 10.3 %collective-permute-start.62 = (bf16[256,1024]{1,0:T(8,128)(2,1)S(1)}, bf16[256,1024]{1,0:T(8,128)(2,1)S(1)}, u32[]{:S(2)}, u32[]{:S(2)}) collective-permute-start(bf16[256,1024]{1,0:T(8,128)(2,1)S(1)} %get-tuple-element.371), channel_id=1, source_target_pairs={{0,1},{1,0},{2,3},{3,2},{4,5},{5,4},{6,7},{7,6},{8,9},{9,8},{10,11... | collective-permute-start | bytes 1572872 | tf_op jit(solution)/shard_map/ppermute | solution.py:56
  403.4 25.3 %collective-permute-start.68 = (bf16[256,1408]{1,0:T(8,128)(2,1)}, bf16[256,1408]{1,0:T(8,128)(2,1)S(1)}, u32[]{:S(2)}, u32[]{:S(2)}) collective-permute-start(bf16[256,1408]{1,0:T(8,128)(2,1)} %add_convert_fusion.3), channel_id=1, source_target_pairs={{0,16},{16,0},{1,17},{17,1},{2,18},{18,2},{3,19},{19,3},{4,20},{20... | collective-permute-start | bytes 2162696 | tf_op jit(solution)/shard_map/ppermute | solution.py:56
  406.1 15.5 %collective-permute-start.65 = (bf16[1,2,128,256]{3,2,1,0:T(8,128)(2,1)}, bf16[1,2,128,256]{3,2,1,0:T(8,128)(2,1)}, u32[]{:S(2)}, u32[]{:S(2)}) collective-permute-start(bf16[1,2,128,256]{3,2,1,0:T(8,128)(2,1)} %fusion.35), channel_id=1, source_target_pairs={{0,4},{4,0},{1,5},{5,1},{2,6},{6,2},{3,7},{7,3},{8,12},{12,8},{9,1... | collective-permute-start | bytes 393224 | tf_op jit(solution)/shard_map/ppermute | solution.py:56
  421.6 13.9 %collective-permute-start.67 = (bf16[128,2048]{1,0:T(8,128)(2,1)S(1)}, bf16[128,2048]{1,0:T(8,128)(2,1)S(1)}, u32[]{:S(2)}, u32[]{:S(2)}) collective-permute-start(bf16[128,2048]{1,0:T(8,128)(2,1)S(1)} %slice.547), channel_id=1, source_target_pairs={{0,2},{2,0},{1,3},{3,1},{4,6},{6,4},{5,7},{7,5},{8,10},{10,8},{9,1... | collective-permute-start | bytes 1572872 | tf_op jit(solution)/shard_map/ppermute | solution.py:56
  424.1 8.0 %collective-permute-start.66 = (bf16[1,128,256]{2,1,0:T(8,128)(2,1)S(1)}, bf16[1,128,256]{2,1,0:T(8,128)(2,1)S(1)}, u32[]{:S(2)}, u32[]{:S(2)}) collective-permute-start(bf16[1,128,256]{2,1,0:T(8,128)(2,1)S(1)} %fusion.39), channel_id=1, source_target_pairs={{0,8},{8,0},{1,9},{9,1},{2,10},{10,2},{3,11},{11,3},{4,12},{12,4},... | collective-permute-start | bytes 196616 | tf_op jit(solution)/shard_map/ppermute | solution.py:56
  428.7 38.8 %collective-permute-start.73 = (bf16[2,2,1,2,64,1024]{5,4,1,0,3,2:T(8,128)(2,1)}, bf16[2,2,1,2,64,1024]{5,4,1,0,3,2:T(8,128)(2,1)}, u32[]{:S(2)}, u32[]{:S(2)}) collective-permute-start(bf16[2,2,1,2,64,1024]{5,4,1,0,3,2:T(8,128)(2,1)} %fusion.22), channel_id=1, source_target_pairs={{0,4},{4,0},{1,5},{5,1},{2,6},{6,2},{3,7},{7,3},{8,12},{12,8},{9,1... | collective-permute-start | bytes 3145736 | tf_op jit(solution)/shard_map/ppermute | solution.py:56
  449.1 28.7 %collective-permute-start.76 = (bf16[256,1408]{1,0:T(8,128)(2,1)}, bf16[256,1408]{1,0:T(8,128)(2,1)}, u32[]{:S(2)}, u32[]{:S(2)}) collective-permute-start(bf16[256,1408]{1,0:T(8,128)(2,1)} %get-tuple-element.363), channel_id=1, source_target_pairs={{0,16},{16,0},{1,17},{17,1},{2,18},{18,2},{3,19},{19,3},{4,20},{20... | collective-permute-start | bytes 2162696 | tf_op jit(solution)/shard_map/ppermute | solution.py:56
  470.0 14.2 %collective-permute-start.75 = (bf16[2,2,1,64,1024]{4,3,1,0,2:T(8,128)(2,1)}, bf16[2,2,1,64,1024]{4,3,1,0,2:T(8,128)(2,1)}, u32[]{:S(2)}, u32[]{:S(2)}) collective-permute-start(bf16[2,2,1,64,1024]{4,3,1,0,2:T(8,128)(2,1)} %fusion.27), channel_id=1, source_target_pairs={{0,2},{2,0},{1,3},{3,1},{4,6},{6,4},{5,7},{7,5},{8,10},{10,8},{9,1... | collective-permute-start | bytes 1572872 | tf_op jit(solution)/shard_map/ppermute | solution.py:56
  474.8 45.8 %collective-permute-start.74 = (bf16[2,2,1,2,64,1408]{5,4,1,0,3,2:T(8,128)(2,1)}, bf16[2,2,1,2,64,1408]{5,4,1,0,3,2:T(8,128)(2,1)}, u32[]{:S(2)}, u32[]{:S(2)}) collective-permute-start(bf16[2,2,1,2,64,1408]{5,4,1,0,3,2:T(8,128)(2,1)} %fusion.8), channel_id=1, source_target_pairs={{0,4},{4,0},{1,5},{5,1},{2,6},{6,2},{3,7},{7,3},{8,12},{12,8},{9,1... | collective-permute-start | bytes 4325384 | tf_op jit(solution)/shard_map/ppermute | solution.py:56
  489.1 13.3 %collective-permute-start.77 = (bf16[2,1,64,2048]{3,2,0,1:T(8,128)(2,1)}, bf16[2,1,64,2048]{3,2,0,1:T(8,128)(2,1)}, u32[]{:S(2)}, u32[]{:S(2)}) collective-permute-start(bf16[2,1,64,2048]{3,2,0,1:T(8,128)(2,1)} %convert_element_type.356), channel_id=1, source_target_pairs={{0,16},{16,0},{1,17},{17,1},{2,18},{18,2},{3,19},{19,3},{4,20},{20... | collective-permute-start | bytes 1572872 | tf_op jit(solution)/shard_map/ppermute | solution.py:56
  492.1 35.7 %collective-permute-start.80 = (bf16[256,1408]{1,0:T(8,128)(2,1)}, bf16[256,1408]{1,0:T(8,128)(2,1)S(1)}, u32[]{:S(2)}, u32[]{:S(2)}) collective-permute-start(bf16[256,1408]{1,0:T(8,128)(2,1)} %get-tuple-element.362), channel_id=1, source_target_pairs={{0,8},{8,0},{1,9},{9,1},{2,10},{10,2},{3,11},{11,3},{4,12},{12,4},... | collective-permute-start | bytes 2162696 | tf_op jit(solution)/shard_map/ppermute | solution.py:56
  523.2 17.5 %collective-permute-start.78 = (bf16[2,2,1,64,1408]{4,3,1,0,2:T(8,128)(2,1)S(1)}, bf16[2,2,1,64,1408]{4,3,1,0,2:T(8,128)(2,1)}, u32[]{:S(2)}, u32[]{:S(2)}) collective-permute-start(bf16[2,2,1,64,1408]{4,3,1,0,2:T(8,128)(2,1)S(1)} %fusion.23), channel_id=1, source_target_pairs={{0,2},{2,0},{1,3},{3,1},{4,6},{6,4},{5,7},{7,5},{8,10},{10,8},{9,1... | collective-permute-start | bytes 2162696 | tf_op jit(solution)/shard_map/ppermute | solution.py:56
  526.7 13.2 %collective-permute-start.79 = (bf16[1,64,2048]{2,1,0:T(8,128)(2,1)S(1)}, bf16[1,64,2048]{2,1,0:T(8,128)(2,1)}, u32[]{:S(2)}, u32[]{:S(2)}) collective-permute-start(bf16[1,64,2048]{2,1,0:T(8,128)(2,1)S(1)} %fusion.31), channel_id=1, source_target_pairs={{0,8},{8,0},{1,9},{9,1},{2,10},{10,2},{3,11},{11,3},{4,12},{12,4},... | collective-permute-start | bytes 786440 | tf_op jit(solution)/shard_map/ppermute | solution.py:56
  543.7 16.0 %collective-permute-start.81 = (bf16[2,1,64,2432]{3,2,0,1:T(8,128)(2,1)}, bf16[2,1,64,2432]{3,2,0,1:T(8,128)(2,1)}, u32[]{:S(2)}, u32[]{:S(2)}) collective-permute-start(bf16[2,1,64,2432]{3,2,0,1:T(8,128)(2,1)} %fusion.24), channel_id=1, source_target_pairs={{0,16},{16,0},{1,17},{17,1},{2,18},{18,2},{3,19},{19,3},{4,20},{20... | collective-permute-start | bytes 1867784 | tf_op jit(solution)/shard_map/ppermute | solution.py:56
  547.8 25.2 %all-to-all-start.5 = ((bf16[4,2,64,1408]{3,2,1,0:T(8,128)(2,1)}), bf16[4,2,64,1408]{3,2,1,0:T(8,128)(2,1)S(1)}, u32[]{:S(2)}, u32[]{:S(2)}) async-start(bf16[4,2,64,1408]{3,2,1,0:T(8,128)(2,1)} %bitcast.276), calls=%async_computation.6 | async-start | bytes 2883584 | tf_op jit(solution)/shard_map/all_to_all | solution.py:784
  561.6 21.4 %collective-permute-start.82 = (bf16[1,64,2432]{2,1,0:T(8,128)(2,1)}, bf16[1,64,2432]{2,1,0:T(8,128)(2,1)}, u32[]{:S(2)}, u32[]{:S(2)}) collective-permute-start(bf16[1,64,2432]{2,1,0:T(8,128)(2,1)} %fusion.30), channel_id=1, source_target_pairs={{0,8},{8,0},{1,9},{9,1},{2,10},{10,2},{3,11},{11,3},{4,12},{12,4},... | collective-permute-start | bytes 933896 | tf_op jit(solution)/shard_map/ppermute | solution.py:56
  577.7 11.9 %all-to-all-start.6 = ((bf16[4,1,64,1408]{3,2,1,0:T(8,128)(2,1)}), bf16[4,1,64,1408]{3,2,1,0:T(8,128)(2,1)S(1)}, u32[]{:S(2)}, u32[]{:S(2)}) async-start(bf16[4,1,64,1408]{3,2,1,0:T(8,128)(2,1)} %bitcast.289), calls=%async_computation.7 | async-start | bytes 1441792 | tf_op jit(solution)/shard_map/all_to_all | solution.py:784
  (115 other events, 927.8 us)
Sparse Core Ops, SparseCore 0:
  339.6 137.0 reduce-scatter.1

commit v8 on v7

--- a/solution.py
+++ b/solution.py
@@ -779,16 +779,16 @@
     query_got, output_got, down_h1, both_grad = sync(query_got, output_got, down_h1, both_grad)
     query_total, query_got = next_fold(take_x(query_total, query_got), "y")
     output_weight_grad = scatter_m(output_total + output_got.astype(F32), 0)
-    def finish_feed(own):
-        own = low(scatter_m(own, 0))
-        got = lax.all_to_all(own, ("l", "x"), 0, 0)
-        return [merge(got[:, i]) for i in range(own.shape[1])]
+    def exchange_feed(own):
+        return lax.all_to_all(low(scatter_m(own, 0)), ("l", "x"), 0, 0)
 
     both_grad = both_grad.reshape(2, M, 4, rows, part).transpose(1, 2, 0, 3, 4)
-    gate_weight_grad, up_weight_grad = finish_feed(both_grad)
+    both_parts = exchange_feed(both_grad)
     query_total, query_got = next_fold(query_total + query_got.astype(F32), "h")
-    down_own = sync(quarter(0, down_h1, down_y2), gate_weight_grad)[0]
-    (down_weight_grad,) = finish_feed(down_own.reshape(M, 4, 1, rows, part))
+    down_own, both_parts = sync(quarter(0, down_h1, down_y2), both_parts)
+    down_parts = exchange_feed(down_own.reshape(M, 4, 1, rows, part))
+    gate_weight_grad, up_weight_grad = (merge(both_parts[:, i]) for i in range(2))
+    down_weight_grad = merge(down_parts[:, 0])
     query_total = scatter_m(query_total + query_got.astype(F32), 0)
     query_weight_grad = query_total[:, :query_width]
     keyvalue_weight_grad = query_total[:, query_width : query_width + 2 * HEAD_DIM]

time: 608 us -> 606 us (level)
  transfers between devices with their start and end apart: 91 -> 91, of which waited for: 34 -> 35; matrix products, arithmetic and copies ran while one was open for 19% -> 19% of each run, Pallas kernels for 16% -> 16%
where the time goes in v8:
time: 606 us; the launch traced here: 600 us
  waiting for transfers between devices  212 us (35%)
  Pallas kernels  117 us (19%)
  starting transfers between devices  111 us (18%)
  other arithmetic  68.2 us (11%)
  local copies, waits for them, and re-layouts  63 us (10%)
  between operations  16.4 us (3%)
  matrix products  12 us (2%)
    ppermute x83, waiting for transfers between devices, swap(): return lax.ppermute(value, axis, [(0, 1), (1, 0)])  193 us
    pallas_call x7, Pallas kernels, local_call(): pl.pallas_call(kernel, out_shape=outs, in_specs=near + [pl.BlockSpec(memo...  103 us
    ppermute x83, starting transfers between devices, swap(): return lax.ppermute(value, axis, [(0, 1), (1, 0)])  67.6 us
    unnamed x190, local copies, waits for them, and re-layouts  23.8 us
    all_to_all x1, starting transfers between devices, on_device(): feed = gather_m(lax.all_to_all(feed_parts, ('l', 'x'), 0, 0), 0)  17 us
  transfers between devices with their start and end apart: 91, of which 35 were waited for; matrix products, arithmetic and copies ran while one was open for 19% of the time, Pallas kernels for 16%

profile of v8, /device:TPU:0, one launch (start us, length us, event | category | flops | bytes accessed | tf_op | source)
XLA Modules:
  0.0 599.5 jit_solution(11606428989711805434)
XLA Ops:
  8.7 2.9 collective-permute-start
  28.1 3.8 shard_map.212
  32.0 6.4 %collective-permute-done.3 = bf16[2,80,256]{2,1,0:T(8,128)(2,1)S(1)} collective-permute-done((bf16[2,80,256]{2,1,0:T(8,128)(2,1)S(1)}, bf16[2,80,256]{2,1,0:T(8,128)(2,1)S(1)}, u32[]{:S(2)}, u32[]{:S(2)}) %collective-permute-start.3) | collective-permute-done | bytes 81952 | tf_op jit(solution)/shard_map/ppermute | solution.py:56
  39.2 2.8 collective-permute-start.7
  43.0 4.9 collective-permute-done.7
  50.2 17.0 %all-to-all-start = ((bf16[4,3,64,1408]{3,2,1,0:T(8,128)(2,1)}), bf16[4,3,64,1408]{3,2,1,0:T(8,128)(2,1)}, u32[]{:S(2)}, u32[]{:S(2)}) async-start(bf16[4,3,64,1408]{3,2,1,0:T(8,128)(2,1)} %shard_map.212), calls=%async_computation | async-start | bytes 4325376 | tf_op jit(solution)/shard_map/all_to_all | solution.py:498
  74.5 10.7 %collective-permute-done.14 = bf16[128,256]{1,0:T(8,128)(2,1)S(1)} collective-permute-done((bf16[128,256]{1,0:T(8,128)(2,1)S(1)}, bf16[128,256]{1,0:T(8,128)(2,1)S(1)}, u32[]{:S(2)}, u32[]{:S(2)}) %collective-permute-start.14) | collective-permute-done | bytes 65568 | tf_op jit(solution)/shard_map/ppermute | solution.py:56
  85.3 9.9 %collective-permute-start.15 = (bf16[1,2,128,256]{3,2,1,0:T(8,128)(2,1)S(1)}, bf16[1,2,128,256]{3,2,1,0:T(8,128)(2,1)S(1)}, u32[]{:S(2)}, u32[]{:S(2)}) collective-permute-start(bf16[1,2,128,256]{3,2,1,0:T(8,128)(2,1)S(1)} %maximum_bitcast_fusion), channel_id=1, source_target_pairs={{0,4},{4,0},{1,5},{5,1},{2,6},{6,2},{3,7},{7,3},{8,12},{12,8},{9,1... | collective-permute-start | bytes 393224 | tf_op jit(solution)/shard_map/ppermute | solution.py:56
  98.8 2.6 slice_bitcast_fusion.5
  104.1 8.1 %collective-permute-done.18 = bf16[1,2,2,64,1024]{4,3,2,1,0:T(8,128)(2,1)} collective-permute-done((bf16[1,2,2,64,1024]{4,3,2,1,0:T(8,128)(2,1)}, bf16[1,2,2,64,1024]{4,3,2,1,0:T(8,128)(2,1)}, u32[]{:S(2)}, u32[]{:S(2)}) %collective-permute-start.18) | collective-permute-done | bytes 524320 | tf_op jit(solution)/shard_map/ppermute | solution.py:56
  116.0 3.2 collective-permute-done.21
  119.4 2.3 pad_maximum_fusion.9
  127.5 2.1 pad_maximum_fusion.10
  129.6 15.6 %shard_map.213 = (bf16[1024,256]{1,0:T(8,128)(2,1)}, f32[1024,256]{1,0:T(8,128)}, bf16[1024,256]{1,0:T(8,128)(2,1)}, f32[8,256]{1,0:T(8,128)}) custom-call(bf16[256,2048]{1,0:T(8,128)(2,1)} %pad_maximum_fusion.7.normed, bf16[1024,1024]{1,0:T(8,128)(2,1)} %bitcast.251, bf16[256,1024]{1,0:T(8,128)(2,1)} %copy-done.53, bf16[256,1024]{1,0:T(8,128)(2,1)} %copy-done.51, ...), custom_call_target="tpu_custom_call" | custom-call | flops 1 | bytes 1 | tf_op jit(solution)/shard_map/pallas_call | solution.py:385
  145.2 18.6 %collective-permute-done.29.refs_2_.refs_10_ = bf16[4,64,1408]{2,1,0:T(8,128)(2,1)} collective-permute-done((bf16[4,64,1408]{2,1,0:T(8,128)(2,1)S(1)}, bf16[4,64,1408]{2,1,0:T(8,128)(2,1)}, u32[]{:S(2)}, u32[]{:S(2)}) %collective-permute-start.29) | collective-permute-done | bytes 720928 | tf_op jit(solution)/shard_map/ppermute | solution.py:56
  178.8 8.8 %collective-permute-done.36.refs_10_.refs_18_ = bf16[4,64,1408]{2,1,0:T(8,128)(2,1)S(1)} collective-permute-done((bf16[4,64,1408]{2,1,0:T(8,128)(2,1)S(1)}, bf16[4,64,1408]{2,1,0:T(8,128)(2,1)S(1)}, u32[]{:S(2)}, u32[]{:S(2)}) %collective-permute-start.36) | collective-permute-done | bytes 720928 | tf_op jit(solution)/shard_map/ppermute | solution.py:56
  187.5 14.1 %collective-permute-done.35.refs_9_.refs_17_ = bf16[4,64,1408]{2,1,0:T(8,128)(2,1)S(1)} collective-permute-done((bf16[4,64,1408]{2,1,0:T(8,128)(2,1)S(1)}, bf16[4,64,1408]{2,1,0:T(8,128)(2,1)S(1)}, u32[]{:S(2)}, u32[]{:S(2)}) %collective-permute-start.35) | collective-permute-done | bytes 720928 | tf_op jit(solution)/shard_map/ppermute | solution.py:56
  205.7 3.6 all-to-all-start.1
  213.3 15.3 %collective-permute-done.38.refs_11_.refs_19_ = bf16[4,64,1408]{2,1,0:T(8,128)(2,1)S(1)} collective-permute-done((bf16[4,64,1408]{2,1,0:T(8,128)(2,1)}, bf16[4,64,1408]{2,1,0:T(8,128)(2,1)S(1)}, u32[]{:S(2)}, u32[]{:S(2)}) %collective-permute-start.38) | collective-permute-done | bytes 720928 | tf_op jit(solution)/shard_map/ppermute | solution.py:56
  229.2 13.6 %collective-permute-done.40.refs_2_ = bf16[4,64,1408]{2,1,0:T(8,128)(2,1)S(1)} collective-permute-done((bf16[4,64,1408]{2,1,0:T(8,128)(2,1)}, bf16[4,64,1408]{2,1,0:T(8,128)(2,1)S(1)}, u32[]{:S(2)}, u32[]{:S(2)}) %collective-permute-start.40) | collective-permute-done | bytes 720928 | tf_op jit(solution)/shard_map/ppermute | solution.py:56
  242.8 4.9 collective-permute-done.39.refs_1_
  254.4 6.2 %all-to-all-start.2 = ((bf16[4,128,2048]{2,1,0:T(8,128)(2,1)}), bf16[4,128,2048]{2,1,0:T(8,128)(2,1)S(1)}, u32[]{:S(2)}, u32[]{:S(2)}) async-start(bf16[4,128,2048]{2,1,0:T(8,128)(2,1)} %broadcast_in_dim.21), calls=%async_computation.2 | async-start | bytes 4194304 | tf_op jit(solution)/shard_map/all_to_all | solution.py:108
  264.3 14.6 %shard_map.214 = (f32[512,1408]{1,0:T(8,128)}, f32[512,1408]{1,0:T(8,128)}) custom-call(bf16[512,2048]{1,0:T(8,128)(2,1)} %bitcast.255, bf16[4,64,1408]{2,1,0:T(8,128)(2,1)} %copy-done.19, bf16[4,64,1408]{2,1,0:T(8,128)(2,1)} %collective-permute-done.28.refs_1_.refs_9_, bf16[4,64,1408]{2,1,0:T(8,128)(2,1)} %collective-permute-done.29.refs_2_.refs_10_, ...), custom_call_target="tpu_custom_call" | custom-call | flops 1 | bytes 1 | tf_op jit(solution)/shard_map/pallas_call | solution.py:385
  282.4 3.4 all-to-all-done.2
  287.3 20.7 %shard_map.215 = (bf16[512,1408]{1,0:T(8,128)(2,1)}, bf16[512,1408]{1,0:T(8,128)(2,1)}, bf16[512,1408]{1,0:T(8,128)(2,1)}, bf16[512,2048]{1,0:T(8,128)(2,1)}) custom-call(bf16[512,2048]{1,0:T(8,128)(2,1)} %bitcast.253, f32[512,1408]{1,0:T(8,128)} %get-tuple-element.256.gate_sum, f32[512,1408]{1,0:T(8,128)} %get-tuple-element.257.up_sum, ...), custom_call_target="tpu_custom_call" | custom-call | flops 1 | bytes 1 | tf_op jit(solution)/shard_map/pallas_call | solution.py:385
  307.9 4.5 all-to-all-start.3
  313.1 14.9 %shard_map.216 = bf16[8,2,256,1408]{3,2,1,0:T(8,128)(2,1)} custom-call(s32[8]{0:T(128)} %stack.417.order, bf16[512,2048]{1,0:T(8,128)(2,1)} %bitcast.256, bf16[512,1408]{1,0:T(8,128)(2,1)} %get-tuple-element.264.refs_0_, bf16[512,1408]{1,0:T(8,128)(2,1)} %get-tuple-element.265.refs_1_), custom_call_target="tpu_custom_call" | custom-call | flops 1 | bytes 1 | tf_op jit(solution)/shard_map/pallas_call | solution.py:385
  328.0 8.3 %shard_map.217 = (bf16[1024,1408]{1,0:T(8,128)(2,1)}, bf16[1024,1408]{1,0:T(8,128)(2,1)}) custom-call(bf16[512,2048]{1,0:T(8,128)(2,1)} %bitcast.254, bf16[512,1408]{1,0:T(8,128)(2,1)} %get-tuple-element.272.refs_0_.mixed), custom_call_target="tpu_custom_call" | custom-call | flops 1 | bytes 1 | tf_op jit(solution)/shard_map/pallas_call | solution.py:385
  343.3 2.2 convert_reduce_fusion.1
  348.1 12.0 %shard_map.218 = bf16[512,2048]{1,0:T(8,128)(2,1)} custom-call(bf16[512,1408]{1,0:T(8,128)(2,1)} %get-tuple-element.272.refs_0_.mixed, bf16[4,64,1408]{2,1,0:T(8,128)(2,1)} %get-tuple-element.235.refs_0_, bf16[4,64,1408]{2,1,0:T(8,128)(2,1)} %copy-done.30, bf16[4,64,1408]{2,1,0:T(8,128)(2,1)} %copy-done.29, bf16[4,64,1408]{2,1,0:T(8,128)(2,1)} %copy-done.34, ...), custom_call_target="tpu_custom_call" | custom-call | flops 1 | bytes 1 | tf_op jit(solution)/shard_map/pallas_call | solution.py:385
  360.2 2.4 add_convert_fusion.3
  363.3 4.6 all-to-all-start.4
  370.0 17.0 %shard_map.219 = (bf16[1024,256]{1,0:T(8,128)(2,1)}, f32[2048,256]{1,0:T(8,128)}) custom-call(bf16[1024,256]{1,0:T(8,128)(2,1)} %get-tuple-element.226.query_rot, bf16[2048,256]{1,0:T(8,128)(2,1)} %bitcast.266, bf16[256,2048]{1,0:T(8,128)(2,1)} %copy-done.11, bf16[2048,1024]{1,0:T(8,128)(2,1)} %copy-done.13, f32[1024,256]{1,0:T(8,128)} %get-tuple-element.274.attended, ...), custom_call_target="tpu_custom_call" | custom-call | flops 1 | bytes 1 | tf_op jit(solution)/shard_map/pallas_call | solution.py:385
  387.1 2.1 convert.73
  395.3 4.8 fusion.63
  400.1 3.3 convolution_convert_fusion
  407.5 2.9 convert_add_fusion.1
  410.4 5.6 all-to-all-done.4
  416.1 2.2 convert_reduce_fusion
  418.4 3.2 collective-permute-done.65
  425.9 2.8 fusion.22
  428.7 3.4 collective-permute-done.66
  432.1 3.4 collective-permute-done.67
  440.8 3.6 fusion.1
  446.2 2.9 add_convert_fusion.1
  450.6 5.1 pad_maximum_fusion.1
  455.7 11.8 %collective-permute-done.73 = bf16[2,2,1,2,64,1024]{5,4,1,0,3,2:T(8,128)(2,1)} collective-permute-done((bf16[2,2,1,2,64,1024]{5,4,1,0,3,2:T(8,128)(2,1)}, bf16[2,2,1,2,64,1024]{5,4,1,0,3,2:T(8,128)(2,1)}, u32[]{:S(2)}, u32[]{:S(2)}) %collective-permute-start.73) | collective-permute-done | bytes 1048608 | tf_op jit(solution)/shard_map/ppermute | solution.py:56
  471.1 2.4 copy-done.8
  477.8 6.3 %collective-permute-done.75 = bf16[2,2,1,64,1024]{4,3,1,0,2:T(8,128)(2,1)} collective-permute-done((bf16[2,2,1,64,1024]{4,3,1,0,2:T(8,128)(2,1)}, bf16[2,2,1,64,1024]{4,3,1,0,2:T(8,128)(2,1)}, u32[]{:S(2)}, u32[]{:S(2)}) %collective-permute-start.75) | collective-permute-done | bytes 524320 | tf_op jit(solution)/shard_map/ppermute | solution.py:56
  486.9 2.2 convert_element_type.356
  493.9 8.5 %collective-permute-done.77 = bf16[2,1,64,2048]{3,2,0,1:T(8,128)(2,1)} collective-permute-done((bf16[2,1,64,2048]{3,2,0,1:T(8,128)(2,1)}, bf16[2,1,64,2048]{3,2,0,1:T(8,128)(2,1)}, u32[]{:S(2)}, u32[]{:S(2)}) %collective-permute-start.77) | collective-permute-done | bytes 524320 | tf_op jit(solution)/shard_map/ppermute | solution.py:56
  502.4 18.2 %collective-permute-done.74 = bf16[2,2,1,2,64,1408]{5,4,1,0,3,2:T(8,128)(2,1)} collective-permute-done((bf16[2,2,1,2,64,1408]{5,4,1,0,3,2:T(8,128)(2,1)}, bf16[2,2,1,2,64,1408]{5,4,1,0,3,2:T(8,128)(2,1)}, u32[]{:S(2)}, u32[]{:S(2)}) %collective-permute-start.74) | collective-permute-done | bytes 1441824 | tf_op jit(solution)/shard_map/ppermute | solution.py:56
  520.6 2.5 bitcast_add_fusion
  523.2 2.3 collective-permute-start.78
  527.8 12.2 %collective-permute-done.79 = bf16[1,64,2048]{2,1,0:T(8,128)(2,1)} collective-permute-done((bf16[1,64,2048]{2,1,0:T(8,128)(2,1)S(1)}, bf16[1,64,2048]{2,1,0:T(8,128)(2,1)}, u32[]{:S(2)}, u32[]{:S(2)}) %collective-permute-start.79) | collective-permute-done | bytes 262176 | tf_op jit(solution)/shard_map/ppermute | solution.py:56
  543.7 2.9 collective-permute-start.81
  547.8 3.6 all-to-all-start.5
  551.4 3.0 add_convert_fusion
  554.6 5.0 collective-permute-done.81
  563.5 9.6 %all-to-all-done.5 = bf16[4,2,64,1408]{3,2,1,0:T(8,128)(2,1)S(1)} async-done(((bf16[4,2,64,1408]{3,2,1,0:T(8,128)(2,1)}), bf16[4,2,64,1408]{3,2,1,0:T(8,128)(2,1)S(1)}, u32[]{:S(2)}, u32[]{:S(2)}) %all-to-all-start.5) | async-done | bytes 1441824 | tf_op jit(solution)/shard_map/all_to_all | solution.py:783
  573.0 3.5 all-to-all-start.6
  581.2 3.4 shard_map.221
  584.6 3.4 shard_map.220
  588.9 3.4 shard_map.222
  (503 shorter events, 151.4 us)
Async XLA Ops:
  8.7 14.6 %collective-permute-start = (bf16[80,256]{1,0:T(8,128)(2,1)S(1)}, bf16[80,256]{1,0:T(8,128)(2,1)S(1)}, u32[]{:S(2)}, u32[]{:S(2)}) collective-permute-start(bf16[80,256]{1,0:T(8,128)(2,1)S(1)} %get-tuple-element.415), channel_id=1, source_target_pairs={{0,2},{2,0},{1,3},{3,1},{4,6},{6,4},{5,7},{7,5},{8,10},{10,8},{9,1... | collective-permute-start | bytes 122888 | tf_op jit(solution)/shard_map/ppermute | solution.py:56
  15.1 8.2 %collective-permute-start.1 = (bf16[64,1024]{1,0:T(8,128)(2,1)S(1)}, bf16[64,1024]{1,0:T(8,128)(2,1)S(1)}, u32[]{:S(2)}, u32[]{:S(2)}) collective-permute-start(bf16[64,1024]{1,0:T(8,128)(2,1)S(1)} %bitcast.321), channel_id=1, source_target_pairs={{0,2},{2,0},{1,3},{3,1},{4,6},{6,4},{5,7},{7,5},{8,10},{10,8},{9,1... | collective-permute-start | bytes 393224 | tf_op jit(solution)/shard_map/ppermute | solution.py:56
  15.2 8.1 %collective-permute-start.2 = (bf16[64,1024]{1,0:T(8,128)(2,1)S(1)}, bf16[64,1024]{1,0:T(8,128)(2,1)S(1)}, u32[]{:S(2)}, u32[]{:S(2)}) collective-permute-start(bf16[64,1024]{1,0:T(8,128)(2,1)S(1)} %bitcast.322), channel_id=1, source_target_pairs={{0,2},{2,0},{1,3},{3,1},{4,6},{6,4},{5,7},{7,5},{8,10},{10,8},{9,1... | collective-permute-start | bytes 393224 | tf_op jit(solution)/shard_map/ppermute | solution.py:56
  23.6 14.8 %collective-permute-start.6 = (bf16[128,2048]{1,0:T(8,128)(2,1)S(1)}, bf16[128,2048]{1,0:T(8,128)(2,1)S(1)}, u32[]{:S(2)}, u32[]{:S(2)}) collective-permute-start(bf16[128,2048]{1,0:T(8,128)(2,1)S(1)} %copy.155), channel_id=1, source_target_pairs={{0,2},{2,0},{1,3},{3,1},{4,6},{6,4},{5,7},{7,5},{8,10},{10,8},{9,1... | collective-permute-start | bytes 1572872 | tf_op jit(solution)/shard_map/ppermute | solution.py:56
  23.7 14.7 %collective-permute-start.4 = (bf16[2,64,1024]{2,1,0:T(8,128)(2,1)S(1)}, bf16[2,64,1024]{2,1,0:T(8,128)(2,1)S(1)}, u32[]{:S(2)}, u32[]{:S(2)}) collective-permute-start(bf16[2,64,1024]{2,1,0:T(8,128)(2,1)S(1)} %maximum_select_fusion.4), channel_id=1, source_target_pairs={{0,4},{4,0},{1,5},{5,1},{2,6},{6,2},{3,7},{7,3},{8,12},{12,8},{9,1... | collective-permute-start | bytes 786440 | tf_op jit(solution)/shard_map/ppermute | solution.py:56
  25.9 12.5 %collective-permute-start.5 = (bf16[2,64,1024]{2,1,0:T(8,128)(2,1)S(1)}, bf16[2,64,1024]{2,1,0:T(8,128)(2,1)S(1)}, u32[]{:S(2)}, u32[]{:S(2)}) collective-permute-start(bf16[2,64,1024]{2,1,0:T(8,128)(2,1)S(1)} %maximum_select_fusion.5), channel_id=1, source_target_pairs={{0,4},{4,0},{1,5},{5,1},{2,6},{6,2},{3,7},{7,3},{8,12},{12,8},{9,1... | collective-permute-start | bytes 786440 | tf_op jit(solution)/shard_map/ppermute | solution.py:56
  26.1 12.3 %collective-permute-start.3 = (bf16[2,80,256]{2,1,0:T(8,128)(2,1)S(1)}, bf16[2,80,256]{2,1,0:T(8,128)(2,1)S(1)}, u32[]{:S(2)}, u32[]{:S(2)}) collective-permute-start(bf16[2,80,256]{2,1,0:T(8,128)(2,1)S(1)} %maximum_select_fusion.9), channel_id=1, source_target_pairs={{0,4},{4,0},{1,5},{5,1},{2,6},{6,2},{3,7},{7,3},{8,12},{12,8},{9,1... | collective-permute-start | bytes 245768 | tf_op jit(solution)/shard_map/ppermute | solution.py:56
  39.2 8.6 %collective-permute-start.7 = (bf16[1,2,2,80,256]{4,3,2,1,0:T(8,128)(2,1)S(1)}, bf16[1,2,2,80,256]{4,3,2,1,0:T(8,128)(2,1)S(1)}, u32[]{:S(2)}, u32[]{:S(2)}) collective-permute-start(bf16[1,2,2,80,256]{4,3,2,1,0:T(8,128)(2,1)S(1)} %maximum_select_fusion.8), channel_id=1, source_target_pairs={{0,8},{8,0},{1,9},{9,1},{2,10},{10,2},{3,11},{11,3},{4,12},{12,4},... | collective-permute-start | bytes 491528 | tf_op jit(solution)/shard_map/ppermute | solution.py:56
  47.9 19.4 %collective-permute-start.8 = (bf16[2,1,2,2,80,256]{5,4,3,2,1,0:T(8,128)(2,1)S(1)}, bf16[2,1,2,2,80,256]{5,4,3,2,1,0:T(8,128)(2,1)S(1)}, u32[]{:S(2)}, u32[]{:S(2)}) collective-permute-start(bf16[2,1,2,2,80,256]{5,4,3,2,1,0:T(8,128)(2,1)S(1)} %pad_maximum_fusion.16), channel_id=1, source_target_pairs={{0,16},{16,0},{1,17},{17,1},{2,18},{18,2},{3,19},{19,3},{4,20},{20... | collective-permute-start | bytes 983048 | tf_op jit(solution)/shard_map/ppermute | solution.py:56
  49.6 20.1 %collective-permute-start.13 = (bf16[1,2,2,64,1024]{4,3,2,1,0:T(8,128)(2,1)S(1)}, bf16[1,2,2,64,1024]{4,3,2,1,0:T(8,128)(2,1)S(1)}, u32[]{:S(2)}, u32[]{:S(2)}) collective-permute-start(bf16[1,2,2,64,1024]{4,3,2,1,0:T(8,128)(2,1)S(1)} %maximum_select_fusion.2), channel_id=1, source_target_pairs={{0,8},{8,0},{1,9},{9,1},{2,10},{10,2},{3,11},{11,3},{4,12},{12,4},... | collective-permute-start | bytes 1572872 | tf_op jit(solution)/shard_map/ppermute | solution.py:56
  50.2 48.6 %all-to-all-start = ((bf16[4,3,64,1408]{3,2,1,0:T(8,128)(2,1)}), bf16[4,3,64,1408]{3,2,1,0:T(8,128)(2,1)}, u32[]{:S(2)}, u32[]{:S(2)}) async-start(bf16[4,3,64,1408]{3,2,1,0:T(8,128)(2,1)} %shard_map.212), calls=%async_computation | async-start | bytes 4325376 | tf_op jit(solution)/shard_map/all_to_all | solution.py:498
  72.3 12.9 %collective-permute-start.14 = (bf16[128,256]{1,0:T(8,128)(2,1)S(1)}, bf16[128,256]{1,0:T(8,128)(2,1)S(1)}, u32[]{:S(2)}, u32[]{:S(2)}) collective-permute-start(bf16[128,256]{1,0:T(8,128)(2,1)S(1)} %pad_maximum_fusion.19), channel_id=1, source_target_pairs={{0,8},{8,0},{1,9},{9,1},{2,10},{10,2},{3,11},{11,3},{4,12},{12,4},... | collective-permute-start | bytes 196616 | tf_op jit(solution)/shard_map/ppermute | solution.py:56
  73.5 38.6 %collective-permute-start.17 = (bf16[2,1,2,2,64,1024]{5,4,3,2,1,0:T(8,128)(2,1)S(1)}, bf16[2,1,2,2,64,1024]{5,4,3,2,1,0:T(8,128)(2,1)}, u32[]{:S(2)}, u32[]{:S(2)}) collective-permute-start(bf16[2,1,2,2,64,1024]{5,4,3,2,1,0:T(8,128)(2,1)S(1)} %pad_maximum_fusion.8), channel_id=1, source_target_pairs={{0,16},{16,0},{1,17},{17,1},{2,18},{18,2},{3,19},{19,3},{4,20},{20... | collective-permute-start | bytes 3145736 | tf_op jit(solution)/shard_map/ppermute | solution.py:56
  85.3 13.5 %collective-permute-start.15 = (bf16[1,2,128,256]{3,2,1,0:T(8,128)(2,1)S(1)}, bf16[1,2,128,256]{3,2,1,0:T(8,128)(2,1)S(1)}, u32[]{:S(2)}, u32[]{:S(2)}) collective-permute-start(bf16[1,2,128,256]{3,2,1,0:T(8,128)(2,1)S(1)} %maximum_bitcast_fusion), channel_id=1, source_target_pairs={{0,4},{4,0},{1,5},{5,1},{2,6},{6,2},{3,7},{7,3},{8,12},{12,8},{9,1... | collective-permute-start | bytes 393224 | tf_op jit(solution)/shard_map/ppermute | solution.py:56
  96.7 15.5 %collective-permute-start.18 = (bf16[1,2,2,64,1024]{4,3,2,1,0:T(8,128)(2,1)}, bf16[1,2,2,64,1024]{4,3,2,1,0:T(8,128)(2,1)}, u32[]{:S(2)}, u32[]{:S(2)}) collective-permute-start(bf16[1,2,2,64,1024]{4,3,2,1,0:T(8,128)(2,1)} %maximum_select_fusion.3), channel_id=1, source_target_pairs={{0,8},{8,0},{1,9},{9,1},{2,10},{10,2},{3,11},{11,3},{4,12},{12,4},... | collective-permute-start | bytes 1572872 | tf_op jit(solution)/shard_map/ppermute | solution.py:56
  102.5 9.7 %collective-permute-start.16 = (bf16[2,1,2,128,256]{4,3,2,0,1:T(8,128)(2,1)S(1)}, bf16[2,1,2,128,256]{4,3,2,0,1:T(8,128)(2,1)S(1)}, u32[]{:S(2)}, u32[]{:S(2)}) collective-permute-start(bf16[2,1,2,128,256]{4,3,2,0,1:T(8,128)(2,1)S(1)} %bitcast.302), channel_id=1, source_target_pairs={{0,2},{2,0},{1,3},{3,1},{4,6},{6,4},{5,7},{7,5},{8,10},{10,8},{9,1... | collective-permute-start | bytes 786440 | tf_op jit(solution)/shard_map/ppermute | solution.py:56
  114.9 7.6 %collective-permute-start.26 = (bf16[256,1024]{1,0:T(8,128)(2,1)S(1)}, bf16[256,1024]{1,0:T(8,128)(2,1)S(1)}, u32[]{:S(2)}, u32[]{:S(2)}) collective-permute-start(bf16[256,1024]{1,0:T(8,128)(2,1)S(1)} %get-tuple-element.381), channel_id=1, source_target_pairs={{0,1},{1,0},{2,3},{3,2},{4,5},{5,4},{6,7},{7,6},{8,9},{9,8},{10,11... | collective-permute-start | bytes 1572872 | tf_op jit(solution)/shard_map/ppermute | solution.py:56
  114.9 7.6 %collective-permute-start.25 = (bf16[256,1024]{1,0:T(8,128)(2,1)S(1)}, bf16[256,1024]{1,0:T(8,128)(2,1)S(1)}, u32[]{:S(2)}, u32[]{:S(2)}) collective-permute-start(bf16[256,1024]{1,0:T(8,128)(2,1)S(1)} %get-tuple-element.382), channel_id=1, source_target_pairs={{0,1},{1,0},{2,3},{3,2},{4,5},{5,4},{6,7},{7,6},{8,9},{9,8},{10,11... | collective-permute-start | bytes 1572872 | tf_op jit(solution)/shard_map/ppermute | solution.py:56
  115.4 7.1 %collective-permute-start.23 = (bf16[256,1024]{1,0:T(8,128)(2,1)S(1)}, bf16[256,1024]{1,0:T(8,128)(2,1)S(1)}, u32[]{:S(2)}, u32[]{:S(2)}) collective-permute-start(bf16[256,1024]{1,0:T(8,128)(2,1)S(1)} %get-tuple-element.384), channel_id=1, source_target_pairs={{0,1},{1,0},{2,3},{3,2},{4,5},{5,4},{6,7},{7,6},{8,9},{9,8},{10,11... | collective-permute-start | bytes 1572872 | tf_op jit(solution)/shard_map/ppermute | solution.py:56
  122.6 41.3 %collective-permute-start.27 = (bf16[2,1,2,2,64,1024]{5,4,3,2,0,1:T(8,128)(2,1)}, bf16[2,1,2,2,64,1024]{5,4,3,2,0,1:T(8,128)(2,1)}, u32[]{:S(2)}, u32[]{:S(2)}) collective-permute-start(bf16[2,1,2,2,64,1024]{5,4,3,2,0,1:T(8,128)(2,1)} %bitcast.72), channel_id=1, source_target_pairs={{0,16},{16,0},{1,17},{17,1},{2,18},{18,2},{3,19},{19,3},{4,20},{20... | collective-permute-start | bytes 3145736 | tf_op jit(solution)/shard_map/ppermute | solution.py:56
  123.6 40.2 %collective-permute-start.29 = (bf16[4,64,1408]{2,1,0:T(8,128)(2,1)S(1)}, bf16[4,64,1408]{2,1,0:T(8,128)(2,1)}, u32[]{:S(2)}, u32[]{:S(2)}) collective-permute-start(bf16[4,64,1408]{2,1,0:T(8,128)(2,1)S(1)} %get-tuple-element.236.refs_0_.refs_8_), channel_id=1, source_target_pairs={{0,16},{16,0},{1,17},{17,1},{2,18},{18,2},{3,19},{19,3},{4,20},{20... | collective-permute-start | bytes 2162696 | tf_op jit(solution)/shard_map/ppermute | solution.py:56
  124.7 39.2 %collective-permute-start.28 = (bf16[4,64,1408]{2,1,0:T(8,128)(2,1)S(1)}, bf16[4,64,1408]{2,1,0:T(8,128)(2,1)}, u32[]{:S(2)}, u32[]{:S(2)}) collective-permute-start(bf16[4,64,1408]{2,1,0:T(8,128)(2,1)S(1)} %get-tuple-element.236.refs_0_.refs_8_), channel_id=1, source_target_pairs={{0,8},{8,0},{1,9},{9,1},{2,10},{10,2},{3,11},{11,3},{4,12},{12,4},... | collective-permute-start | bytes 2162696 | tf_op jit(solution)/shard_map/ppermute | solution.py:56
  168.5 19.0 %collective-permute-start.36 = (bf16[4,64,1408]{2,1,0:T(8,128)(2,1)S(1)}, bf16[4,64,1408]{2,1,0:T(8,128)(2,1)S(1)}, u32[]{:S(2)}, u32[]{:S(2)}) collective-permute-start(bf16[4,64,1408]{2,1,0:T(8,128)(2,1)S(1)} %get-tuple-element.240.refs_8_.refs_16_), channel_id=1, source_target_pairs={{0,16},{16,0},{1,17},{17,1},{2,18},{18,2},{3,19},{19,3},{4,20},{20... | collective-permute-start | bytes 2162696 | tf_op jit(solution)/shard_map/ppermute | solution.py:56
  169.5 32.1 %collective-permute-start.35 = (bf16[4,64,1408]{2,1,0:T(8,128)(2,1)S(1)}, bf16[4,64,1408]{2,1,0:T(8,128)(2,1)S(1)}, u32[]{:S(2)}, u32[]{:S(2)}) collective-permute-start(bf16[4,64,1408]{2,1,0:T(8,128)(2,1)S(1)} %get-tuple-element.240.refs_8_.refs_16_), channel_id=1, source_target_pairs={{0,8},{8,0},{1,9},{9,1},{2,10},{10,2},{3,11},{11,3},{4,12},{12,4},... | collective-permute-start | bytes 2162696 | tf_op jit(solution)/shard_map/ppermute | solution.py:56
  175.0 27.2 %collective-permute-start.37 = (bf16[4,64,1408]{2,1,0:T(8,128)(2,1)}, bf16[4,64,1408]{2,1,0:T(8,128)(2,1)}, u32[]{:S(2)}, u32[]{:S(2)}) collective-permute-start(bf16[4,64,1408]{2,1,0:T(8,128)(2,1)} %collective-permute-done.28.refs_1_.refs_9_), channel_id=1, source_target_pairs={{0,16},{16,0},{1,17},{17,1},{2,18},{18,2},{3,19},{19,3},{4,20},{20... | collective-permute-start | bytes 2162696 | tf_op jit(solution)/shard_map/ppermute | solution.py:56
  176.4 25.2 %collective-permute-start.34 = (bf16[128,2048]{1,0:T(8,128)(2,1)S(1)}, bf16[128,2048]{1,0:T(8,128)(2,1)}, u32[]{:S(2)}, u32[]{:S(2)}) collective-permute-start(bf16[128,2048]{1,0:T(8,128)(2,1)S(1)} %slice.548), channel_id=1, source_target_pairs={{0,2},{2,0},{1,3},{3,1},{4,6},{6,4},{5,7},{7,5},{8,10},{10,8},{9,1... | collective-permute-start | bytes 1572872 | tf_op jit(solution)/shard_map/ppermute | solution.py:56
  205.7 47.4 %all-to-all-start.1 = ((bf16[4,128,2048]{2,1,0:T(8,128)(2,1)}), bf16[4,128,2048]{2,1,0:T(8,128)(2,1)S(1)}, u32[]{:S(2)}, u32[]{:S(2)}) async-start(bf16[4,128,2048]{2,1,0:T(8,128)(2,1)} %broadcast_in_dim.22), calls=%async_computation.1 | async-start | bytes 4194304 | tf_op jit(solution)/shard_map/all_to_all | solution.py:108
  209.3 19.3 %collective-permute-start.38 = (bf16[4,64,1408]{2,1,0:T(8,128)(2,1)}, bf16[4,64,1408]{2,1,0:T(8,128)(2,1)S(1)}, u32[]{:S(2)}, u32[]{:S(2)}) collective-permute-start(bf16[4,64,1408]{2,1,0:T(8,128)(2,1)} %copy-done.38), channel_id=1, source_target_pairs={{0,16},{16,0},{1,17},{17,1},{2,18},{18,2},{3,19},{19,3},{4,20},{20... | collective-permute-start | bytes 2162696 | tf_op jit(solution)/shard_map/ppermute | solution.py:56
  210.4 32.4 %collective-permute-start.40 = (bf16[4,64,1408]{2,1,0:T(8,128)(2,1)}, bf16[4,64,1408]{2,1,0:T(8,128)(2,1)S(1)}, u32[]{:S(2)}, u32[]{:S(2)}) collective-permute-start(bf16[4,64,1408]{2,1,0:T(8,128)(2,1)} %get-tuple-element.235.refs_0_), channel_id=1, source_target_pairs={{0,16},{16,0},{1,17},{17,1},{2,18},{18,2},{3,19},{19,3},{4,20},{20... | collective-permute-start | bytes 2162696 | tf_op jit(solution)/shard_map/ppermute | solution.py:56
  211.4 36.2 %collective-permute-start.39 = (bf16[4,64,1408]{2,1,0:T(8,128)(2,1)}, bf16[4,64,1408]{2,1,0:T(8,128)(2,1)S(1)}, u32[]{:S(2)}, u32[]{:S(2)}) collective-permute-start(bf16[4,64,1408]{2,1,0:T(8,128)(2,1)} %get-tuple-element.235.refs_0_), channel_id=1, source_target_pairs={{0,8},{8,0},{1,9},{9,1},{2,10},{10,2},{3,11},{11,3},{4,12},{12,4},... | collective-permute-start | bytes 2162696 | tf_op jit(solution)/shard_map/ppermute | solution.py:56
  228.7 19.0 %collective-permute-start.41 = (bf16[4,64,1408]{2,1,0:T(8,128)(2,1)}, bf16[4,64,1408]{2,1,0:T(8,128)(2,1)S(1)}, u32[]{:S(2)}, u32[]{:S(2)}) collective-permute-start(bf16[4,64,1408]{2,1,0:T(8,128)(2,1)} %copy-done.19), channel_id=1, source_target_pairs={{0,1},{1,0},{2,3},{3,2},{4,5},{5,4},{6,7},{7,6},{8,9},{9,8},{10,11... | collective-permute-start | bytes 2162696 | tf_op jit(solution)/shard_map/ppermute | solution.py:56
  228.7 19.5 %collective-permute-start.42 = (bf16[4,64,1408]{2,1,0:T(8,128)(2,1)}, bf16[4,64,1408]{2,1,0:T(8,128)(2,1)S(1)}, u32[]{:S(2)}, u32[]{:S(2)}) collective-permute-start(bf16[4,64,1408]{2,1,0:T(8,128)(2,1)} %collective-permute-done.28.refs_1_.refs_9_), channel_id=1, source_target_pairs={{0,1},{1,0},{2,3},{3,2},{4,5},{5,4},{6,7},{7,6},{8,9},{9,8},{10,11... | collective-permute-start | bytes 2162696 | tf_op jit(solution)/shard_map/ppermute | solution.py:56
  229.2 19.1 %collective-permute-start.43 = (bf16[4,64,1408]{2,1,0:T(8,128)(2,1)}, bf16[4,64,1408]{2,1,0:T(8,128)(2,1)S(1)}, u32[]{:S(2)}, u32[]{:S(2)}) collective-permute-start(bf16[4,64,1408]{2,1,0:T(8,128)(2,1)} %collective-permute-done.29.refs_2_.refs_10_), channel_id=1, source_target_pairs={{0,1},{1,0},{2,3},{3,2},{4,5},{5,4},{6,7},{7,6},{8,9},{9,8},{10,11... | collective-permute-start | bytes 2162696 | tf_op jit(solution)/shard_map/ppermute | solution.py:56
  254.4 31.4 %all-to-all-start.2 = ((bf16[4,128,2048]{2,1,0:T(8,128)(2,1)}), bf16[4,128,2048]{2,1,0:T(8,128)(2,1)S(1)}, u32[]{:S(2)}, u32[]{:S(2)}) async-start(bf16[4,128,2048]{2,1,0:T(8,128)(2,1)} %broadcast_in_dim.21), calls=%async_computation.2 | async-start | bytes 4194304 | tf_op jit(solution)/shard_map/all_to_all | solution.py:108
  260.8 18.1 %collective-permute-start.50 = (bf16[4,64,1408]{2,1,0:T(8,128)(2,1)}, bf16[4,64,1408]{2,1,0:T(8,128)(2,1)S(1)}, u32[]{:S(2)}, u32[]{:S(2)}) collective-permute-start(bf16[4,64,1408]{2,1,0:T(8,128)(2,1)} %get-tuple-element.235.refs_0_), channel_id=1, source_target_pairs={{0,1},{1,0},{2,3},{3,2},{4,5},{5,4},{6,7},{7,6},{8,9},{9,8},{10,11... | collective-permute-start | bytes 2162696 | tf_op jit(solution)/shard_map/ppermute | solution.py:56
  261.3 17.6 %collective-permute-start.52 = (bf16[4,64,1408]{2,1,0:T(8,128)(2,1)}, bf16[4,64,1408]{2,1,0:T(8,128)(2,1)S(1)}, u32[]{:S(2)}, u32[]{:S(2)}) collective-permute-start(bf16[4,64,1408]{2,1,0:T(8,128)(2,1)} %copy-done.29), channel_id=1, source_target_pairs={{0,1},{1,0},{2,3},{3,2},{4,5},{5,4},{6,7},{7,6},{8,9},{9,8},{10,11... | collective-permute-start | bytes 2162696 | tf_op jit(solution)/shard_map/ppermute | solution.py:56
  261.4 17.5 %collective-permute-start.51 = (bf16[4,64,1408]{2,1,0:T(8,128)(2,1)}, bf16[4,64,1408]{2,1,0:T(8,128)(2,1)S(1)}, u32[]{:S(2)}, u32[]{:S(2)}) collective-permute-start(bf16[4,64,1408]{2,1,0:T(8,128)(2,1)} %copy-done.30), channel_id=1, source_target_pairs={{0,1},{1,0},{2,3},{3,2},{4,5},{5,4},{6,7},{7,6},{8,9},{9,8},{10,11... | collective-permute-start | bytes 2162696 | tf_op jit(solution)/shard_map/ppermute | solution.py:56
  261.8 18.3 %collective-permute-start.48 = (bf16[4,64,1408]{2,1,0:T(8,128)(2,1)}, bf16[4,64,1408]{2,1,0:T(8,128)(2,1)S(1)}, u32[]{:S(2)}, u32[]{:S(2)}) collective-permute-start(bf16[4,64,1408]{2,1,0:T(8,128)(2,1)} %copy-done.30), channel_id=1, source_target_pairs={{0,16},{16,0},{1,17},{17,1},{2,18},{18,2},{3,19},{19,3},{4,20},{20... | collective-permute-start | bytes 2162696 | tf_op jit(solution)/shard_map/ppermute | solution.py:56
  307.9 35.3 %all-to-all-start.3 = ((bf16[4,128,2048]{2,1,0:T(8,128)(2,1)}), bf16[4,128,2048]{2,1,0:T(8,128)(2,1)}, u32[]{:S(2)}, u32[]{:S(2)}) async-start(bf16[4,128,2048]{2,1,0:T(8,128)(2,1)} %bitcast.290), calls=%async_computation.3 | async-start | bytes 4194304 | tf_op jit(solution)/shard_map/all_to_all | solution.py:112
  312.4 228.4 %reduce-scatter.2.cloned.1.call-start = ((), (), s32[]{:S(2)}) async-start(), calls=%async_computation.8 | async-start | bytes 12976128 | tf_op jit(solution)/shard_map/reduce_scatter | solution.py:656
  336.4 9.1 %collective-permute-start.54 = (bf16[1024,1408]{1,0:T(8,128)(2,1)}, bf16[1024,1408]{1,0:T(8,128)(2,1)}, u32[]{:S(2)}, u32[]{:S(2)}) collective-permute-start(bf16[1024,1408]{1,0:T(8,128)(2,1)} %get-tuple-element.268), channel_id=1, source_target_pairs={{0,1},{1,0},{2,3},{3,2},{4,5},{5,4},{6,7},{7,6},{8,9},{9,8},{10,11... | collective-permute-start | bytes 8650760 | tf_op jit(solution)/shard_map/ppermute | solution.py:56
  346.1 16.4 %collective-permute-start.55 = (bf16[128,2048]{1,0:T(8,128)(2,1)S(1)}, bf16[128,2048]{1,0:T(8,128)(2,1)S(1)}, u32[]{:S(2)}, u32[]{:S(2)}) collective-permute-start(bf16[128,2048]{1,0:T(8,128)(2,1)S(1)} %fusion.54), channel_id=1, source_target_pairs={{0,2},{2,0},{1,3},{3,1},{4,6},{6,4},{5,7},{7,5},{8,10},{10,8},{9,1... | collective-permute-start | bytes 1572872 | tf_op jit(solution)/shard_map/ppermute | solution.py:56
  363.3 52.7 %all-to-all-start.4 = ((bf16[4,128,2048]{2,1,0:T(8,128)(2,1)}), bf16[4,128,2048]{2,1,0:T(8,128)(2,1)}, u32[]{:S(2)}, u32[]{:S(2)}) async-start(bf16[4,128,2048]{2,1,0:T(8,128)(2,1)} %bitcast.269), calls=%async_computation.4 | async-start | bytes 4194304 | tf_op jit(solution)/shard_map/all_to_all | solution.py:112
  392.1 13.2 %collective-permute-start.60 = (bf16[2,1,2,128,256]{4,3,2,1,0:T(8,128)(2,1)S(1)}, bf16[2,1,2,128,256]{4,3,2,1,0:T(8,128)(2,1)S(1)}, u32[]{:S(2)}, u32[]{:S(2)}) collective-permute-start(bf16[2,1,2,128,256]{4,3,2,1,0:T(8,128)(2,1)S(1)} %slice.549), channel_id=1, source_target_pairs={{0,2},{2,0},{1,3},{3,1},{4,6},{6,4},{5,7},{7,5},{8,10},{10,8},{9,1... | collective-permute-start | bytes 786440 | tf_op jit(solution)/shard_map/ppermute | solution.py:56
  394.2 9.2 %collective-permute-start.61 = (bf16[256,1024]{1,0:T(8,128)(2,1)S(1)}, bf16[256,1024]{1,0:T(8,128)(2,1)S(1)}, u32[]{:S(2)}, u32[]{:S(2)}) collective-permute-start(bf16[256,1024]{1,0:T(8,128)(2,1)S(1)} %get-tuple-element.370), channel_id=1, source_target_pairs={{0,1},{1,0},{2,3},{3,2},{4,5},{5,4},{6,7},{7,6},{8,9},{9,8},{10,11... | collective-permute-start | bytes 1572872 | tf_op jit(solution)/shard_map/ppermute | solution.py:56
  394.3 10.8 %collective-permute-start.64 = (bf16[256,1024]{1,0:T(8,128)(2,1)S(1)}, bf16[256,1024]{1,0:T(8,128)(2,1)S(1)}, u32[]{:S(2)}, u32[]{:S(2)}) collective-permute-start(bf16[256,1024]{1,0:T(8,128)(2,1)S(1)} %get-tuple-element.371), channel_id=1, source_target_pairs={{0,1},{1,0},{2,3},{3,2},{4,5},{5,4},{6,7},{7,6},{8,9},{9,8},{10,11... | collective-permute-start | bytes 1572872 | tf_op jit(solution)/shard_map/ppermute | solution.py:56
  394.8 10.3 %collective-permute-start.63 = (bf16[256,1024]{1,0:T(8,128)(2,1)S(1)}, bf16[256,1024]{1,0:T(8,128)(2,1)S(1)}, u32[]{:S(2)}, u32[]{:S(2)}) collective-permute-start(bf16[256,1024]{1,0:T(8,128)(2,1)S(1)} %get-tuple-element.372), channel_id=1, source_target_pairs={{0,1},{1,0},{2,3},{3,2},{4,5},{5,4},{6,7},{7,6},{8,9},{9,8},{10,11... | collective-permute-start | bytes 1572872 | tf_op jit(solution)/shard_map/ppermute | solution.py:56
  394.9 10.3 %collective-permute-start.62 = (bf16[256,1024]{1,0:T(8,128)(2,1)S(1)}, bf16[256,1024]{1,0:T(8,128)(2,1)S(1)}, u32[]{:S(2)}, u32[]{:S(2)}) collective-permute-start(bf16[256,1024]{1,0:T(8,128)(2,1)S(1)} %get-tuple-element.373), channel_id=1, source_target_pairs={{0,1},{1,0},{2,3},{3,2},{4,5},{5,4},{6,7},{7,6},{8,9},{9,8},{10,11... | collective-permute-start | bytes 1572872 | tf_op jit(solution)/shard_map/ppermute | solution.py:56
  403.4 25.3 %collective-permute-start.68 = (bf16[256,1408]{1,0:T(8,128)(2,1)}, bf16[256,1408]{1,0:T(8,128)(2,1)S(1)}, u32[]{:S(2)}, u32[]{:S(2)}) collective-permute-start(bf16[256,1408]{1,0:T(8,128)(2,1)} %add_convert_fusion.3), channel_id=1, source_target_pairs={{0,16},{16,0},{1,17},{17,1},{2,18},{18,2},{3,19},{19,3},{4,20},{20... | collective-permute-start | bytes 2162696 | tf_op jit(solution)/shard_map/ppermute | solution.py:56
  406.1 15.5 %collective-permute-start.65 = (bf16[1,2,128,256]{3,2,1,0:T(8,128)(2,1)}, bf16[1,2,128,256]{3,2,1,0:T(8,128)(2,1)}, u32[]{:S(2)}, u32[]{:S(2)}) collective-permute-start(bf16[1,2,128,256]{3,2,1,0:T(8,128)(2,1)} %fusion.35), channel_id=1, source_target_pairs={{0,4},{4,0},{1,5},{5,1},{2,6},{6,2},{3,7},{7,3},{8,12},{12,8},{9,1... | collective-permute-start | bytes 393224 | tf_op jit(solution)/shard_map/ppermute | solution.py:56
  421.6 13.9 %collective-permute-start.67 = (bf16[128,2048]{1,0:T(8,128)(2,1)S(1)}, bf16[128,2048]{1,0:T(8,128)(2,1)S(1)}, u32[]{:S(2)}, u32[]{:S(2)}) collective-permute-start(bf16[128,2048]{1,0:T(8,128)(2,1)S(1)} %slice.547), channel_id=1, source_target_pairs={{0,2},{2,0},{1,3},{3,1},{4,6},{6,4},{5,7},{7,5},{8,10},{10,8},{9,1... | collective-permute-start | bytes 1572872 | tf_op jit(solution)/shard_map/ppermute | solution.py:56
  424.1 8.0 %collective-permute-start.66 = (bf16[1,128,256]{2,1,0:T(8,128)(2,1)S(1)}, bf16[1,128,256]{2,1,0:T(8,128)(2,1)S(1)}, u32[]{:S(2)}, u32[]{:S(2)}) collective-permute-start(bf16[1,128,256]{2,1,0:T(8,128)(2,1)S(1)} %fusion.39), channel_id=1, source_target_pairs={{0,8},{8,0},{1,9},{9,1},{2,10},{10,2},{3,11},{11,3},{4,12},{12,4},... | collective-permute-start | bytes 196616 | tf_op jit(solution)/shard_map/ppermute | solution.py:56
  428.7 38.8 %collective-permute-start.73 = (bf16[2,2,1,2,64,1024]{5,4,1,0,3,2:T(8,128)(2,1)}, bf16[2,2,1,2,64,1024]{5,4,1,0,3,2:T(8,128)(2,1)}, u32[]{:S(2)}, u32[]{:S(2)}) collective-permute-start(bf16[2,2,1,2,64,1024]{5,4,1,0,3,2:T(8,128)(2,1)} %fusion.22), channel_id=1, source_target_pairs={{0,4},{4,0},{1,5},{5,1},{2,6},{6,2},{3,7},{7,3},{8,12},{12,8},{9,1... | collective-permute-start | bytes 3145736 | tf_op jit(solution)/shard_map/ppermute | solution.py:56
  449.1 28.7 %collective-permute-start.76 = (bf16[256,1408]{1,0:T(8,128)(2,1)}, bf16[256,1408]{1,0:T(8,128)(2,1)}, u32[]{:S(2)}, u32[]{:S(2)}) collective-permute-start(bf16[256,1408]{1,0:T(8,128)(2,1)} %get-tuple-element.365), channel_id=1, source_target_pairs={{0,16},{16,0},{1,17},{17,1},{2,18},{18,2},{3,19},{19,3},{4,20},{20... | collective-permute-start | bytes 2162696 | tf_op jit(solution)/shard_map/ppermute | solution.py:56
  470.0 14.2 %collective-permute-start.75 = (bf16[2,2,1,64,1024]{4,3,1,0,2:T(8,128)(2,1)}, bf16[2,2,1,64,1024]{4,3,1,0,2:T(8,128)(2,1)}, u32[]{:S(2)}, u32[]{:S(2)}) collective-permute-start(bf16[2,2,1,64,1024]{4,3,1,0,2:T(8,128)(2,1)} %fusion.27), channel_id=1, source_target_pairs={{0,2},{2,0},{1,3},{3,1},{4,6},{6,4},{5,7},{7,5},{8,10},{10,8},{9,1... | collective-permute-start | bytes 1572872 | tf_op jit(solution)/shard_map/ppermute | solution.py:56
  474.8 45.8 %collective-permute-start.74 = (bf16[2,2,1,2,64,1408]{5,4,1,0,3,2:T(8,128)(2,1)}, bf16[2,2,1,2,64,1408]{5,4,1,0,3,2:T(8,128)(2,1)}, u32[]{:S(2)}, u32[]{:S(2)}) collective-permute-start(bf16[2,2,1,2,64,1408]{5,4,1,0,3,2:T(8,128)(2,1)} %fusion.8), channel_id=1, source_target_pairs={{0,4},{4,0},{1,5},{5,1},{2,6},{6,2},{3,7},{7,3},{8,12},{12,8},{9,1... | collective-permute-start | bytes 4325384 | tf_op jit(solution)/shard_map/ppermute | solution.py:56
  489.1 13.3 %collective-permute-start.77 = (bf16[2,1,64,2048]{3,2,0,1:T(8,128)(2,1)}, bf16[2,1,64,2048]{3,2,0,1:T(8,128)(2,1)}, u32[]{:S(2)}, u32[]{:S(2)}) collective-permute-start(bf16[2,1,64,2048]{3,2,0,1:T(8,128)(2,1)} %convert_element_type.356), channel_id=1, source_target_pairs={{0,16},{16,0},{1,17},{17,1},{2,18},{18,2},{3,19},{19,3},{4,20},{20... | collective-permute-start | bytes 1572872 | tf_op jit(solution)/shard_map/ppermute | solution.py:56
  492.1 35.7 %collective-permute-start.80 = (bf16[256,1408]{1,0:T(8,128)(2,1)}, bf16[256,1408]{1,0:T(8,128)(2,1)S(1)}, u32[]{:S(2)}, u32[]{:S(2)}) collective-permute-start(bf16[256,1408]{1,0:T(8,128)(2,1)} %get-tuple-element.364), channel_id=1, source_target_pairs={{0,8},{8,0},{1,9},{9,1},{2,10},{10,2},{3,11},{11,3},{4,12},{12,4},... | collective-permute-start | bytes 2162696 | tf_op jit(solution)/shard_map/ppermute | solution.py:56
  523.2 17.5 %collective-permute-start.78 = (bf16[2,2,1,64,1408]{4,3,1,0,2:T(8,128)(2,1)S(1)}, bf16[2,2,1,64,1408]{4,3,1,0,2:T(8,128)(2,1)}, u32[]{:S(2)}, u32[]{:S(2)}) collective-permute-start(bf16[2,2,1,64,1408]{4,3,1,0,2:T(8,128)(2,1)S(1)} %fusion.23), channel_id=1, source_target_pairs={{0,2},{2,0},{1,3},{3,1},{4,6},{6,4},{5,7},{7,5},{8,10},{10,8},{9,1... | collective-permute-start | bytes 2162696 | tf_op jit(solution)/shard_map/ppermute | solution.py:56
  526.7 13.2 %collective-permute-start.79 = (bf16[1,64,2048]{2,1,0:T(8,128)(2,1)S(1)}, bf16[1,64,2048]{2,1,0:T(8,128)(2,1)}, u32[]{:S(2)}, u32[]{:S(2)}) collective-permute-start(bf16[1,64,2048]{2,1,0:T(8,128)(2,1)S(1)} %fusion.31), channel_id=1, source_target_pairs={{0,8},{8,0},{1,9},{9,1},{2,10},{10,2},{3,11},{11,3},{4,12},{12,4},... | collective-permute-start | bytes 786440 | tf_op jit(solution)/shard_map/ppermute | solution.py:56
  543.7 16.0 %collective-permute-start.81 = (bf16[2,1,64,2432]{3,2,0,1:T(8,128)(2,1)}, bf16[2,1,64,2432]{3,2,0,1:T(8,128)(2,1)}, u32[]{:S(2)}, u32[]{:S(2)}) collective-permute-start(bf16[2,1,64,2432]{3,2,0,1:T(8,128)(2,1)} %fusion.24), channel_id=1, source_target_pairs={{0,16},{16,0},{1,17},{17,1},{2,18},{18,2},{3,19},{19,3},{4,20},{20... | collective-permute-start | bytes 1867784 | tf_op jit(solution)/shard_map/ppermute | solution.py:56
  547.8 25.2 %all-to-all-start.5 = ((bf16[4,2,64,1408]{3,2,1,0:T(8,128)(2,1)}), bf16[4,2,64,1408]{3,2,1,0:T(8,128)(2,1)S(1)}, u32[]{:S(2)}, u32[]{:S(2)}) async-start(bf16[4,2,64,1408]{3,2,1,0:T(8,128)(2,1)} %bitcast.272), calls=%async_computation.6 | async-start | bytes 2883584 | tf_op jit(solution)/shard_map/all_to_all | solution.py:783
  561.6 15.2 %collective-permute-start.82 = (bf16[1,64,2432]{2,1,0:T(8,128)(2,1)}, bf16[1,64,2432]{2,1,0:T(8,128)(2,1)}, u32[]{:S(2)}, u32[]{:S(2)}) collective-permute-start(bf16[1,64,2432]{2,1,0:T(8,128)(2,1)} %fusion.30), channel_id=1, source_target_pairs={{0,8},{8,0},{1,9},{9,1},{2,10},{10,2},{3,11},{11,3},{4,12},{12,4},... | collective-permute-start | bytes 933896 | tf_op jit(solution)/shard_map/ppermute | solution.py:56
  573.0 15.0 %all-to-all-start.6 = ((bf16[4,1,64,1408]{3,2,1,0:T(8,128)(2,1)}), bf16[4,1,64,1408]{3,2,1,0:T(8,128)(2,1)S(1)}, u32[]{:S(2)}, u32[]{:S(2)}) async-start(bf16[4,1,64,1408]{3,2,1,0:T(8,128)(2,1)} %bitcast.143), calls=%async_computation.7 | async-start | bytes 1441792 | tf_op jit(solution)/shard_map/all_to_all | solution.py:783
  (115 other events, 929.6 us)
Sparse Core Ops, SparseCore 0:
  339.6 137.0 reduce-scatter.1
